TPU v7x, 32 devices: a whole 2x2x4 slice. The times are simulated.
32 devices in a mesh: dp: 8 (over z, y), fsdp: 4 (over x, core).
Axes of the slice: x: 2, y: 2, z: 4, core: 2. Of those that a mesh axis runs over, the one named last changes fastest.
Arguments:
- tokens: bfloat16 [32768, 512], P(('dp', 'fsdp')), may hold values from -6 to 6
- first_gain: bfloat16 [512], P('fsdp'), may hold values from 0.5 to 1.5
- first_shift: bfloat16 [512], P('fsdp'), may hold values from -4 to 4
- w_query: bfloat16 [512, 512], P('fsdp'), may hold values from -0.375 to 0.375
- w_key: bfloat16 [512, 512], P('fsdp'), may hold values from -0.375 to 0.375
- w_value: bfloat16 [512, 512], P('fsdp'), may hold values from -0.25 to 0.25
- w_control: bfloat16 [512, 512], P('fsdp'), may hold values from -0.625 to 0.625
- w_output: bfloat16 [512, 512], P('fsdp'), may hold values from -0.375 to 0.375
- second_gain: bfloat16 [512], P('fsdp'), may hold values from 0.5 to 1.5
- second_shift: bfloat16 [512], P('fsdp'), may hold values from -4 to 4
- w_inner: bfloat16 [512, 2048], P('fsdp'), may hold values from -0.25 to 0.25
- inner_bias: bfloat16 [2048], P('fsdp'), may hold values from -4 to 4
- w_outer: bfloat16 [2048, 512], P('fsdp'), may hold values from -0.1875 to 0.1875
- outer_bias: bfloat16 [512], P('fsdp'), may hold values from -4 to 4
- cotangent: bfloat16 [32768, 512], P(('dp', 'fsdp')), may hold values from -6 to 6
Outputs:
- output: bfloat16 [32768, 512], P(('dp', 'fsdp'))
- grad_tokens: bfloat16 [32768, 512], P(('dp', 'fsdp'))
- grad_first_gain: float32 [512], P('fsdp')
- grad_first_shift: float32 [512], P('fsdp')
- grad_w_query: float32 [512, 512], P('fsdp')
- grad_w_key: float32 [512, 512], P('fsdp')
- grad_w_value: float32 [512, 512], P('fsdp')
- grad_w_control: float32 [512, 512], P('fsdp')
- grad_w_output: float32 [512, 512], P('fsdp')
- grad_second_gain: float32 [512], P('fsdp')
- grad_second_shift: float32 [512], P('fsdp')
- grad_w_inner: float32 [512, 2048], P('fsdp')
- grad_inner_bias: float32 [2048], P('fsdp')
- grad_w_outer: float32 [2048, 512], P('fsdp')
- grad_outer_bias: float32 [512], P('fsdp')
All inputs are finite; a program needn't handle non-finite values.
Results may differ from a plain program's by a relative error of at most 0.022.
Values may be sent and summed in bfloat16 or wider, within the bound.
No kernel may reach another device: no remote copies, remote signals or barrier semaphores. Data moves between devices by JAX's collectives and lax.ppermute only.
A program may use at most 128 MiB of HBM per device.

v0:
```python
import jax
import jax.numpy as jnp
from jax import lax
from jax.sharding import PartitionSpec as P

D = 512
HEAD = 64
SLOTS = 64
LEN = 1024


EPSILON = 1e-05


def normalize(values):
    average = jnp.mean(values, axis=-1, keepdims=True)
    centred = values - average
    inv_scale = lax.rsqrt(jnp.mean(centred * centred, axis=-1, keepdims=True) + EPSILON)
    return (centred * inv_scale, inv_scale)


def norm_back(grad_normed, normed, inv_scale):
    first_mean = jnp.mean(grad_normed, axis=-1, keepdims=True)
    second_mean = jnp.mean(grad_normed * normed, axis=-1, keepdims=True)
    return inv_scale * (grad_normed - first_mean - normed * second_mean)


def causal_mask(length):
    row_index = lax.broadcasted_iota(jnp.int32, (length, length), 0)
    col_index = lax.broadcasted_iota(jnp.int32, (length, length), 1)
    return row_index >= col_index


def to_items(array, item_width):
    row_count = array.shape[0]
    return (
        array.reshape(row_count // LEN, LEN, -1, item_width)
        .transpose(0, 2, 1, 3)
        .reshape(-1, LEN, item_width)
    )


def from_items(array, row_count):
    item_width = array.shape[-1]
    return (
        array.reshape(row_count // LEN, -1, LEN, item_width)
        .transpose(0, 2, 1, 3)
        .reshape(row_count, -1)
    )


def head_forward(queries, keys, control):
    causal = causal_mask(queries.shape[0])
    nothing = jnp.zeros((), jnp.bfloat16)
    raw_scores = jnp.einsum("td,sd->ts", queries, keys, preferred_element_type=jnp.float32)
    scores = jnp.where(causal, raw_scores.astype(jnp.bfloat16), nothing)
    numerator = jnp.dot(scores, control, preferred_element_type=jnp.float32)
    denominator = jnp.dot(causal.astype(jnp.bfloat16), control, preferred_element_type=jnp.float32)
    logits = numerator / denominator * queries.shape[1] ** (-0.5)
    probabilities = jax.nn.softmax(logits, axis=-1)
    weights = (probabilities / denominator).astype(jnp.bfloat16)
    raw_mixing = jnp.einsum("tm,sm->ts", weights, control, preferred_element_type=jnp.float32)
    mixing = jnp.where(causal, raw_mixing.astype(jnp.bfloat16), nothing)
    return (causal, scores, denominator, logits, probabilities, weights, mixing)


def head_output(packed):
    queries, keys, values, control = packed
    mixing = head_forward(queries, keys, control)[6]
    return jnp.dot(mixing, values, preferred_element_type=jnp.float32)


def head_backward(packed):
    queries, keys, values, control, grad_out = packed
    causal, scores, denominator, logits, probabilities, weights, mixing = head_forward(
        queries, keys, control
    )
    raw_mixing = jnp.einsum("td,sd->ts", grad_out, values, preferred_element_type=jnp.float32)
    grad_mixing = jnp.where(causal, raw_mixing, 0.0).astype(jnp.bfloat16)
    grad_values = jnp.einsum("ts,td->sd", mixing, grad_out, preferred_element_type=jnp.float32)
    grad_weights = jnp.dot(grad_mixing, control, preferred_element_type=jnp.float32)
    grad_control = jnp.einsum("ts,tm->sm", grad_mixing, weights, preferred_element_type=jnp.float32)
    grad_probs = grad_weights / denominator
    grad_denominator = -grad_weights * probabilities / (denominator * denominator)
    grad_logits = probabilities * (
        grad_probs - jnp.sum(grad_probs * probabilities, axis=-1, keepdims=True)
    )
    grad_numerator = (grad_logits * queries.shape[1] ** (-0.5) / denominator).astype(jnp.bfloat16)
    grad_denominator = grad_denominator - grad_logits * logits / denominator
    raw_scores = jnp.einsum(
        "tm,sm->ts", grad_numerator, control, preferred_element_type=jnp.float32
    )
    grad_scores = jnp.where(causal, raw_scores, 0.0).astype(jnp.bfloat16)
    grad_control = grad_control + jnp.einsum(
        "ts,tm->sm", scores, grad_numerator, preferred_element_type=jnp.float32
    )
    grad_control = grad_control + jnp.einsum(
        "ts,tm->sm", causal.astype(jnp.float32), grad_denominator, precision=lax.Precision.HIGHEST
    )
    grad_queries = jnp.dot(grad_scores, keys, preferred_element_type=jnp.float32)
    grad_keys = jnp.einsum("ts,td->sd", grad_scores, queries, preferred_element_type=jnp.float32)
    return (grad_queries, grad_keys, grad_values, grad_control)


def per_device(
    tokens,
    first_gain,
    first_shift,
    w_query,
    w_key,
    w_value,
    w_control,
    w_output,
    second_gain,
    second_shift,
    w_inner,
    inner_bias,
    w_outer,
    outer_bias,
    cotangent,
):
    gathered = (
        lax.all_gather(first_gain, "fsdp", axis=0, tiled=True),
        lax.all_gather(first_shift, "fsdp", axis=0, tiled=True),
        lax.all_gather(w_query, "fsdp", axis=0, tiled=True),
        lax.all_gather(w_key, "fsdp", axis=0, tiled=True),
        lax.all_gather(w_value, "fsdp", axis=0, tiled=True),
        lax.all_gather(w_control, "fsdp", axis=0, tiled=True),
        lax.all_gather(w_output, "fsdp", axis=0, tiled=True),
        lax.all_gather(second_gain, "fsdp", axis=0, tiled=True),
        lax.all_gather(second_shift, "fsdp", axis=0, tiled=True),
        lax.all_gather(w_inner, "fsdp", axis=0, tiled=True),
        lax.all_gather(inner_bias, "fsdp", axis=0, tiled=True),
        lax.all_gather(w_outer, "fsdp", axis=0, tiled=True),
        lax.all_gather(outer_bias, "fsdp", axis=0, tiled=True),
    )
    (
        gain_one,
        shift_one,
        query_full,
        key_full,
        value_full,
        control_full,
        output_full,
        gain_two,
        shift_two,
        inner_full,
        inner_shift,
        outer_full,
        outer_shift,
    ) = gathered
    row_count = tokens.shape[0]
    tokens_f = tokens.astype(jnp.float32)
    normed_one, scale_one = normalize(tokens_f)
    hidden_one = (normed_one * gain_one.astype(jnp.float32) + shift_one.astype(jnp.float32)).astype(
        jnp.bfloat16
    )
    project_all = jnp.concatenate((query_full, key_full, value_full, control_full), axis=1)
    projected = jnp.dot(hidden_one, project_all, preferred_element_type=jnp.float32)
    queries = projected[:, :D].astype(jnp.bfloat16)
    keys = projected[:, D : 2 * D].astype(jnp.bfloat16)
    values = projected[:, 2 * D : 3 * D].astype(jnp.bfloat16)
    control_exp = jnp.exp(projected[:, 3 * D :])
    control = control_exp.astype(jnp.bfloat16)
    query_items = to_items(queries, HEAD)
    key_items = to_items(keys, HEAD)
    value_items = to_items(values, HEAD)
    control_items = to_items(control, SLOTS)
    heads_out = lax.map(head_output, (query_items, key_items, value_items, control_items))
    mixed = from_items(heads_out, row_count).astype(jnp.bfloat16)
    resid = tokens_f + jnp.dot(mixed, output_full, preferred_element_type=jnp.float32)
    normed_two, scale_two = normalize(resid)
    hidden_two = (normed_two * gain_two.astype(jnp.float32) + shift_two.astype(jnp.float32)).astype(
        jnp.bfloat16
    )
    inner = jnp.dot(
        hidden_two, inner_full, preferred_element_type=jnp.float32
    ) + inner_shift.astype(jnp.float32)
    activated, gelu_back = jax.vjp(jax.nn.gelu, inner)
    act_low = activated.astype(jnp.bfloat16)
    result = (
        resid
        + jnp.dot(act_low, outer_full, preferred_element_type=jnp.float32)
        + outer_shift.astype(jnp.float32)
    )
    output = result.astype(jnp.bfloat16)
    regathered = (
        lax.all_gather(first_gain, "fsdp", axis=0, tiled=True),
        lax.all_gather(w_query, "fsdp", axis=0, tiled=True),
        lax.all_gather(w_key, "fsdp", axis=0, tiled=True),
        lax.all_gather(w_value, "fsdp", axis=0, tiled=True),
        lax.all_gather(w_control, "fsdp", axis=0, tiled=True),
        lax.all_gather(w_output, "fsdp", axis=0, tiled=True),
        lax.all_gather(second_gain, "fsdp", axis=0, tiled=True),
        lax.all_gather(w_inner, "fsdp", axis=0, tiled=True),
        lax.all_gather(w_outer, "fsdp", axis=0, tiled=True),
    )
    (
        gain_one,
        query_full,
        key_full,
        value_full,
        control_full,
        output_full,
        gain_two,
        inner_full,
        outer_full,
    ) = regathered
    project_all = jnp.concatenate((query_full, key_full, value_full, control_full), axis=1)
    grad_result = cotangent.astype(jnp.float32)
    grad_outer_shift = jnp.sum(grad_result, axis=0)
    grad_outer = jnp.einsum("tf,td->fd", act_low, cotangent, preferred_element_type=jnp.float32)
    grad_act = jnp.einsum("td,fd->tf", cotangent, outer_full, preferred_element_type=jnp.float32)
    grad_inner = gelu_back(grad_act)[0].astype(jnp.bfloat16)
    grad_inner_shift = jnp.sum(grad_inner.astype(jnp.float32), axis=0)
    grad_inner_full = jnp.einsum(
        "td,tf->df", hidden_two, grad_inner, preferred_element_type=jnp.float32
    )
    grad_hidden_two = jnp.einsum(
        "tf,df->td", grad_inner, inner_full, preferred_element_type=jnp.float32
    )
    grad_gain_two = jnp.sum(grad_hidden_two * normed_two, axis=0)
    grad_shift_two = jnp.sum(grad_hidden_two, axis=0)
    grad_resid = grad_result + norm_back(
        grad_hidden_two * gain_two.astype(jnp.float32), normed_two, scale_two
    )
    grad_attn = grad_resid.astype(jnp.bfloat16)
    grad_output_full = jnp.einsum("td,te->de", mixed, grad_attn, preferred_element_type=jnp.float32)
    grad_mixed = jnp.einsum(
        "te,de->td", grad_attn, output_full, preferred_element_type=jnp.float32
    ).astype(jnp.bfloat16)
    head_grads = lax.map(
        head_backward,
        (query_items, key_items, value_items, control_items, to_items(grad_mixed, HEAD)),
    )
    grad_project = jnp.concatenate(
        (
            from_items(head_grads[0], row_count),
            from_items(head_grads[1], row_count),
            from_items(head_grads[2], row_count),
            from_items(head_grads[3], row_count) * control_exp,
        ),
        axis=1,
    ).astype(jnp.bfloat16)
    grad_project_all = jnp.einsum(
        "td,tc->dc", hidden_one, grad_project, preferred_element_type=jnp.float32
    )
    grad_hidden_one = jnp.einsum(
        "tc,dc->td", grad_project, project_all, preferred_element_type=jnp.float32
    )
    grad_gain_one = jnp.sum(grad_hidden_one * normed_one, axis=0)
    grad_shift_one = jnp.sum(grad_hidden_one, axis=0)
    grad_inputs = grad_resid + norm_back(
        grad_hidden_one * gain_one.astype(jnp.float32), normed_one, scale_one
    )
    grad_tokens = grad_inputs.astype(jnp.bfloat16)
    grad_query_full = grad_project_all[:, :D]
    grad_key_full = grad_project_all[:, D : 2 * D]
    grad_value_full = grad_project_all[:, 2 * D : 3 * D]
    grad_control_full = grad_project_all[:, 3 * D :]
    reduced = tuple(
        lax.psum(
            (
                lax.psum_scatter(
                    grad_gain_one.astype(jnp.bfloat16), "fsdp", scatter_dimension=0, tiled=True
                ).astype(jnp.float32),
                lax.psum_scatter(
                    grad_shift_one.astype(jnp.bfloat16), "fsdp", scatter_dimension=0, tiled=True
                ).astype(jnp.float32),
                lax.psum_scatter(
                    grad_query_full.astype(jnp.bfloat16), "fsdp", scatter_dimension=0, tiled=True
                ).astype(jnp.float32),
                lax.psum_scatter(
                    grad_key_full.astype(jnp.bfloat16), "fsdp", scatter_dimension=0, tiled=True
                ).astype(jnp.float32),
                lax.psum_scatter(
                    grad_value_full.astype(jnp.bfloat16), "fsdp", scatter_dimension=0, tiled=True
                ).astype(jnp.float32),
                lax.psum_scatter(
                    grad_control_full.astype(jnp.bfloat16), "fsdp", scatter_dimension=0, tiled=True
                ).astype(jnp.float32),
                lax.psum_scatter(
                    grad_output_full.astype(jnp.bfloat16), "fsdp", scatter_dimension=0, tiled=True
                ).astype(jnp.float32),
                lax.psum_scatter(
                    grad_gain_two.astype(jnp.bfloat16), "fsdp", scatter_dimension=0, tiled=True
                ).astype(jnp.float32),
                lax.psum_scatter(
                    grad_shift_two.astype(jnp.bfloat16), "fsdp", scatter_dimension=0, tiled=True
                ).astype(jnp.float32),
                lax.psum_scatter(
                    grad_inner_full.astype(jnp.bfloat16), "fsdp", scatter_dimension=0, tiled=True
                ).astype(jnp.float32),
                lax.psum_scatter(
                    grad_inner_shift.astype(jnp.bfloat16), "fsdp", scatter_dimension=0, tiled=True
                ).astype(jnp.float32),
                lax.psum_scatter(
                    grad_outer.astype(jnp.bfloat16), "fsdp", scatter_dimension=0, tiled=True
                ).astype(jnp.float32),
                lax.psum_scatter(
                    grad_outer_shift.astype(jnp.bfloat16), "fsdp", scatter_dimension=0, tiled=True
                ).astype(jnp.float32),
            ),
            "dp",
        )
    )
    return (output, grad_tokens) + reduced


def solution(mesh):
    return jax.shard_map(
        per_device,
        mesh=mesh,
        in_specs=(
            P(("dp", "fsdp"), None),
            P("fsdp"),
            P("fsdp"),
            P("fsdp", None),
            P("fsdp", None),
            P("fsdp", None),
            P("fsdp", None),
            P("fsdp", None),
            P("fsdp"),
            P("fsdp"),
            P("fsdp", None),
            P("fsdp"),
            P("fsdp", None),
            P("fsdp"),
            P(("dp", "fsdp"), None),
        ),
        out_specs=(
            P(("dp", "fsdp"), None),
            P(("dp", "fsdp"), None),
            P("fsdp"),
            P("fsdp"),
            P("fsdp", None),
            P("fsdp", None),
            P("fsdp", None),
            P("fsdp", None),
            P("fsdp", None),
            P("fsdp"),
            P("fsdp"),
            P("fsdp", None),
            P("fsdp"),
            P("fsdp", None),
            P("fsdp"),
        ),
        check_vma=False,
    )
```

profile of v0, /device:TPU:0, one launch (start us, length us, event | category | flops | bytes accessed | tf_op | source)
XLA Modules:
  0.0 698.2 jit_solution(9187283005854391818)
XLA Ops:
  10.0 6.0 all-gather
  16.0 8.6 %all_gather.50 = bf16[512,512]{1,0:T(8,128)(2,1)S(1)} all-gather(bf16[128,512]{1,0:T(8,128)(2,1)S(1)} %copy-done.11), channel_id=1, replica_groups=mesh['dp'=8,'fsdp'=4] {'fsdp'}, dimensions={0}, use_global_device_ids=true | all-gather | bytes 655360 | tf_op jit(solution)/shard_map/all_gather | solution.py:125
  24.7 12.0 %all_gather.51 = bf16[512,512]{1,0:T(8,128)(2,1)S(1)} all-gather(bf16[128,512]{1,0:T(8,128)(2,1)S(1)} %copy-done.12), channel_id=1, replica_groups=mesh['dp'=8,'fsdp'=4] {'fsdp'}, dimensions={0}, use_global_device_ids=true | all-gather | bytes 655360 | tf_op jit(solution)/shard_map/all_gather | solution.py:126
  36.6 7.3 %all_gather.52 = bf16[512,512]{1,0:T(8,128)(2,1)S(1)} all-gather(bf16[128,512]{1,0:T(8,128)(2,1)S(1)} %copy-done.13), channel_id=1, replica_groups=mesh['dp'=8,'fsdp'=4] {'fsdp'}, dimensions={0}, use_global_device_ids=true | all-gather | bytes 655360 | tf_op jit(solution)/shard_map/all_gather | solution.py:127
  44.0 7.3 %all_gather.53 = bf16[512,512]{1,0:T(8,128)(2,1)S(1)} all-gather(bf16[128,512]{1,0:T(8,128)(2,1)S(1)} %copy-done.14), channel_id=1, replica_groups=mesh['dp'=8,'fsdp'=4] {'fsdp'}, dimensions={0}, use_global_device_ids=true | all-gather | bytes 655360 | tf_op jit(solution)/shard_map/all_gather | solution.py:128
  51.3 6.0 all-gather.1
  57.5 5.8 fusion.169
  81.1 54.1 %while.28 = (s32[]{:T(128)}, bf16[8,1024,64]{1,2,0:T(8,128)(2,1)S(1)}, bf16[8,1024,64]{2,1,0:T(8,128)(2,1)}, bf16[8,1024,64]{2,1,0:T(8,128)(2,1)}, bf16[8,1024,64]{2,1,0:T(8,128)(2,1)}, /*index=5*/bf16[8,1024,64]{2,1,0:T(8,128)(2,1)}) while((s32[]{:T(128)}, bf16[8,1024,64]{1,2,0:T(8,128)(2,1)S(1)}, bf16[8,1024,64]{2,1,0:T(8,128)(2,1)}, ...), condition=%wide.region_5.6_spmd.clone, body=%wide.region_2.5_spmd.sunk.clone | while | flops 679016448 | bytes 3432005 | solution.py:169
  137.2 5.0 all-gather.2
  142.3 5.2 all-gather.4
  147.5 5.0 all-gather.3
  154.8 7.5 %all_gather.54 = bf16[512,512]{1,0:T(8,128)(2,1)S(1)} all-gather(bf16[128,512]{1,0:T(8,128)(2,1)S(1)} %copy-done.15), channel_id=1, replica_groups=mesh['dp'=8,'fsdp'=4] {'fsdp'}, dimensions={0}, use_global_device_ids=true | all-gather | bytes 655360 | tf_op jit(solution)/shard_map/all_gather | solution.py:129
  164.9 9.5 %multiply_convert_fusion = (bf16[1024,2048]{1,0:T(8,128)(2,1)}, f32[1024,2048]{1,0:T(8,128)}) fusion(f32[2048]{0:T(1024)S(1)} %bitcast.286, bf16[512,2048]{1,0:T(8,128)(2,1)} %all-gather.9.cloned.1.call-done, f32[1024,512]{0,1:T(8,128)S(1)} %get-tuple-element.264, f32[512]{0:T(512)S(1)} %bitcast.288, f32[512]{0:T(512)S(1)} %bitcast.282, ...), kind=kOutput, calls=%fused_computation.120 | convolution fusion | flops 2171076608 | bytes 16797696 | tf_op jit(solution)/shard_map/dot_general | solution.py:176
  174.3 10.2 %fusion.173 = (bf16[2048]{0:T(1024)(128)(2,1)S(1)}, bf16[1024,2048]{1,0:T(8,128)(2,1)S(1)}) fusion(f32[1024,2048]{1,0:T(8,128)} %get-tuple-element.266, f32[2048]{0:T(1024)S(1)} %bitcast.287, bf16[1024,512]{1,0:T(8,128)(2,1)} %param.33, bf16[2048,512]{1,0:T(8,128)(2,1)} %all-gather.11.cloned.1.call-done), kind=kOutput, calls=%fused_computation.191 | convolution fusion | flops 2193618944 | bytes 15740928 | tf_op jit(solution)/shard_map/td,fd->tf/dot_general | solution.py:213
  184.6 3.7 fusion.172
  200.5 3.0 copy.86
  203.5 164.3 %while.29 = (s32[]{:T(128)}, bf16[8,1024,64]{1,2,0:T(8,128)(2,1)}, bf16[8,1024,64]{1,2,0:T(8,128)(2,1)}, bf16[8,1024,64]{1,2,0:T(8,128)(2,1)}, f32[8,1024,64]{1,...) while((s32[]{:T(128)}, bf16[8,1024,64]{1,2,0:T(8,128)(2,1)}, ...), condition=%wide.region_14.15_spmd.clone, body=%wide.region_10.0_spmd.sunk.clone | while | flops 2432758784 | bytes 28893284 | solution.py:232
  367.8 2.9 copy.91
  370.7 3.7 multiply_convert_fusion.1
  381.3 4.6 convolution_convert_fusion.2
  389.5 6.7 convolution_convert_fusion.1
  396.3 6.3 convolution_convert_fusion
  405.9 5.0 all-gather.5
  411.0 6.6 fusion.171
  417.6 3.0 copy.95
  427.1 5.3 add_convert_fusion
  433.8 7.3 %all-reduce.7 = (bf16[512]{0:T(512)(128)(2,1)S(1)}, bf16[512]{0:T(512)(128)(2,1)S(1)}, bf16[512]{0:T(512)(128)(2,1)S(1)}, bf16[512]{0:T(512)(128)(2,1)S(1)}, bf1...) all-reduce(bf16[512]{0:T(512)(128)(2,1)S(1)} %get-tuple-element.186, ...), channel_id=2, replica_groups=mesh['dp'=8,'fsdp'=4] {'fsdp'}, use_global_device_ids=true, to_apply=%region_18.19.clone | all-reduce | flops 4608 | bytes 18432
  441.6 17.3 %reduce-scatter.12.cloned.1.call-done = bf16[128,512]{1,0:T(8,128)(2,1)} async-done(((bf16[512,512]{1,0:T(8,128)(2,1)}), bf16[128,512]{1,0:T(8,128)(2,1)}) %reduce-scatter.12.cloned.1.call-update) | async-done | bytes 131088 | tf_op jit(solution)/shard_map/reduce_scatter | solution.py:276
  458.9 24.2 %reduce-scatter.14.cloned.1.call-done = bf16[128,512]{1,0:T(8,128)(2,1)} async-done(((bf16[512,512]{1,0:T(8,128)(2,1)}), bf16[128,512]{1,0:T(8,128)(2,1)}) %reduce-scatter.14.cloned.1.call-update) | async-done | bytes 131088 | tf_op jit(solution)/shard_map/reduce_scatter | solution.py:279
  483.1 34.2 %reduce-scatter.18.cloned.1.call-done = bf16[128,2048]{1,0:T(8,128)(2,1)} async-done(((bf16[512,2048]{1,0:T(8,128)(2,1)}), bf16[128,2048]{1,0:T(8,128)(2,1)}) %reduce-scatter.18.cloned.1.call-update) | async-done | bytes 524304 | tf_op jit(solution)/shard_map/reduce_scatter | solution.py:291
  517.3 34.0 %reduce-scatter.20.cloned.1.call-done = bf16[512,512]{1,0:T(8,128)(2,1)} async-done(((bf16[2048,512]{1,0:T(8,128)(2,1)}), bf16[512,512]{1,0:T(8,128)(2,1)}) %reduce-scatter.20.cloned.1.call-update) | async-done | bytes 524304 | tf_op jit(solution)/shard_map/reduce_scatter | solution.py:297
  551.3 140.0 %all-reduce.9 = (f32[128]{0:T(128)}, f32[128]{0:T(128)}, f32[128,512]{1,0:T(8,128)}, f32[128,512]{1,0:T(8,128)}, f32[128,512]{1,0:T(8,128)}, /*index=5*/f32[128,...) all-reduce(f32[128]{0:T(128)S(1)} %dynamic-slice_convert_fusion.5, ...), channel_id=1, replica_groups=mesh['dp'=8,'fsdp'=4] {'dp'}, use_global_device_ids=true, to_apply=%region_19.20 | all-reduce | flops 853120 | bytes 5121024 | tf_op jit(solution)/shard_map/psum | solution.py:262
  (277 shorter events, 278.1 us)
Async XLA Ops:
  7.2 1.7 copy-start.10
  7.2 157.7 %all-gather.9.cloned.1.call-start = ((), (), s32[]{:S(2)}) async-start(), calls=%async_computation.7 | async-start | bytes 2621440 | tf_op jit(solution)/shard_map/all_gather | solution.py:132
  7.9 166.4 %all-gather.11.cloned.1.call-start = ((), (), s32[]{:S(2)}) async-start(), calls=%async_computation.8 | async-start | bytes 2621440 | tf_op jit(solution)/shard_map/all_gather | solution.py:134
  8.7 432.9 %reduce-scatter.16.cloned.1.call-start = ((), (), s32[]{:S(2)}) async-start(), calls=%async_computation.13 | async-start | bytes 655360 | tf_op jit(solution)/shard_map/reduce_scatter | solution.py:282
  8.9 127.4 %copy-start.2 = (bf16[8,1024,64]{1,2,0:T(8,128)(2,1)}, bf16[8,1024,64]{1,2,0:T(8,128)(2,1)S(1)}, u32[]{:S(2)}) copy-start(bf16[8,1024,64]{1,2,0:T(8,128)(2,1)S(1)} %fusion.168) | copy-start | bytes 3145732
  8.9 7.1 %copy-start.11 = (bf16[128,512]{1,0:T(8,128)(2,1)S(1)}, bf16[128,512]{1,0:T(8,128)(2,1)}, u32[]{:S(2)}) copy-start(bf16[128,512]{1,0:T(8,128)(2,1)} %param.22) | copy-start | bytes 393220
  9.4 15.2 %copy-start.12 = (bf16[128,512]{1,0:T(8,128)(2,1)S(1)}, bf16[128,512]{1,0:T(8,128)(2,1)}, u32[]{:S(2)}) copy-start(bf16[128,512]{1,0:T(8,128)(2,1)} %param.23) | copy-start | bytes 393220
  9.4 27.2 %copy-start.13 = (bf16[128,512]{1,0:T(8,128)(2,1)S(1)}, bf16[128,512]{1,0:T(8,128)(2,1)}, u32[]{:S(2)}) copy-start(bf16[128,512]{1,0:T(8,128)(2,1)} %param.24) | copy-start | bytes 393220
  9.6 34.4 %copy-start.14 = (bf16[128,512]{1,0:T(8,128)(2,1)S(1)}, bf16[128,512]{1,0:T(8,128)(2,1)}, u32[]{:S(2)}) copy-start(bf16[128,512]{1,0:T(8,128)(2,1)} %param.25) | copy-start | bytes 393220
  10.0 41.3 %copy-start.18 = (bf16[128]{0:T(256)(128)(2,1)S(1)}, bf16[128]{0:T(256)(128)(2,1)}, u32[]{:S(2)}) copy-start(bf16[128]{0:T(256)(128)(2,1)} %param.21) | copy-start | bytes 772
  57.5 5.8 copy-start.9
  135.2 2.0 copy-start.5
  135.2 2.0 copy-start.19
  135.2 7.0 %copy-start.16 = (bf16[512]{0:T(512)(128)(2,1)S(1)}, bf16[512]{0:T(512)(128)(2,1)}, u32[]{:S(2)}) copy-start(bf16[512]{0:T(512)(128)(2,1)} %param.30) | copy-start | bytes 3076
  135.2 12.2 %copy-start.20 = (bf16[128]{0:T(256)(128)(2,1)S(1)}, bf16[128]{0:T(256)(128)(2,1)}, u32[]{:S(2)}) copy-start(bf16[128]{0:T(256)(128)(2,1)} %param.28) | copy-start | bytes 772
  136.2 18.5 %copy-start.15 = (bf16[128,512]{1,0:T(8,128)(2,1)S(1)}, bf16[128,512]{1,0:T(8,128)(2,1)}, u32[]{:S(2)}) copy-start(bf16[128,512]{1,0:T(8,128)(2,1)} %param.26) | copy-start | bytes 393220
  162.3 2.2 copy-start.7
  164.5 26.7 %copy-start = (f32[1024,512]{0,1:T(8,128)}, f32[1024,512]{0,1:T(8,128)S(1)}, u32[]{:S(2)}) copy-start(f32[1024,512]{0,1:T(8,128)S(1)} %get-tuple-element.264) | copy-start | bytes 6291460
  174.3 10.3 %copy-start.22 = (bf16[512,2048]{1,0:T(8,128)(2,1)S(1)}, bf16[512,2048]{1,0:T(8,128)(2,1)}, u32[]{:S(2)}) copy-start(bf16[512,2048]{1,0:T(8,128)(2,1)} %all-gather.9.cloned.1.call-done) | copy-start | bytes 6291460
  184.6 3.7 copy-start.24
  191.3 2.5 copy-start.4
  191.3 2.5 copy-start.8
  193.7 2.4 copy-start.6
  200.5 241.1 %reduce-scatter.8.cloned.1.call-start = ((), (), s32[]{:S(2)}) async-start(), calls=%async_computation.9 | async-start | bytes 655360 | tf_op jit(solution)/shard_map/reduce_scatter | solution.py:270
  387.3 54.3 %reduce-scatter.10.cloned.1.call-start = ((), (), s32[]{:S(2)}) async-start(), calls=%async_computation.10 | async-start | bytes 655360 | tf_op jit(solution)/shard_map/reduce_scatter | solution.py:273
  387.9 71.0 %reduce-scatter.12.cloned.1.call-start = ((), (), s32[]{:S(2)}) async-start(), calls=%async_computation.11 | async-start | bytes 655360 | tf_op jit(solution)/shard_map/reduce_scatter | solution.py:276
  388.5 94.6 %reduce-scatter.14.cloned.1.call-start = ((), (), s32[]{:S(2)}) async-start(), calls=%async_computation.12 | async-start | bytes 655360 | tf_op jit(solution)/shard_map/reduce_scatter | solution.py:279
  389.2 128.1 %reduce-scatter.18.cloned.1.call-start = ((), (), s32[]{:S(2)}) async-start(), calls=%async_computation.14 | async-start | bytes 2621440 | tf_op jit(solution)/shard_map/reduce_scatter | solution.py:291
  396.2 155.0 %reduce-scatter.20.cloned.1.call-start = ((), (), s32[]{:S(2)}) async-start(), calls=%async_computation.15 | async-start | bytes 2621440 | tf_op jit(solution)/shard_map/reduce_scatter | solution.py:297
  402.5 3.4 copy-start.21
  420.5 2.5 copy-start.3
  424.7 2.4 copy-start.1
  (2 other events, 2.6 us)
Sparse Core Ops, SparseCore 0:
  9.6 28.7 all-gather.8
  39.9 23.9 all-gather.10
  200.6 23.2 reduce-scatter.15
  387.4 23.2 reduce-scatter.7
  413.1 21.6 reduce-scatter.9
  437.2 21.6 reduce-scatter.11
  461.4 21.6 reduce-scatter.13
  485.8 31.4 reduce-scatter.17
  519.8 31.4 reduce-scatter.19
where the time goes:
time: 710 us; the launch traced here: 698 us
  matrix products  281 us (40%)
  blocking collectives  222 us (31%)
  waiting for transfers between devices  113 us (16%)
  local copies, waits for them, and re-layouts  44.4 us (6%)
  other arithmetic  20.3 us (3%)
  between operations  16 us (2%)
    psum x1, blocking collectives, per_device(): lax.psum((lax.psum_scatter(grad_gain_one.astype(jnp.bfloat16), 'fsdp', sc...  140 us
    reduce_scatter x1, waiting for transfers between devices, per_device(): lax.psum_scatter(grad_inner_full.astype(jnp.bfloat16), 'fsdp', scatter_di...  34.2 us
    reduce_scatter x1, waiting for transfers between devices, per_device(): lax.psum_scatter(grad_outer.astype(jnp.bfloat16), 'fsdp', scatter_dimensi...  34 us
    dot_general x16, matrix products, head_forward(): numerator = jnp.dot(scores, control, preferred_element_type=jnp.float32)  31.9 us
    dot_general x16, matrix products, head_forward(): jnp.dot(causal.astype(jnp.bfloat16), control, preferred_element_type=jnp....  29.5 us
    reduce_scatter x1, waiting for transfers between devices, per_device(): lax.psum_scatter(grad_control_full.astype(jnp.bfloat16), 'fsdp', scatter_...  24.2 us
    dot_general x8, matrix products, head_backward(): jnp.einsum('ts,td->sd', mixing, grad_out, preferred_element_type=jnp.floa...  21.4 us
    dot_general x8, matrix products, head_backward(): jnp.dot(grad_scores, keys, preferred_element_type=jnp.float32)  19 us
  transfers between devices with their start and end apart: 9, of which 4 were waited for; matrix products, arithmetic and copies ran while one was open for 46% of the time, Pallas kernels for 0%

commit v1 on v0

v1 whole, which is shorter than its diff:
```python
import functools
import jax
import jax.numpy as jnp
from jax import lax
from jax.experimental import pallas as pl
from jax.experimental.pallas import tpu as pltpu
from jax.sharding import PartitionSpec as P

F32 = jnp.float32
BF16 = jnp.bfloat16
PAIR = 128
SCALE = 64 ** -0.5


def mm(a, b):
    return lax.dot_general(a, b, (((1,), (0,)), ((), ())), preferred_element_type=F32)


def mm_nt(a, b):
    return lax.dot_general(a, b, (((1,), (1,)), ((), ())), preferred_element_type=F32)


def mm_tn(a, b):
    return lax.dot_general(a, b, (((0,), (0,)), ((), ())), preferred_element_type=F32)


def left_half(rows):
    return lax.broadcasted_iota(jnp.int32, (rows, PAIR), 1) < 64


def split_pair(x, left):
    zero = jnp.zeros((), x.dtype)
    return jnp.concatenate((jnp.where(left, x, zero), jnp.where(left, zero, x)), axis=0)


def same_head():
    r = lax.broadcasted_iota(jnp.int32, (PAIR, PAIR), 0) < 64
    c = lax.broadcasted_iota(jnp.int32, (PAIR, PAIR), 1) < 64
    return r == c


def causal_pair(rows):
    r = lax.broadcasted_iota(jnp.int32, (rows, 2 * rows), 0)
    c = lax.broadcasted_iota(jnp.int32, (rows, 2 * rows), 1)
    return r >= jnp.where(c >= rows, c - rows, c)


def half_reduce(x, left, fn, fill):
    a = fn(jnp.where(left, x, fill), axis=1, keepdims=True)
    b = fn(jnp.where(left, fill, x), axis=1, keepdims=True)
    return jnp.where(left, a, b)


def forward_kernel(C, qkvf, mixed, a_out, b_out, s_out, p_out, rden_out, s1_out, s2_out, s1, s2, carry):
    c = pl.program_id(0)

    @pl.when(c == 0)
    def _():
        s1[...] = jnp.zeros_like(s1)
        s2[...] = jnp.zeros_like(s2)
        carry[...] = jnp.zeros_like(carry)

    left = left_half(C)
    causal = causal_pair(C)
    same = same_head()
    lower = (lax.broadcasted_iota(jnp.int32, (C, C), 0) >= lax.broadcasted_iota(jnp.int32, (C, C), 1)).astype(BF16)
    zero = jnp.zeros((), BF16)
    denom = mm(lower, qkvf[:, 1536:2048]) + carry[0:1, :]
    carry[0:1, :] = denom[C - 1 :, :]
    rden_all = 1.0 / denom
    rden_out[...] = rden_all
    for j in range(4):
        sl = slice(PAIR * j, PAIR * (j + 1))
        q = qkvf[:, PAIR * j : PAIR * (j + 1)]
        k = qkvf[:, 512 + PAIR * j : 512 + PAIR * (j + 1)]
        v = qkvf[:, 1024 + PAIR * j : 1024 + PAIR * (j + 1)]
        f = qkvf[:, 1536 + PAIR * j : 1536 + PAIR * (j + 1)]
        rden = rden_all[:, sl]
        f2 = split_pair(f, left)
        a2 = jnp.where(causal, mm_nt(q, split_pair(k, left)).astype(BF16), zero)
        a_out[:, 2 * C * j : 2 * C * (j + 1)] = a2
        s1b = s1[j].astype(BF16)
        s2b = s2[j].astype(BF16)
        s1_out[0, :, sl] = s1b
        s2_out[0, :, sl] = s2b
        numer = mm(a2, f2) + mm(q, s1b)
        s = numer * rden * SCALE
        s_out[:, sl] = s
        top = half_reduce(s, left, jnp.max, -jnp.inf)
        e = jnp.exp(s - top)
        p = e / half_reduce(e, left, jnp.sum, 0.0)
        p_out[:, sl] = p
        g = (p * rden).astype(BF16)
        b2 = jnp.where(causal, mm_nt(g, f2).astype(BF16), zero)
        b_out[:, 2 * C * j : 2 * C * (j + 1)] = b2
        o = mm(b2, split_pair(v, left)) + mm(g, s2b)
        mixed[:, sl] = o.astype(BF16)
        s1[j] += jnp.where(same, mm_tn(k, f), 0.0)
        s2[j] += jnp.where(same, mm_tn(f, v), 0.0)


def attention_forward(qkvf, C=128):
    T = qkvf.shape[0]
    n = T // C
    row = lambda w: pl.BlockSpec((C, w), lambda i: (i, 0))
    st = pl.BlockSpec((1, PAIR, 512), lambda i: (i, 0, 0))
    return pl.pallas_call(
        functools.partial(forward_kernel, C),
        grid=(n,),
        in_specs=[row(2048)],
        out_specs=[row(512), row(8 * C), row(8 * C), row(512), row(512), row(512), st, st],
        out_shape=[
            jax.ShapeDtypeStruct((T, 512), BF16),
            jax.ShapeDtypeStruct((T, 8 * C), BF16),
            jax.ShapeDtypeStruct((T, 8 * C), BF16),
            jax.ShapeDtypeStruct((T, 512), F32),
            jax.ShapeDtypeStruct((T, 512), F32),
            jax.ShapeDtypeStruct((T, 512), F32),
            jax.ShapeDtypeStruct((n, PAIR, 512), BF16),
            jax.ShapeDtypeStruct((n, PAIR, 512), BF16),
        ],
        scratch_shapes=[pltpu.VMEM((4, PAIR, PAIR), F32), pltpu.VMEM((4, PAIR, PAIR), F32), pltpu.VMEM((8, 512), F32)],
        compiler_params=pltpu.CompilerParams(vmem_limit_bytes=48 << 20),
        name="attention_forward",
    )(qkvf)


def backward_kernel(C, qkvf, a_in, b_in, s_in, p_in, rden_in, s1_in, s2_in, do_in, grad, r1, r2, carry):
    c = pl.program_id(0)

    @pl.when(c == 0)
    def _():
        r1[...] = jnp.zeros_like(r1)
        r2[...] = jnp.zeros_like(r2)
        carry[...] = jnp.zeros_like(carry)

    left = left_half(C)
    causal = causal_pair(C)
    same = same_head()
    upper = (lax.broadcasted_iota(jnp.int32, (C, C), 0) <= lax.broadcasted_iota(jnp.int32, (C, C), 1)).astype(BF16)
    upper2 = jnp.concatenate((upper, upper), axis=1)
    zero = jnp.zeros((), BF16)
    for j in range(4):
        sl = slice(PAIR * j, PAIR * (j + 1))
        sl2 = slice(2 * C * j, 2 * C * (j + 1))
        q = qkvf[:, PAIR * j : PAIR * (j + 1)]
        k = qkvf[:, 512 + PAIR * j : 512 + PAIR * (j + 1)]
        v = qkvf[:, 1024 + PAIR * j : 1024 + PAIR * (j + 1)]
        f = qkvf[:, 1536 + PAIR * j : 1536 + PAIR * (j + 1)]
        do = do_in[:, sl]
        a2 = a_in[:, sl2]
        b2 = b_in[:, sl2]
        s = s_in[:, sl]
        p = p_in[:, sl]
        rden = rden_in[:, sl]
        s1b = s1_in[0, :, sl]
        s2b = s2_in[0, :, sl]
        f2 = split_pair(f, left)
        g = (p * rden).astype(BF16)
        db2 = jnp.where(causal, mm_nt(do, split_pair(v, left)).astype(BF16), zero)
        dg = mm(db2, f2) + mm_nt(do, s2b)
        dp = dg * rden
        dpp = dp * p
        ds = dpp - p * half_reduce(dpp, left, jnp.sum, 0.0)
        ddenom = -(dpp + ds * s) * rden
        dn = (ds * SCALE * rden).astype(BF16)
        da2 = jnp.where(causal, mm_nt(dn, f2).astype(BF16), zero)
        r1b = r1[j].astype(BF16)
        r2b = r2[j].astype(BF16)
        dq = mm(da2, split_pair(k, left)) + mm_nt(dn, s1b)
        grad[:, PAIR * j : PAIR * (j + 1)] = dq.astype(BF16)
        dk2 = mm_tn(da2, q)
        dk = jnp.where(left, dk2[:C], dk2[C:]) + mm_nt(f, r1b)
        grad[:, 512 + PAIR * j : 512 + PAIR * (j + 1)] = dk.astype(BF16)
        dv2 = mm_tn(b2, do)
        dv = jnp.where(left, dv2[:C], dv2[C:]) + mm(f, r2b)
        grad[:, 1024 + PAIR * j : 1024 + PAIR * (j + 1)] = dv.astype(BF16)
        df2 = mm_tn(db2, g) + mm_tn(a2, dn)
        hi = ddenom.astype(BF16)
        lo = (ddenom - hi.astype(F32)).astype(BF16)
        df = jnp.where(left, df2[:C], df2[C:]) + mm_nt(v, r2b) + mm(k, r1b)
        df = df + mm(upper2, jnp.concatenate((hi, lo), axis=0)) + carry[0:1, sl]
        grad[:, 1536 + PAIR * j : 1536 + PAIR * (j + 1)] = (df * f.astype(F32)).astype(BF16)
        carry[0:1, sl] += jnp.sum(ddenom, axis=0, keepdims=True)
        r1[j] += jnp.where(same, mm_tn(q, dn), 0.0)
        r2[j] += jnp.where(same, mm_tn(g, do), 0.0)


def attention_backward(saved, d_o, C=128):
    qkvf, a, b, s, p, rden, s1, s2 = saved
    T = qkvf.shape[0]
    n = T // C
    row = lambda w: pl.BlockSpec((C, w), lambda i: (n - 1 - i, 0))
    st = pl.BlockSpec((1, PAIR, 512), lambda i: (n - 1 - i, 0, 0))
    return pl.pallas_call(
        functools.partial(backward_kernel, C),
        grid=(n,),
        in_specs=[row(2048), row(8 * C), row(8 * C), row(512), row(512), row(512), st, st, row(512)],
        out_specs=row(2048),
        out_shape=jax.ShapeDtypeStruct((T, 2048), BF16),
        scratch_shapes=[pltpu.VMEM((4, PAIR, PAIR), F32), pltpu.VMEM((4, PAIR, PAIR), F32), pltpu.VMEM((8, 512), F32)],
        compiler_params=pltpu.CompilerParams(vmem_limit_bytes=48 << 20),
        name="attention_backward",
    )(qkvf, a, b, s, p, rden, s1, s2, d_o)


EPS = 1e-5
MASKS = (0, 2, 1, 3)
ROWS = 256


def blocks_of(me):
    return [me ^ mask for mask in MASKS]


def take_blocks(ref, blocks, width):
    return jnp.concatenate([ref[:, pl.ds(pl.multiple_of(b * width, width), width)] for b in blocks], axis=1)


def put_blocks(ref, values, blocks, width):
    for i, b in enumerate(blocks):
        ref[:, pl.ds(pl.multiple_of(b * width, width), width)] = values[:, i * width : (i + 1) * width]


def stats(x):
    mean = jnp.mean(x, axis=1, keepdims=True)
    centred = x - mean
    inv = lax.rsqrt(jnp.mean(centred * centred, axis=1, keepdims=True) + EPS)
    return centred * inv, inv


def vector(refs, start, width):
    return jnp.concatenate([r[0:1, start : start + width] for r in refs], axis=1).astype(F32)


def project_kernel(me_ref, tokens, w0, w1, w2, w3, v0, v1, v2, v3, qkvf, n1_out, a1, scr):
    t = pl.program_id(0)

    @pl.when(t == 0)
    def _():
        blocks = blocks_of(me_ref[0])
        gain = vector((v0, v1, v2, v3), 0, 128)
        shift = vector((v0, v1, v2, v3), 128, 128)

        def chunk(c, carry):
            rows = pl.ds(pl.multiple_of(c * ROWS, ROWS), ROWS)
            n, _ = stats(tokens[rows, :].astype(F32))
            scr[...] = n
            n_rel = take_blocks(scr, blocks, 128)
            n1_out[rows, :] = n_rel.astype(BF16)
            a1[rows, :] = (n_rel * gain + shift).astype(BF16)
            return carry

        lax.fori_loop(0, tokens.shape[0] // ROWS, chunk, 0)

    w = jnp.concatenate((w0[...], w1[...], w2[...], w3[...]), axis=0)
    out = mm(a1[...], w)

    @pl.when(t < 6)
    def _():
        qkvf[...] = out.astype(BF16)

    @pl.when(t >= 6)
    def _():
        qkvf[...] = jnp.exp(out).astype(BF16)


SMEM = pl.BlockSpec(memory_space=pltpu.SMEM)


def whole(shape):
    return pl.BlockSpec(shape, lambda i: (0,) * len(shape))


def params():
    return pltpu.CompilerParams(vmem_limit_bytes=56 << 20)


VEC = pl.BlockSpec((16, 2048), lambda i: (8, 0))


def project(me, tokens, packs):
    T = tokens.shape[0]
    return pl.pallas_call(
        project_kernel,
        grid=(8,),
        in_specs=[SMEM, whole((T, 512))] + [pl.BlockSpec((128, 256), lambda t: (0, t))] * 4 + [VEC] * 4,
        out_specs=[pl.BlockSpec((T, 256), lambda t: (0, t)), whole((T, 512))],
        out_shape=[jax.ShapeDtypeStruct((T, 2048), BF16), jax.ShapeDtypeStruct((T, 512), BF16)],
        scratch_shapes=[pltpu.VMEM((T, 512), BF16), pltpu.VMEM((ROWS, 512), F32)],
        compiler_params=params(),
        name="project",
    )(me, tokens, *packs, *packs)


def gelu_parts(v):
    c = 0.7978845608028654
    v2 = v * v
    t = jnp.tanh(c * v * (1.0 + 0.044715 * v2))
    half = 0.5 * (1.0 + t)
    slope = half + 0.5 * v * (1.0 - t * t) * (c * (1.0 + 3 * 0.044715 * v2))
    return v * half, slope


def ffn_forward_kernel(me_ref, tokens, mixed, dy, o0, o1, o2, o3, i0, i1, i2, i3, u0, u1, u2, u3, v0, v1, v2, v3,
                       out, n2_out, r2_out, slope_out, keep, send, acc, scr, bias):
    c = pl.program_id(0)
    blocks = blocks_of(me_ref[0])
    vs = (v0, v1, v2, v3)

    @pl.when(c == 0)
    def _():
        acc[...] = jnp.zeros_like(acc)
        put_blocks(bias, jnp.broadcast_to(vector(vs, 512, 128), (8, 512)), blocks, 128)

    wo = jnp.concatenate((o0[...], o1[...], o2[...], o3[...]), axis=0)
    resid = tokens[...].astype(F32) + mm(take_blocks(mixed, blocks, 128), wo)
    n2, r2 = stats(resid)
    scr[...] = n2
    n2 = take_blocks(scr, blocks, 128)
    n2_out[...] = n2.astype(BF16)
    r2_out[...] = jnp.broadcast_to(r2, r2_out.shape)
    a2 = (n2 * vector(vs, 256, 128) + vector(vs, 384, 128)).astype(BF16)
    total = resid + bias[0:1, :]
    dyt = dy[...].T
    for i, (u, v) in enumerate(zip((u0, u1, u2, u3), vs)):
        cols = pl.ds(pl.multiple_of(blocks[i] * 512, 512), 512)
        w = jnp.concatenate((i0[:, cols], i1[:, cols], i2[:, cols], i3[:, cols]), axis=0)
        act, slope = gelu_parts(mm(a2, w) + v[0:1, 640:1152].astype(F32))
        act = act.astype(BF16)
        slope_out[:, 512 * i : 512 * (i + 1)] = slope.astype(BF16)
        total = total + mm(act, u[...])
        acc[i] += mm(dyt, act)
    out[...] = total.astype(BF16)

    @pl.when(c == pl.num_programs(0) - 1)
    def _():
        keep[...] = acc[0:2].astype(BF16)
        send[...] = acc[2:4].astype(BF16)


def ffn_forward(me, tokens, mixed, dy, wo, wi, wu, packs):
    T = tokens.shape[0]
    row = lambda w: pl.BlockSpec((ROWS, w), lambda i: (i, 0))
    S = jax.ShapeDtypeStruct
    return pl.pallas_call(
        ffn_forward_kernel,
        grid=(T // ROWS,),
        in_specs=[SMEM, row(512), row(512), row(512)] + [whole((128, 512))] * 4 + [whole((128, 2048))] * 4 + [whole((512, 512))] * 4 + [VEC] * 4,
        out_specs=[row(512), row(512), row(128), row(2048), whole((2, 512, 512)), whole((2, 512, 512))],
        out_shape=[S((T, 512), BF16), S((T, 512), BF16), S((T, 128), F32), S((T, 2048), BF16), S((2, 512, 512), BF16), S((2, 512, 512), BF16)],
        scratch_shapes=[pltpu.VMEM((4, 512, 512), F32), pltpu.VMEM((ROWS, 512), F32), pltpu.VMEM((8, 512), F32)],
        compiler_params=params(),
        name="ffn_forward",
    )(me, tokens, mixed, dy, *wo, *wi, *wu, *packs)


def ffn_backward_kernel(me_ref, dy_ref, n2_ref, r2_ref, slope, mixed, o0, o1, o2, o3, i0, i1, i2, i3, u0, u1, u2, u3, v0, v1, v2, v3,
                        dres_out, do_out, keep, send, keep_o, send_o, acc, acc_o, sums, scr):
    c = pl.program_id(0)
    blocks = blocks_of(me_ref[0])
    vs = (v0, v1, v2, v3)

    @pl.when(c == 0)
    def _():
        acc[...] = jnp.zeros_like(acc)
        acc_o[...] = jnp.zeros_like(acc_o)
        sums[...] = jnp.zeros_like(sums)

    dy = dy_ref[...]
    n2b = n2_ref[...]
    n2t = n2b.T
    da2 = jnp.zeros((ROWS, 512), F32)
    for i, u in enumerate((u0, u1, u2, u3)):
        cols = pl.ds(pl.multiple_of(blocks[i] * 512, 512), 512)
        w = jnp.concatenate((i0[:, cols], i1[:, cols], i2[:, cols], i3[:, cols]), axis=0)
        din = (mm_nt(dy, u[...]) * slope[:, 512 * i : 512 * (i + 1)].astype(F32)).astype(BF16)
        da2 = da2 + mm_nt(din, w)
        acc[:, cols] += mm(n2t, din)
        sums[0:1, cols] += jnp.sum(din.astype(F32), axis=0, keepdims=True)
    n2 = n2b.astype(F32)
    e = da2 * vector(vs, 256, 128)
    dn = r2_ref[:, 0:1] * (e - jnp.mean(e, axis=1, keepdims=True) - n2 * jnp.mean(e * n2, axis=1, keepdims=True))
    put_blocks(scr, dn, blocks, 128)
    dyf = dy.astype(F32)
    sums[1:2, 0:512] += jnp.sum(dyf, axis=0, keepdims=True)
    dres = dyf + scr[...]
    dres_out[...] = dres
    dattn = dres.astype(BF16)
    wo = jnp.concatenate((o0[...], o1[...], o2[...], o3[...]), axis=0)
    acc_o[...] += mm_tn(take_blocks(mixed, blocks, 128), dattn)
    put_blocks(do_out, mm_nt(dattn, wo).astype(BF16), blocks, 128)

    @pl.when(c == pl.num_programs(0) - 1)
    def _():
        tail = jnp.concatenate((sums[...], jnp.zeros_like(sums)), axis=0).astype(BF16)
        for i in range(2):
            keep[i, 0:128, :] = acc[128 * i : 128 * (i + 1), :].astype(BF16)
            send[i, 0:128, :] = acc[128 * (i + 2) : 128 * (i + 3), :].astype(BF16)
            keep[i, 128:144, :] = tail
            send[i, 128:144, :] = tail
            keep_o[i] = acc_o[128 * i : 128 * (i + 1), :].astype(BF16)
            send_o[i] = acc_o[128 * (i + 2) : 128 * (i + 3), :].astype(BF16)


def ffn_backward(me, dy, n2, r2, slope, mixed, wo, wi, wu, packs):
    T = dy.shape[0]
    row = lambda w: pl.BlockSpec((ROWS, w), lambda i: (i, 0))
    S = jax.ShapeDtypeStruct
    return pl.pallas_call(
        ffn_backward_kernel,
        grid=(T // ROWS,),
        in_specs=[SMEM, row(512), row(512), row(128), row(2048), row(512)]
        + [whole((128, 512))] * 4 + [whole((128, 2048))] * 4 + [whole((512, 512))] * 4 + [VEC] * 4,
        out_specs=[row(512), row(512), whole((2, 144, 2048)), whole((2, 144, 2048)), whole((2, 128, 512)), whole((2, 128, 512))],
        out_shape=[S((T, 512), F32), S((T, 512), BF16), S((2, 144, 2048), BF16), S((2, 144, 2048), BF16), S((2, 128, 512), BF16), S((2, 128, 512), BF16)],
        scratch_shapes=[pltpu.VMEM((512, 2048), F32), pltpu.VMEM((512, 512), F32), pltpu.VMEM((8, 2048), F32), pltpu.VMEM((ROWS, 512), F32)],
        compiler_params=params(),
        name="ffn_backward",
    )(me, dy, n2, r2, slope, mixed, *wo, *wi, *wu, *packs)


def project_grad_kernel(n1, d, keep, send, n1t):
    @pl.when(pl.program_id(0) == 0)
    def _():
        n1t[...] = n1[...].T

    dv = d[...]
    out = mm(n1t[...], dv).astype(BF16)
    total = jnp.sum(dv.astype(F32), axis=0, keepdims=True)
    tail = jnp.broadcast_to(total, (16, total.shape[1])).astype(BF16)
    for i in range(2):
        keep[i, 0:128, :] = out[128 * i : 128 * (i + 1)]
        send[i, 0:128, :] = out[128 * (i + 2) : 128 * (i + 3)]
        keep[i, 128:144, :] = tail
        send[i, 128:144, :] = tail


def project_grad(n1, d):
    T = n1.shape[0]
    spec = pl.BlockSpec((2, 144, 256), lambda t: (0, 0, t))
    S = jax.ShapeDtypeStruct((2, 144, 2048), BF16)
    return pl.pallas_call(
        project_grad_kernel,
        grid=(8,),
        in_specs=[whole((T, 512)), pl.BlockSpec((T, 256), lambda t: (0, t))],
        out_specs=[spec, spec],
        out_shape=[S, S],
        scratch_shapes=[pltpu.VMEM((512, T), BF16)],
        compiler_params=params(),
        name="project_grad",
    )(n1, d)


def input_grad_kernel(me_ref, tokens, d, dres, w0, w1, w2, w3, v0, v1, v2, v3, out, scr):
    blocks = blocks_of(me_ref[0])
    n, r = stats(tokens[...].astype(F32))
    scr[...] = n
    n = take_blocks(scr, blocks, 128)
    w = jnp.concatenate((w0[...], w1[...], w2[...], w3[...]), axis=0)
    e = mm_nt(d[...], w) * vector((v0, v1, v2, v3), 0, 128)
    dn = r * (e - jnp.mean(e, axis=1, keepdims=True) - n * jnp.mean(e * n, axis=1, keepdims=True))
    put_blocks(scr, dn, blocks, 128)
    out[...] = (dres[...] + scr[...]).astype(BF16)


def input_grad(me, tokens, d, dres, packs):
    T = tokens.shape[0]
    row = lambda w: pl.BlockSpec((ROWS, w), lambda i: (i, 0))
    return pl.pallas_call(
        input_grad_kernel,
        grid=(T // ROWS,),
        in_specs=[SMEM, row(512), row(2048), row(512)] + [whole((128, 2048))] * 4 + [VEC] * 4,
        out_specs=row(512),
        out_shape=jax.ShapeDtypeStruct((T, 512), BF16),
        scratch_shapes=[pltpu.VMEM((ROWS, 512), F32)],
        compiler_params=params(),
        name="input_grad",
    )(me, tokens, d, dres, *packs, *packs)


def add(a, b):
    return (a.astype(F32) + b.astype(F32)).astype(BF16)


def exchange(value, axis, size, mask):
    return lax.ppermute(value, axis, [(i, i ^ mask) for i in range(size)])


def gather(own):
    across = exchange(own, "fsdp", 4, 2)
    return own, across, exchange(own, "fsdp", 4, 1), exchange(across, "fsdp", 4, 1)


def reduce_to_owner(keep, send, dp):
    both = add(keep, exchange(send, "fsdp", 4, 1))
    part = add(both[0], exchange(both[1], "fsdp", 4, 2))
    odd = (lax.axis_index("dp") & 1) == 1
    half = part.shape[1] // 2
    low, high = part[:, :half], part[:, half:]
    part = add(jnp.where(odd, high, low), exchange(jnp.where(odd, low, high), "dp", dp, 1))
    mask = 2
    while mask < dp:
        part = add(part, exchange(part, "dp", dp, mask))
        mask *= 2
    other = exchange(part, "dp", dp, 1)
    return jnp.concatenate((jnp.where(odd, other, part), jnp.where(odd, part, other)), axis=1).astype(F32)


def per_device(dp, tokens, first_gain, first_shift, w_query, w_key, w_value, w_control, w_output, second_gain, second_shift, w_inner, inner_bias, w_outer, outer_bias, cotangent):
    me = lax.axis_index("fsdp").astype(jnp.int32)
    me_arr = me.reshape(1)
    vec = jnp.concatenate((first_gain, first_shift, second_gain, second_shift, outer_bias, inner_bias, jnp.zeros((896,), BF16)))
    own = jnp.concatenate((jnp.concatenate((w_query, w_key, w_value, w_control), axis=1), jnp.broadcast_to(vec, (16, 2048))), axis=0)
    packs = gather(own)
    wo = gather(w_output)
    wi = gather(w_inner)
    wu = gather(w_outer)
    qkvf, n1 = project(me_arr, tokens, packs)
    mixed, *saved = attention_forward(qkvf, ROWS)
    output, n2, r2, slope, keep_u, send_u = ffn_forward(me_arr, tokens, mixed, cotangent, wo, wi, wu, packs)
    dres, d_o, keep_i, send_i, keep_o, send_o = ffn_backward(me_arr, cotangent, n2, r2, slope, mixed, wo, wi, wu, packs)
    grad = attention_backward((qkvf, *saved), d_o, ROWS)
    keep_p, send_p = project_grad(n1, grad)
    grad_tokens = input_grad(me_arr, tokens, grad, dres, packs)
    sum_u = reduce_to_owner(keep_u, send_u, dp)
    sum_i = reduce_to_owner(keep_i, send_i, dp)
    sum_o = reduce_to_owner(keep_o, send_o, dp)
    sum_p = reduce_to_owner(keep_p, send_p, dp)
    f32 = lambda v: v.astype(F32)
    col = sum_i[128]
    grad_inner = f32(second_gain)[:, None] * sum_i[:128] + f32(second_shift)[:, None] * col
    grad_second_gain = jnp.sum(f32(w_inner) * sum_i[:128], axis=1)
    grad_second_shift = jnp.sum(f32(w_inner) * col, axis=1)
    grad_inner_bias = lax.dynamic_slice(col, (me * 512,), (512,))
    grad_outer_bias = lax.dynamic_slice(sum_i[129], (me * 128,), (128,))
    colp = sum_p[128]
    grad_p = f32(first_gain)[:, None] * sum_p[:128] + f32(first_shift)[:, None] * colp
    wp = f32(own[:128])
    grad_first_gain = jnp.sum(wp * sum_p[:128], axis=1)
    grad_first_shift = jnp.sum(wp * colp, axis=1)
    return (
        output, grad_tokens, grad_first_gain, grad_first_shift,
        grad_p[:, :512], grad_p[:, 512:1024], grad_p[:, 1024:1536], grad_p[:, 1536:],
        sum_o, grad_second_gain, grad_second_shift, grad_inner, grad_inner_bias, sum_u.T, grad_outer_bias,
    )


def solution(mesh):
    row, vec, mat = P(("dp", "fsdp"), None), P("fsdp"), P("fsdp", None)
    return jax.shard_map(
        functools.partial(per_device, mesh.shape["dp"]),
        mesh=mesh,
        in_specs=(row, vec, vec, mat, mat, mat, mat, mat, vec, vec, mat, vec, mat, vec, row),
        out_specs=(row, row, vec, vec, mat, mat, mat, mat, mat, vec, vec, mat, vec, mat, vec),
        check_vma=False,
    )
```

time: 710 us -> 281 us (0.40); the launches traced: 698 us -> 280 us
  matrix products: 281 us -> 0 us
  blocking collectives: 222 us -> 0 us
  Pallas kernels: 0 us -> 98.2 us
  starting transfers between devices: 0.6 us -> 33.1 us
  local copies, waits for them, and re-layouts: 44.4 us -> 18.3 us
  between operations: 16 us -> 1.14 us
  other arithmetic: 20.3 us -> 10.6 us
    dot_general x132 -> x0, matrix products: 281 us -> none  [the longest x16 31.9 us: head_forward(): numerator = jnp.dot(scores, control, preferred_element_type=jnp.float32)]
    psum x1 -> x0, blocking collectives: 140 us -> none  [per_device(): lax.psum((lax.psum_scatter(grad_gain_one.astype(jnp.bfloat16), 'fsdp', sc...]
    ppermute x0 -> x36, waiting for transfers between devices: none -> 119 us  [exchange(): return lax.ppermute(value, axis, [(i, i ^ mask) for i in range(size)])]
    reduce_scatter x7 -> x0, waiting for transfers between devices: 110 us -> none  [the longest x1 34.2 us: per_device(): lax.psum_scatter(grad_inner_full.astype(jnp.bfloat16), 'fsdp', scatter_di...]
    pallas_call x0 -> x7, Pallas kernels: none -> 98.2 us  [the longest x1 20.5 us: attention_backward(): pl.pallas_call(functools.partial(backward_kernel, C), grid=(n,), in_specs...]
    all_gather x11 -> x0, blocking collectives: 75 us -> none  [the longest x1 12 us: per_device(): lax.all_gather(w_key, 'fsdp', axis=0, tiled=True)]
    ppermute x0 -> x36, starting transfers between devices: none -> 33.1 us  [exchange(): return lax.ppermute(value, axis, [(i, i ^ mask) for i in range(size)])]
    reshape x5 -> x0, local copies, waits for them, and re-layouts: 12.7 us -> none  [the longest x4 9.76 us: from_items(): return array.reshape(row_count // LEN, -1, LEN, item_width).transpose(0,...]
  transfers between devices with their start and end apart: 9 -> 36, of which waited for: 4 -> 16; matrix products, arithmetic and copies ran while one was open for 46% -> 2% of each run, Pallas kernels for 0% -> 22%
where the time goes in v1:
time: 281 us; the launch traced here: 280 us
  waiting for transfers between devices  119 us (42%)
  Pallas kernels  98.2 us (35%)
  starting transfers between devices  33.1 us (12%)
  local copies, waits for them, and re-layouts  18.3 us (7%)
  other arithmetic  10.6 us (4%)
    ppermute x36, waiting for transfers between devices, exchange(): return lax.ppermute(value, axis, [(i, i ^ mask) for i in range(size)])  119 us
    ppermute x36, starting transfers between devices, exchange(): return lax.ppermute(value, axis, [(i, i ^ mask) for i in range(size)])  33.1 us
    pallas_call x1, Pallas kernels, attention_backward(): pl.pallas_call(functools.partial(backward_kernel, C), grid=(n,), in_specs...  20.5 us
    pallas_call x1, Pallas kernels, ffn_forward(): pl.pallas_call(ffn_forward_kernel, grid=(T // ROWS,), in_specs=[SMEM, row...  19.1 us
    pallas_call x1, Pallas kernels, ffn_backward(): pl.pallas_call(ffn_backward_kernel, grid=(T // ROWS,), in_specs=[SMEM, ro...  17.7 us
    unnamed x56, local copies, waits for them, and re-layouts  14.8 us
    pallas_call x1, Pallas kernels, attention_forward(): pl.pallas_call(functools.partial(forward_kernel, C), grid=(n,), in_specs=...  14.2 us
    pallas_call x1, Pallas kernels, project(): pl.pallas_call(project_kernel, grid=(8,), in_specs=[SMEM, whole((T, 512))...  10.4 us
  transfers between devices with their start and end apart: 36, of which 16 were waited for; matrix products, arithmetic and copies ran while one was open for 2% of the time, Pallas kernels for 22%

profile of v1, /device:TPU:0, one launch (start us, length us, event | category | flops | bytes accessed | tf_op | source)
XLA Modules:
  0.0 280.3 jit_solution(10231520595967010323)
XLA Ops:
  9.8 3.0 %collective-permute-start = (bf16[144,2048]{1,0:T(8,128)(2,1)S(1)}, bf16[144,2048]{1,0:T(8,128)(2,1)S(1)}, u32[]{:S(2)}, u32[]{:S(2)}) collective-permute-start(bf16[144,2048]{1,0:T(8,128)(2,1)S(1)} %pad_maximum_fusion.w0.v0), channel_id=1, source_target_pairs={{0,2},{1,3},{2,0},{3,1},{4,6},{5,7},{6,4},{7,5},{8,10},{9,11},{10,... | collective-permute-start | bytes 1769480 | tf_op jit(solution)/shard_map/ppermute | solution.py:487
  12.9 1.9 collective-permute-start.6
  14.8 12.1 %collective-permute-done.w1.v1 = bf16[144,2048]{1,0:T(8,128)(2,1)S(1)} collective-permute-done((bf16[144,2048]{1,0:T(8,128)(2,1)S(1)}, bf16[144,2048]{1,0:T(8,128)(2,1)S(1)}, u32[]{:S(2)}, u32[]{:S(2)}) %collective-permute-start) | collective-permute-done | bytes 589856 | tf_op jit(solution)/shard_map/ppermute | solution.py:487
  27.0 2.1 collective-permute-start.3
  29.1 22.4 %collective-permute-done.3.o1 = bf16[128,512]{1,0:T(8,128)(2,1)} collective-permute-done((bf16[128,512]{1,0:T(8,128)(2,1)S(1)}, bf16[128,512]{1,0:T(8,128)(2,1)}, u32[]{:S(2)}, u32[]{:S(2)}) %collective-permute-start.3) | collective-permute-done | bytes 131104 | tf_op jit(solution)/shard_map/ppermute | solution.py:487
  53.4 10.4 %project.1 = (bf16[1024,2048]{1,0:T(8,128)(2,1)}, bf16[1024,512]{1,0:T(8,128)(2,1)}) custom-call(s32[1]{0:T(128)} %bitcast.me_ref, bf16[1024,512]{1,0:T(8,128)(2,1)} %tokens.5, bf16[144,2048]{1,0:T(8,128)(2,1)} %copy-done.6, bf16[144,2048]{1,0:T(8,128)(2,1)} %copy-done.7, bf16[144,2048]{1,0:T(8,128)(2,1)} %copy-done.8, bf16[144,2048]{1,0:T(8,128)(2,1)} %copy-done.9, ...), custom_call_target="tpu_custom_call" | custom-call | tf_op jit(solution)/shard_map/project/pallas_call | solution.py:284
  63.8 14.2 %attention_forward.1 = (bf16[1024,512]{1,0:T(8,128)(2,1)S(1)}, bf16[1024,2048]{1,0:T(8,128)(2,1)}, bf16[1024,2048]{1,0:T(8,128)(2,1)}, f32[1024,512]{1,0:T(8,128...) custom-call(bf16[1024,2048]{1,0:T(8,128)(2,1)} %get-tuple-element.39, ...), custom_call_target="tpu_custom_call" | custom-call | tf_op jit(solution)/shard_map/attention_forward/pallas_call | solution.py:107
  81.2 19.1 %ffn_forward.1 = (bf16[1024,512]{1,0:T(8,128)(2,1)}, bf16[1024,512]{1,0:T(8,128)(2,1)}, f32[1024,128]{1,0:T(8,128)}, bf16[1024,2048]{1,0:T(8,128)(2,1)}, bf16[2,...) custom-call(s32[1]{0:T(128)} %bitcast.me_ref, bf16[1024,512]{1,0:T(8,128)(2,1)} %tokens.5, bf16[1024,512]{1,0:T(8,128)(2,1)} %copy-done, ...), custom_call_target="tpu_custom_call" | custom-call | tf_op jit(solution)/shard_map/ffn_forward/pallas_call | solution.py:346
  100.4 17.7 %ffn_backward.1 = (f32[1024,512]{1,0:T(8,128)}, bf16[1024,512]{1,0:T(8,128)(2,1)}, bf16[2,144,2048]{2,1,0:T(8,128)(2,1)}, bf16[2,144,2048]{2,1,0:T(8,128)(2,1)},...) custom-call(s32[1]{0:T(128)} %bitcast.me_ref, bf16[1024,512]{1,0:T(8,128)(2,1)} %dy_ref.1, ...), custom_call_target="tpu_custom_call" | custom-call | tf_op jit(solution)/shard_map/ffn_backward/pallas_call | solution.py:410
  121.6 1.9 collective-permute-start.19
  123.4 4.0 %collective-permute-done.19 = bf16[128,512]{1,0:T(8,128)(2,1)S(1)} collective-permute-done((bf16[128,512]{1,0:T(8,128)(2,1)}, bf16[128,512]{1,0:T(8,128)(2,1)S(1)}, u32[]{:S(2)}, u32[]{:S(2)}) %collective-permute-start.19) | collective-permute-done | bytes 131104 | tf_op jit(solution)/shard_map/ppermute | solution.py:487
  127.5 1.7 collective-permute-start.20
  129.2 2.6 collective-permute-done.20
  131.9 1.8 collective-permute-start.21
  133.6 2.5 collective-permute-done.21
  136.2 3.2 %collective-permute-start.22 = (bf16[128,256]{1,0:T(8,128)(2,1)S(1)}, bf16[128,256]{1,0:T(8,128)(2,1)S(1)}, u32[]{:S(2)}, u32[]{:S(2)}) collective-permute-start(bf16[128,256]{1,0:T(8,128)(2,1)S(1)} %add_convert_fusion.14), channel_id=1, source_target_pairs={{0,16},{4,20},{8,24},{12,28},{16,0},{20,4},{24,8},{28,12},{1,17},{... | collective-permute-start | bytes 196616 | tf_op jit(solution)/shard_map/ppermute | solution.py:487
  139.4 20.5 %attention_backward.1.d = bf16[1024,2048]{1,0:T(8,128)(2,1)} custom-call(bf16[1024,2048]{1,0:T(8,128)(2,1)} %get-tuple-element.39.qkvf, bf16[1024,2048]{1,0:T(8,128)(2,1)} %get-tuple-element.42.a_in, bf16[1024,2048]{1,0:T(8,128)(2,1)} %get-tuple-element.43.b_in, f32[1024,512]{1,0:T(8,128)S(1)} %get-tuple-element.44.s_in, ...), custom_call_target="tpu_custom_call" | custom-call | tf_op jit(solution)/shard_map/attention_backward/pallas_call | solution.py:195
  159.9 8.4 %project_grad.1 = (bf16[2,144,2048]{2,1,0:T(8,128)(2,1)}, bf16[2,144,2048]{2,1,0:T(8,128)(2,1)}) custom-call(bf16[1024,512]{1,0:T(8,128)(2,1)} %get-tuple-element.54.n1, bf16[1024,2048]{1,0:T(8,128)(2,1)} %attention_backward.1.d), custom_call_target="tpu_custom_call" | custom-call | tf_op jit(solution)/shard_map/project_grad/pallas_call | solution.py:443
  170.3 7.9 %input_grad.1 = bf16[1024,512]{1,0:T(8,128)(2,1)} custom-call(s32[1]{0:T(128)} %bitcast.me_ref, bf16[1024,512]{1,0:T(8,128)(2,1)} %tokens.5, bf16[1024,2048]{1,0:T(8,128)(2,1)} %attention_backward.1.d, f32[1024,512]{1,0:T(8,128)} %get-tuple-element.53.dres, bf16[144,2048]{1,0:T(8,128)(2,1)} %copy-done.6, bf16[144,2048]{1,0:T(8,128)(2,1)} %copy-done.7, ...), custom_call_target="tpu_custom_call" | custom-call | tf_op jit(solution)/shard_map/input_grad/pallas_call | solution.py:470
  180.6 1.7 collective-permute-start.31
  185.5 9.9 %collective-permute-done.31 = bf16[512,512]{1,0:T(8,128)(2,1)S(1)} collective-permute-done((bf16[512,512]{1,0:T(8,128)(2,1)S(1)}, bf16[512,512]{1,0:T(8,128)(2,1)S(1)}, u32[]{:S(2)}, u32[]{:S(2)}) %collective-permute-start.31) | collective-permute-done | bytes 524320 | tf_op jit(solution)/shard_map/ppermute | solution.py:487
  196.2 11.9 %collective-permute-done.13 = bf16[144,2048]{1,0:T(8,128)(2,1)S(1)} collective-permute-done((bf16[144,2048]{1,0:T(8,128)(2,1)S(1)}, bf16[144,2048]{1,0:T(8,128)(2,1)S(1)}, u32[]{:S(2)}, u32[]{:S(2)}) %collective-permute-start.13) | collective-permute-done | bytes 589856 | tf_op jit(solution)/shard_map/ppermute | solution.py:487
  210.2 9.9 %collective-permute-done.25 = bf16[144,2048]{1,0:T(8,128)(2,1)S(1)} collective-permute-done((bf16[144,2048]{1,0:T(8,128)(2,1)S(1)}, bf16[144,2048]{1,0:T(8,128)(2,1)S(1)}, u32[]{:S(2)}, u32[]{:S(2)}) %collective-permute-start.25) | collective-permute-done | bytes 589856 | tf_op jit(solution)/shard_map/ppermute | solution.py:487
  222.7 6.1 %collective-permute-done.26 = bf16[144,1024]{1,0:T(8,128)(2,1)S(1)} collective-permute-done((bf16[144,1024]{1,0:T(8,128)(2,1)S(1)}, bf16[144,1024]{1,0:T(8,128)(2,1)S(1)}, u32[]{:S(2)}, u32[]{:S(2)}) %collective-permute-start.26) | collective-permute-done | bytes 294944 | tf_op jit(solution)/shard_map/ppermute | solution.py:487
  230.1 4.9 %collective-permute-done.34 = bf16[512,256]{1,0:T(8,128)(2,1)S(1)} collective-permute-done((bf16[512,256]{1,0:T(8,128)(2,1)S(1)}, bf16[512,256]{1,0:T(8,128)(2,1)S(1)}, u32[]{:S(2)}, u32[]{:S(2)}) %collective-permute-start.34) | collective-permute-done | bytes 262176 | tf_op jit(solution)/shard_map/ppermute | solution.py:487
  236.8 2.0 collective-permute-start.16
  238.8 5.8 %collective-permute-done.27 = bf16[144,1024]{1,0:T(8,128)(2,1)S(1)} collective-permute-done((bf16[144,1024]{1,0:T(8,128)(2,1)S(1)}, bf16[144,1024]{1,0:T(8,128)(2,1)S(1)}, u32[]{:S(2)}, u32[]{:S(2)}) %collective-permute-start.27) | collective-permute-done | bytes 294944 | tf_op jit(solution)/shard_map/ppermute | solution.py:487
  245.1 15.0 %collective-permute-done.16 = bf16[144,1024]{1,0:T(8,128)(2,1)S(1)} collective-permute-done((bf16[144,1024]{1,0:T(8,128)(2,1)S(1)}, bf16[144,1024]{1,0:T(8,128)(2,1)S(1)}, u32[]{:S(2)}, u32[]{:S(2)}) %collective-permute-start.16) | collective-permute-done | bytes 294944 | tf_op jit(solution)/shard_map/ppermute | solution.py:487
  262.4 2.3 collective-permute-done.28
  265.3 2.8 collective-permute-done.17
  268.3 5.0 %collective-permute-done.29 = bf16[144,1024]{1,0:T(8,128)(2,1)S(1)} collective-permute-done((bf16[144,1024]{1,0:T(8,128)(2,1)S(1)}, bf16[144,1024]{1,0:T(8,128)(2,1)S(1)}, u32[]{:S(2)}, u32[]{:S(2)}) %collective-permute-start.29) | collective-permute-done | bytes 294944 | tf_op jit(solution)/shard_map/ppermute | solution.py:487
  277.3 3.0 %fusion.5 = (f32[128]{0:T(128)}, f32[128]{0:T(128)}, f32[128,2048]{1,0:T(8,128)}) fusion(bf16[128,2048]{1,0:T(8,128)(2,1)} %i0.3, f32[2048]{0:T(1024)S(1)} %bitcast.36, f32[144,2048]{1,0:T(8,128)S(1)} %maximum_convert_fusion.1, f32[128]{0:T(128)S(1)} %convert_element_type.277, f32[128]{0:T(128)S(1)} %convert_element_type.276), kind=kLoop, calls=%fused_computation.14 | loop fusion | flops 2096896 | bytes 2631680 | tf_op jit(solution)/shard_map/reduce_sum | solution.py:534
  (156 shorter events, 41.5 us)
Async XLA Ops:
  9.8 17.2 %collective-permute-start = (bf16[144,2048]{1,0:T(8,128)(2,1)S(1)}, bf16[144,2048]{1,0:T(8,128)(2,1)S(1)}, u32[]{:S(2)}, u32[]{:S(2)}) collective-permute-start(bf16[144,2048]{1,0:T(8,128)(2,1)S(1)} %pad_maximum_fusion.w0.v0), channel_id=1, source_target_pairs={{0,2},{1,3},{2,0},{3,1},{4,6},{5,7},{6,4},{7,5},{8,10},{9,11},{10,... | collective-permute-start | bytes 1769480 | tf_op jit(solution)/shard_map/ppermute | solution.py:487
  12.8 39.3 %collective-permute-start.1 = (bf16[144,2048]{1,0:T(8,128)(2,1)S(1)}, bf16[144,2048]{1,0:T(8,128)(2,1)S(1)}, u32[]{:S(2)}, u32[]{:S(2)}) collective-permute-start(bf16[144,2048]{1,0:T(8,128)(2,1)S(1)} %pad_maximum_fusion.w0.v0), channel_id=1, source_target_pairs={{0,1},{1,0},{2,3},{3,2},{4,5},{5,4},{6,7},{7,6},{8,9},{9,8},{10,11... | collective-permute-start | bytes 1769480 | tf_op jit(solution)/shard_map/ppermute | solution.py:487
  12.8 38.7 %collective-permute-start.9 = (bf16[512,512]{1,0:T(8,128)(2,1)}, bf16[512,512]{1,0:T(8,128)(2,1)}, u32[]{:S(2)}, u32[]{:S(2)}) collective-permute-start(bf16[512,512]{1,0:T(8,128)(2,1)} %u0.3), channel_id=1, source_target_pairs={{0,2},{1,3},{2,0},{3,1},{4,6},{5,7},{6,4},{7,5},{8,10},{9,11},{10,... | collective-permute-start | bytes 1572872 | tf_op jit(solution)/shard_map/ppermute | solution.py:487
  12.9 39.1 %collective-permute-start.6 = (bf16[128,2048]{1,0:T(8,128)(2,1)}, bf16[128,2048]{1,0:T(8,128)(2,1)}, u32[]{:S(2)}, u32[]{:S(2)}) collective-permute-start(bf16[128,2048]{1,0:T(8,128)(2,1)} %i0.3), channel_id=1, source_target_pairs={{0,2},{1,3},{2,0},{3,1},{4,6},{5,7},{6,4},{7,5},{8,10},{9,11},{10,... | collective-permute-start | bytes 1572872 | tf_op jit(solution)/shard_map/ppermute | solution.py:487
  14.8 12.1 %collective-permute-start.4 = (bf16[128,512]{1,0:T(8,128)(2,1)S(1)}, bf16[128,512]{1,0:T(8,128)(2,1)S(1)}, u32[]{:S(2)}, u32[]{:S(2)}) collective-permute-start(bf16[128,512]{1,0:T(8,128)(2,1)S(1)} %copy-done.15), channel_id=1, source_target_pairs={{0,1},{1,0},{2,3},{3,2},{4,5},{5,4},{6,7},{7,6},{8,9},{9,8},{10,11... | collective-permute-start | bytes 393224 | tf_op jit(solution)/shard_map/ppermute | solution.py:487
  26.9 25.6 %collective-permute-start.2 = (bf16[144,2048]{1,0:T(8,128)(2,1)S(1)}, bf16[144,2048]{1,0:T(8,128)(2,1)S(1)}, u32[]{:S(2)}, u32[]{:S(2)}) collective-permute-start(bf16[144,2048]{1,0:T(8,128)(2,1)S(1)} %collective-permute-done.w1.v1), channel_id=1, source_target_pairs={{0,1},{1,0},{2,3},{3,2},{4,5},{5,4},{6,7},{7,6},{8,9},{9,8},{10,11... | collective-permute-start | bytes 1769480 | tf_op jit(solution)/shard_map/ppermute | solution.py:487
  27.0 24.5 %collective-permute-start.3 = (bf16[128,512]{1,0:T(8,128)(2,1)S(1)}, bf16[128,512]{1,0:T(8,128)(2,1)}, u32[]{:S(2)}, u32[]{:S(2)}) collective-permute-start(bf16[128,512]{1,0:T(8,128)(2,1)S(1)} %copy-done.15), channel_id=1, source_target_pairs={{0,2},{1,3},{2,0},{3,1},{4,6},{5,7},{6,4},{7,5},{8,10},{9,11},{10,... | collective-permute-start | bytes 393224 | tf_op jit(solution)/shard_map/ppermute | solution.py:487
  51.5 29.1 %collective-permute-start.10 = (bf16[512,512]{1,0:T(8,128)(2,1)}, bf16[512,512]{1,0:T(8,128)(2,1)}, u32[]{:S(2)}, u32[]{:S(2)}) collective-permute-start(bf16[512,512]{1,0:T(8,128)(2,1)} %u0.3), channel_id=1, source_target_pairs={{0,1},{1,0},{2,3},{3,2},{4,5},{5,4},{6,7},{7,6},{8,9},{9,8},{10,11... | collective-permute-start | bytes 1572872 | tf_op jit(solution)/shard_map/ppermute | solution.py:487
  51.5 29.1 %collective-permute-start.7 = (bf16[128,2048]{1,0:T(8,128)(2,1)}, bf16[128,2048]{1,0:T(8,128)(2,1)}, u32[]{:S(2)}, u32[]{:S(2)}) collective-permute-start(bf16[128,2048]{1,0:T(8,128)(2,1)} %i0.3), channel_id=1, source_target_pairs={{0,1},{1,0},{2,3},{3,2},{4,5},{5,4},{6,7},{7,6},{8,9},{9,8},{10,11... | collective-permute-start | bytes 1572872 | tf_op jit(solution)/shard_map/ppermute | solution.py:487
  52.0 28.6 %collective-permute-start.11 = (bf16[512,512]{1,0:T(8,128)(2,1)}, bf16[512,512]{1,0:T(8,128)(2,1)}, u32[]{:S(2)}, u32[]{:S(2)}) collective-permute-start(bf16[512,512]{1,0:T(8,128)(2,1)} %collective-permute-done.9.u1), channel_id=1, source_target_pairs={{0,1},{1,0},{2,3},{3,2},{4,5},{5,4},{6,7},{7,6},{8,9},{9,8},{10,11... | collective-permute-start | bytes 1572872 | tf_op jit(solution)/shard_map/ppermute | solution.py:487
  52.1 28.5 %collective-permute-start.8 = (bf16[128,2048]{1,0:T(8,128)(2,1)}, bf16[128,2048]{1,0:T(8,128)(2,1)}, u32[]{:S(2)}, u32[]{:S(2)}) collective-permute-start(bf16[128,2048]{1,0:T(8,128)(2,1)} %collective-permute-done.6.i1), channel_id=1, source_target_pairs={{0,1},{1,0},{2,3},{3,2},{4,5},{5,4},{6,7},{7,6},{8,9},{9,8},{10,11... | collective-permute-start | bytes 1572872 | tf_op jit(solution)/shard_map/ppermute | solution.py:487
  52.5 28.1 %collective-permute-start.5 = (bf16[128,512]{1,0:T(8,128)(2,1)}, bf16[128,512]{1,0:T(8,128)(2,1)S(1)}, u32[]{:S(2)}, u32[]{:S(2)}) collective-permute-start(bf16[128,512]{1,0:T(8,128)(2,1)} %collective-permute-done.3.o1), channel_id=1, source_target_pairs={{0,1},{1,0},{2,3},{3,2},{4,5},{5,4},{6,7},{7,6},{8,9},{9,8},{10,11... | collective-permute-start | bytes 393224 | tf_op jit(solution)/shard_map/ppermute | solution.py:487
  129.2 49.7 %collective-permute-start.30 = (bf16[2,512,512]{2,1,0:T(8,128)(2,1)}, bf16[2,512,512]{2,1,0:T(8,128)(2,1)}, u32[]{:S(2)}, u32[]{:S(2)}) collective-permute-start(bf16[2,512,512]{2,1,0:T(8,128)(2,1)} %get-tuple-element.62), channel_id=1, source_target_pairs={{0,1},{1,0},{2,3},{3,2},{4,5},{5,4},{6,7},{7,6},{8,9},{9,8},{10,11... | collective-permute-start | bytes 3145736 | tf_op jit(solution)/shard_map/ppermute | solution.py:487
  136.2 32.1 %collective-permute-start.22 = (bf16[128,256]{1,0:T(8,128)(2,1)S(1)}, bf16[128,256]{1,0:T(8,128)(2,1)S(1)}, u32[]{:S(2)}, u32[]{:S(2)}) collective-permute-start(bf16[128,256]{1,0:T(8,128)(2,1)S(1)} %add_convert_fusion.14), channel_id=1, source_target_pairs={{0,16},{4,20},{8,24},{12,28},{16,0},{20,4},{24,8},{28,12},{1,17},{... | collective-permute-start | bytes 196616 | tf_op jit(solution)/shard_map/ppermute | solution.py:487
  168.3 14.0 %collective-permute-start.12 = (bf16[2,144,2048]{2,1,0:T(8,128)(2,1)}, bf16[2,144,2048]{2,1,0:T(8,128)(2,1)S(1)}, u32[]{:S(2)}, u32[]{:S(2)}) collective-permute-start(bf16[2,144,2048]{2,1,0:T(8,128)(2,1)} %get-tuple-element.56), channel_id=1, source_target_pairs={{0,1},{1,0},{2,3},{3,2},{4,5},{5,4},{6,7},{7,6},{8,9},{9,8},{10,11... | collective-permute-start | bytes 3538952 | tf_op jit(solution)/shard_map/ppermute | solution.py:487
  168.4 9.8 %collective-permute-start.23 = (bf16[128,256]{1,0:T(8,128)(2,1)S(1)}, bf16[128,256]{1,0:T(8,128)(2,1)S(1)}, u32[]{:S(2)}, u32[]{:S(2)}) collective-permute-start(bf16[128,256]{1,0:T(8,128)(2,1)S(1)} %add_convert_fusion.13), channel_id=1, source_target_pairs={{0,4},{4,0},{8,12},{12,8},{16,20},{20,16},{24,28},{28,24},{1,5},{5... | collective-permute-start | bytes 196616 | tf_op jit(solution)/shard_map/ppermute | solution.py:487
  170.0 13.3 %collective-permute-start.24 = (bf16[2,144,2048]{2,1,0:T(8,128)(2,1)S(1)}, bf16[2,144,2048]{2,1,0:T(8,128)(2,1)S(1)}, u32[]{:S(2)}, u32[]{:S(2)}) collective-permute-start(bf16[2,144,2048]{2,1,0:T(8,128)(2,1)S(1)} %copy-done.22), channel_id=1, source_target_pairs={{0,1},{1,0},{2,3},{3,2},{4,5},{5,4},{6,7},{7,6},{8,9},{9,8},{10,11... | collective-permute-start | bytes 3538952 | tf_op jit(solution)/shard_map/ppermute | solution.py:487
  180.6 14.8 %collective-permute-start.31 = (bf16[512,512]{1,0:T(8,128)(2,1)S(1)}, bf16[512,512]{1,0:T(8,128)(2,1)S(1)}, u32[]{:S(2)}, u32[]{:S(2)}) collective-permute-start(bf16[512,512]{1,0:T(8,128)(2,1)S(1)} %slice_bitcast_fusion.4), channel_id=1, source_target_pairs={{0,2},{1,3},{2,0},{3,1},{4,6},{5,7},{6,4},{7,5},{8,10},{9,11},{10,... | collective-permute-start | bytes 1572872 | tf_op jit(solution)/shard_map/ppermute | solution.py:487
  182.8 25.3 %collective-permute-start.13 = (bf16[144,2048]{1,0:T(8,128)(2,1)S(1)}, bf16[144,2048]{1,0:T(8,128)(2,1)S(1)}, u32[]{:S(2)}, u32[]{:S(2)}) collective-permute-start(bf16[144,2048]{1,0:T(8,128)(2,1)S(1)} %slice_bitcast_fusion.2), channel_id=1, source_target_pairs={{0,2},{1,3},{2,0},{3,1},{4,6},{5,7},{6,4},{7,5},{8,10},{9,11},{10,... | collective-permute-start | bytes 1769480 | tf_op jit(solution)/shard_map/ppermute | solution.py:487
  184.5 35.6 %collective-permute-start.25 = (bf16[144,2048]{1,0:T(8,128)(2,1)S(1)}, bf16[144,2048]{1,0:T(8,128)(2,1)S(1)}, u32[]{:S(2)}, u32[]{:S(2)}) collective-permute-start(bf16[144,2048]{1,0:T(8,128)(2,1)S(1)} %slice_bitcast_fusion), channel_id=1, source_target_pairs={{0,2},{1,3},{2,0},{3,1},{4,6},{5,7},{6,4},{7,5},{8,10},{9,11},{10,... | collective-permute-start | bytes 1769480 | tf_op jit(solution)/shard_map/ppermute | solution.py:487
  195.6 13.2 %collective-permute-start.32 = (bf16[512,256]{1,0:T(8,128)(2,1)S(1)}, bf16[512,256]{1,0:T(8,128)(2,1)S(1)}, u32[]{:S(2)}, u32[]{:S(2)}) collective-permute-start(bf16[512,256]{1,0:T(8,128)(2,1)S(1)} %broadcast_select_fusion.8), channel_id=1, source_target_pairs={{0,4},{4,0},{8,12},{12,8},{16,20},{20,16},{24,28},{28,24},{1,5},{5... | collective-permute-start | bytes 786440 | tf_op jit(solution)/shard_map/ppermute | solution.py:487
  208.3 12.8 %collective-permute-start.14 = (bf16[144,1024]{1,0:T(8,128)(2,1)S(1)}, bf16[144,1024]{1,0:T(8,128)(2,1)S(1)}, u32[]{:S(2)}, u32[]{:S(2)}) collective-permute-start(bf16[144,1024]{1,0:T(8,128)(2,1)S(1)} %broadcast_select_fusion.5), channel_id=1, source_target_pairs={{0,4},{4,0},{8,12},{12,8},{16,20},{20,16},{24,28},{28,24},{1,5},{5... | collective-permute-start | bytes 884744 | tf_op jit(solution)/shard_map/ppermute | solution.py:487
  209.0 11.9 %collective-permute-start.33 = (bf16[512,256]{1,0:T(8,128)(2,1)S(1)}, bf16[512,256]{1,0:T(8,128)(2,1)S(1)}, u32[]{:S(2)}, u32[]{:S(2)}) collective-permute-start(bf16[512,256]{1,0:T(8,128)(2,1)S(1)} %add_convert_fusion.11), channel_id=1, source_target_pairs={{0,8},{4,12},{8,0},{12,4},{16,24},{20,28},{24,16},{28,20},{1,9},{5... | collective-permute-start | bytes 786440 | tf_op jit(solution)/shard_map/ppermute | solution.py:487
  220.3 8.5 %collective-permute-start.26 = (bf16[144,1024]{1,0:T(8,128)(2,1)S(1)}, bf16[144,1024]{1,0:T(8,128)(2,1)S(1)}, u32[]{:S(2)}, u32[]{:S(2)}) collective-permute-start(bf16[144,1024]{1,0:T(8,128)(2,1)S(1)} %broadcast_select_fusion.2), channel_id=1, source_target_pairs={{0,4},{4,0},{8,12},{12,8},{16,20},{20,16},{24,28},{28,24},{1,5},{5... | collective-permute-start | bytes 884744 | tf_op jit(solution)/shard_map/ppermute | solution.py:487
  220.9 14.1 %collective-permute-start.34 = (bf16[512,256]{1,0:T(8,128)(2,1)S(1)}, bf16[512,256]{1,0:T(8,128)(2,1)S(1)}, u32[]{:S(2)}, u32[]{:S(2)}) collective-permute-start(bf16[512,256]{1,0:T(8,128)(2,1)S(1)} %add_convert_fusion.10), channel_id=1, source_target_pairs={{0,16},{4,20},{8,24},{12,28},{16,0},{20,4},{24,8},{28,12},{1,17},{... | collective-permute-start | bytes 786440 | tf_op jit(solution)/shard_map/ppermute | solution.py:487
  221.2 15.5 %collective-permute-start.15 = (bf16[144,1024]{1,0:T(8,128)(2,1)S(1)}, bf16[144,1024]{1,0:T(8,128)(2,1)S(1)}, u32[]{:S(2)}, u32[]{:S(2)}) collective-permute-start(bf16[144,1024]{1,0:T(8,128)(2,1)S(1)} %add_convert_fusion.8), channel_id=1, source_target_pairs={{0,8},{4,12},{8,0},{12,4},{16,24},{20,28},{24,16},{28,20},{1,9},{5... | collective-permute-start | bytes 884744 | tf_op jit(solution)/shard_map/ppermute | solution.py:487
  228.9 15.7 %collective-permute-start.27 = (bf16[144,1024]{1,0:T(8,128)(2,1)S(1)}, bf16[144,1024]{1,0:T(8,128)(2,1)S(1)}, u32[]{:S(2)}, u32[]{:S(2)}) collective-permute-start(bf16[144,1024]{1,0:T(8,128)(2,1)S(1)} %add_convert_fusion.5), channel_id=1, source_target_pairs={{0,8},{4,12},{8,0},{12,4},{16,24},{20,28},{24,16},{28,20},{1,9},{5... | collective-permute-start | bytes 884744 | tf_op jit(solution)/shard_map/ppermute | solution.py:487
  235.1 10.0 %collective-permute-start.35 = (bf16[512,256]{1,0:T(8,128)(2,1)S(1)}, bf16[512,256]{1,0:T(8,128)(2,1)S(1)}, u32[]{:S(2)}, u32[]{:S(2)}) collective-permute-start(bf16[512,256]{1,0:T(8,128)(2,1)S(1)} %add_convert_fusion.9), channel_id=1, source_target_pairs={{0,4},{4,0},{8,12},{12,8},{16,20},{20,16},{24,28},{28,24},{1,5},{5... | collective-permute-start | bytes 786440 | tf_op jit(solution)/shard_map/ppermute | solution.py:487
  236.8 23.3 %collective-permute-start.16 = (bf16[144,1024]{1,0:T(8,128)(2,1)S(1)}, bf16[144,1024]{1,0:T(8,128)(2,1)S(1)}, u32[]{:S(2)}, u32[]{:S(2)}) collective-permute-start(bf16[144,1024]{1,0:T(8,128)(2,1)S(1)} %add_convert_fusion.7), channel_id=1, source_target_pairs={{0,16},{4,20},{8,24},{12,28},{16,0},{20,4},{24,8},{28,12},{1,17},{... | collective-permute-start | bytes 884744 | tf_op jit(solution)/shard_map/ppermute | solution.py:487
  244.7 20.0 %collective-permute-start.28 = (bf16[144,1024]{1,0:T(8,128)(2,1)S(1)}, bf16[144,1024]{1,0:T(8,128)(2,1)S(1)}, u32[]{:S(2)}, u32[]{:S(2)}) collective-permute-start(bf16[144,1024]{1,0:T(8,128)(2,1)S(1)} %add_convert_fusion.4), channel_id=1, source_target_pairs={{0,16},{4,20},{8,24},{12,28},{16,0},{20,4},{24,8},{28,12},{1,17},{... | collective-permute-start | bytes 884744 | tf_op jit(solution)/shard_map/ppermute | solution.py:487
  260.2 7.9 %collective-permute-start.17 = (bf16[144,1024]{1,0:T(8,128)(2,1)S(1)}, bf16[144,1024]{1,0:T(8,128)(2,1)S(1)}, u32[]{:S(2)}, u32[]{:S(2)}) collective-permute-start(bf16[144,1024]{1,0:T(8,128)(2,1)S(1)} %add_convert_fusion.6), channel_id=1, source_target_pairs={{0,4},{4,0},{8,12},{12,8},{16,20},{20,16},{24,28},{28,24},{1,5},{5... | collective-permute-start | bytes 884744 | tf_op jit(solution)/shard_map/ppermute | solution.py:487
  264.8 8.5 %collective-permute-start.29 = (bf16[144,1024]{1,0:T(8,128)(2,1)S(1)}, bf16[144,1024]{1,0:T(8,128)(2,1)S(1)}, u32[]{:S(2)}, u32[]{:S(2)}) collective-permute-start(bf16[144,1024]{1,0:T(8,128)(2,1)S(1)} %add_convert_fusion.3), channel_id=1, source_target_pairs={{0,4},{4,0},{8,12},{12,8},{16,20},{20,16},{24,28},{28,24},{1,5},{5... | collective-permute-start | bytes 884744 | tf_op jit(solution)/shard_map/ppermute | solution.py:487
  (27 other events, 278.3 us)

commit v2 on v0

v2 whole, which is shorter than its diff:
```python
import functools

import jax
import jax.numpy as jnp
from jax import lax
from jax.experimental import pallas as pl
from jax.experimental.pallas import tpu as pltpu
from jax.sharding import PartitionSpec as P

F32 = jnp.float32
BF16 = jnp.bfloat16
PAIR = 128
PAIRS = range(4)
SCALE = 64 ** -0.5
CHUNK = 128
UNROLL = 2
JOIN = 4
ROWS = 512
EPS = 1e-5
WEIGHT = 10**9
MASKS = (0, 2, 1, 3)
VM = pl.BlockSpec(memory_space=pltpu.VMEM)
SM = pl.BlockSpec(memory_space=pltpu.SMEM)
ANY = pl.BlockSpec(memory_space=pl.ANY)


def mm(a, b):
    return lax.dot_general(a, b, (((1,), (0,)), ((), ())), preferred_element_type=F32)


def mm_nt(a, b):
    return lax.dot_general(a, b, (((1,), (1,)), ((), ())), preferred_element_type=F32)


def mm_tn(a, b):
    return lax.dot_general(a, b, (((0,), (0,)), ((), ())), preferred_element_type=F32)


def shape(dims, dtype=BF16):
    return jax.ShapeDtypeStruct(dims, dtype)


class Clock:
    def __init__(self, me):
        self.me = me
        self.token = jnp.zeros((8, 128), F32)

    def sync(self, *values):
        self.token, values = lax.optimization_barrier((self.token, values))
        return values if len(values) > 1 else values[0]


def call(clock, kernel, name, outs, args, scratch=(), limit=8, outside=(), aliases=None):
    n_in, n_out = len(args), len(outs)

    def body(me, token, *refs):
        outs_at = n_in + n_out
        refs[outs_at][...] = token[...]
        kernel(me, *refs[:outs_at], *refs[outs_at + 1 :])

    place = lambda k, o: (pltpu.HBM if k in outside else pltpu.VMEM)(o.shape, o.dtype)
    *results, clock.token = pl.pallas_call(
        body,
        in_specs=[SM] + [VM] * (n_in + 1),
        out_specs=[ANY if k in outside else VM for k in range(n_out)] + [VM],
        out_shape=[place(k, o) for k, o in enumerate(outs)] + [pltpu.VMEM((8, 128), F32)],
        scratch_shapes=list(scratch),
        input_output_aliases={i + 2: o for i, o in (aliases or {}).items()},
        compiler_params=pltpu.CompilerParams(vmem_limit_bytes=limit << 20),
        cost_estimate=pl.CostEstimate(flops=WEIGHT, bytes_accessed=1 << 10, transcendentals=0),
        name=name,
    )(clock.me, *[pltpu.with_memory_space_constraint(a, pltpu.VMEM) for a in (clock.token, *args)])
    return results


def blocks_of(me):
    return [me ^ mask for mask in MASKS]


def wide(blocks, width):
    return [pl.ds(pl.multiple_of(b * width, width), width) for b in blocks]


def take_blocks(ref, rows, blocks, width):
    return jnp.concatenate([ref[rows, cols] for cols in wide(blocks, width)], axis=1)


def put_blocks(ref, rows, values, blocks, width):
    for i, cols in enumerate(wide(blocks, width)):
        ref[rows, cols] = values[:, i * width : (i + 1) * width]


def stack(refs, cols=slice(None)):
    return jnp.concatenate([r[:, cols] for r in refs], axis=0)


def vector(vecs, start, width):
    return jnp.concatenate([r[0:1, start : start + width] for r in vecs], axis=1).astype(F32)


def row_loop(T, body):
    def step(c, _):
        body(pl.ds(pl.multiple_of(c * ROWS, ROWS), ROWS))
        return 0

    lax.fori_loop(0, T // ROWS, step, 0)


def stats(x):
    mean = jnp.mean(x, axis=1, keepdims=True)
    centred = x - mean
    inv = lax.rsqrt(jnp.mean(centred * centred, axis=1, keepdims=True) + EPS)
    return centred * inv, inv


def norm_back(grad, normed, inv):
    return inv * (grad - jnp.mean(grad, axis=1, keepdims=True) - normed * jnp.mean(grad * normed, axis=1, keepdims=True))


def vectors_kernel(*refs):
    parts, out, bufs, sems = refs[:6], refs[6], refs[7:13], refs[13]
    copies = [pltpu.make_async_copy(src, dst, sems.at[i]) for i, (src, dst) in enumerate(zip(parts, bufs))]
    for copy in copies:
        copy.start()
    for copy in copies:
        copy.wait()
    vec = jnp.concatenate([b[...].reshape(1, -1).astype(F32) for b in bufs], axis=1)
    out[...] = jnp.broadcast_to(vec, out.shape).astype(BF16)


def pack_vectors(*parts):
    return pl.pallas_call(
        vectors_kernel,
        in_specs=[ANY] * len(parts),
        out_specs=VM,
        out_shape=shape((16, sum(p.shape[0] for p in parts))),
        scratch_shapes=[pltpu.VMEM(p.shape, BF16) for p in parts] + [pltpu.SemaphoreType.DMA((len(parts),))],
        compiler_params=pltpu.CompilerParams(vmem_limit_bytes=1 << 20),
        cost_estimate=pl.CostEstimate(flops=WEIGHT, bytes_accessed=1 << 10, transcendentals=0),
        name="pack_vectors",
    )(*parts)


def first_norm_kernel(me_ref, tokens, n1, n1_low, scr):
    blocks = blocks_of(me_ref[0])

    def body(rows):
        n, _ = stats(tokens[rows, :].astype(F32))
        scr[...] = n
        n = take_blocks(scr, slice(None), blocks, 128)
        n1[rows, :] = n
        n1_low[rows, :] = n.astype(BF16)

    row_loop(tokens.shape[0], body)


def first_norm(clock, tokens):
    T = tokens.shape[0]
    return call(clock, first_norm_kernel, "first_norm", [shape((T, 512), F32), shape((T, 512))], [tokens], [pltpu.VMEM((ROWS, 512), F32)])


def project_kernel(_, n1, *refs):
    weights, vecs, (qkvf, a1) = refs[:16], refs[16:20], refs[20:]
    a1[...] = (n1[...] * vector(vecs, 0, 128) + vector(vecs, 128, 128)).astype(BF16)
    for n in range(4):
        out = mm(a1[...], stack(weights[4 * n : 4 * n + 4]))
        qkvf[:, 512 * n : 512 * (n + 1)] = (jnp.exp(out) if n == 3 else out).astype(BF16)


def flat(weights):
    return [w for group in weights for w in group]


def project(clock, n1, weights, vecs):
    T = n1.shape[0]
    return call(clock, project_kernel, "project", [shape((T, 2048))], [n1, *flat(weights), *vecs], [pltpu.VMEM((T, 512), BF16)])[0]


def left_half(rows):
    return lax.broadcasted_iota(jnp.int32, (rows, PAIR), 1) < 64


def split_pair(x, left):
    zero = jnp.zeros((), x.dtype)
    return jnp.concatenate((jnp.where(left, x, zero), jnp.where(left, zero, x)), axis=0)


def same_head():
    r = lax.broadcasted_iota(jnp.int32, (PAIR, PAIR), 0) < 64
    c = lax.broadcasted_iota(jnp.int32, (PAIR, PAIR), 1) < 64
    return r == c


def causal_pair(rows):
    r = lax.broadcasted_iota(jnp.int32, (rows, 2 * rows), 0)
    c = lax.broadcasted_iota(jnp.int32, (rows, 2 * rows), 1)
    return r >= jnp.where(c >= rows, c - rows, c)


def triangle(rows):
    return lax.broadcasted_iota(jnp.int32, (rows, rows), 0) >= lax.broadcasted_iota(jnp.int32, (rows, rows), 1)


def half_reduce(x, left, fn, fill):
    a = fn(jnp.where(left, x, fill), axis=1, keepdims=True)
    b = fn(jnp.where(left, fill, x), axis=1, keepdims=True)
    return jnp.where(left, a, b)


def pair_of(j):
    return slice(PAIR * j, PAIR * (j + 1))


def a_of(j):
    return slice(256 * j, 256 * (j + 1))


def b_of(j):
    return slice(1024 + 256 * j, 1024 + 256 * (j + 1))


def s_of(j):
    return slice(2048 + PAIR * j, 2048 + PAIR * (j + 1))


def g_of(j):
    return slice(2560 + PAIR * j, 2560 + PAIR * (j + 1))


KEPT = 3072


def chunk_rows(c):
    return pl.ds(pl.multiple_of(c * CHUNK, CHUNK), CHUNK)


def forward_kernel(_, qkvf, mixed, kept, states, carry_out, s1, s2, carry):
    C = CHUNK
    s1[...] = jnp.zeros_like(s1)
    s2[...] = jnp.zeros_like(s2)
    carry[...] = jnp.zeros_like(carry)
    left = left_half(C)
    causal = causal_pair(C)
    same = same_head()
    lower = triangle(C).astype(BF16)
    zero = jnp.zeros((), BF16)

    def step(c, _):
        rows = chunk_rows(c)
        part = lambda n, j: qkvf[rows, 512 * n + PAIR * j : 512 * n + PAIR * (j + 1)]
        raw = [mm_nt(part(0, j), split_pair(part(1, j), left)) for j in PAIRS]
        carry_out[c] = carry[...]
        denom = mm(lower, qkvf[rows, 1536:2048]) + carry[0:1, :]
        carry[0:1, :] = denom[C - 1 :, :]
        rden_all = 1.0 / denom
        f2 = [split_pair(part(3, j), left) for j in PAIRS]
        numer = []
        for j in PAIRS:
            a2 = jnp.where(causal, raw[j].astype(BF16), zero)
            kept[rows, a_of(j)] = a2
            s1b = s1[j].astype(BF16)
            states[c, :, pair_of(j)] = s1b
            numer.append(mm(a2, f2[j]) + mm(part(0, j), s1b))
        g = []
        for j in PAIRS:
            rden = rden_all[:, pair_of(j)]
            s = numer[j] * rden * SCALE
            kept[rows, s_of(j)] = s.astype(BF16)
            e = jnp.exp(s - half_reduce(s, left, jnp.max, -jnp.inf))
            p = e / half_reduce(e, left, jnp.sum, 0.0)
            g.append((p * rden).astype(BF16))
            kept[rows, g_of(j)] = g[j]
        raw = [mm_nt(g[j], f2[j]) for j in PAIRS]
        for j in PAIRS:
            b2 = jnp.where(causal, raw[j].astype(BF16), zero)
            kept[rows, b_of(j)] = b2
            s2b = s2[j].astype(BF16)
            states[c, :, pair_of(4 + j)] = s2b
            o = mm(b2, split_pair(part(2, j), left)) + mm(g[j], s2b)
            mixed[rows, pair_of(j)] = o.astype(BF16)
        for j in PAIRS:
            s1[j] += jnp.where(same, mm_tn(part(1, j), part(3, j)), 0.0)
            s2[j] += jnp.where(same, mm_tn(part(3, j), part(2, j)), 0.0)
        return 0

    lax.fori_loop(0, qkvf.shape[0] // C, step, 0, unroll=UNROLL)


def state_scratch():
    return [pltpu.VMEM((4, PAIR, PAIR), F32), pltpu.VMEM((4, PAIR, PAIR), F32), pltpu.VMEM((8, 512), F32)]


def attention_forward(clock, qkvf):
    T = qkvf.shape[0]
    n = T // CHUNK
    outs = [shape((T, 512)), shape((T, KEPT)), shape((n, PAIR, 1024)), shape((n, 8, 512), F32)]
    return call(clock, forward_kernel, "attention_forward", outs, [qkvf], state_scratch())


def backward_kernel(first, count, last, _, qkvf, kept, states, carry_in, do_in, *refs):
    C = CHUNK
    r1, r2, carry = refs[-3:]
    begins, (grad, *ends) = (refs[:3], refs[3:-3]) if first < last else ((), refs[:-3])
    for ref, old in zip((r1, r2, carry), begins or (None,) * 3):
        ref[...] = jnp.zeros_like(ref) if old is None else old[...]
    left = left_half(C)
    causal = causal_pair(C)
    same = same_head()
    lower = triangle(C).astype(BF16)
    upper = lower.T
    upper2 = jnp.concatenate((upper, upper), axis=1)
    zero = jnp.zeros((), BF16)

    def step(t, _):
        c = first - t
        rows = chunk_rows(c)
        here = chunk_rows(count - 1 - t)
        part = lambda n, j: qkvf[rows, 512 * n + PAIR * j : 512 * n + PAIR * (j + 1)]
        do = [do_in[rows, pair_of(j)] for j in PAIRS]
        denoms = mm(lower, qkvf[rows, 1536:2048]) + carry_in[c][0:1, :]
        s1b = [states[c, :, pair_of(j)] for j in PAIRS]
        s2b = [states[c, :, pair_of(4 + j)] for j in PAIRS]
        r1b = [r1[j].astype(BF16) for j in PAIRS]
        r2b = [r2[j].astype(BF16) for j in PAIRS]
        g = [kept[rows, g_of(j)] for j in PAIRS]
        raw = [mm_nt(do[j], split_pair(part(2, j), left)) for j in PAIRS]
        f2 = [split_pair(part(3, j), left) for j in PAIRS]
        db2, dg, dn, dd = [], [], [], []
        for j in PAIRS:
            db2.append(jnp.where(causal, raw[j].astype(BF16), zero))
            dg.append(mm(db2[j], f2[j]) + mm_nt(do[j], s2b[j]))
        for j in PAIRS:
            dv2 = mm_tn(kept[rows, b_of(j)], do[j])
            dv = jnp.where(left, dv2[:C], dv2[C:]) + mm(part(3, j), r2b[j])
            grad[here, 1024 + PAIR * j : 1024 + PAIR * (j + 1)] = dv.astype(BF16)
        for j in PAIRS:
            denom = denoms[:, pair_of(j)]
            rden = 1.0 / denom
            p = g[j].astype(F32) * denom
            dpp = dg[j] * rden * p
            ds = dpp - p * half_reduce(dpp, left, jnp.sum, 0.0)
            dd.append(-(dpp + ds * kept[rows, s_of(j)].astype(F32)) * rden)
            dn.append((ds * SCALE * rden).astype(BF16))
        raw = [mm_nt(dn[j], f2[j]) for j in PAIRS]
        for j in PAIRS:
            df2 = mm_tn(db2[j], g[j]) + mm_tn(kept[rows, a_of(j)], dn[j])
            hi = dd[j].astype(BF16)
            lo = (dd[j] - hi.astype(F32)).astype(BF16)
            df = jnp.where(left, df2[:C], df2[C:]) + mm_nt(part(2, j), r2b[j]) + mm(part(1, j), r1b[j])
            df = df + mm(upper2, jnp.concatenate((hi, lo), axis=0)) + carry[0:1, pair_of(j)]
            grad[here, 1536 + PAIR * j : 1536 + PAIR * (j + 1)] = (df * part(3, j).astype(F32)).astype(BF16)
            carry[0:1, pair_of(j)] += jnp.sum(dd[j], axis=0, keepdims=True)
        for j in PAIRS:
            da2 = jnp.where(causal, raw[j].astype(BF16), zero)
            dq = mm(da2, split_pair(part(1, j), left)) + mm_nt(dn[j], s1b[j])
            grad[here, pair_of(j)] = dq.astype(BF16)
            dk2 = mm_tn(da2, part(0, j))
            dk = jnp.where(left, dk2[:C], dk2[C:]) + mm_nt(part(3, j), r1b[j])
            grad[here, 512 + PAIR * j : 512 + PAIR * (j + 1)] = dk.astype(BF16)
        for j in PAIRS:
            r1[j] += jnp.where(same, mm_tn(part(0, j), dn[j]), 0.0)
            r2[j] += jnp.where(same, mm_tn(g[j], do[j]), 0.0)
        return 0

    lax.fori_loop(0, count, step, 0, unroll=UNROLL)
    for ref, end in zip((r1, r2, carry), ends):
        end[...] = ref[...]


def attention_backward(clock, qkvf, saved, d_o, first, count, states=()):
    rows = count * CHUNK
    outs = [shape((rows, 2048))]
    if first - count >= 0:
        outs += [shape((4, PAIR, PAIR), F32), shape((4, PAIR, PAIR), F32), shape((8, 512), F32)]
    kernel = functools.partial(backward_kernel, first, count, qkvf.shape[0] // CHUNK - 1)
    return call(clock, kernel, "attention_backward", outs, [qkvf, *saved, d_o, *states], state_scratch())


def gelu_parts(v):
    c = 0.7978845608028654
    k = c * 0.044715
    v2 = v * v
    half = 0.5 * jnp.tanh(v * (c + k * v2)) + 0.5
    act = v * half
    return act, half + act * (1.0 - half) * (2 * c + (6 * k) * v2)


def ffn_inner_kernel(me_ref, tokens, mixed, *refs):
    wo, wi, vs = refs[:4], refs[4:8], refs[8:12]
    resid_out, n2_out, r2_out, act_out, slope_out, scr = refs[12:]
    blocks = blocks_of(me_ref[0])
    gain, shift = vector(vs, 256, 128), vector(vs, 384, 128)
    cols = wide(blocks, 512)

    def body(rows):
        resid = tokens[rows, :].astype(F32) + mm(take_blocks(mixed, rows, blocks, 128), stack(wo))
        resid_out[rows, :] = resid
        n2, r2 = stats(resid)
        scr[...] = n2
        n2 = take_blocks(scr, slice(None), blocks, 128)
        n2_out[rows, :] = n2.astype(BF16)
        r2_out[rows, :] = jnp.broadcast_to(r2, (ROWS, 128))
        a2 = (n2 * gain + shift).astype(BF16)
        inner = mm(a2, stack(wi, cols[0]))
        for i in range(4):
            after = mm(a2, stack(wi, cols[i + 1])) if i < 3 else None
            act, slope = gelu_parts(inner + vs[i][0:1, 640:1152].astype(F32))
            act_out[rows, 512 * i : 512 * (i + 1)] = act.astype(BF16)
            slope_out[rows, cols[i]] = slope.astype(BF16)
            inner = after

    row_loop(tokens.shape[0], body)


def ffn_inner(clock, tokens, mixed, wo, wi, vecs):
    T = tokens.shape[0]
    outs = [shape((T, 512), F32), shape((T, 512)), shape((T, 128), F32), shape((T, 2048)), shape((T, 2048))]
    return call(clock, ffn_inner_kernel, "ffn_inner", outs, [tokens, mixed, *wo, *wi, *vecs], [pltpu.VMEM((ROWS, 512), F32)])


def outer_grad_kernel(_, act, dy, keep, send):
    for i in range(4):
        out = mm_tn(act[:, 512 * i : 512 * (i + 1)], dy[...]).astype(BF16)
        (keep if i < 2 else send)[i % 2] = out


def outer_grad(clock, act, dy):
    return call(clock, outer_grad_kernel, "outer_grad", [shape((2, 512, 512))] * 2, [act, dy])


def ffn_outer_kernel(me_ref, resid, act, *refs):
    wu, vs, (out, bias, result, sem) = refs[:4], refs[4:8], refs[8:]
    put_blocks(bias, slice(None), jnp.broadcast_to(vector(vs, 512, 128), (8, 512)), blocks_of(me_ref[0]), 128)
    total = mm(act[...], stack(wu))
    result[...] = (total + resid[...] + bias[0:1, :]).astype(BF16)
    copy = pltpu.make_async_copy(result, out, sem)
    copy.start()
    copy.wait()


def ffn_outer(clock, resid, act, wu, vecs):
    scratch = [pltpu.VMEM((8, 512), F32), pltpu.VMEM(resid.shape, BF16), pltpu.SemaphoreType.DMA]
    return call(clock, ffn_outer_kernel, "ffn_outer", [shape(resid.shape)], [resid, act, *wu, *vecs], scratch, outside=(0,))[0]


def inner_back_kernel(me_ref, dy, slope, u0, u1, u2, u3, din, sums):
    cols = wide(blocks_of(me_ref[0]), 512)
    sums[...] = jnp.zeros_like(sums)
    sums[1:2, 0:512] = jnp.sum(dy[...].astype(F32), axis=0, keepdims=True)
    for i, u in enumerate((u0, u1, u2, u3)):
        d = (mm_nt(dy[...], u[...]) * slope[:, cols[i]].astype(F32)).astype(BF16)
        din[:, cols[i]] = d
        sums[0:1, cols[i]] = jnp.sum(d.astype(F32), axis=0, keepdims=True)


def inner_back(clock, dy, slope, wu):
    T = dy.shape[0]
    return call(clock, inner_back_kernel, "inner_back", [shape((T, 2048)), shape((8, 2048), F32)], [dy, slope, *wu], aliases={1: 0})


def inner_grad_kernel(_, n2, din, sums, keep, send):
    tail = jnp.concatenate((sums[...], jnp.zeros_like(sums)), axis=0).astype(BF16)
    for i in range(4):
        dest = keep if i < 2 else send
        dest[i % 2, 0:128, :] = mm_tn(n2[:, 128 * i : 128 * (i + 1)], din[...]).astype(BF16)
        dest[i % 2, 128:144, :] = tail


def inner_grad(clock, n2, din, sums):
    return call(clock, inner_grad_kernel, "inner_grad", [shape((2, 144, 2048))] * 2, [n2, din, sums])


def resid_back_kernel(me_ref, dy, n2, r2, din, *refs):
    wo, wi, vs = refs[:4], refs[4:8], refs[8:12]
    dres_out, do_out, scr = refs[12:]
    blocks = blocks_of(me_ref[0])
    gain = vector(vs, 256, 128)

    def body(rows):
        da2 = mm_nt(din[rows, :], stack(wi))
        put_blocks(scr, slice(None), norm_back(da2 * gain, n2[rows, :].astype(F32), r2[rows, 0:1]), blocks, 128)
        dres = dy[rows, :].astype(F32) + scr[...]
        dres_out[rows, :] = dres
        d_o = mm_nt(dres.astype(BF16), stack(wo))
        put_blocks(do_out, rows, d_o.astype(BF16), blocks, 128)

    row_loop(dy.shape[0], body)


def resid_back(clock, dy, n2, r2, din, wo, wi, vecs):
    T = dy.shape[0]
    return call(clock, resid_back_kernel, "resid_back", [shape((T, 512), F32), shape((T, 512))], [dy, n2, r2, din, *wo, *wi, *vecs], [pltpu.VMEM((ROWS, 512), F32)])


def project_grad_kernel(start, width, extra, me_ref, n1, early, late, *refs):
    keep, send = refs[-2:]
    cols = slice(start, start + width)
    half = early.shape[0]
    out = mm_tn(n1[0:half, :], early[:, cols]) + mm_tn(n1[half:, :], late[:, cols])
    out = out.astype(BF16)
    total = sum(jnp.sum(r[:, cols].astype(F32), axis=0, keepdims=True) for r in (early, late))
    tail = jnp.broadcast_to(total, (16, width)).astype(BF16)
    for i, block in enumerate(wide(blocks_of(me_ref[0]), 128)):
        dest = keep if i < 2 else send
        dest[i % 2, 0:128, 0:width] = out[128 * i : 128 * (i + 1)]
        dest[i % 2, 128:144, 0:width] = tail
        if extra:
            mixed, dres = refs[:2]
            m = mm_tn(mixed[:, block], dres[...].astype(BF16))
            dest[i % 2, 0:128, width:] = m.astype(BF16)
            dest[i % 2, 128:144, width:] = jnp.zeros((16, extra), BF16)


def project_grad(clock, n1, early, late, start, width, *more):
    extra = 512 if more else 0
    kernel = functools.partial(project_grad_kernel, start, width, extra)
    return call(clock, kernel, "project_grad", [shape((2, 144, width + extra))] * 2, [n1, early, late, *more])


def input_grad_kernel(me_ref, tokens, early, late, dres, *refs):
    weights, vecs, (out, scr, result, sems) = refs[:16], refs[16:20], refs[20:]
    blocks = blocks_of(me_ref[0])
    gain = vector(vecs, 0, 128)
    for h, d in enumerate((early, late)):
        rows = slice(ROWS * h, ROWS * (h + 1))
        e = mm_nt(d[:, 0:512], stack(weights[0:4]))
        for n in range(1, 4):
            e = e + mm_nt(d[:, 512 * n : 512 * (n + 1)], stack(weights[4 * n : 4 * n + 4]))
        n1, r1 = stats(tokens[rows, :].astype(F32))
        scr[...] = n1
        put_blocks(scr, slice(None), norm_back(e * gain, take_blocks(scr, slice(None), blocks, 128), r1), blocks, 128)
        result[rows, :] = (dres[rows, :] + scr[...]).astype(BF16)
        pltpu.make_async_copy(result.at[rows, :], out.at[rows, :], sems.at[h]).start()
    for h in range(2):
        rows = slice(ROWS * h, ROWS * (h + 1))
        pltpu.make_async_copy(result.at[rows, :], out.at[rows, :], sems.at[h]).wait()


def input_grad(clock, tokens, early, late, dres, weights, vecs):
    args = [tokens, early, late, dres, *flat(weights), *vecs]
    scratch = [pltpu.VMEM((ROWS, 512), F32), pltpu.VMEM(dres.shape, BF16), pltpu.SemaphoreType.DMA((2,))]
    return call(clock, input_grad_kernel, "input_grad", [shape(dres.shape)], args, scratch, outside=(0,))[0]


def exchange(value, axis, size, mask):
    return lax.ppermute(value, axis, [(i, i ^ mask) for i in range(size)])


def over_x(value):
    return exchange(value, "fsdp", 4, 2)


def over_core(value):
    return exchange(value, "fsdp", 4, 1)


def add(a, b):
    return a.astype(F32) + b.astype(F32)


def half_at(bit, width):
    return pl.ds(pl.multiple_of(bit * (width // 2), width // 2), width // 2)


def join_core_kernel(_, keep, got, mine, send):
    mine[...] = add(keep[0], got[0]).astype(BF16)
    send[...] = add(keep[1], got[1]).astype(BF16)


def join_kernel(split, place, me_ref, keep, got, *refs):
    if place is None:
        total = add(keep[...], got[...]).astype(BF16)
    if split is None:
        out = refs[0]
        if place is None:
            out[...] = total
        else:
            bit = lax.rem(lax.div(me_ref[1], place), 2)
            out[:, half_at(bit, out.shape[1])] = keep[...]
            out[:, half_at(1 - bit, out.shape[1])] = got[...]
    else:
        mine, send, whole = refs
        bit = lax.rem(lax.div(me_ref[1], split), 2)
        whole[...] = total
        mine[...] = whole[:, half_at(bit, whole.shape[1])]
        send[...] = whole[:, half_at(1 - bit, whole.shape[1])]


class Chain:
    def __init__(self, clock, dp, halved, pair):
        self.clock, self.dp = clock, dp
        masks = [1 << k for k in range(dp.bit_length() - 1)]
        self.todo = [("core", 0), ("x", 0)] + [("half" if m in halved else "all", m) for m in masks] + [("beside", m) for m in reversed(masks) if m in halved]
        self.keep, self.send = pair
        self.busy = True
        self.launch()

    def launch(self):
        self.kind, self.mask = self.todo.pop(0)
        if self.kind == "core":
            self.got = over_core(self.send)
        elif self.kind == "x":
            self.got = over_x(self.send)
        else:
            self.got = exchange(self.send, "dp", self.dp, self.mask)

    def step(self):
        rows, width = self.keep.shape[-2:]
        if self.kind == "core":
            self.keep, self.send = call(self.clock, join_core_kernel, "join_core", [shape((rows, width))] * 2, [self.keep, self.got], limit=JOIN)
        else:
            split = self.todo[0][1] if self.todo and self.todo[0][0] == "half" else None
            place = self.mask if self.kind == "beside" else None
            kernel = functools.partial(join_kernel, split, place)
            if split is None:
                outs, scratch = [shape((rows, 2 * width if place else width))], []
            else:
                outs, scratch = [shape((rows, width // 2))] * 2, [pltpu.VMEM((rows, width), BF16)]
            out = call(self.clock, kernel, "join", outs, [self.keep, self.got], scratch, limit=JOIN)
            self.keep, self.send = out if split else (out[0], out[0])
        self.busy = bool(self.todo)
        if self.busy:
            self.launch()


def steps(*chains):
    for chain in chains:
        chain.step()


def column(row):
    r = lax.broadcasted_iota(jnp.int32, (128, 128), 0)
    c = lax.broadcasted_iota(jnp.int32, (128, 128), 1)
    return jnp.sum(jnp.where(r == c, row, 0.0), axis=1, keepdims=True)


def as_row(col):
    r = lax.broadcasted_iota(jnp.int32, (128, 128), 0)
    c = lax.broadcasted_iota(jnp.int32, (128, 128), 1)
    return jnp.sum(jnp.where(r == c, col, 0.0), axis=0, keepdims=True)


def send_out(pairs, sems):
    copies = [pltpu.make_async_copy(src, dst, sems.at[k]) for k, (src, dst) in enumerate(pairs)]
    for copy in copies:
        copy.start()
    for copy in copies:
        copy.wait()


def finish_outer_kernel(_, u, out, buf, sems):
    buf[...] = u[...].astype(F32)
    send_out([(buf, out)], sems)


def finish_outer(clock, u):
    return call(clock, finish_outer_kernel, "finish_outer", [shape(u.shape, F32)], [u], [pltpu.VMEM(u.shape, F32), pltpu.SemaphoreType.DMA((1,))], limit=JOIN, outside=(0,))[0]


def finish_inner_kernel(me_ref, total, w, vec, out, gain_out, shift_out, inner_out, outer_out, buf, small, sems):
    gain, shift = (column(vec[0:1, k : k + 128].astype(F32)) for k in (256, 384))
    m = total[0:128, :].astype(F32)
    tail = total[128:144, :].astype(F32)
    buf[...] = gain * m + shift * tail[0:1, :]
    wf = w[...].astype(F32)
    small[0:1, 0:128] = as_row(jnp.sum(wf * m, axis=1, keepdims=True))
    small[1:2, 0:128] = as_row(jnp.sum(wf * tail[0:1, :], axis=1, keepdims=True))
    me = me_ref[0]
    small[2:3, :] = total[128:144, pl.ds(pl.multiple_of(me * 512, 512), 512)].astype(F32)[0:1, :]
    small[3:4, 0:128] = total[128:144, pl.ds(pl.multiple_of(me * 128, 128), 128)].astype(F32)[1:2, :]
    gain_out[...] = small[0:1, 0:128]
    shift_out[...] = small[1:2, 0:128]
    inner_out[...] = small[2:3, :]
    outer_out[...] = small[3:4, 0:128]
    send_out([(buf, out)], sems)


def finish_inner(clock, total, w, vec):
    outs = [shape((128, 2048), F32), shape((1, 128), F32), shape((1, 128), F32), shape((1, 512), F32), shape((1, 128), F32)]
    scratch = [pltpu.VMEM((128, 2048), F32), pltpu.VMEM((8, 512), F32), pltpu.SemaphoreType.DMA((1,))]
    return call(clock, finish_inner_kernel, "finish_inner", outs, [total, w, vec], scratch, limit=JOIN, outside=(0,))


def finish_project_kernel(more, _, total, w0, w1, vec, *refs):
    before, refs = refs[:1], refs[1:]
    out0, out1, *rest = refs
    sums = rest[1] if more else rest[0]
    buf, sems = rest[-2:]
    gain, shift = (column(vec[0:1, k : k + 128].astype(F32)) for k in (0, 128))
    m = total[0:128, 0:1024].astype(F32)
    tail = total[128:144, 0:1024].astype(F32)[0:1, :]
    buf[:, 0:1024] = gain * m + shift * tail
    w = jnp.concatenate((w0[...], w1[...]), axis=1).astype(F32)
    sums[0:1, :] = before[0][0:1, :] + as_row(jnp.sum(w * m, axis=1, keepdims=True))
    sums[1:2, :] = before[0][1:2, :] + as_row(jnp.sum(w * tail, axis=1, keepdims=True))
    pairs = [(buf.at[:, 0:512], out0), (buf.at[:, 512:1024], out1)]
    if more:
        buf[:, 1024:1536] = total[0:128, 1024:1536].astype(F32)
        pairs.append((buf.at[:, 1024:1536], rest[0]))
    send_out(pairs, sems)


def finish_project(clock, total, w0, w1, vec, before):
    more = total.shape[1] > 1024
    n = 3 if more else 2
    outs = [shape((128, 512), F32)] * n + [shape((8, 128), F32)]
    scratch = [pltpu.VMEM((128, 512 * n), F32), pltpu.SemaphoreType.DMA((n,))]
    return call(clock, functools.partial(finish_project_kernel, more), "finish_project", outs, [total, w0, w1, vec, before], scratch, limit=JOIN, outside=range(n))


def per_device(dp, tokens, first_gain, first_shift, w_query, w_key, w_value, w_control, w_output, second_gain, second_shift, w_inner, inner_bias, w_outer, outer_bias, cotangent):
    me = lax.axis_index("fsdp").astype(jnp.int32)
    place = lax.axis_index("dp").astype(jnp.int32)
    clock = Clock(jnp.stack((me, place)))
    own = [w_query, w_key, w_value, w_control, pack_vectors(first_gain, first_shift, second_gain, second_shift, outer_bias, inner_bias)]
    across = [over_x(v) for v in own]
    own_core = [over_core(v) for v in own]
    n1, n1_low = first_norm(clock, tokens)
    *across, w_output, w_inner, w_outer = clock.sync(*across, w_output, w_inner, w_outer)
    across_core = [over_core(v) for v in across]
    wo_x, wi_x = over_x(w_output), over_x(w_inner)
    *weights, vecs = [list(group) for group in zip(own, across, own_core, across_core)]
    qkvf = project(clock, n1, weights, vecs)
    wo_x, w_output, w_inner = clock.sync(wo_x, w_output, w_inner)
    wo = [w_output, wo_x, over_core(w_output), over_core(wo_x)]
    wi_c = over_core(w_inner)
    mixed, *saved = attention_forward(clock, qkvf)
    wi_x, w_outer = clock.sync(wi_x, w_outer)
    wi = [w_inner, wi_x, wi_c, over_core(wi_x)]
    wu_x, wu_c = over_x(w_outer), over_core(w_outer)
    resid, n2, r2, act, slope = ffn_inner(clock, tokens, mixed, wo, wi, vecs)
    u = Chain(clock, dp, (1, 2), outer_grad(clock, act, cotangent))
    wu_x = clock.sync(wu_x)
    wu = [w_outer, wu_x, wu_c, over_core(wu_x)]
    din, sums = inner_back(clock, cotangent, slope, wu)
    u.step()
    i = Chain(clock, dp, (1, 2), inner_grad(clock, n2, din, sums))
    dres, d_o = resid_back(clock, cotangent, n2, r2, din, wo, wi, vecs)
    i.step()
    early = attention_backward(clock, qkvf, saved, d_o, 7, 4)
    u.step()
    late = attention_backward(clock, qkvf, saved, d_o, 3, 4, early[1:])
    u.step()
    a = Chain(clock, dp, (1,), project_grad(clock, n1_low, late[0], early[0], 0, 1024, mixed, dres))
    b = Chain(clock, dp, (1,), project_grad(clock, n1_low, late[0], early[0], 1024, 1024))
    a.step()
    i.step()
    u.step()
    b.step()
    grad_tokens = input_grad(clock, tokens, late[0], early[0], dres, weights, vecs)
    i.step()
    u.step()
    a.step()
    output = ffn_outer(clock, resid, act, wu, vecs)
    chains = [a, b, i, u]
    while any(c.busy for c in chains):
        for c in chains:
            if c.busy:
                c.step()
    grad_outer = finish_outer(clock, u.keep)
    grad_inner, *vectors = finish_inner(clock, i.keep, w_inner, vecs[0])
    grad_query, grad_key, grad_output, before = finish_project(clock, a.keep, w_query, w_key, vecs[0], jnp.zeros((8, 128), F32))
    grad_value, grad_control, before = finish_project(clock, b.keep, w_value, w_control, vecs[0], before)
    second_gain_grad, second_shift_grad, inner_bias_grad, outer_bias_grad = [v.reshape(-1) for v in vectors]
    return (
        output, grad_tokens, before[0], before[1], grad_query, grad_key, grad_value, grad_control,
        grad_output, second_gain_grad, second_shift_grad, grad_inner, inner_bias_grad, grad_outer, outer_bias_grad,
    )


def solution(mesh):
    row, vec, mat = P(("dp", "fsdp"), None), P("fsdp"), P("fsdp", None)
    return jax.shard_map(
        functools.partial(per_device, mesh.shape["dp"]),
        mesh=mesh,
        in_specs=(row, vec, vec, mat, mat, mat, mat, mat, vec, vec, mat, vec, mat, vec, row),
        out_specs=(row, row, vec, vec, mat, mat, mat, mat, mat, vec, vec, mat, vec, mat, vec),
        check_vma=False,
    )
```

time: 710 us -> 182 us (0.26); the launches traced: 698 us -> 182 us
  matrix products: 281 us -> 0 us
  blocking collectives: 222 us -> 0 us
  Pallas kernels: 0 us -> 83.8 us
  waiting for transfers between devices: 113 us -> 43.2 us
  starting transfers between devices: 0.6 us -> 47.4 us
  local copies, waits for them, and re-layouts: 44.4 us -> 6.74 us
  other arithmetic: 20.3 us -> 0.07 us
  between operations: 16 us -> 1.17 us
    dot_general x132 -> x0, matrix products: 281 us -> none  [the longest x16 31.9 us: head_forward(): numerator = jnp.dot(scores, control, preferred_element_type=jnp.float32)]
    psum x1 -> x0, blocking collectives: 140 us -> none  [per_device(): lax.psum((lax.psum_scatter(grad_gain_one.astype(jnp.bfloat16), 'fsdp', sc...]
    reduce_scatter x7 -> x0, waiting for transfers between devices: 110 us -> none  [the longest x1 34.2 us: per_device(): lax.psum_scatter(grad_inner_full.astype(jnp.bfloat16), 'fsdp', scatter_di...]
    pallas_call x0 -> x45, Pallas kernels: none -> 83.8 us  [the longest x44 83.7 us: call(): pl.pallas_call(body, in_specs=[SM] + [VM] * (n_in + 1), out_specs=[ANY if...]
    all_gather x11 -> x0, blocking collectives: 75 us -> none  [the longest x1 12 us: per_device(): lax.all_gather(w_key, 'fsdp', axis=0, tiled=True)]
    ppermute x0 -> x50, starting transfers between devices: none -> 47.4 us  [exchange(): return lax.ppermute(value, axis, [(i, i ^ mask) for i in range(size)])]
    ppermute x0 -> x50, waiting for transfers between devices: none -> 43.2 us  [exchange(): return lax.ppermute(value, axis, [(i, i ^ mask) for i in range(size)])]
    reshape x5 -> x0, local copies, waits for them, and re-layouts: 12.7 us -> none  [the longest x4 9.76 us: from_items(): return array.reshape(row_count // LEN, -1, LEN, item_width).transpose(0,...]
  transfers between devices with their start and end apart: 9 -> 50, of which waited for: 4 -> 24; matrix products, arithmetic and copies ran while one was open for 46% -> 0% of each run, Pallas kernels for 0% -> 37%
where the time goes in v2:
time: 182 us
  Pallas kernels  83.8 us (46%)
  starting transfers between devices  47.4 us (26%)
  waiting for transfers between devices  43.2 us (24%)
  local copies, waits for them, and re-layouts  6.74 us (4%)
    pallas_call x44, Pallas kernels, call(): pl.pallas_call(body, in_specs=[SM] + [VM] * (n_in + 1), out_specs=[ANY if...  83.7 us
    ppermute x50, starting transfers between devices, exchange(): return lax.ppermute(value, axis, [(i, i ^ mask) for i in range(size)])  47.4 us
    ppermute x50, waiting for transfers between devices, exchange(): return lax.ppermute(value, axis, [(i, i ^ mask) for i in range(size)])  43.2 us
    unnamed x34, local copies, waits for them, and re-layouts  6.22 us
  transfers between devices with their start and end apart: 50, of which 24 were waited for; matrix products, arithmetic and copies ran while one was open for 0% of the time, Pallas kernels for 37%

profile of v2, /device:TPU:0, one launch (start us, length us, event | category | flops | bytes accessed | tf_op | source)
XLA Modules:
  0.0 182.3 jit_solution(17251322633800975896)
XLA Ops:
  4.9 3.0 %collective-permute-start.4 = (bf16[16,1152]{1,0:T(8,128)(2,1)S(1)}, bf16[16,1152]{1,0:T(8,128)(2,1)S(1)}, u32[]{:S(2)}, u32[]{:S(2)}) collective-permute-start(bf16[16,1152]{1,0:T(8,128)(2,1)S(1)} %pack_vectors.1.refs_17_.refs_10_.refs_12_.refs_20_.refs_6_.refs_2_.refs_3_), channel_id=1, source_target_pairs={{0,2},{1,3},{2,0},{3,1},{4,6},{5,7},{6,4},{7,5},{8,10},{9,11},{10,... | collective-permute-start | bytes 110600 | tf_op jit(solution)/shard_map/ppermute | solution.py:546
  8.0 1.9 %collective-permute-start.1 = (bf16[128,512]{1,0:T(8,128)(2,1)S(1)}, bf16[128,512]{1,0:T(8,128)(2,1)S(1)}, u32[]{:S(2)}, u32[]{:S(2)}) collective-permute-start(bf16[128,512]{1,0:T(8,128)(2,1)S(1)} %copy-done.6), channel_id=1, source_target_pairs={{0,2},{1,3},{2,0},{3,1},{4,6},{5,7},{6,4},{7,5},{8,10},{9,11},{10,... | collective-permute-start | bytes 393224 | tf_op jit(solution)/shard_map/ppermute | solution.py:546
  10.0 1.9 %collective-permute-start.3 = (bf16[128,512]{1,0:T(8,128)(2,1)S(1)}, bf16[128,512]{1,0:T(8,128)(2,1)S(1)}, u32[]{:S(2)}, u32[]{:S(2)}) collective-permute-start(bf16[128,512]{1,0:T(8,128)(2,1)S(1)} %copy-done.8), channel_id=1, source_target_pairs={{0,2},{1,3},{2,0},{3,1},{4,6},{5,7},{6,4},{7,5},{8,10},{9,11},{10,... | collective-permute-start | bytes 393224 | tf_op jit(solution)/shard_map/ppermute | solution.py:546
  14.3 2.8 %collective-permute-done.1.refs_6_.refs_9_ = bf16[128,512]{1,0:T(8,128)(2,1)S(1)} collective-permute-done((bf16[128,512]{1,0:T(8,128)(2,1)S(1)}, bf16[128,512]{1,0:T(8,128)(2,1)S(1)}, u32[]{:S(2)}, u32[]{:S(2)}) %collective-permute-start.1) | collective-permute-done | bytes 131104 | tf_op jit(solution)/shard_map/ppermute | solution.py:546
  17.1 2.7 %collective-permute-done.2.refs_10_.refs_13_ = bf16[128,512]{1,0:T(8,128)(2,1)S(1)} collective-permute-done((bf16[128,512]{1,0:T(8,128)(2,1)S(1)}, bf16[128,512]{1,0:T(8,128)(2,1)S(1)}, u32[]{:S(2)}, u32[]{:S(2)}) %collective-permute-start.2) | collective-permute-done | bytes 131104 | tf_op jit(solution)/shard_map/ppermute | solution.py:546
  26.8 2.9 %project.1 = (bf16[1024,2048]{1,0:T(8,128)(2,1)S(1)}, f32[8,128]{1,0:T(8,128)S(1)}) custom-call(s32[2]{0:T(128)S(1)} %pad_add_fusion.me, f32[8,128]{1,0:T(8,128)S(1)} %get-tuple-element.157.token, f32[1024,512]{1,0:T(8,128)S(1)} %get-tuple-element.158.refs_0_, bf16[128,512]{1,0:T(8,128)(2,1)S(1)} %copy-done.5, ...), custom_call_target="tpu_custom_call" | custom-call | flops 1000000000 | bytes 1024 | tf_op jit(solution)/shard_map/project/pallas_call | solution.py:62
  29.7 6.8 %collective-permute-done.15.refs_3_.refs_5_ = bf16[128,512]{1,0:T(8,128)(2,1)S(1)} collective-permute-done((bf16[128,512]{1,0:T(8,128)(2,1)S(1)}, bf16[128,512]{1,0:T(8,128)(2,1)S(1)}, u32[]{:S(2)}, u32[]{:S(2)}) %collective-permute-start.15) | collective-permute-done | bytes 131104 | tf_op jit(solution)/shard_map/ppermute | solution.py:546
  36.6 7.9 %attention_forward.1 = (bf16[1024,512]{1,0:T(8,128)(2,1)S(1)}, bf16[1024,3072]{1,0:T(8,128)(2,1)S(1)}, bf16[8,128,1024]{2,1,0:T(8,128)(2,1)S(1)}, f32[8,8,512]{2,1,0:T(8,128)S(1)}, f32[8,128]{1,0:T(8,128)S(1)}) custom-call(s32[2]{0:T(128)S(1)} %pad_add_fusion.me, f32[8,128]{1,0:T(8,128)S(1)} %get-tuple-element.167.token, ...), custom_call_target="tpu_custom_call" | custom-call | flops 1000000000 | bytes 1024 | tf_op jit(solution)/shard_map/attention_forward/pallas_call | solution.py:62
  47.0 7.9 %ffn_inner.1 = (f32[1024,512]{1,0:T(8,128)S(1)}, bf16[1024,512]{1,0:T(8,128)(2,1)S(1)}, f32[1024,128]{1,0:T(8,128)S(1)}, bf16[1024,2048]{1,0:T(8,128)(2,1)S(1)},...) custom-call(s32[2]{0:T(128)S(1)} %pad_add_fusion.me, f32[8,128]{1,0:T(8,128)S(1)} %get-tuple-element.171.token, ...), custom_call_target="tpu_custom_call" | custom-call | flops 1000000000 | bytes 1024 | tf_op jit(solution)/shard_map/ffn_inner/pallas_call | solution.py:62
  54.9 2.9 %outer_grad.1 = (bf16[2,512,512]{2,1,0:T(8,128)(2,1)S(1)}, bf16[2,512,512]{2,1,0:T(8,128)(2,1)S(1)}, f32[8,128]{1,0:T(8,128)S(1)}) custom-call(s32[2]{0:T(128)S(1)} %pad_add_fusion.me, f32[8,128]{1,0:T(8,128)S(1)} %get-tuple-element.177.token, bf16[1024,2048]{1,0:T(8,128)(2,1)S(1)} %get-tuple-element.178.refs_0_.refs_1_, bf16[1024,512]{1,0:T(8,128)(2,1)S(1)} %copy-done), custom_call_target="tpu_custom_call" | custom-call | flops 1000000000 | bytes 1024 | tf_op jit(solution)/shard_map/outer_grad/pallas_call | solution.py:62
  59.4 1.9 %collective-permute-done.22.refs_4_ = bf16[512,512]{1,0:T(8,128)(2,1)S(1)} collective-permute-done((bf16[512,512]{1,0:T(8,128)(2,1)S(1)}, bf16[512,512]{1,0:T(8,128)(2,1)S(1)}, u32[]{:S(2)}, u32[]{:S(2)}) %collective-permute-start.22) | collective-permute-done | bytes 524320 | tf_op jit(solution)/shard_map/ppermute | solution.py:546
  62.1 3.4 %inner_back.1 = (bf16[1024,2048]{1,0:T(8,128)(2,1)S(1)}, f32[8,2048]{1,0:T(8,128)S(1)}, f32[8,128]{1,0:T(8,128)S(1)}) custom-call(s32[2]{0:T(128)S(1)} %pad_add_fusion.me, f32[8,128]{1,0:T(8,128)S(1)} %get-tuple-element.181.token, bf16[1024,512]{1,0:T(8,128)(2,1)S(1)} %copy-done, ...), custom_call_target="tpu_custom_call", output_to_operand_aliasing={{0}: (3, {})} | custom-call | flops 1000000000 | bytes 1024 | tf_op jit(solution)/shard_map/inner_back/pallas_call | solution.py:62
  66.3 3.0 %inner_grad.1 = (bf16[2,144,2048]{2,1,0:T(8,128)(2,1)S(1)}, bf16[2,144,2048]{2,1,0:T(8,128)(2,1)S(1)}, f32[8,128]{1,0:T(8,128)S(1)}) custom-call(s32[2]{0:T(128)S(1)} %pad_add_fusion.me, f32[8,128]{1,0:T(8,128)S(1)} %get-tuple-element.187.token, bf16[1024,512]{1,0:T(8,128)(2,1)S(1)} %get-tuple-element.188.refs_0_.refs_1_, ...), custom_call_target="tpu_custom_call" | custom-call | flops 1000000000 | bytes 1024 | tf_op jit(solution)/shard_map/inner_grad/pallas_call | solution.py:62
  71.1 4.8 %resid_back.1 = (f32[1024,512]{1,0:T(8,128)S(1)}, bf16[1024,512]{1,0:T(8,128)(2,1)S(1)}, f32[8,128]{1,0:T(8,128)S(1)}) custom-call(s32[2]{0:T(128)S(1)} %pad_add_fusion.me, f32[8,128]{1,0:T(8,128)S(1)} %get-tuple-element.191.token, bf16[1024,512]{1,0:T(8,128)(2,1)S(1)} %copy-done, bf16[1024,512]{1,0:T(8,128)(2,1)S(1)} %get-tuple-element.188.refs_0_.refs_1_, ...), custom_call_target="tpu_custom_call" | custom-call | flops 1000000000 | bytes 1024 | tf_op jit(solution)/shard_map/resid_back/pallas_call | solution.py:62
  76.8 5.8 %attention_backward.2 = (bf16[512,2048]{1,0:T(8,128)(2,1)S(1)}, f32[4,128,128]{2,1,0:T(8,128)S(1)}, f32[4,128,128]{2,1,0:T(8,128)S(1)}, f32[8,512]{1,0:T(8,128)S(1)}, f32[8,128]{1,0:T(8,128)S(1)}) custom-call(s32[2]{0:T(128)S(1)} %pad_add_fusion.me, f32[8,128]{1,0:T(8,128)S(1)} %get-tuple-element.196.token, ...), custom_call_target="tpu_custom_call" | custom-call | flops 1000000000 | bytes 1024 | tf_op jit(solution)/shard_map/attention_backward/pallas_call | solution.py:62
  84.6 2.2 %collective-permute-start.27 = (bf16[512,256]{1,0:T(8,128)(2,1)S(1)}, bf16[512,256]{1,0:T(8,128)(2,1)S(1)}, u32[]{:S(2)}, u32[]{:S(2)}) collective-permute-start(bf16[512,256]{1,0:T(8,128)(2,1)S(1)} %get-tuple-element.210), channel_id=1, source_target_pairs={{0,4},{4,0},{8,12},{12,8},{16,20},{20,16},{24,28},{28,24},{1,5},{5... | collective-permute-start | bytes 786440 | tf_op jit(solution)/shard_map/ppermute | solution.py:546
  86.8 5.9 %attention_backward.3 = (bf16[512,2048]{1,0:T(8,128)(2,1)S(1)}, f32[8,128]{1,0:T(8,128)S(1)}) custom-call(s32[2]{0:T(128)S(1)} %pad_add_fusion.me, f32[8,128]{1,0:T(8,128)S(1)} %get-tuple-element.204.token, bf16[1024,2048]{1,0:T(8,128)(2,1)S(1)} %get-tuple-element.168.refs_0_, bf16[1024,3072]{1,0:T(8,128)(2,1)S(1)} %get-tuple-element.197.refs_1_, ...), custom_call_target="tpu_custom_call" | custom-call | flops 1000000000 | bytes 1024 | tf_op jit(solution)/shard_map/attention_backward/pallas_call | solution.py:62
  93.5 2.4 %project_grad.2 = (bf16[2,144,1536]{2,1,0:T(8,128)(2,1)S(1)}, bf16[2,144,1536]{2,1,0:T(8,128)(2,1)S(1)}, f32[8,128]{1,0:T(8,128)S(1)}) custom-call(s32[2]{0:T(128)S(1)} %pad_add_fusion.me, f32[8,128]{1,0:T(8,128)S(1)} %get-tuple-element.211.token, bf16[1024,512]{1,0:T(8,128)(2,1)S(1)} %get-tuple-element.212.refs_0_, ...), custom_call_target="tpu_custom_call" | custom-call | flops 1000000000 | bytes 1024 | tf_op jit(solution)/shard_map/project_grad/pallas_call | solution.py:62
  96.8 1.8 %project_grad.3 = (bf16[2,144,1024]{2,1,0:T(8,128)(2,1)S(1)}, bf16[2,144,1024]{2,1,0:T(8,128)(2,1)S(1)}, f32[8,128]{1,0:T(8,128)S(1)}) custom-call(s32[2]{0:T(128)S(1)} %pad_add_fusion.me, f32[8,128]{1,0:T(8,128)S(1)} %get-tuple-element.216.token, bf16[1024,512]{1,0:T(8,128)(2,1)S(1)} %get-tuple-element.212.refs_0_, ...), custom_call_target="tpu_custom_call" | custom-call | flops 1000000000 | bytes 1024 | tf_op jit(solution)/shard_map/project_grad/pallas_call | solution.py:62
  101.2 10.5 %collective-permute-done.29.refs_1_ = bf16[144,2048]{1,0:T(8,128)(2,1)S(1)} collective-permute-done((bf16[144,2048]{1,0:T(8,128)(2,1)S(1)}, bf16[144,2048]{1,0:T(8,128)(2,1)S(1)}, u32[]{:S(2)}, u32[]{:S(2)}) %collective-permute-start.29) | collective-permute-done | bytes 589856 | tf_op jit(solution)/shard_map/ppermute | solution.py:546
  115.6 2.6 %collective-permute-start.33 = (bf16[512,128]{1,0:T(8,128)(2,1)S(1)}, bf16[512,128]{1,0:T(8,128)(2,1)S(1)}, u32[]{:S(2)}, u32[]{:S(2)}) collective-permute-start(bf16[512,128]{1,0:T(8,128)(2,1)S(1)} %get-tuple-element.234.refs_0_), channel_id=1, source_target_pairs={{0,16},{4,20},{8,24},{12,28},{16,0},{20,4},{24,8},{28,12},{1,17},{... | collective-permute-start | bytes 393224 | tf_op jit(solution)/shard_map/ppermute | solution.py:546
  118.9 5.0 %input_grad.1 = (bf16[1024,512]{1,0:T(8,128)(2,1)}, f32[8,128]{1,0:T(8,128)S(1)}) custom-call(s32[2]{0:T(128)S(1)} %pad_add_fusion.me, f32[8,128]{1,0:T(8,128)S(1)} %get-tuple-element.229.token, bf16[1024,512]{1,0:T(8,128)(2,1)S(1)} %copy-done.1, bf16[512,2048]{1,0:T(8,128)(2,1)S(1)} %get-tuple-element.213.refs_1_, ...), custom_call_target="tpu_custom_call" | custom-call | flops 1000000000 | bytes 1024 | tf_op jit(solution)/shard_map/input_grad/pallas_call | solution.py:62
  130.0 3.9 %ffn_outer.1 = (bf16[1024,512]{1,0:T(8,128)(2,1)}, f32[8,128]{1,0:T(8,128)S(1)}) custom-call(s32[2]{0:T(128)S(1)} %pad_add_fusion.me, f32[8,128]{1,0:T(8,128)S(1)} %get-tuple-element.238.token, f32[1024,512]{1,0:T(8,128)S(1)} %get-tuple-element.239.refs_0_, bf16[1024,2048]{1,0:T(8,128)(2,1)S(1)} %get-tuple-element.178.refs_0_.refs_1_, ...), custom_call_target="tpu_custom_call" | custom-call | flops 1000000000 | bytes 1024 | tf_op jit(solution)/shard_map/ffn_outer/pallas_call | solution.py:62
  137.3 2.6 %collective-permute-start.41 = (bf16[144,512]{1,0:T(8,128)(2,1)S(1)}, bf16[144,512]{1,0:T(8,128)(2,1)S(1)}, u32[]{:S(2)}, u32[]{:S(2)}) collective-permute-start(bf16[144,512]{1,0:T(8,128)(2,1)S(1)} %get-tuple-element.259.refs_0_), channel_id=1, source_target_pairs={{0,16},{4,20},{8,24},{12,28},{16,0},{20,4},{24,8},{28,12},{1,17},{... | collective-permute-start | bytes 442376 | tf_op jit(solution)/shard_map/ppermute | solution.py:546
  148.4 2.3 %collective-permute-start.45 = (bf16[144,512]{1,0:T(8,128)(2,1)S(1)}, bf16[144,512]{1,0:T(8,128)(2,1)S(1)}, u32[]{:S(2)}, u32[]{:S(2)}) collective-permute-start(bf16[144,512]{1,0:T(8,128)(2,1)S(1)} %get-tuple-element.267.refs_0_), channel_id=1, source_target_pairs={{0,8},{4,12},{8,0},{12,4},{16,24},{20,28},{24,16},{28,20},{1,9},{5... | collective-permute-start | bytes 442376 | tf_op jit(solution)/shard_map/ppermute | solution.py:546
  151.5 3.2 %collective-permute-done.43.refs_1_ = bf16[144,768]{1,0:T(8,128)(2,1)S(1)} collective-permute-done((bf16[144,768]{1,0:T(8,128)(2,1)S(1)}, bf16[144,768]{1,0:T(8,128)(2,1)S(1)}, u32[]{:S(2)}, u32[]{:S(2)}) %collective-permute-start.43) | collective-permute-done | bytes 221216 | tf_op jit(solution)/shard_map/ppermute | solution.py:546
  158.1 2.4 %collective-permute-start.47 = (bf16[144,512]{1,0:T(8,128)(2,1)S(1)}, bf16[144,512]{1,0:T(8,128)(2,1)S(1)}, u32[]{:S(2)}, u32[]{:S(2)}) collective-permute-start(bf16[144,512]{1,0:T(8,128)(2,1)S(1)} %get-tuple-element.271.refs_0_), channel_id=1, source_target_pairs={{0,16},{4,20},{8,24},{12,28},{16,0},{20,4},{24,8},{28,12},{1,17},{... | collective-permute-start | bytes 442376 | tf_op jit(solution)/shard_map/ppermute | solution.py:546
  161.0 2.5 %collective-permute-start.48 = (bf16[144,1024]{1,0:T(8,128)(2,1)S(1)}, bf16[144,1024]{1,0:T(8,128)(2,1)S(1)}, u32[]{:S(2)}, u32[]{:S(2)}) collective-permute-start(bf16[144,1024]{1,0:T(8,128)(2,1)S(1)} %get-tuple-element.273.refs_0_), channel_id=1, source_target_pairs={{0,4},{4,0},{8,12},{12,8},{16,20},{20,16},{24,28},{28,24},{1,5},{5... | collective-permute-start | bytes 884744 | tf_op jit(solution)/shard_map/ppermute | solution.py:546
  166.3 1.9 %collective-permute-start.49 = (bf16[144,512]{1,0:T(8,128)(2,1)S(1)}, bf16[144,512]{1,0:T(8,128)(2,1)S(1)}, u32[]{:S(2)}, u32[]{:S(2)}) collective-permute-start(bf16[144,512]{1,0:T(8,128)(2,1)S(1)} %get-tuple-element.275.refs_0_), channel_id=1, source_target_pairs={{0,4},{4,0},{8,12},{12,8},{16,20},{20,16},{24,28},{28,24},{1,5},{5... | collective-permute-start | bytes 442376 | tf_op jit(solution)/shard_map/ppermute | solution.py:546
  168.2 1.8 collective-permute-done.48.refs_1_
  173.8 2.0 %finish_inner.1 = (f32[128,2048]{1,0:T(8,128)}, f32[1,128]{1,0:T(1,128)S(1)}, f32[1,128]{1,0:T(1,128)S(1)}, f32[1,512]{1,0:T(1,128)S(1)}, f32[1,128]{1,0:T(1,128)S(1)}, /*index=5*/f32[8,128]{1,0:T(8,128)S(1)}) custom-call(s32[2]{0:T(128)S(1)} %pad_add_fusion.me, f32[8,128]{1,0:T(8,128)S(1)} %get-tuple-element.278.token, ...), custom_call_target="tpu_custom_call" | custom-call | flops 1000000000 | bytes 1024 | tf_op jit(solution)/shard_map/finish_inner/pallas_call | solution.py:62
  179.6 2.2 %finish_project.3 = (f32[128,512]{1,0:T(8,128)}, f32[128,512]{1,0:T(8,128)}, f32[8,128]{1,0:T(8,128)S(1)}, f32[8,128]{1,0:T(8,128)}) custom-call(s32[2]{0:T(128)S(1)} %pad_add_fusion.me, f32[8,128]{1,0:T(8,128)S(1)} %get-tuple-element.282.token, bf16[144,1024]{1,0:T(8,128)(2,1)S(1)} %get-tuple-element.283.refs_0_, bf16[128,512]{1,0:T(8,128)(2,1)S(1)} %copy-done.7, ...), custom_call_target="tpu_custom_call" | custom-call | flops 1000000000 | bytes 1024 | tf_op jit(solution)/shard_map/finish_project/pallas_call | solution.py:62
  (150 shorter events, 66.1 us)
Async XLA Ops:
  4.9 8.7 %collective-permute-start.4 = (bf16[16,1152]{1,0:T(8,128)(2,1)S(1)}, bf16[16,1152]{1,0:T(8,128)(2,1)S(1)}, u32[]{:S(2)}, u32[]{:S(2)}) collective-permute-start(bf16[16,1152]{1,0:T(8,128)(2,1)S(1)} %pack_vectors.1.refs_17_.refs_10_.refs_12_.refs_20_.refs_6_.refs_2_.refs_3_), channel_id=1, source_target_pairs={{0,2},{1,3},{2,0},{3,1},{4,6},{5,7},{6,4},{7,5},{8,10},{9,11},{10,... | collective-permute-start | bytes 110600 | tf_op jit(solution)/shard_map/ppermute | solution.py:546
  7.9 6.4 %collective-permute-start = (bf16[128,512]{1,0:T(8,128)(2,1)S(1)}, bf16[128,512]{1,0:T(8,128)(2,1)S(1)}, u32[]{:S(2)}, u32[]{:S(2)}) collective-permute-start(bf16[128,512]{1,0:T(8,128)(2,1)S(1)} %copy-done.5), channel_id=1, source_target_pairs={{0,2},{1,3},{2,0},{3,1},{4,6},{5,7},{6,4},{7,5},{8,10},{9,11},{10,... | collective-permute-start | bytes 393224 | tf_op jit(solution)/shard_map/ppermute | solution.py:546
  8.0 9.1 %collective-permute-start.1 = (bf16[128,512]{1,0:T(8,128)(2,1)S(1)}, bf16[128,512]{1,0:T(8,128)(2,1)S(1)}, u32[]{:S(2)}, u32[]{:S(2)}) collective-permute-start(bf16[128,512]{1,0:T(8,128)(2,1)S(1)} %copy-done.6), channel_id=1, source_target_pairs={{0,2},{1,3},{2,0},{3,1},{4,6},{5,7},{6,4},{7,5},{8,10},{9,11},{10,... | collective-permute-start | bytes 393224 | tf_op jit(solution)/shard_map/ppermute | solution.py:546
  9.9 9.9 %collective-permute-start.2 = (bf16[128,512]{1,0:T(8,128)(2,1)S(1)}, bf16[128,512]{1,0:T(8,128)(2,1)S(1)}, u32[]{:S(2)}, u32[]{:S(2)}) collective-permute-start(bf16[128,512]{1,0:T(8,128)(2,1)S(1)} %copy-done.7), channel_id=1, source_target_pairs={{0,2},{1,3},{2,0},{3,1},{4,6},{5,7},{6,4},{7,5},{8,10},{9,11},{10,... | collective-permute-start | bytes 393224 | tf_op jit(solution)/shard_map/ppermute | solution.py:546
  10.0 11.3 %collective-permute-start.3 = (bf16[128,512]{1,0:T(8,128)(2,1)S(1)}, bf16[128,512]{1,0:T(8,128)(2,1)S(1)}, u32[]{:S(2)}, u32[]{:S(2)}) collective-permute-start(bf16[128,512]{1,0:T(8,128)(2,1)S(1)} %copy-done.8), channel_id=1, source_target_pairs={{0,2},{1,3},{2,0},{3,1},{4,6},{5,7},{6,4},{7,5},{8,10},{9,11},{10,... | collective-permute-start | bytes 393224 | tf_op jit(solution)/shard_map/ppermute | solution.py:546
  21.3 23.2 %collective-permute-start.16 = (bf16[128,2048]{1,0:T(8,128)(2,1)S(1)}, bf16[128,2048]{1,0:T(8,128)(2,1)S(1)}, u32[]{:S(2)}, u32[]{:S(2)}) collective-permute-start(bf16[128,2048]{1,0:T(8,128)(2,1)S(1)} %copy-done.2), channel_id=1, source_target_pairs={{0,2},{1,3},{2,0},{3,1},{4,6},{5,7},{6,4},{7,5},{8,10},{9,11},{10,... | collective-permute-start | bytes 1572872 | tf_op jit(solution)/shard_map/ppermute | solution.py:546
  25.8 10.8 %collective-permute-start.15 = (bf16[128,512]{1,0:T(8,128)(2,1)S(1)}, bf16[128,512]{1,0:T(8,128)(2,1)S(1)}, u32[]{:S(2)}, u32[]{:S(2)}) collective-permute-start(bf16[128,512]{1,0:T(8,128)(2,1)S(1)} %copy-done.4), channel_id=1, source_target_pairs={{0,2},{1,3},{2,0},{3,1},{4,6},{5,7},{6,4},{7,5},{8,10},{9,11},{10,... | collective-permute-start | bytes 393224 | tf_op jit(solution)/shard_map/ppermute | solution.py:546
  36.6 10.4 %collective-permute-start.19 = (bf16[128,2048]{1,0:T(8,128)(2,1)S(1)}, bf16[128,2048]{1,0:T(8,128)(2,1)S(1)}, u32[]{:S(2)}, u32[]{:S(2)}) collective-permute-start(bf16[128,2048]{1,0:T(8,128)(2,1)S(1)} %copy-done.2), channel_id=1, source_target_pairs={{0,1},{1,0},{2,3},{3,2},{4,5},{5,4},{6,7},{7,6},{8,9},{9,8},{10,11... | collective-permute-start | bytes 1572872 | tf_op jit(solution)/shard_map/ppermute | solution.py:546
  45.5 13.9 %collective-permute-start.21 = (bf16[512,512]{1,0:T(8,128)(2,1)S(1)}, bf16[512,512]{1,0:T(8,128)(2,1)S(1)}, u32[]{:S(2)}, u32[]{:S(2)}) collective-permute-start(bf16[512,512]{1,0:T(8,128)(2,1)S(1)} %copy-done.3), channel_id=1, source_target_pairs={{0,2},{1,3},{2,0},{3,1},{4,6},{5,7},{6,4},{7,5},{8,10},{9,11},{10,... | collective-permute-start | bytes 1572872 | tf_op jit(solution)/shard_map/ppermute | solution.py:546
  57.8 7.7 %collective-permute-start.24 = (bf16[2,512,512]{2,1,0:T(8,128)(2,1)S(1)}, bf16[2,512,512]{2,1,0:T(8,128)(2,1)S(1)}, u32[]{:S(2)}, u32[]{:S(2)}) collective-permute-start(bf16[2,512,512]{2,1,0:T(8,128)(2,1)S(1)} %get-tuple-element.186), channel_id=1, source_target_pairs={{0,1},{1,0},{2,3},{3,2},{4,5},{5,4},{6,7},{7,6},{8,9},{9,8},{10,11... | collective-permute-start | bytes 3145736 | tf_op jit(solution)/shard_map/ppermute | solution.py:546
  69.3 6.6 %collective-permute-start.25 = (bf16[2,144,2048]{2,1,0:T(8,128)(2,1)S(1)}, bf16[2,144,2048]{2,1,0:T(8,128)(2,1)S(1)}, u32[]{:S(2)}, u32[]{:S(2)}) collective-permute-start(bf16[2,144,2048]{2,1,0:T(8,128)(2,1)S(1)} %get-tuple-element.195), channel_id=1, source_target_pairs={{0,1},{1,0},{2,3},{3,2},{4,5},{5,4},{6,7},{7,6},{8,9},{9,8},{10,11... | collective-permute-start | bytes 3538952 | tf_op jit(solution)/shard_map/ppermute | solution.py:546
  69.8 14.0 %collective-permute-start.26 = (bf16[512,512]{1,0:T(8,128)(2,1)S(1)}, bf16[512,512]{1,0:T(8,128)(2,1)S(1)}, u32[]{:S(2)}, u32[]{:S(2)}) collective-permute-start(bf16[512,512]{1,0:T(8,128)(2,1)S(1)} %get-tuple-element.203), channel_id=1, source_target_pairs={{0,2},{1,3},{2,0},{3,1},{4,6},{5,7},{6,4},{7,5},{8,10},{9,11},{10,... | collective-permute-start | bytes 1572872 | tf_op jit(solution)/shard_map/ppermute | solution.py:546
  84.6 8.1 %collective-permute-start.27 = (bf16[512,256]{1,0:T(8,128)(2,1)S(1)}, bf16[512,256]{1,0:T(8,128)(2,1)S(1)}, u32[]{:S(2)}, u32[]{:S(2)}) collective-permute-start(bf16[512,256]{1,0:T(8,128)(2,1)S(1)} %get-tuple-element.210), channel_id=1, source_target_pairs={{0,4},{4,0},{8,12},{12,8},{16,20},{20,16},{24,28},{28,24},{1,5},{5... | collective-permute-start | bytes 786440 | tf_op jit(solution)/shard_map/ppermute | solution.py:546
  96.0 15.7 %collective-permute-start.29 = (bf16[144,2048]{1,0:T(8,128)(2,1)S(1)}, bf16[144,2048]{1,0:T(8,128)(2,1)S(1)}, u32[]{:S(2)}, u32[]{:S(2)}) collective-permute-start(bf16[144,2048]{1,0:T(8,128)(2,1)S(1)} %get-tuple-element.222), channel_id=1, source_target_pairs={{0,2},{1,3},{2,0},{3,1},{4,6},{5,7},{6,4},{7,5},{8,10},{9,11},{10,... | collective-permute-start | bytes 1769480 | tf_op jit(solution)/shard_map/ppermute | solution.py:546
  98.7 19.5 %collective-permute-start.31 = (bf16[2,144,1024]{2,1,0:T(8,128)(2,1)S(1)}, bf16[2,144,1024]{2,1,0:T(8,128)(2,1)S(1)}, u32[]{:S(2)}, u32[]{:S(2)}) collective-permute-start(bf16[2,144,1024]{2,1,0:T(8,128)(2,1)S(1)} %get-tuple-element.228), channel_id=1, source_target_pairs={{0,1},{1,0},{2,3},{3,2},{4,5},{5,4},{6,7},{7,6},{8,9},{9,8},{10,11... | collective-permute-start | bytes 1769480 | tf_op jit(solution)/shard_map/ppermute | solution.py:546
  98.9 16.1 %collective-permute-start.30 = (bf16[512,128]{1,0:T(8,128)(2,1)S(1)}, bf16[512,128]{1,0:T(8,128)(2,1)S(1)}, u32[]{:S(2)}, u32[]{:S(2)}) collective-permute-start(bf16[512,128]{1,0:T(8,128)(2,1)S(1)} %get-tuple-element.225), channel_id=1, source_target_pairs={{0,8},{4,12},{8,0},{12,4},{16,24},{20,28},{24,16},{28,20},{1,9},{5... | collective-permute-start | bytes 393224 | tf_op jit(solution)/shard_map/ppermute | solution.py:546
  112.6 11.2 %collective-permute-start.32 = (bf16[144,1024]{1,0:T(8,128)(2,1)S(1)}, bf16[144,1024]{1,0:T(8,128)(2,1)S(1)}, u32[]{:S(2)}, u32[]{:S(2)}) collective-permute-start(bf16[144,1024]{1,0:T(8,128)(2,1)S(1)} %get-tuple-element.232), channel_id=1, source_target_pairs={{0,4},{4,0},{8,12},{12,8},{16,20},{20,16},{24,28},{28,24},{1,5},{5... | collective-permute-start | bytes 884744 | tf_op jit(solution)/shard_map/ppermute | solution.py:546
  114.3 11.5 %collective-permute-start.34 = (bf16[144,1536]{1,0:T(8,128)(2,1)S(1)}, bf16[144,1536]{1,0:T(8,128)(2,1)S(1)}, u32[]{:S(2)}, u32[]{:S(2)}) collective-permute-start(bf16[144,1536]{1,0:T(8,128)(2,1)S(1)} %get-tuple-element.237), channel_id=1, source_target_pairs={{0,2},{1,3},{2,0},{3,1},{4,6},{5,7},{6,4},{7,5},{8,10},{9,11},{10,... | collective-permute-start | bytes 1327112 | tf_op jit(solution)/shard_map/ppermute | solution.py:546
  115.6 9.0 %collective-permute-start.33 = (bf16[512,128]{1,0:T(8,128)(2,1)S(1)}, bf16[512,128]{1,0:T(8,128)(2,1)S(1)}, u32[]{:S(2)}, u32[]{:S(2)}) collective-permute-start(bf16[512,128]{1,0:T(8,128)(2,1)S(1)} %get-tuple-element.234.refs_0_), channel_id=1, source_target_pairs={{0,16},{4,20},{8,24},{12,28},{16,0},{20,4},{24,8},{28,12},{1,17},{... | collective-permute-start | bytes 393224 | tf_op jit(solution)/shard_map/ppermute | solution.py:546
  126.5 7.3 %collective-permute-start.35 = (bf16[144,768]{1,0:T(8,128)(2,1)S(1)}, bf16[144,768]{1,0:T(8,128)(2,1)S(1)}, u32[]{:S(2)}, u32[]{:S(2)}) collective-permute-start(bf16[144,768]{1,0:T(8,128)(2,1)S(1)} %get-tuple-element.244), channel_id=1, source_target_pairs={{0,4},{4,0},{8,12},{12,8},{16,20},{20,16},{24,28},{28,24},{1,5},{5... | collective-permute-start | bytes 663560 | tf_op jit(solution)/shard_map/ppermute | solution.py:546
  127.1 9.0 %collective-permute-start.36 = (bf16[144,1024]{1,0:T(8,128)(2,1)S(1)}, bf16[144,1024]{1,0:T(8,128)(2,1)S(1)}, u32[]{:S(2)}, u32[]{:S(2)}) collective-permute-start(bf16[144,1024]{1,0:T(8,128)(2,1)S(1)} %get-tuple-element.247), channel_id=1, source_target_pairs={{0,2},{1,3},{2,0},{3,1},{4,6},{5,7},{6,4},{7,5},{8,10},{9,11},{10,... | collective-permute-start | bytes 884744 | tf_op jit(solution)/shard_map/ppermute | solution.py:546
  127.9 13.5 %collective-permute-start.38 = (bf16[512,128]{1,0:T(8,128)(2,1)S(1)}, bf16[512,128]{1,0:T(8,128)(2,1)S(1)}, u32[]{:S(2)}, u32[]{:S(2)}) collective-permute-start(bf16[512,128]{1,0:T(8,128)(2,1)S(1)} %get-tuple-element.252.refs_0_), channel_id=1, source_target_pairs={{0,8},{4,12},{8,0},{12,4},{16,24},{20,28},{24,16},{28,20},{1,9},{5... | collective-permute-start | bytes 393224 | tf_op jit(solution)/shard_map/ppermute | solution.py:546
  129.5 7.3 %collective-permute-start.37 = (bf16[144,512]{1,0:T(8,128)(2,1)S(1)}, bf16[144,512]{1,0:T(8,128)(2,1)S(1)}, u32[]{:S(2)}, u32[]{:S(2)}) collective-permute-start(bf16[144,512]{1,0:T(8,128)(2,1)S(1)} %get-tuple-element.250), channel_id=1, source_target_pairs={{0,8},{4,12},{8,0},{12,4},{16,24},{20,28},{24,16},{28,20},{1,9},{5... | collective-permute-start | bytes 442376 | tf_op jit(solution)/shard_map/ppermute | solution.py:546
  134.4 8.7 %collective-permute-start.39 = (bf16[144,768]{1,0:T(8,128)(2,1)S(1)}, bf16[144,768]{1,0:T(8,128)(2,1)S(1)}, u32[]{:S(2)}, u32[]{:S(2)}) collective-permute-start(bf16[144,768]{1,0:T(8,128)(2,1)S(1)} %get-tuple-element.254.refs_0_), channel_id=1, source_target_pairs={{0,8},{4,12},{8,0},{12,4},{16,24},{20,28},{24,16},{28,20},{1,9},{5... | collective-permute-start | bytes 663560 | tf_op jit(solution)/shard_map/ppermute | solution.py:546
  137.3 10.5 %collective-permute-start.41 = (bf16[144,512]{1,0:T(8,128)(2,1)S(1)}, bf16[144,512]{1,0:T(8,128)(2,1)S(1)}, u32[]{:S(2)}, u32[]{:S(2)}) collective-permute-start(bf16[144,512]{1,0:T(8,128)(2,1)S(1)} %get-tuple-element.259.refs_0_), channel_id=1, source_target_pairs={{0,16},{4,20},{8,24},{12,28},{16,0},{20,4},{24,8},{28,12},{1,17},{... | collective-permute-start | bytes 442376 | tf_op jit(solution)/shard_map/ppermute | solution.py:546
  142.1 8.8 %collective-permute-start.42 = (bf16[512,256]{1,0:T(8,128)(2,1)S(1)}, bf16[512,256]{1,0:T(8,128)(2,1)S(1)}, u32[]{:S(2)}, u32[]{:S(2)}) collective-permute-start(bf16[512,256]{1,0:T(8,128)(2,1)S(1)} %get-tuple-element.261.refs_0_), channel_id=1, source_target_pairs={{0,4},{4,0},{8,12},{12,8},{16,20},{20,16},{24,28},{28,24},{1,5},{5... | collective-permute-start | bytes 786440 | tf_op jit(solution)/shard_map/ppermute | solution.py:546
  143.8 10.9 %collective-permute-start.43 = (bf16[144,768]{1,0:T(8,128)(2,1)S(1)}, bf16[144,768]{1,0:T(8,128)(2,1)S(1)}, u32[]{:S(2)}, u32[]{:S(2)}) collective-permute-start(bf16[144,768]{1,0:T(8,128)(2,1)S(1)} %get-tuple-element.263.refs_0_), channel_id=1, source_target_pairs={{0,16},{4,20},{8,24},{12,28},{16,0},{20,4},{24,8},{28,12},{1,17},{... | collective-permute-start | bytes 663560 | tf_op jit(solution)/shard_map/ppermute | solution.py:546
  148.4 12.0 %collective-permute-start.45 = (bf16[144,512]{1,0:T(8,128)(2,1)S(1)}, bf16[144,512]{1,0:T(8,128)(2,1)S(1)}, u32[]{:S(2)}, u32[]{:S(2)}) collective-permute-start(bf16[144,512]{1,0:T(8,128)(2,1)S(1)} %get-tuple-element.267.refs_0_), channel_id=1, source_target_pairs={{0,8},{4,12},{8,0},{12,4},{16,24},{20,28},{24,16},{28,20},{1,9},{5... | collective-permute-start | bytes 442376 | tf_op jit(solution)/shard_map/ppermute | solution.py:546
  150.8 6.7 %collective-permute-start.44 = (bf16[144,512]{1,0:T(8,128)(2,1)S(1)}, bf16[144,512]{1,0:T(8,128)(2,1)S(1)}, u32[]{:S(2)}, u32[]{:S(2)}) collective-permute-start(bf16[144,512]{1,0:T(8,128)(2,1)S(1)} %get-tuple-element.265.refs_0_), channel_id=1, source_target_pairs={{0,8},{4,12},{8,0},{12,4},{16,24},{20,28},{24,16},{28,20},{1,9},{5... | collective-permute-start | bytes 442376 | tf_op jit(solution)/shard_map/ppermute | solution.py:546
  155.3 8.4 %collective-permute-start.46 = (bf16[144,768]{1,0:T(8,128)(2,1)S(1)}, bf16[144,768]{1,0:T(8,128)(2,1)S(1)}, u32[]{:S(2)}, u32[]{:S(2)}) collective-permute-start(bf16[144,768]{1,0:T(8,128)(2,1)S(1)} %get-tuple-element.269.refs_0_), channel_id=1, source_target_pairs={{0,4},{4,0},{8,12},{12,8},{16,20},{20,16},{24,28},{28,24},{1,5},{5... | collective-permute-start | bytes 663560 | tf_op jit(solution)/shard_map/ppermute | solution.py:546
  158.1 7.7 %collective-permute-start.47 = (bf16[144,512]{1,0:T(8,128)(2,1)S(1)}, bf16[144,512]{1,0:T(8,128)(2,1)S(1)}, u32[]{:S(2)}, u32[]{:S(2)}) collective-permute-start(bf16[144,512]{1,0:T(8,128)(2,1)S(1)} %get-tuple-element.271.refs_0_), channel_id=1, source_target_pairs={{0,16},{4,20},{8,24},{12,28},{16,0},{20,4},{24,8},{28,12},{1,17},{... | collective-permute-start | bytes 442376 | tf_op jit(solution)/shard_map/ppermute | solution.py:546
  161.0 9.0 %collective-permute-start.48 = (bf16[144,1024]{1,0:T(8,128)(2,1)S(1)}, bf16[144,1024]{1,0:T(8,128)(2,1)S(1)}, u32[]{:S(2)}, u32[]{:S(2)}) collective-permute-start(bf16[144,1024]{1,0:T(8,128)(2,1)S(1)} %get-tuple-element.273.refs_0_), channel_id=1, source_target_pairs={{0,4},{4,0},{8,12},{12,8},{16,20},{20,16},{24,28},{28,24},{1,5},{5... | collective-permute-start | bytes 884744 | tf_op jit(solution)/shard_map/ppermute | solution.py:546
  (33 other events, 146.3 us)

commit v3 on v2

v3 whole, which is shorter than its diff:
```python
import functools

import jax
import jax.numpy as jnp
from jax import lax
from jax.experimental import pallas as pl
from jax.experimental.pallas import tpu as pltpu
from jax.sharding import PartitionSpec as P

F32 = jnp.float32
BF16 = jnp.bfloat16
PAIR = 128
PAIRS = range(4)
SCALE = 64 ** -0.5
CHUNK = 128
UNROLL = 2
JOIN = 4
ROWS = 512
EPS = 1e-5
WEIGHT = 1000
MASKS = (0, 2, 1, 3)
VM = pl.BlockSpec(memory_space=pltpu.VMEM)
SM = pl.BlockSpec(memory_space=pltpu.SMEM)
ANY = pl.BlockSpec(memory_space=pl.ANY)


def mm(a, b):
    return lax.dot_general(a, b, (((1,), (0,)), ((), ())), preferred_element_type=F32)


def mm_nt(a, b):
    return lax.dot_general(a, b, (((1,), (1,)), ((), ())), preferred_element_type=F32)


def mm_tn(a, b):
    return lax.dot_general(a, b, (((0,), (0,)), ((), ())), preferred_element_type=F32)


def shape(dims, dtype=BF16):
    return jax.ShapeDtypeStruct(dims, dtype)


class Clock:
    def __init__(self, me, place):
        row = lax.broadcasted_iota(jnp.int32, (8, 128), 0)
        self.token = jnp.where(row == 0, me, place)

    def sync(self, *values):
        self.token, values = lax.optimization_barrier((self.token, values))
        return values if len(values) > 1 else values[0]


def call(clock, kernel, name, outs, args, scratch=(), limit=8, outside=(), raw=(), aliases=None):
    n_in, n_out = len(args), len(outs)

    def body(token, *refs):
        outs_at = n_in + n_out
        refs[outs_at][...] = token[...]
        kernel(token, *refs[:outs_at], *refs[outs_at + 1 :])

    place = lambda k, o: (pltpu.HBM if k in outside else pltpu.VMEM)(o.shape, o.dtype)
    args = [pltpu.with_memory_space_constraint(a, pltpu.HBM if k in raw else pltpu.VMEM) for k, a in enumerate(args)]
    *results, clock.token = pl.pallas_call(
        body,
        in_specs=[VM] + [ANY if k in raw else VM for k in range(n_in)],
        out_specs=[ANY if k in outside else VM for k in range(n_out)] + [VM],
        out_shape=[place(k, o) for k, o in enumerate(outs)] + [pltpu.VMEM((8, 128), jnp.int32)],
        scratch_shapes=list(scratch),
        input_output_aliases={i + 1: o for i, o in (aliases or {}).items()},
        compiler_params=pltpu.CompilerParams(vmem_limit_bytes=limit << 20),
        cost_estimate=pl.CostEstimate(flops=WEIGHT, bytes_accessed=1 << 10, transcendentals=0),
        name=name,
    )(pltpu.with_memory_space_constraint(clock.token, pltpu.VMEM), *args)
    return results


def position(token, row):
    return jnp.max(token[row : row + 1, :])


def blocks_of(token):
    me = position(token, 0)
    return [me ^ mask for mask in MASKS]


def wide(blocks, width):
    return [pl.ds(pl.multiple_of(b * width, width), width) for b in blocks]


def take_blocks(ref, rows, blocks, width):
    return jnp.concatenate([ref[rows, cols] for cols in wide(blocks, width)], axis=1)


def put_blocks(ref, rows, values, blocks, width):
    for i, cols in enumerate(wide(blocks, width)):
        ref[rows, cols] = values[:, i * width : (i + 1) * width]


def stack(refs, cols=slice(None)):
    return jnp.concatenate([r[:, cols] for r in refs], axis=0)


def stack_packs(packs, cols):
    return jnp.concatenate([r[0:128, cols] for r in packs], axis=0)


def vector(packs, start, width):
    return jnp.concatenate([r[128:129, start : start + width] for r in packs], axis=1).astype(F32)


def row_loop(T, body):
    def step(c, _):
        body(pl.ds(pl.multiple_of(c * ROWS, ROWS), ROWS))
        return 0

    lax.fori_loop(0, T // ROWS, step, 0)


def stats(x):
    mean = jnp.mean(x, axis=1, keepdims=True)
    centred = x - mean
    inv = lax.rsqrt(jnp.mean(centred * centred, axis=1, keepdims=True) + EPS)
    return centred * inv, inv


def norm_back(grad, normed, inv):
    return inv * (grad - jnp.mean(grad, axis=1, keepdims=True) - normed * jnp.mean(grad * normed, axis=1, keepdims=True))


def begin_kernel(token, *refs):
    weights, vecs, inner, (out, first, second, wi0, wi1), rest = refs[:4], refs[4:10], refs[10], refs[11:16], refs[16:]
    bufs, sems = rest[:6], rest[6]
    cols = [slice(512 * n, 512 * (n + 1)) for n in range(4)]
    copies = [pltpu.make_async_copy(w, out.at[0:128, c], sems.at[n]) for n, (w, c) in enumerate(zip(weights, cols))]
    copies += [pltpu.make_async_copy(v, b, sems.at[4 + n]) for n, (v, b) in enumerate(zip(vecs, bufs))]
    copies += [pltpu.make_async_copy(inner.at[64 * n : 64 * (n + 1), :], w, sems.at[10 + n]) for n, w in enumerate((wi0, wi1))]
    for copy in copies:
        copy.start()
    for copy in copies:
        copy.wait()
    vec = jnp.concatenate([b[...].reshape(1, -1).astype(F32) for b in bufs] + [jnp.zeros((1, 896), F32)], axis=1)
    out[128:144, :] = jnp.broadcast_to(vec, (16, 2048)).astype(BF16)
    odd = lax.rem(position(token, 1), 2)
    for k, piece in enumerate((first, second)):
        piece[...] = out[:, pl.ds(pl.multiple_of(odd * 1024 + 512 * k, 512), 512)]


def begin(clock, weights, vecs, inner):
    scratch = [pltpu.VMEM(v.shape, BF16) for v in vecs] + [pltpu.SemaphoreType.DMA((12,))]
    outs = [shape((144, 2048)), shape((144, 512)), shape((144, 512)), shape((64, 2048)), shape((64, 2048))]
    return call(clock, begin_kernel, "begin", outs, [*weights, *vecs, inner], scratch, limit=JOIN, raw=range(11))


def assemble_kernel(token, mine0, mine1, other0, other1, _, out):
    odd = lax.rem(position(token, 1), 2)
    for half, pieces in ((odd, (mine0, mine1)), (1 - odd, (other0, other1))):
        for k, piece in enumerate(pieces):
            out[:, pl.ds(pl.multiple_of(half * 1024 + 512 * k, 512), 512)] = piece[...]


def assemble(clock, mine, other, waited):
    return call(clock, assemble_kernel, "assemble", [shape((144, 2048))], [*mine, *other, waited], limit=JOIN)[0]


def first_norm_kernel(token, tokens, n1, n1_low, scr):
    blocks = blocks_of(token)

    def body(rows):
        n, _ = stats(tokens[rows, :].astype(F32))
        scr[...] = n
        n = take_blocks(scr, slice(None), blocks, 128)
        n1[rows, :] = n
        n1_low[rows, :] = n.astype(BF16)

    row_loop(tokens.shape[0], body)


def first_norm(clock, tokens):
    T = tokens.shape[0]
    return call(clock, first_norm_kernel, "first_norm", [shape((T, 512), F32), shape((T, 512))], [tokens], [pltpu.VMEM((ROWS, 512), F32)])


def project_kernel(_, n1, p0, p1, p2, p3, qkvf, a1):
    packs = (p0, p1, p2, p3)
    a1[...] = (n1[...] * vector(packs, 0, 128) + vector(packs, 128, 128)).astype(BF16)
    for n in range(4):
        cols = slice(512 * n, 512 * (n + 1))
        out = mm(a1[...], stack_packs(packs, cols))
        qkvf[:, cols] = (jnp.exp(out) if n == 3 else out).astype(BF16)


def project(clock, n1, packs):
    T = n1.shape[0]
    return call(clock, project_kernel, "project", [shape((T, 2048))], [n1, *packs], [pltpu.VMEM((T, 512), BF16)])[0]


def left_half(rows):
    return lax.broadcasted_iota(jnp.int32, (rows, PAIR), 1) < 64


def split_pair(x, left):
    zero = jnp.zeros((), x.dtype)
    return jnp.concatenate((jnp.where(left, x, zero), jnp.where(left, zero, x)), axis=0)


def same_head():
    r = lax.broadcasted_iota(jnp.int32, (PAIR, PAIR), 0) < 64
    c = lax.broadcasted_iota(jnp.int32, (PAIR, PAIR), 1) < 64
    return r == c


def causal_pair(rows):
    r = lax.broadcasted_iota(jnp.int32, (rows, 2 * rows), 0)
    c = lax.broadcasted_iota(jnp.int32, (rows, 2 * rows), 1)
    return r >= jnp.where(c >= rows, c - rows, c)


def triangle(rows):
    return lax.broadcasted_iota(jnp.int32, (rows, rows), 0) >= lax.broadcasted_iota(jnp.int32, (rows, rows), 1)


def half_reduce(x, left, fn, fill):
    a = fn(jnp.where(left, x, fill), axis=1, keepdims=True)
    b = fn(jnp.where(left, fill, x), axis=1, keepdims=True)
    return jnp.where(left, a, b)


def pair_of(j):
    return slice(PAIR * j, PAIR * (j + 1))


def a_of(j):
    return slice(256 * j, 256 * (j + 1))


def b_of(j):
    return slice(1024 + 256 * j, 1024 + 256 * (j + 1))


def s_of(j):
    return slice(2048 + PAIR * j, 2048 + PAIR * (j + 1))


def g_of(j):
    return slice(2560 + PAIR * j, 2560 + PAIR * (j + 1))


KEPT = 3072


def chunk_rows(c):
    return pl.ds(pl.multiple_of(c * CHUNK, CHUNK), CHUNK)


def forward_kernel(_, qkvf, mixed, kept, states, carry_out, s1, s2, carry):
    C = CHUNK
    s1[...] = jnp.zeros_like(s1)
    s2[...] = jnp.zeros_like(s2)
    carry[...] = jnp.zeros_like(carry)
    left = left_half(C)
    causal = causal_pair(C)
    same = same_head()
    lower = triangle(C).astype(BF16)
    zero = jnp.zeros((), BF16)

    def step(c, _):
        rows = chunk_rows(c)
        part = lambda n, j: qkvf[rows, 512 * n + PAIR * j : 512 * n + PAIR * (j + 1)]
        raw = [mm_nt(part(0, j), split_pair(part(1, j), left)) for j in PAIRS]
        carry_out[c] = carry[...]
        denom = mm(lower, qkvf[rows, 1536:2048]) + carry[0:1, :]
        carry[0:1, :] = denom[C - 1 :, :]
        rden_all = 1.0 / denom
        f2 = [split_pair(part(3, j), left) for j in PAIRS]
        numer = []
        for j in PAIRS:
            a2 = jnp.where(causal, raw[j].astype(BF16), zero)
            kept[rows, a_of(j)] = a2
            s1b = s1[j].astype(BF16)
            states[c, :, pair_of(j)] = s1b
            numer.append(mm(a2, f2[j]) + mm(part(0, j), s1b))
        g = []
        for j in PAIRS:
            rden = rden_all[:, pair_of(j)]
            s = numer[j] * rden * SCALE
            kept[rows, s_of(j)] = s.astype(BF16)
            e = jnp.exp(s - half_reduce(s, left, jnp.max, -jnp.inf))
            p = e / half_reduce(e, left, jnp.sum, 0.0)
            g.append((p * rden).astype(BF16))
            kept[rows, g_of(j)] = g[j]
        raw = [mm_nt(g[j], f2[j]) for j in PAIRS]
        for j in PAIRS:
            b2 = jnp.where(causal, raw[j].astype(BF16), zero)
            kept[rows, b_of(j)] = b2
            s2b = s2[j].astype(BF16)
            states[c, :, pair_of(4 + j)] = s2b
            o = mm(b2, split_pair(part(2, j), left)) + mm(g[j], s2b)
            mixed[rows, pair_of(j)] = o.astype(BF16)
        for j in PAIRS:
            s1[j] += jnp.where(same, mm_tn(part(1, j), part(3, j)), 0.0)
            s2[j] += jnp.where(same, mm_tn(part(3, j), part(2, j)), 0.0)
        return 0

    lax.fori_loop(0, qkvf.shape[0] // C, step, 0, unroll=UNROLL)


def state_scratch():
    return [pltpu.VMEM((4, PAIR, PAIR), F32), pltpu.VMEM((4, PAIR, PAIR), F32), pltpu.VMEM((8, 512), F32)]


def attention_forward(clock, qkvf):
    T = qkvf.shape[0]
    n = T // CHUNK
    outs = [shape((T, 512)), shape((T, KEPT)), shape((n, PAIR, 1024)), shape((n, 8, 512), F32)]
    return call(clock, forward_kernel, "attention_forward", outs, [qkvf], state_scratch())


def backward_kernel(first, count, last, _, qkvf, kept, states, carry_in, do_in, *refs):
    C = CHUNK
    r1, r2, carry = refs[-3:]
    begins, (grad, *ends) = (refs[:3], refs[3:-3]) if first < last else ((), refs[:-3])
    for ref, old in zip((r1, r2, carry), begins or (None,) * 3):
        ref[...] = jnp.zeros_like(ref) if old is None else old[...]
    left = left_half(C)
    causal = causal_pair(C)
    same = same_head()
    lower = triangle(C).astype(BF16)
    upper = lower.T
    upper2 = jnp.concatenate((upper, upper), axis=1)
    zero = jnp.zeros((), BF16)

    def step(t, _):
        c = first - t
        rows = chunk_rows(c)
        here = chunk_rows(count - 1 - t)
        part = lambda n, j: qkvf[rows, 512 * n + PAIR * j : 512 * n + PAIR * (j + 1)]
        do = [do_in[rows, pair_of(j)] for j in PAIRS]
        denoms = mm(lower, qkvf[rows, 1536:2048]) + carry_in[c][0:1, :]
        s1b = [states[c, :, pair_of(j)] for j in PAIRS]
        s2b = [states[c, :, pair_of(4 + j)] for j in PAIRS]
        r1b = [r1[j].astype(BF16) for j in PAIRS]
        r2b = [r2[j].astype(BF16) for j in PAIRS]
        g = [kept[rows, g_of(j)] for j in PAIRS]
        raw = [mm_nt(do[j], split_pair(part(2, j), left)) for j in PAIRS]
        f2 = [split_pair(part(3, j), left) for j in PAIRS]
        db2, dg, dn, dd = [], [], [], []
        for j in PAIRS:
            db2.append(jnp.where(causal, raw[j].astype(BF16), zero))
            dg.append(mm(db2[j], f2[j]) + mm_nt(do[j], s2b[j]))
        for j in PAIRS:
            dv2 = mm_tn(kept[rows, b_of(j)], do[j])
            dv = jnp.where(left, dv2[:C], dv2[C:]) + mm(part(3, j), r2b[j])
            grad[here, 1024 + PAIR * j : 1024 + PAIR * (j + 1)] = dv.astype(BF16)
        for j in PAIRS:
            denom = denoms[:, pair_of(j)]
            rden = 1.0 / denom
            p = g[j].astype(F32) * denom
            dpp = dg[j] * rden * p
            ds = dpp - p * half_reduce(dpp, left, jnp.sum, 0.0)
            dd.append(-(dpp + ds * kept[rows, s_of(j)].astype(F32)) * rden)
            dn.append((ds * SCALE * rden).astype(BF16))
        raw = [mm_nt(dn[j], f2[j]) for j in PAIRS]
        for j in PAIRS:
            df2 = mm_tn(db2[j], g[j]) + mm_tn(kept[rows, a_of(j)], dn[j])
            hi = dd[j].astype(BF16)
            lo = (dd[j] - hi.astype(F32)).astype(BF16)
            df = jnp.where(left, df2[:C], df2[C:]) + mm_nt(part(2, j), r2b[j]) + mm(part(1, j), r1b[j])
            df = df + mm(upper2, jnp.concatenate((hi, lo), axis=0)) + carry[0:1, pair_of(j)]
            grad[here, 1536 + PAIR * j : 1536 + PAIR * (j + 1)] = (df * part(3, j).astype(F32)).astype(BF16)
            carry[0:1, pair_of(j)] += jnp.sum(dd[j], axis=0, keepdims=True)
        for j in PAIRS:
            da2 = jnp.where(causal, raw[j].astype(BF16), zero)
            dq = mm(da2, split_pair(part(1, j), left)) + mm_nt(dn[j], s1b[j])
            grad[here, pair_of(j)] = dq.astype(BF16)
            dk2 = mm_tn(da2, part(0, j))
            dk = jnp.where(left, dk2[:C], dk2[C:]) + mm_nt(part(3, j), r1b[j])
            grad[here, 512 + PAIR * j : 512 + PAIR * (j + 1)] = dk.astype(BF16)
        for j in PAIRS:
            r1[j] += jnp.where(same, mm_tn(part(0, j), dn[j]), 0.0)
            r2[j] += jnp.where(same, mm_tn(g[j], do[j]), 0.0)
        return 0

    lax.fori_loop(0, count, step, 0, unroll=UNROLL)
    for ref, end in zip((r1, r2, carry), ends):
        end[...] = ref[...]


def attention_backward(clock, qkvf, saved, d_o, first, count, states=()):
    rows = count * CHUNK
    outs = [shape((rows, 2048))]
    if first - count >= 0:
        outs += [shape((4, PAIR, PAIR), F32), shape((4, PAIR, PAIR), F32), shape((8, 512), F32)]
    kernel = functools.partial(backward_kernel, first, count, qkvf.shape[0] // CHUNK - 1)
    return call(clock, kernel, "attention_backward", outs, [qkvf, *saved, d_o, *states], state_scratch())


def gelu_parts(v):
    c = 0.7978845608028654
    k = c * 0.044715
    v2 = v * v
    half = 0.5 * jnp.tanh(v * (c + k * v2)) + 0.5
    act = v * half
    return act, half + act * (1.0 - half) * (2 * c + (6 * k) * v2)


def middle_kernel(token, tokens, mixed, *refs):
    wo, packs, (resid_out, n2_out, r2_out, a2_out, scr) = refs[:4], refs[4:8], refs[8:]
    blocks = blocks_of(token)
    gain, shift = vector(packs, 256, 128), vector(packs, 384, 128)

    def body(rows):
        resid = tokens[rows, :].astype(F32) + mm(take_blocks(mixed, rows, blocks, 128), stack(wo))
        resid_out[rows, :] = resid
        n2, r2 = stats(resid)
        scr[...] = n2
        n2 = take_blocks(scr, slice(None), blocks, 128)
        n2_out[rows, :] = n2.astype(BF16)
        r2_out[rows, :] = jnp.broadcast_to(r2, (ROWS, 128))
        a2_out[rows, :] = (n2 * gain + shift).astype(BF16)

    row_loop(tokens.shape[0], body)


def middle(clock, tokens, mixed, wo, packs):
    T = tokens.shape[0]
    outs = [shape((T, 512), F32), shape((T, 512)), shape((T, 128), F32), shape((T, 512))]
    return call(clock, middle_kernel, "middle", outs, [tokens, mixed, *wo, *packs], [pltpu.VMEM((ROWS, 512), F32)])


def ffn_inner_kernel(token, a2_ref, *refs):
    wi, packs, (act_out, slope_out) = refs[:-6], refs[-6:-2], refs[-2:]
    cols = wide(blocks_of(token), 512)

    def body(rows):
        a2 = a2_ref[rows, :]
        inner = mm(a2, stack(wi, cols[0]))
        for i in range(4):
            after = mm(a2, stack(wi, cols[i + 1])) if i < 3 else None
            act, slope = gelu_parts(inner + packs[i][128:129, 640:1152].astype(F32))
            act_out[rows, 512 * i : 512 * (i + 1)] = act.astype(BF16)
            slope_out[rows, cols[i]] = slope.astype(BF16)
            inner = after

    row_loop(a2_ref.shape[0], body)


def ffn_inner(clock, a2, wi, packs):
    T = a2.shape[0]
    return call(clock, ffn_inner_kernel, "ffn_inner", [shape((T, 2048)), shape((T, 2048))], [a2, *wi, *packs])


def outer_grad_kernel(_, act, dy, keep, send):
    for i in range(4):
        out = mm_tn(act[:, 512 * i : 512 * (i + 1)], dy[...]).astype(BF16)
        (keep if i < 2 else send)[i % 2] = out


def outer_grad(clock, act, dy):
    return call(clock, outer_grad_kernel, "outer_grad", [shape((2, 512, 512))] * 2, [act, dy])


def ffn_outer_kernel(token, resid, act, *refs):
    wu, vs, (out, bias, result, sem) = refs[:4], refs[4:8], refs[8:]
    put_blocks(bias, slice(None), jnp.broadcast_to(vector(vs, 512, 128), (8, 512)), blocks_of(token), 128)
    total = mm(act[...], stack(wu))
    result[...] = (total + resid[...] + bias[0:1, :]).astype(BF16)
    copy = pltpu.make_async_copy(result, out, sem)
    copy.start()
    copy.wait()


def ffn_outer(clock, resid, act, wu, vecs):
    scratch = [pltpu.VMEM((8, 512), F32), pltpu.VMEM(resid.shape, BF16), pltpu.SemaphoreType.DMA]
    return call(clock, ffn_outer_kernel, "ffn_outer", [shape(resid.shape)], [resid, act, *wu, *vecs], scratch, outside=(0,))[0]


def inner_back_kernel(token, dy, slope, u0, u1, u2, u3, din, sums):
    cols = wide(blocks_of(token), 512)
    sums[...] = jnp.zeros_like(sums)
    sums[1:2, 0:512] = jnp.sum(dy[...].astype(F32), axis=0, keepdims=True)
    for i, u in enumerate((u0, u1, u2, u3)):
        d = (mm_nt(dy[...], u[...]) * slope[:, cols[i]].astype(F32)).astype(BF16)
        din[:, cols[i]] = d
        sums[0:1, cols[i]] = jnp.sum(d.astype(F32), axis=0, keepdims=True)


def inner_back(clock, dy, slope, wu):
    T = dy.shape[0]
    return call(clock, inner_back_kernel, "inner_back", [shape((T, 2048)), shape((8, 2048), F32)], [dy, slope, *wu], aliases={1: 0})


def inner_grad_kernel(n2, din, sums, keep, send):
    tail = jnp.concatenate((sums[...], jnp.zeros_like(sums)), axis=0).astype(BF16)
    for i in range(4):
        dest = keep if i < 2 else send
        dest[i % 2, 0:128, :] = mm_tn(n2[:, 128 * i : 128 * (i + 1)], din[...]).astype(BF16)
        dest[i % 2, 128:144, :] = tail


def resid_back_kernel(token, dy, n2, r2, din, sums, *refs):
    wo, wi, packs = refs[:4], refs[4:-9], refs[-9:-5]
    keep, send, dres_out, do_out, scr = refs[-5:]
    inner_grad_kernel(n2, din, sums, keep, send)
    blocks = blocks_of(token)
    gain = vector(packs, 256, 128)

    def body(rows):
        da2 = mm_nt(din[rows, :], stack(wi))
        put_blocks(scr, slice(None), norm_back(da2 * gain, n2[rows, :].astype(F32), r2[rows, 0:1]), blocks, 128)
        dres = dy[rows, :].astype(F32) + scr[...]
        dres_out[rows, :] = dres
        d_o = mm_nt(dres.astype(BF16), stack(wo))
        put_blocks(do_out, rows, d_o.astype(BF16), blocks, 128)

    row_loop(dy.shape[0], body)


def resid_back(clock, dy, n2, r2, din, sums, wo, wi, packs):
    T = dy.shape[0]
    outs = [shape((2, 144, 2048))] * 2 + [shape((T, 512), F32), shape((T, 512))]
    return call(clock, resid_back_kernel, "resid_back", outs, [dy, n2, r2, din, sums, *wo, *wi, *packs], [pltpu.VMEM((ROWS, 512), F32)])


def project_grad_kernel(token, n1, early, late, mixed, dres, *dests):
    half = early.shape[0]
    blocks = wide(blocks_of(token), 128)
    for keep, send, start in ((*dests[:2], 0), (*dests[2:], 1024)):
        cols = slice(start, start + 1024)
        out = (mm_tn(n1[0:half, :], early[:, cols]) + mm_tn(n1[half:, :], late[:, cols])).astype(BF16)
        total = sum(jnp.sum(r[:, cols].astype(F32), axis=0, keepdims=True) for r in (early, late))
        tail = jnp.broadcast_to(total, (16, 1024)).astype(BF16)
        for i in range(4):
            dest = keep if i < 2 else send
            dest[i % 2, 0:128, 0:1024] = out[128 * i : 128 * (i + 1)]
            dest[i % 2, 128:144, 0:1024] = tail
    keep, send = dests[:2]
    d = dres[...].astype(BF16)
    for i in range(4):
        dest = keep if i < 2 else send
        dest[i % 2, 0:128, 1024:] = mm_tn(mixed[:, blocks[i]], d).astype(BF16)
        dest[i % 2, 128:144, 1024:] = jnp.zeros((16, 512), BF16)


def project_grad(clock, n1, early, late, mixed, dres):
    outs = [shape((2, 144, 1536))] * 2 + [shape((2, 144, 1024))] * 2
    keep_a, send_a, keep_b, send_b = call(clock, project_grad_kernel, "project_grad", outs, [n1, early, late, mixed, dres])
    return (keep_a, send_a), (keep_b, send_b)


def input_grad_kernel(token, tokens, early, late, dres, p0, p1, p2, p3, out, scr, result, sems):
    packs = (p0, p1, p2, p3)
    blocks = blocks_of(token)
    gain = vector(packs, 0, 128)
    w = stack_packs(packs, slice(0, 2048))
    copies = []
    for h, d in enumerate((early, late)):
        rows = slice(ROWS * h, ROWS * (h + 1))
        e = mm_nt(d[...], w) * gain
        n1, r1 = stats(tokens[rows, :].astype(F32))
        scr[...] = n1
        put_blocks(scr, slice(None), norm_back(e, take_blocks(scr, slice(None), blocks, 128), r1), blocks, 128)
        result[rows, :] = (dres[rows, :] + scr[...]).astype(BF16)
        copies.append(pltpu.make_async_copy(result.at[rows, :], out.at[rows, :], sems.at[h]))
        copies[-1].start()
    for copy in copies:
        copy.wait()


def input_grad(clock, tokens, early, late, dres, packs):
    scratch = [pltpu.VMEM((ROWS, 512), F32), pltpu.VMEM(dres.shape, BF16), pltpu.SemaphoreType.DMA((2,))]
    return call(clock, input_grad_kernel, "input_grad", [shape(dres.shape)], [tokens, early, late, dres, *packs], scratch, outside=(0,))[0]


def exchange(value, axis, size, mask):
    return lax.ppermute(value, axis, [(i, i ^ mask) for i in range(size)])


def over_x(value):
    return exchange(value, "fsdp", 4, 2)


def over_core(value):
    return exchange(value, "fsdp", 4, 1)


def add(a, b):
    return a.astype(F32) + b.astype(F32)


def half_at(bit, width):
    return pl.ds(pl.multiple_of(bit * (width // 2), width // 2), width // 2)


def gate_kernel(*refs):
    pass


def gate(clock, waited, values):
    n = len(waited)
    outs = [shape(v.shape, v.dtype) for v in values]
    return call(clock, gate_kernel, "gate", outs, [*waited, *values], limit=1, aliases={n + k: k for k in range(len(values))})


def join_core_kernel(_, keep, got, mine, *pieces):
    mine[...] = add(keep[0], got[0]).astype(BF16)
    start = 0
    for piece in pieces:
        rows = slice(start, start + piece.shape[0])
        piece[...] = add(keep[1, rows, :], got[1, rows, :]).astype(BF16)
        start += piece.shape[0]


def join_kernel(split, place, token, keep, *refs):
    outs_at = len(refs) - (1 if split is None else 3)
    gots, refs = refs[:outs_at], refs[outs_at:]
    if place is not None:
        out = refs[0]
        bit = lax.rem(lax.div(position(token, 1), place), 2)
        out[:, half_at(bit, out.shape[1])] = keep[...]
        out[:, half_at(1 - bit, out.shape[1])] = gots[0][...]
        return
    whole = refs[-1]
    start = 0
    for got in gots:
        rows = slice(start, start + got.shape[0])
        whole[rows, :] = add(keep[rows, :], got[...]).astype(BF16)
        start += got.shape[0]
    if split is not None:
        mine, send, _ = refs
        bit = lax.rem(lax.div(position(token, 1), split), 2)
        mine[...] = whole[:, half_at(bit, whole.shape[1])]
        send[...] = whole[:, half_at(1 - bit, whole.shape[1])]


class Chain:
    def __init__(self, clock, dp, halved, pieces, pair):
        self.clock, self.dp, self.pieces = clock, dp, pieces
        masks = [1 << k for k in range(dp.bit_length() - 1)]
        self.todo = [("core", 0), ("x", 0)] + [("half" if m in halved else "all", m) for m in masks] + [("beside", m) for m in reversed(masks) if m in halved]
        self.keep, self.send = pair
        self.busy = True

    def launch(self):
        self.kind, self.mask = self.todo.pop(0)
        if self.kind == "core":
            self.got = [over_core(self.send)]
        elif self.kind == "x":
            self.got = [over_x(self.send.pop(0))]
        else:
            self.got = [exchange(self.send, "dp", self.dp, self.mask)]

    def more(self, *others):
        piece, *sends = gate(self.clock, [self.got[-1]], [self.send.pop(0)] + [c.send for c in others])
        self.got.append(over_x(piece))
        for chain, send in zip(others, sends):
            chain.send = send
            chain.launch()

    def step(self):
        rows, width = self.keep.shape[-2:]
        if self.kind == "core":
            outs = [shape((rows, width))] + [shape((n, width)) for n in self.pieces]
            self.keep, *self.send = call(self.clock, join_core_kernel, "join_core", outs, [self.keep, *self.got], limit=JOIN)
        else:
            split = self.todo[0][1] if self.todo and self.todo[0][0] == "half" else None
            place = self.mask if self.kind == "beside" else None
            kernel = functools.partial(join_kernel, split, place)
            if split is None:
                outs, scratch = [shape((rows, 2 * width if place else width))], []
            else:
                outs, scratch = [shape((rows, width // 2))] * 2, [pltpu.VMEM((rows, width), BF16)]
            out = call(self.clock, kernel, "join", outs, [self.keep, *self.got], scratch, limit=JOIN)
            self.keep, self.send = out if split else (out[0], out[0])
        self.busy = bool(self.todo)
        if self.busy:
            self.launch()


def column(row):
    r = lax.broadcasted_iota(jnp.int32, (128, 128), 0)
    c = lax.broadcasted_iota(jnp.int32, (128, 128), 1)
    return jnp.sum(jnp.where(r == c, row, 0.0), axis=1, keepdims=True)


def as_row(col):
    r = lax.broadcasted_iota(jnp.int32, (128, 128), 0)
    c = lax.broadcasted_iota(jnp.int32, (128, 128), 1)
    return jnp.sum(jnp.where(r == c, col, 0.0), axis=0, keepdims=True)


def send_out(pairs, sems):
    copies = [pltpu.make_async_copy(src, dst, sems.at[k]) for k, (src, dst) in enumerate(pairs)]
    for copy in copies:
        copy.start()
    for copy in copies:
        copy.wait()


def finish_outer_kernel(_, u, out, buf, sems):
    buf[...] = u[...].astype(F32)
    send_out([(buf, out)], sems)


def finish_outer(clock, u):
    return call(clock, finish_outer_kernel, "finish_outer", [shape(u.shape, F32)], [u], [pltpu.VMEM(u.shape, F32), pltpu.SemaphoreType.DMA((1,))], limit=JOIN, outside=(0,))[0]


def finish_inner_kernel(token, total, w, pack, out, gain_out, shift_out, inner_out, outer_out, buf, small, sems):
    gain, shift = (column(pack[128:129, k : k + 128].astype(F32)) for k in (256, 384))
    m = total[0:128, :].astype(F32)
    tail = total[128:144, :].astype(F32)
    buf[...] = gain * m + shift * tail[0:1, :]
    wf = w[...].astype(F32)
    small[0:1, 0:128] = as_row(jnp.sum(wf * m, axis=1, keepdims=True))
    small[1:2, 0:128] = as_row(jnp.sum(wf * tail[0:1, :], axis=1, keepdims=True))
    me = position(token, 0)
    small[2:3, :] = total[128:144, pl.ds(pl.multiple_of(me * 512, 512), 512)].astype(F32)[0:1, :]
    small[3:4, 0:128] = total[128:144, pl.ds(pl.multiple_of(me * 128, 128), 128)].astype(F32)[1:2, :]
    send_out([(buf, out), (small.at[0, 0:128], gain_out), (small.at[1, 0:128], shift_out), (small.at[2], inner_out), (small.at[3, 0:128], outer_out)], sems)


def finish_inner(clock, total, w, pack):
    outs = [shape((128, 2048), F32), shape((128,), F32), shape((128,), F32), shape((512,), F32), shape((128,), F32)]
    scratch = [pltpu.VMEM((128, 2048), F32), pltpu.VMEM((8, 512), F32), pltpu.SemaphoreType.DMA((5,))]
    return call(clock, finish_inner_kernel, "finish_inner", outs, [total, w, pack], scratch, limit=JOIN, outside=range(5))


def project_parts(total, pack, start, buf):
    gain, shift = (column(pack[128:129, k : k + 128].astype(F32)) for k in (0, 128))
    m = total[0:128, 0:1024].astype(F32)
    tail = total[128:144, 0:1024].astype(F32)[0:1, :]
    buf[:, 0:1024] = gain * m + shift * tail
    w = pack[0:128, start : start + 1024].astype(F32)
    return as_row(jnp.sum(w * m, axis=1, keepdims=True)), as_row(jnp.sum(w * tail, axis=1, keepdims=True))


def finish_first_kernel(_, total, pack, out0, out1, out2, before, buf, sems):
    gain, shift = project_parts(total, pack, 0, buf)
    buf[:, 1024:1536] = total[0:128, 1024:1536].astype(F32)
    before[0:1, :] = gain
    before[1:2, :] = shift
    send_out([(buf.at[:, 512 * n : 512 * (n + 1)], out) for n, out in enumerate((out0, out1, out2))], sems)


def finish_first(clock, total, pack):
    outs = [shape((128, 512), F32)] * 3 + [shape((8, 128), F32)]
    scratch = [pltpu.VMEM((128, 1536), F32), pltpu.SemaphoreType.DMA((3,))]
    return call(clock, finish_first_kernel, "finish_first", outs, [total, pack], scratch, limit=JOIN, outside=range(3))


def finish_last_kernel(_, total, pack, before, out0, out1, gain_out, shift_out, buf, small, sems):
    gain, shift = project_parts(total, pack, 1024, buf)
    small[0:1, :] = before[0:1, :] + gain
    small[1:2, :] = before[1:2, :] + shift
    send_out([(buf.at[:, 0:512], out0), (buf.at[:, 512:1024], out1), (small.at[0], gain_out), (small.at[1], shift_out)], sems)


def finish_last(clock, total, pack, before):
    outs = [shape((128, 512), F32)] * 2 + [shape((128,), F32)] * 2
    scratch = [pltpu.VMEM((128, 1024), F32), pltpu.VMEM((8, 128), F32), pltpu.SemaphoreType.DMA((4,))]
    return call(clock, finish_last_kernel, "finish_last", outs, [total, pack, before], scratch, limit=JOIN, outside=range(4))


def per_device(dp, tokens, first_gain, first_shift, w_query, w_key, w_value, w_control, w_output, second_gain, second_shift, w_inner, inner_bias, w_outer, outer_bias, cotangent):
    clock = Clock(lax.axis_index("fsdp").astype(jnp.int32), lax.axis_index("dp").astype(jnp.int32))
    vectors = (first_gain, first_shift, second_gain, second_shift, outer_bias, inner_bias)
    own, first, second, wi0, wi1 = begin(clock, (w_query, w_key, w_value, w_control), vectors, w_inner)
    mine = [over_x(first), over_x(second)]
    own_core, wi_c = over_core(own), over_core(w_inner)
    n1, n1_low = first_norm(clock, tokens)
    *mine, wi0, wi1, w_output = clock.sync(*mine, wi0, wi1, w_output)
    wi_x0 = over_x(wi0)
    across = assemble(clock, mine, [exchange(v, "dp", dp, 1) for v in mine], wi_x0)
    packs = [own, across, own_core, over_core(across)]
    wi1, w_output = clock.sync(wi1, w_output)
    wi_x1, wo_x, wo_c = over_x(wi1), over_x(w_output), over_core(w_output)
    qkvf = project(clock, n1, packs)
    mixed, *saved = attention_forward(clock, qkvf)
    wo_x, wi_x1, w_outer = clock.sync(wo_x, wi_x1, w_outer)
    wo = [w_output, wo_x, wo_c, over_core(wo_x)]
    wi = [w_inner, wi_x0, wi_x1, wi_c, over_core(wi_x0), over_core(wi_x1)]
    wu_x, wu_c = over_x(w_outer), over_core(w_outer)
    resid, n2, r2, a2 = middle(clock, tokens, mixed, wo, packs)
    act, slope = ffn_inner(clock, a2, wi, packs)
    u = Chain(clock, dp, (1, 2), (272, 240), outer_grad(clock, act, cotangent))
    u.launch()
    wu_x = clock.sync(wu_x)
    wu = [w_outer, wu_x, wu_c, over_core(wu_x)]
    din, sums = inner_back(clock, cotangent, slope, wu)
    u.step()
    *pair, dres, d_o = resid_back(clock, cotangent, n2, r2, din, sums, wo, wi, packs)
    i = Chain(clock, dp, (1, 2), (48, 32, 64), pair)
    u.more(i)
    early = attention_backward(clock, qkvf, saved, d_o, 7, 4)
    u.step()
    i.step()
    late = attention_backward(clock, qkvf, saved, d_o, 3, 4, early[1:])
    i.more()
    u.step()
    pair_a, pair_b = project_grad(clock, n1_low, late[0], early[0], mixed, dres)
    a, b = Chain(clock, dp, (1, 2), (144,), pair_a), Chain(clock, dp, (1,), (144,), pair_b)
    u.step()
    i.more(a, b)
    a.step()
    grad_tokens = input_grad(clock, tokens, late[0], early[0], dres, packs)
    for c in (u, b, i):
        c.step()
    output = ffn_outer(clock, resid, act, wu, packs)
    order = [a, u, i, a, i, b, a, u, b, i, a, b, i, a, i, b, a, b]
    while any(c.busy for c in (u, i, a, b)):
        c = order.pop(0) if order else next(c for c in (u, i, a, b) if c.busy)
        if not c.busy:
            continue
        c.step()
        if not c.busy and c is u:
            grad_outer = finish_outer(clock, u.keep)
        elif not c.busy and c is i:
            grad_inner, *vectors = finish_inner(clock, i.keep, w_inner, packs[0])
        elif not c.busy and c is a:
            grad_query, grad_key, grad_output, before = finish_first(clock, a.keep, packs[0])
    grad_value, grad_control, first_gain_grad, first_shift_grad = finish_last(clock, b.keep, packs[0], before)
    second_gain_grad, second_shift_grad, inner_bias_grad, outer_bias_grad = vectors
    return (
        output, grad_tokens, first_gain_grad, first_shift_grad, grad_query, grad_key, grad_value, grad_control,
        grad_output, second_gain_grad, second_shift_grad, grad_inner, inner_bias_grad, grad_outer, outer_bias_grad,
    )


def solution(mesh):
    row, vec, mat = P(("dp", "fsdp"), None), P("fsdp"), P("fsdp", None)
    return jax.shard_map(
        functools.partial(per_device, mesh.shape["dp"]),
        mesh=mesh,
        in_specs=(row, vec, vec, mat, mat, mat, mat, mat, vec, vec, mat, vec, mat, vec, row),
        out_specs=(row, row, vec, vec, mat, mat, mat, mat, mat, vec, vec, mat, vec, mat, vec),
        check_vma=False,
    )
```

time: 182 us -> 159 us (0.87)
  Pallas kernels: 83.8 us -> 64.6 us
  waiting for transfers between devices: 43.2 us -> 52.9 us
  starting transfers between devices: 47.4 us -> 38.4 us
  local copies, waits for them, and re-layouts: 6.74 us -> 1.32 us
    pallas_call x45 -> x49, Pallas kernels: 83.8 us -> 64.6 us  [call(): pl.pallas_call(body, in_specs=[VM] + [ANY if k in raw else VM for k in ra...]
    ppermute x50 -> x47, waiting for transfers between devices: 43.2 us -> 52.9 us  [exchange(): return lax.ppermute(value, axis, [(i, i ^ mask) for i in range(size)])]
    ppermute x50 -> x47, starting transfers between devices: 47.4 us -> 38.4 us  [exchange(): return lax.ppermute(value, axis, [(i, i ^ mask) for i in range(size)])]
    unnamed x34 -> x12, local copies, waits for them, and re-layouts: 6.22 us -> 1.25 us
  transfers between devices with their start and end apart: 50 -> 47, of which waited for: 24 -> 22; matrix products, arithmetic and copies ran while one was open for 0% -> 0% of each run, Pallas kernels for 37% -> 38%
where the time goes in v3:
time: 159 us
  Pallas kernels  64.6 us (41%)
  waiting for transfers between devices  52.9 us (33%)
  starting transfers between devices  38.4 us (24%)
    pallas_call x49, Pallas kernels, call(): pl.pallas_call(body, in_specs=[VM] + [ANY if k in raw else VM for k in ra...  64.6 us
    ppermute x47, waiting for transfers between devices, exchange(): return lax.ppermute(value, axis, [(i, i ^ mask) for i in range(size)])  52.9 us
    ppermute x47, starting transfers between devices, exchange(): return lax.ppermute(value, axis, [(i, i ^ mask) for i in range(size)])  38.4 us
  transfers between devices with their start and end apart: 47, of which 22 were waited for; matrix products, arithmetic and copies ran while one was open for 0% of the time, Pallas kernels for 38%

profile of v3, /device:TPU:0, one launch (start us, length us, event | category | flops | bytes accessed | tf_op | source)
XLA Modules:
  0.0 158.6 jit_solution(10558532024197409993)
XLA Ops:
  0.8 1.7 %begin.1 = (bf16[144,2048]{1,0:T(8,128)(2,1)S(1)}, bf16[144,512]{1,0:T(8,128)(2,1)S(1)}, bf16[144,512]{1,0:T(8,128)(2,1)S(1)}, bf16[64,2048]{1,0:T(8,128)(2,1)S(...) custom-call(s32[8,128]{1,0:T(8,128)S(1)} %iota.7.token, bf16[128,512]{1,0:T(8,128)(2,1)} %refs_0_.6, ...), custom_call_target="tpu_custom_call" | custom-call | flops 1000 | bytes 1024 | tf_op jit(solution)/shard_map/begin/pallas_call | solution.py:63
  2.5 3.0 %collective-permute-start = (bf16[144,512]{1,0:T(8,128)(2,1)S(1)}, bf16[144,512]{1,0:T(8,128)(2,1)S(1)}, u32[]{:S(2)}, u32[]{:S(2)}) collective-permute-start(bf16[144,512]{1,0:T(8,128)(2,1)S(1)} %get-tuple-element.179), channel_id=1, source_target_pairs={{0,2},{1,3},{2,0},{3,1},{4,6},{5,7},{6,4},{7,5},{8,10},{9,11},{10,... | collective-permute-start | bytes 442376 | tf_op jit(solution)/shard_map/ppermute | solution.py:575
  8.0 2.2 %collective-permute-done.refs_0_ = bf16[144,512]{1,0:T(8,128)(2,1)S(1)} collective-permute-done((bf16[144,512]{1,0:T(8,128)(2,1)S(1)}, bf16[144,512]{1,0:T(8,128)(2,1)S(1)}, u32[]{:S(2)}, u32[]{:S(2)}) %collective-permute-start) | collective-permute-done | bytes 147488 | tf_op jit(solution)/shard_map/ppermute | solution.py:575
  10.2 2.3 %collective-permute-done.1.refs_1_ = bf16[144,512]{1,0:T(8,128)(2,1)S(1)} collective-permute-done((bf16[144,512]{1,0:T(8,128)(2,1)S(1)}, bf16[144,512]{1,0:T(8,128)(2,1)S(1)}, u32[]{:S(2)}, u32[]{:S(2)}) %collective-permute-start.1) | collective-permute-done | bytes 147488 | tf_op jit(solution)/shard_map/ppermute | solution.py:575
  12.5 1.7 %collective-permute-start.4 = (bf16[64,2048]{1,0:T(8,128)(2,1)S(1)}, bf16[64,2048]{1,0:T(8,128)(2,1)S(1)}, u32[]{:S(2)}, u32[]{:S(2)}) collective-permute-start(bf16[64,2048]{1,0:T(8,128)(2,1)S(1)} %get-tuple-element.186), channel_id=1, source_target_pairs={{0,2},{1,3},{2,0},{3,1},{4,6},{5,7},{6,4},{7,5},{8,10},{9,11},{10,... | collective-permute-start | bytes 786440 | tf_op jit(solution)/shard_map/ppermute | solution.py:575
  16.3 4.0 %collective-permute-done.2.refs_2_ = bf16[144,512]{1,0:T(8,128)(2,1)S(1)} collective-permute-done((bf16[144,512]{1,0:T(8,128)(2,1)S(1)}, bf16[144,512]{1,0:T(8,128)(2,1)S(1)}, u32[]{:S(2)}, u32[]{:S(2)}) %collective-permute-start.2) | collective-permute-done | bytes 147488 | tf_op jit(solution)/shard_map/ppermute | solution.py:575
  24.5 2.4 %project.1 = (bf16[1024,2048]{1,0:T(8,128)(2,1)S(1)}, s32[8,128]{1,0:T(8,128)S(1)}) custom-call(s32[8,128]{1,0:T(8,128)S(1)} %get-tuple-element.190.token, f32[1024,512]{1,0:T(8,128)S(1)} %get-tuple-element.191.refs_0_, bf16[144,2048]{1,0:T(8,128)(2,1)S(1)} %get-tuple-element.192.refs_1_.refs_6_.refs_7_.refs_15_.refs_4_.refs_2_, ...), custom_call_target="tpu_custom_call" | custom-call | flops 1000 | bytes 1024 | tf_op jit(solution)/shard_map/project/pallas_call | solution.py:63
  26.9 7.4 %attention_forward.1 = (bf16[1024,512]{1,0:T(8,128)(2,1)S(1)}, bf16[1024,3072]{1,0:T(8,128)(2,1)S(1)}, bf16[8,128,1024]{2,1,0:T(8,128)(2,1)S(1)}, f32[8,8,512]{2,1,0:T(8,128)S(1)}, s32[8,128]{1,0:T(8,128)S(1)}) custom-call(s32[8,128]{1,0:T(8,128)S(1)} %get-tuple-element.194.token, bf16[1024,2048]{1,0:T(8,128)(2,1)S(1)} %get-tuple-element.195.refs_0_), custom_call_target="tpu_custom_call" | custom-call | flops 1000 | bytes 1024 | tf_op jit(solution)/shard_map/attention_forward/pallas_call | solution.py:63
  36.8 2.0 %middle.1 = (f32[1024,512]{1,0:T(8,128)S(1)}, bf16[1024,512]{1,0:T(8,128)(2,1)S(1)}, f32[1024,128]{1,0:T(8,128)S(1)}, bf16[1024,512]{1,0:T(8,128)(2,1)S(1)}, s32[8,128]{1,0:T(8,128)S(1)}) custom-call(s32[8,128]{1,0:T(8,128)S(1)} %get-tuple-element.199.token, bf16[1024,512]{1,0:T(8,128)(2,1)S(1)} %copy-done.1, ...), custom_call_target="tpu_custom_call" | custom-call | flops 1000 | bytes 1024 | tf_op jit(solution)/shard_map/middle/pallas_call | solution.py:63
  38.9 6.2 %ffn_inner.1 = (bf16[1024,2048]{1,0:T(8,128)(2,1)S(1)}, bf16[1024,2048]{1,0:T(8,128)(2,1)S(1)}, s32[8,128]{1,0:T(8,128)S(1)}) custom-call(s32[8,128]{1,0:T(8,128)S(1)} %get-tuple-element.202.token, bf16[1024,512]{1,0:T(8,128)(2,1)S(1)} %get-tuple-element.203.refs_0_, bf16[128,2048]{1,0:T(8,128)(2,1)S(1)} %copy-done.3, ...), custom_call_target="tpu_custom_call" | custom-call | flops 1000 | bytes 1024 | tf_op jit(solution)/shard_map/ffn_inner/pallas_call | solution.py:63
  45.1 2.4 %outer_grad.1 = (bf16[2,512,512]{2,1,0:T(8,128)(2,1)S(1)}, bf16[2,512,512]{2,1,0:T(8,128)(2,1)S(1)}, s32[8,128]{1,0:T(8,128)S(1)}) custom-call(s32[8,128]{1,0:T(8,128)S(1)} %get-tuple-element.205.token, bf16[1024,2048]{1,0:T(8,128)(2,1)S(1)} %get-tuple-element.206.refs_0_.refs_1_, bf16[1024,512]{1,0:T(8,128)(2,1)S(1)} %copy-done.2), custom_call_target="tpu_custom_call" | custom-call | flops 1000 | bytes 1024 | tf_op jit(solution)/shard_map/outer_grad/pallas_call | solution.py:63
  48.0 2.3 %collective-permute-done.14.refs_3_ = bf16[512,512]{1,0:T(8,128)(2,1)S(1)} collective-permute-done((bf16[512,512]{1,0:T(8,128)(2,1)S(1)}, bf16[512,512]{1,0:T(8,128)(2,1)S(1)}, u32[]{:S(2)}, u32[]{:S(2)}) %collective-permute-start.14) | collective-permute-done | bytes 524320 | tf_op jit(solution)/shard_map/ppermute | solution.py:575
  52.2 2.9 %inner_back.1 = (bf16[1024,2048]{1,0:T(8,128)(2,1)S(1)}, f32[8,2048]{1,0:T(8,128)S(1)}, s32[8,128]{1,0:T(8,128)S(1)}) custom-call(s32[8,128]{1,0:T(8,128)S(1)} %get-tuple-element.209.token, bf16[1024,512]{1,0:T(8,128)(2,1)S(1)} %copy-done.2, bf16[1024,2048]{1,0:T(8,128)(2,1)S(1)} %get-tuple-element.210.refs_1_, ...), custom_call_target="tpu_custom_call", output_to_operand_aliasing={{0}: (2, {})} | custom-call | flops 1000 | bytes 1024 | tf_op jit(solution)/shard_map/inner_back/pallas_call | solution.py:63
  56.3 6.7 %resid_back.1 = (bf16[2,144,2048]{2,1,0:T(8,128)(2,1)S(1)}, bf16[2,144,2048]{2,1,0:T(8,128)(2,1)S(1)}, f32[1024,512]{1,0:T(8,128)S(1)}, bf16[1024,512]{1,0:T(8,128)(2,1)S(1)}, s32[8,128]{1,0:T(8,128)S(1)}) custom-call(s32[8,128]{1,0:T(8,128)S(1)} %get-tuple-element.215.token, bf16[1024,512]{1,0:T(8,128)(2,1)S(1)} %copy-done.2, ...), custom_call_target="tpu_custom_call" | custom-call | flops 1000 | bytes 1024 | tf_op jit(solution)/shard_map/resid_back/pallas_call | solution.py:63
  65.0 5.2 %attention_backward.2 = (bf16[512,2048]{1,0:T(8,128)(2,1)S(1)}, f32[4,128,128]{2,1,0:T(8,128)S(1)}, f32[4,128,128]{2,1,0:T(8,128)S(1)}, f32[8,512]{1,0:T(8,128)S(1)}, s32[8,128]{1,0:T(8,128)S(1)}) custom-call(s32[8,128]{1,0:T(8,128)S(1)} %get-tuple-element.224.token, bf16[1024,2048]{1,0:T(8,128)(2,1)S(1)} %get-tuple-element.195.refs_0_, ...), custom_call_target="tpu_custom_call" | custom-call | flops 1000 | bytes 1024 | tf_op jit(solution)/shard_map/attention_backward/pallas_call | solution.py:63
  70.2 2.3 %collective-permute-done.19.refs_2_ = bf16[240,512]{1,0:T(8,128)(2,1)S(1)} collective-permute-done((bf16[240,512]{1,0:T(8,128)(2,1)S(1)}, bf16[240,512]{1,0:T(8,128)(2,1)S(1)}, u32[]{:S(2)}, u32[]{:S(2)}) %collective-permute-start.19) | collective-permute-done | bytes 245792 | tf_op jit(solution)/shard_map/ppermute | solution.py:575
  75.7 5.4 %attention_backward.3 = (bf16[512,2048]{1,0:T(8,128)(2,1)S(1)}, s32[8,128]{1,0:T(8,128)S(1)}) custom-call(s32[8,128]{1,0:T(8,128)S(1)} %get-tuple-element.235.token, bf16[1024,2048]{1,0:T(8,128)(2,1)S(1)} %get-tuple-element.195.refs_0_, bf16[1024,3072]{1,0:T(8,128)(2,1)S(1)} %get-tuple-element.225.refs_1_, ...), custom_call_target="tpu_custom_call" | custom-call | flops 1000 | bytes 1024 | tf_op jit(solution)/shard_map/attention_backward/pallas_call | solution.py:63
  84.2 3.0 %project_grad.1 = (bf16[2,144,1536]{2,1,0:T(8,128)(2,1)S(1)}, bf16[2,144,1536]{2,1,0:T(8,128)(2,1)S(1)}, bf16[2,144,1024]{2,1,0:T(8,128)(2,1)S(1)}, bf16[2,144,1024]{2,1,0:T(8,128)(2,1)S(1)}, s32[8,128]{1,0:T(8,128)S(1)}) custom-call(s32[8,128]{1,0:T(8,128)S(1)} %get-tuple-element.245.token, bf16[1024,512]{1,0:T(8,128)(2,1)S(1)} %get-tuple-element.246.refs_0_, ...), custom_call_target="tpu_custom_call" | custom-call | flops 1000 | bytes 1024 | tf_op jit(solution)/shard_map/project_grad/pallas_call | solution.py:63
  91.8 2.6 %collective-permute-start.26 = (bf16[512,128]{1,0:T(8,128)(2,1)S(1)}, bf16[512,128]{1,0:T(8,128)(2,1)S(1)}, u32[]{:S(2)}, u32[]{:S(2)}) collective-permute-start(bf16[512,128]{1,0:T(8,128)(2,1)S(1)} %get-tuple-element.263.refs_0_), channel_id=1, source_target_pairs={{0,16},{4,20},{8,24},{12,28},{16,0},{20,4},{24,8},{28,12},{1,17},{... | collective-permute-start | bytes 393224 | tf_op jit(solution)/shard_map/ppermute | solution.py:575
  94.4 4.4 %input_grad.1 = (bf16[1024,512]{1,0:T(8,128)(2,1)}, s32[8,128]{1,0:T(8,128)S(1)}) custom-call(s32[8,128]{1,0:T(8,128)S(1)} %get-tuple-element.261.token, bf16[1024,512]{1,0:T(8,128)(2,1)S(1)} %copy-done.1, bf16[512,2048]{1,0:T(8,128)(2,1)S(1)} %get-tuple-element.247.refs_1_, bf16[512,2048]{1,0:T(8,128)(2,1)S(1)} %get-tuple-element.248.refs_2_, ...), custom_call_target="tpu_custom_call" | custom-call | flops 1000 | bytes 1024 | tf_op jit(solution)/shard_map/input_grad/pallas_call | solution.py:63
  98.9 1.8 %collective-permute-done.26.refs_1_ = bf16[512,128]{1,0:T(8,128)(2,1)S(1)} collective-permute-done((bf16[512,128]{1,0:T(8,128)(2,1)S(1)}, bf16[512,128]{1,0:T(8,128)(2,1)S(1)}, u32[]{:S(2)}, u32[]{:S(2)}) %collective-permute-start.26) | collective-permute-done | bytes 131104 | tf_op jit(solution)/shard_map/ppermute | solution.py:575
  103.5 3.3 %ffn_outer.1 = (bf16[1024,512]{1,0:T(8,128)(2,1)}, s32[8,128]{1,0:T(8,128)S(1)}) custom-call(s32[8,128]{1,0:T(8,128)S(1)} %get-tuple-element.270.token, f32[1024,512]{1,0:T(8,128)S(1)} %get-tuple-element.271.refs_0_, bf16[1024,2048]{1,0:T(8,128)(2,1)S(1)} %get-tuple-element.206.refs_0_.refs_1_, bf16[512,512]{1,0:T(8,128)(2,1)S(1)} %copy-done.4, ...), custom_call_target="tpu_custom_call" | custom-call | flops 1000 | bytes 1024 | tf_op jit(solution)/shard_map/ffn_outer/pallas_call | solution.py:63
  109.1 2.1 %collective-permute-done.31.refs_1_ = bf16[144,1024]{1,0:T(8,128)(2,1)S(1)} collective-permute-done((bf16[144,1024]{1,0:T(8,128)(2,1)S(1)}, bf16[144,1024]{1,0:T(8,128)(2,1)S(1)}, u32[]{:S(2)}, u32[]{:S(2)}) %collective-permute-start.31) | collective-permute-done | bytes 294944 | tf_op jit(solution)/shard_map/ppermute | solution.py:575
  112.6 3.3 %collective-permute-done.32.refs_1_ = bf16[144,768]{1,0:T(8,128)(2,1)S(1)} collective-permute-done((bf16[144,768]{1,0:T(8,128)(2,1)S(1)}, bf16[144,768]{1,0:T(8,128)(2,1)S(1)}, u32[]{:S(2)}, u32[]{:S(2)}) %collective-permute-start.32) | collective-permute-done | bytes 221216 | tf_op jit(solution)/shard_map/ppermute | solution.py:575
  118.1 2.4 %collective-permute-start.38 = (bf16[144,512]{1,0:T(8,128)(2,1)S(1)}, bf16[144,512]{1,0:T(8,128)(2,1)S(1)}, u32[]{:S(2)}, u32[]{:S(2)}) collective-permute-start(bf16[144,512]{1,0:T(8,128)(2,1)S(1)} %get-tuple-element.302.refs_0_), channel_id=1, source_target_pairs={{0,16},{4,20},{8,24},{12,28},{16,0},{20,4},{24,8},{28,12},{1,17},{... | collective-permute-start | bytes 442376 | tf_op jit(solution)/shard_map/ppermute | solution.py:575
  120.9 6.8 %collective-permute-done.35.refs_1_ = bf16[144,384]{1,0:T(8,128)(2,1)S(1)} collective-permute-done((bf16[144,384]{1,0:T(8,128)(2,1)S(1)}, bf16[144,384]{1,0:T(8,128)(2,1)S(1)}, u32[]{:S(2)}, u32[]{:S(2)}) %collective-permute-start.35) | collective-permute-done | bytes 110624 | tf_op jit(solution)/shard_map/ppermute | solution.py:575
  129.2 2.1 %collective-permute-start.41 = (bf16[144,512]{1,0:T(8,128)(2,1)S(1)}, bf16[144,512]{1,0:T(8,128)(2,1)S(1)}, u32[]{:S(2)}, u32[]{:S(2)}) collective-permute-start(bf16[144,512]{1,0:T(8,128)(2,1)S(1)} %get-tuple-element.308.refs_0_), channel_id=1, source_target_pairs={{0,8},{4,12},{8,0},{12,4},{16,24},{20,28},{24,16},{28,20},{1,9},{5... | collective-permute-start | bytes 442376 | tf_op jit(solution)/shard_map/ppermute | solution.py:575
  131.3 9.2 %collective-permute-done.39.refs_1_ = bf16[144,384]{1,0:T(8,128)(2,1)S(1)} collective-permute-done((bf16[144,384]{1,0:T(8,128)(2,1)S(1)}, bf16[144,384]{1,0:T(8,128)(2,1)S(1)}, u32[]{:S(2)}, u32[]{:S(2)}) %collective-permute-start.39) | collective-permute-done | bytes 110624 | tf_op jit(solution)/shard_map/ppermute | solution.py:575
  142.1 5.1 %collective-permute-done.42.refs_1_ = bf16[144,384]{1,0:T(8,128)(2,1)S(1)} collective-permute-done((bf16[144,384]{1,0:T(8,128)(2,1)S(1)}, bf16[144,384]{1,0:T(8,128)(2,1)S(1)}, u32[]{:S(2)}, u32[]{:S(2)}) %collective-permute-start.42) | collective-permute-done | bytes 110624 | tf_op jit(solution)/shard_map/ppermute | solution.py:575
  147.4 2.1 %collective-permute-start.45 = (bf16[144,768]{1,0:T(8,128)(2,1)S(1)}, bf16[144,768]{1,0:T(8,128)(2,1)S(1)}, u32[]{:S(2)}, u32[]{:S(2)}) collective-permute-start(bf16[144,768]{1,0:T(8,128)(2,1)S(1)} %get-tuple-element.318.refs_0_), channel_id=1, source_target_pairs={{0,4},{4,0},{8,12},{12,8},{16,20},{20,16},{24,28},{28,24},{1,5},{5... | collective-permute-start | bytes 663560 | tf_op jit(solution)/shard_map/ppermute | solution.py:575
  151.4 2.0 %collective-permute-done.45.refs_1_ = bf16[144,768]{1,0:T(8,128)(2,1)S(1)} collective-permute-done((bf16[144,768]{1,0:T(8,128)(2,1)S(1)}, bf16[144,768]{1,0:T(8,128)(2,1)S(1)}, u32[]{:S(2)}, u32[]{:S(2)}) %collective-permute-start.45) | collective-permute-done | bytes 221216 | tf_op jit(solution)/shard_map/ppermute | solution.py:575
  154.8 1.7 %collective-permute-done.46.refs_1_ = bf16[144,512]{1,0:T(8,128)(2,1)S(1)} collective-permute-done((bf16[144,512]{1,0:T(8,128)(2,1)S(1)}, bf16[144,512]{1,0:T(8,128)(2,1)S(1)}, u32[]{:S(2)}, u32[]{:S(2)}) %collective-permute-start.46) | collective-permute-done | bytes 147488 | tf_op jit(solution)/shard_map/ppermute | solution.py:575
  (125 shorter events, 45.3 us)
Async XLA Ops:
  2.5 7.7 %collective-permute-start = (bf16[144,512]{1,0:T(8,128)(2,1)S(1)}, bf16[144,512]{1,0:T(8,128)(2,1)S(1)}, u32[]{:S(2)}, u32[]{:S(2)}) collective-permute-start(bf16[144,512]{1,0:T(8,128)(2,1)S(1)} %get-tuple-element.179), channel_id=1, source_target_pairs={{0,2},{1,3},{2,0},{3,1},{4,6},{5,7},{6,4},{7,5},{8,10},{9,11},{10,... | collective-permute-start | bytes 442376 | tf_op jit(solution)/shard_map/ppermute | solution.py:575
  5.5 7.0 %collective-permute-start.1 = (bf16[144,512]{1,0:T(8,128)(2,1)S(1)}, bf16[144,512]{1,0:T(8,128)(2,1)S(1)}, u32[]{:S(2)}, u32[]{:S(2)}) collective-permute-start(bf16[144,512]{1,0:T(8,128)(2,1)S(1)} %get-tuple-element.180), channel_id=1, source_target_pairs={{0,2},{1,3},{2,0},{3,1},{4,6},{5,7},{6,4},{7,5},{8,10},{9,11},{10,... | collective-permute-start | bytes 442376 | tf_op jit(solution)/shard_map/ppermute | solution.py:575
  12.5 9.3 %collective-permute-start.4 = (bf16[64,2048]{1,0:T(8,128)(2,1)S(1)}, bf16[64,2048]{1,0:T(8,128)(2,1)S(1)}, u32[]{:S(2)}, u32[]{:S(2)}) collective-permute-start(bf16[64,2048]{1,0:T(8,128)(2,1)S(1)} %get-tuple-element.186), channel_id=1, source_target_pairs={{0,2},{1,3},{2,0},{3,1},{4,6},{5,7},{6,4},{7,5},{8,10},{9,11},{10,... | collective-permute-start | bytes 786440 | tf_op jit(solution)/shard_map/ppermute | solution.py:575
  16.3 8.2 %collective-permute-start.5 = (bf16[144,2048]{1,0:T(8,128)(2,1)S(1)}, bf16[144,2048]{1,0:T(8,128)(2,1)S(1)}, u32[]{:S(2)}, u32[]{:S(2)}) collective-permute-start(bf16[144,2048]{1,0:T(8,128)(2,1)S(1)} %get-tuple-element.192.refs_1_.refs_6_.refs_7_.refs_15_.refs_4_.refs_2_), channel_id=1, source_target_pairs={{0,1},{1,0},{2,3},{3,2},{4,5},{5,4},{6,7},{7,6},{8,9},{9,8},{10,11... | collective-permute-start | bytes 1769480 | tf_op jit(solution)/shard_map/ppermute | solution.py:575
  22.2 12.1 %collective-permute-start.8 = (bf16[64,2048]{1,0:T(8,128)(2,1)S(1)}, bf16[64,2048]{1,0:T(8,128)(2,1)S(1)}, u32[]{:S(2)}, u32[]{:S(2)}) collective-permute-start(bf16[64,2048]{1,0:T(8,128)(2,1)S(1)} %get-tuple-element.198), channel_id=1, source_target_pairs={{0,2},{1,3},{2,0},{3,1},{4,6},{5,7},{6,4},{7,5},{8,10},{9,11},{10,... | collective-permute-start | bytes 786440 | tf_op jit(solution)/shard_map/ppermute | solution.py:575
  22.8 16.0 %collective-permute-start.11 = (bf16[128,2048]{1,0:T(8,128)(2,1)S(1)}, bf16[128,2048]{1,0:T(8,128)(2,1)S(1)}, u32[]{:S(2)}, u32[]{:S(2)}) collective-permute-start(bf16[128,2048]{1,0:T(8,128)(2,1)S(1)} %copy-done.3), channel_id=1, source_target_pairs={{0,1},{1,0},{2,3},{3,2},{4,5},{5,4},{6,7},{7,6},{8,9},{9,8},{10,11... | collective-permute-start | bytes 1572872 | tf_op jit(solution)/shard_map/ppermute | solution.py:575
  23.0 11.2 %collective-permute-start.7 = (bf16[128,512]{1,0:T(8,128)(2,1)S(1)}, bf16[128,512]{1,0:T(8,128)(2,1)S(1)}, u32[]{:S(2)}, u32[]{:S(2)}) collective-permute-start(bf16[128,512]{1,0:T(8,128)(2,1)S(1)} %copy-done.5), channel_id=1, source_target_pairs={{0,2},{1,3},{2,0},{3,1},{4,6},{5,7},{6,4},{7,5},{8,10},{9,11},{10,... | collective-permute-start | bytes 393224 | tf_op jit(solution)/shard_map/ppermute | solution.py:575
  24.4 14.4 %collective-permute-start.12 = (bf16[64,2048]{1,0:T(8,128)(2,1)S(1)}, bf16[64,2048]{1,0:T(8,128)(2,1)S(1)}, u32[]{:S(2)}, u32[]{:S(2)}) collective-permute-start(bf16[64,2048]{1,0:T(8,128)(2,1)S(1)} %collective-permute-done.4.refs_4_.refs_2_.refs_10_), channel_id=1, source_target_pairs={{0,1},{1,0},{2,3},{3,2},{4,5},{5,4},{6,7},{7,6},{8,9},{9,8},{10,11... | collective-permute-start | bytes 786440 | tf_op jit(solution)/shard_map/ppermute | solution.py:575
  36.1 14.2 %collective-permute-start.14 = (bf16[512,512]{1,0:T(8,128)(2,1)S(1)}, bf16[512,512]{1,0:T(8,128)(2,1)S(1)}, u32[]{:S(2)}, u32[]{:S(2)}) collective-permute-start(bf16[512,512]{1,0:T(8,128)(2,1)S(1)} %copy-done.4), channel_id=1, source_target_pairs={{0,2},{1,3},{2,0},{3,1},{4,6},{5,7},{6,4},{7,5},{8,10},{9,11},{10,... | collective-permute-start | bytes 1572872 | tf_op jit(solution)/shard_map/ppermute | solution.py:575
  47.4 7.7 %collective-permute-start.17 = (bf16[2,512,512]{2,1,0:T(8,128)(2,1)S(1)}, bf16[2,512,512]{2,1,0:T(8,128)(2,1)S(1)}, u32[]{:S(2)}, u32[]{:S(2)}) collective-permute-start(bf16[2,512,512]{2,1,0:T(8,128)(2,1)S(1)} %get-tuple-element.214), channel_id=1, source_target_pairs={{0,1},{1,0},{2,3},{3,2},{4,5},{5,4},{6,7},{7,6},{8,9},{9,8},{10,11... | collective-permute-start | bytes 3145736 | tf_op jit(solution)/shard_map/ppermute | solution.py:575
  55.4 8.8 %collective-permute-start.18 = (bf16[272,512]{1,0:T(8,128)(2,1)S(1)}, bf16[272,512]{1,0:T(8,128)(2,1)S(1)}, u32[]{:S(2)}, u32[]{:S(2)}) collective-permute-start(bf16[272,512]{1,0:T(8,128)(2,1)S(1)} %get-tuple-element.221), channel_id=1, source_target_pairs={{0,2},{1,3},{2,0},{3,1},{4,6},{5,7},{6,4},{7,5},{8,10},{9,11},{10,... | collective-permute-start | bytes 835592 | tf_op jit(solution)/shard_map/ppermute | solution.py:575
  64.2 10.3 %collective-permute-start.20 = (bf16[2,144,2048]{2,1,0:T(8,128)(2,1)S(1)}, bf16[2,144,2048]{2,1,0:T(8,128)(2,1)S(1)}, u32[]{:S(2)}, u32[]{:S(2)}) collective-permute-start(bf16[2,144,2048]{2,1,0:T(8,128)(2,1)S(1)} %get-tuple-element.234), channel_id=1, source_target_pairs={{0,1},{1,0},{2,3},{3,2},{4,5},{5,4},{6,7},{7,6},{8,9},{9,8},{10,11... | collective-permute-start | bytes 3538952 | tf_op jit(solution)/shard_map/ppermute | solution.py:575
  64.2 8.4 %collective-permute-start.19 = (bf16[240,512]{1,0:T(8,128)(2,1)S(1)}, bf16[240,512]{1,0:T(8,128)(2,1)S(1)}, u32[]{:S(2)}, u32[]{:S(2)}) collective-permute-start(bf16[240,512]{1,0:T(8,128)(2,1)S(1)} %get-tuple-element.231), channel_id=1, source_target_pairs={{0,2},{1,3},{2,0},{3,1},{4,6},{5,7},{6,4},{7,5},{8,10},{9,11},{10,... | collective-permute-start | bytes 737288 | tf_op jit(solution)/shard_map/ppermute | solution.py:575
  72.9 8.2 %collective-permute-start.22 = (bf16[512,256]{1,0:T(8,128)(2,1)S(1)}, bf16[512,256]{1,0:T(8,128)(2,1)S(1)}, u32[]{:S(2)}, u32[]{:S(2)}) collective-permute-start(bf16[512,256]{1,0:T(8,128)(2,1)S(1)} %get-tuple-element.244), channel_id=1, source_target_pairs={{0,4},{4,0},{8,12},{12,8},{16,20},{20,16},{24,28},{28,24},{1,5},{5... | collective-permute-start | bytes 786440 | tf_op jit(solution)/shard_map/ppermute | solution.py:575
  74.8 6.3 %collective-permute-start.21 = (bf16[48,2048]{1,0:T(8,128)(2,1)S(1)}, bf16[48,2048]{1,0:T(8,128)(2,1)S(1)}, u32[]{:S(2)}, u32[]{:S(2)}) collective-permute-start(bf16[48,2048]{1,0:T(8,128)(2,1)S(1)} %get-tuple-element.240), channel_id=1, source_target_pairs={{0,2},{1,3},{2,0},{3,1},{4,6},{5,7},{6,4},{7,5},{8,10},{9,11},{10,... | collective-permute-start | bytes 589832 | tf_op jit(solution)/shard_map/ppermute | solution.py:575
  88.0 12.8 %collective-permute-start.27 = (bf16[2,144,1024]{2,1,0:T(8,128)(2,1)S(1)}, bf16[2,144,1024]{2,1,0:T(8,128)(2,1)S(1)}, u32[]{:S(2)}, u32[]{:S(2)}) collective-permute-start(bf16[2,144,1024]{2,1,0:T(8,128)(2,1)S(1)} %get-tuple-element.266), channel_id=1, source_target_pairs={{0,1},{1,0},{2,3},{3,2},{4,5},{5,4},{6,7},{7,6},{8,9},{9,8},{10,11... | collective-permute-start | bytes 1769480 | tf_op jit(solution)/shard_map/ppermute | solution.py:575
  88.5 12.4 %collective-permute-start.28 = (bf16[64,2048]{1,0:T(8,128)(2,1)S(1)}, bf16[64,2048]{1,0:T(8,128)(2,1)S(1)}, u32[]{:S(2)}, u32[]{:S(2)}) collective-permute-start(bf16[64,2048]{1,0:T(8,128)(2,1)S(1)} %get-tuple-element.269), channel_id=1, source_target_pairs={{0,2},{1,3},{2,0},{3,1},{4,6},{5,7},{6,4},{7,5},{8,10},{9,11},{10,... | collective-permute-start | bytes 786440 | tf_op jit(solution)/shard_map/ppermute | solution.py:575
  90.6 16.5 %collective-permute-start.29 = (bf16[144,1536]{1,0:T(8,128)(2,1)S(1)}, bf16[144,1536]{1,0:T(8,128)(2,1)S(1)}, u32[]{:S(2)}, u32[]{:S(2)}) collective-permute-start(bf16[144,1536]{1,0:T(8,128)(2,1)S(1)} %get-tuple-element.276), channel_id=1, source_target_pairs={{0,2},{1,3},{2,0},{3,1},{4,6},{5,7},{6,4},{7,5},{8,10},{9,11},{10,... | collective-permute-start | bytes 1327112 | tf_op jit(solution)/shard_map/ppermute | solution.py:575
  91.8 8.9 %collective-permute-start.26 = (bf16[512,128]{1,0:T(8,128)(2,1)S(1)}, bf16[512,128]{1,0:T(8,128)(2,1)S(1)}, u32[]{:S(2)}, u32[]{:S(2)}) collective-permute-start(bf16[512,128]{1,0:T(8,128)(2,1)S(1)} %get-tuple-element.263.refs_0_), channel_id=1, source_target_pairs={{0,16},{4,20},{8,24},{12,28},{16,0},{20,4},{24,8},{28,12},{1,17},{... | collective-permute-start | bytes 393224 | tf_op jit(solution)/shard_map/ppermute | solution.py:575
  101.3 9.9 %collective-permute-start.31 = (bf16[144,1024]{1,0:T(8,128)(2,1)S(1)}, bf16[144,1024]{1,0:T(8,128)(2,1)S(1)}, u32[]{:S(2)}, u32[]{:S(2)}) collective-permute-start(bf16[144,1024]{1,0:T(8,128)(2,1)S(1)} %get-tuple-element.281), channel_id=1, source_target_pairs={{0,4},{4,0},{8,12},{12,8},{16,20},{20,16},{24,28},{28,24},{1,5},{5... | collective-permute-start | bytes 884744 | tf_op jit(solution)/shard_map/ppermute | solution.py:575
  102.3 14.4 %collective-permute-start.34 = (bf16[144,1024]{1,0:T(8,128)(2,1)S(1)}, bf16[144,1024]{1,0:T(8,128)(2,1)S(1)}, u32[]{:S(2)}, u32[]{:S(2)}) collective-permute-start(bf16[144,1024]{1,0:T(8,128)(2,1)S(1)} %get-tuple-element.290), channel_id=1, source_target_pairs={{0,2},{1,3},{2,0},{3,1},{4,6},{5,7},{6,4},{7,5},{8,10},{9,11},{10,... | collective-permute-start | bytes 884744 | tf_op jit(solution)/shard_map/ppermute | solution.py:575
  107.5 8.5 %collective-permute-start.32 = (bf16[144,768]{1,0:T(8,128)(2,1)S(1)}, bf16[144,768]{1,0:T(8,128)(2,1)S(1)}, u32[]{:S(2)}, u32[]{:S(2)}) collective-permute-start(bf16[144,768]{1,0:T(8,128)(2,1)S(1)} %get-tuple-element.284), channel_id=1, source_target_pairs={{0,4},{4,0},{8,12},{12,8},{16,20},{20,16},{24,28},{28,24},{1,5},{5... | collective-permute-start | bytes 663560 | tf_op jit(solution)/shard_map/ppermute | solution.py:575
  111.5 16.2 %collective-permute-start.36 = (bf16[512,256]{1,0:T(8,128)(2,1)S(1)}, bf16[512,256]{1,0:T(8,128)(2,1)S(1)}, u32[]{:S(2)}, u32[]{:S(2)}) collective-permute-start(bf16[512,256]{1,0:T(8,128)(2,1)S(1)} %get-tuple-element.295.refs_0_), channel_id=1, source_target_pairs={{0,4},{4,0},{8,12},{12,8},{16,20},{20,16},{24,28},{28,24},{1,5},{5... | collective-permute-start | bytes 786440 | tf_op jit(solution)/shard_map/ppermute | solution.py:575
  117.0 12.1 %collective-permute-start.37 = (bf16[144,512]{1,0:T(8,128)(2,1)S(1)}, bf16[144,512]{1,0:T(8,128)(2,1)S(1)}, u32[]{:S(2)}, u32[]{:S(2)}) collective-permute-start(bf16[144,512]{1,0:T(8,128)(2,1)S(1)} %get-tuple-element.300), channel_id=1, source_target_pairs={{0,4},{4,0},{8,12},{12,8},{16,20},{20,16},{24,28},{28,24},{1,5},{5... | collective-permute-start | bytes 442376 | tf_op jit(solution)/shard_map/ppermute | solution.py:575
  118.1 11.1 %collective-permute-start.38 = (bf16[144,512]{1,0:T(8,128)(2,1)S(1)}, bf16[144,512]{1,0:T(8,128)(2,1)S(1)}, u32[]{:S(2)}, u32[]{:S(2)}) collective-permute-start(bf16[144,512]{1,0:T(8,128)(2,1)S(1)} %get-tuple-element.302.refs_0_), channel_id=1, source_target_pairs={{0,16},{4,20},{8,24},{12,28},{16,0},{20,4},{24,8},{28,12},{1,17},{... | collective-permute-start | bytes 442376 | tf_op jit(solution)/shard_map/ppermute | solution.py:575
  120.5 7.2 %collective-permute-start.35 = (bf16[144,384]{1,0:T(8,128)(2,1)S(1)}, bf16[144,384]{1,0:T(8,128)(2,1)S(1)}, u32[]{:S(2)}, u32[]{:S(2)}) collective-permute-start(bf16[144,384]{1,0:T(8,128)(2,1)S(1)} %get-tuple-element.293), channel_id=1, source_target_pairs={{0,8},{4,12},{8,0},{12,4},{16,24},{20,28},{24,16},{28,20},{1,9},{5... | collective-permute-start | bytes 331784 | tf_op jit(solution)/shard_map/ppermute | solution.py:575
  129.1 11.5 %collective-permute-start.40 = (bf16[144,512]{1,0:T(8,128)(2,1)S(1)}, bf16[144,512]{1,0:T(8,128)(2,1)S(1)}, u32[]{:S(2)}, u32[]{:S(2)}) collective-permute-start(bf16[144,512]{1,0:T(8,128)(2,1)S(1)} %get-tuple-element.306.refs_0_), channel_id=1, source_target_pairs={{0,8},{4,12},{8,0},{12,4},{16,24},{20,28},{24,16},{28,20},{1,9},{5... | collective-permute-start | bytes 442376 | tf_op jit(solution)/shard_map/ppermute | solution.py:575
  129.2 11.4 %collective-permute-start.41 = (bf16[144,512]{1,0:T(8,128)(2,1)S(1)}, bf16[144,512]{1,0:T(8,128)(2,1)S(1)}, u32[]{:S(2)}, u32[]{:S(2)}) collective-permute-start(bf16[144,512]{1,0:T(8,128)(2,1)S(1)} %get-tuple-element.308.refs_0_), channel_id=1, source_target_pairs={{0,8},{4,12},{8,0},{12,4},{16,24},{20,28},{24,16},{28,20},{1,9},{5... | collective-permute-start | bytes 442376 | tf_op jit(solution)/shard_map/ppermute | solution.py:575
  131.3 9.2 %collective-permute-start.39 = (bf16[144,384]{1,0:T(8,128)(2,1)S(1)}, bf16[144,384]{1,0:T(8,128)(2,1)S(1)}, u32[]{:S(2)}, u32[]{:S(2)}) collective-permute-start(bf16[144,384]{1,0:T(8,128)(2,1)S(1)} %get-tuple-element.304.refs_0_), channel_id=1, source_target_pairs={{0,16},{4,20},{8,24},{12,28},{16,0},{20,4},{24,8},{28,12},{1,17},{... | collective-permute-start | bytes 331784 | tf_op jit(solution)/shard_map/ppermute | solution.py:575
  140.8 8.7 %collective-permute-start.43 = (bf16[144,1024]{1,0:T(8,128)(2,1)S(1)}, bf16[144,1024]{1,0:T(8,128)(2,1)S(1)}, u32[]{:S(2)}, u32[]{:S(2)}) collective-permute-start(bf16[144,1024]{1,0:T(8,128)(2,1)S(1)} %get-tuple-element.312.refs_0_), channel_id=1, source_target_pairs={{0,4},{4,0},{8,12},{12,8},{16,20},{20,16},{24,28},{28,24},{1,5},{5... | collective-permute-start | bytes 884744 | tf_op jit(solution)/shard_map/ppermute | solution.py:575
  140.9 6.3 %collective-permute-start.42 = (bf16[144,384]{1,0:T(8,128)(2,1)S(1)}, bf16[144,384]{1,0:T(8,128)(2,1)S(1)}, u32[]{:S(2)}, u32[]{:S(2)}) collective-permute-start(bf16[144,384]{1,0:T(8,128)(2,1)S(1)} %get-tuple-element.310.refs_0_), channel_id=1, source_target_pairs={{0,8},{4,12},{8,0},{12,4},{16,24},{20,28},{24,16},{28,20},{1,9},{5... | collective-permute-start | bytes 331784 | tf_op jit(solution)/shard_map/ppermute | solution.py:575
  141.0 10.2 %collective-permute-start.44 = (bf16[144,512]{1,0:T(8,128)(2,1)S(1)}, bf16[144,512]{1,0:T(8,128)(2,1)S(1)}, u32[]{:S(2)}, u32[]{:S(2)}) collective-permute-start(bf16[144,512]{1,0:T(8,128)(2,1)S(1)} %get-tuple-element.316.refs_0_), channel_id=1, source_target_pairs={{0,16},{4,20},{8,24},{12,28},{16,0},{20,4},{24,8},{28,12},{1,17},{... | collective-permute-start | bytes 442376 | tf_op jit(solution)/shard_map/ppermute | solution.py:575
  (21 other events, 133.7 us)

commit v4 on v3

--- a/solution.py
+++ b/solution.py
@@ -127,6 +127,11 @@
     return inv * (grad - jnp.mean(grad, axis=1, keepdims=True) - normed * jnp.mean(grad * normed, axis=1, keepdims=True))
 
 
+def parity(token):
+    place = position(token, 1)
+    return lax.rem(place + lax.div(place, 2), 2)
+
+
 def begin_kernel(token, *refs):
     weights, vecs, inner, (out, first, second, wi0, wi1), rest = refs[:4], refs[4:10], refs[10], refs[11:16], refs[16:]
     bufs, sems = rest[:6], rest[6]
@@ -140,7 +145,7 @@
         copy.wait()
     vec = jnp.concatenate([b[...].reshape(1, -1).astype(F32) for b in bufs] + [jnp.zeros((1, 896), F32)], axis=1)
     out[128:144, :] = jnp.broadcast_to(vec, (16, 2048)).astype(BF16)
-    odd = lax.rem(position(token, 1), 2)
+    odd = parity(token)
     for k, piece in enumerate((first, second)):
         piece[...] = out[:, pl.ds(pl.multiple_of(odd * 1024 + 512 * k, 512), 512)]
 
@@ -152,7 +157,7 @@
 
 
 def assemble_kernel(token, mine0, mine1, other0, other1, _, out):
-    odd = lax.rem(position(token, 1), 2)
+    odd = parity(token)
     for half, pieces in ((odd, (mine0, mine1)), (1 - odd, (other0, other1))):
         for k, piece in enumerate(pieces):
             out[:, pl.ds(pl.multiple_of(half * 1024 + 512 * k, 512), 512)] = piece[...]
@@ -180,18 +185,23 @@
     return call(clock, first_norm_kernel, "first_norm", [shape((T, 512), F32), shape((T, 512))], [tokens], [pltpu.VMEM((ROWS, 512), F32)])
 
 
-def project_kernel(_, n1, p0, p1, p2, p3, qkvf, a1):
+def project_kernel(_, n1, p0, p1, p2, p3, qkvf):
     packs = (p0, p1, p2, p3)
-    a1[...] = (n1[...] * vector(packs, 0, 128) + vector(packs, 128, 128)).astype(BF16)
-    for n in range(4):
-        cols = slice(512 * n, 512 * (n + 1))
-        out = mm(a1[...], stack_packs(packs, cols))
-        qkvf[:, cols] = (jnp.exp(out) if n == 3 else out).astype(BF16)
+    gain, shift = vector(packs, 0, 128), vector(packs, 128, 128)
+
+    def body(rows):
+        a1 = (n1[rows, :] * gain + shift).astype(BF16)
+        for n in range(4):
+            cols = slice(512 * n, 512 * (n + 1))
+            out = mm(a1, stack_packs(packs, cols))
+            qkvf[rows, cols] = (jnp.exp(out) if n == 3 else out).astype(BF16)
+
+    row_loop(n1.shape[0], body)
 
 
 def project(clock, n1, packs):
     T = n1.shape[0]
-    return call(clock, project_kernel, "project", [shape((T, 2048))], [n1, *packs], [pltpu.VMEM((T, 512), BF16)])[0]
+    return call(clock, project_kernel, "project", [shape((T, 2048))], [n1, *packs])[0]
 
 
 def left_half(rows):
@@ -317,13 +327,14 @@
 
 def backward_kernel(first, count, last, _, qkvf, kept, states, carry_in, do_in, *refs):
     C = CHUNK
-    r1, r2, carry = refs[-3:]
-    begins, (grad, *ends) = (refs[:3], refs[3:-3]) if first < last else ((), refs[:-3])
-    for ref, old in zip((r1, r2, carry), begins or (None,) * 3):
+    r, carry = refs[-2:]
+    begins, (grad, *ends) = (refs[:2], refs[2:-2]) if first < last else ((), refs[:-2])
+    for ref, old in zip((r, carry), begins or (None,) * 2):
         ref[...] = jnp.zeros_like(ref) if old is None else old[...]
     left = left_half(C)
     causal = causal_pair(C)
     same = same_head()
+    same2 = jnp.concatenate((same, same), axis=1)
     lower = triangle(C).astype(BF16)
     upper = lower.T
     upper2 = jnp.concatenate((upper, upper), axis=1)
@@ -338,18 +349,18 @@
         denoms = mm(lower, qkvf[rows, 1536:2048]) + carry_in[c][0:1, :]
         s1b = [states[c, :, pair_of(j)] for j in PAIRS]
         s2b = [states[c, :, pair_of(4 + j)] for j in PAIRS]
-        r1b = [r1[j].astype(BF16) for j in PAIRS]
-        r2b = [r2[j].astype(BF16) for j in PAIRS]
+        rb = [r[j].astype(BF16) for j in PAIRS]
         g = [kept[rows, g_of(j)] for j in PAIRS]
         raw = [mm_nt(do[j], split_pair(part(2, j), left)) for j in PAIRS]
         f2 = [split_pair(part(3, j), left) for j in PAIRS]
-        db2, dg, dn, dd = [], [], [], []
+        db2, dg, dn, dd, later = [], [], [], [], []
         for j in PAIRS:
             db2.append(jnp.where(causal, raw[j].astype(BF16), zero))
             dg.append(mm(db2[j], f2[j]) + mm_nt(do[j], s2b[j]))
         for j in PAIRS:
+            later.append(mm(part(3, j), rb[j]))
             dv2 = mm_tn(kept[rows, b_of(j)], do[j])
-            dv = jnp.where(left, dv2[:C], dv2[C:]) + mm(part(3, j), r2b[j])
+            dv = jnp.where(left, dv2[:C], dv2[C:]) + later[j][:, :PAIR]
             grad[here, 1024 + PAIR * j : 1024 + PAIR * (j + 1)] = dv.astype(BF16)
         for j in PAIRS:
             denom = denoms[:, pair_of(j)]
@@ -360,12 +371,17 @@
             dd.append(-(dpp + ds * kept[rows, s_of(j)].astype(F32)) * rden)
             dn.append((ds * SCALE * rden).astype(BF16))
         raw = [mm_nt(dn[j], f2[j]) for j in PAIRS]
+        sums = []
+        for k in (0, 2):
+            d = jnp.concatenate((dd[k], dd[k + 1]), axis=1)
+            hi = d.astype(BF16)
+            lo = (d - hi.astype(F32)).astype(BF16)
+            total = mm(upper2, jnp.concatenate((hi, lo), axis=0))
+            sums += [total[:, :PAIR], total[:, PAIR:]]
         for j in PAIRS:
-            df2 = mm_tn(db2[j], g[j]) + mm_tn(kept[rows, a_of(j)], dn[j])
-            hi = dd[j].astype(BF16)
-            lo = (dd[j] - hi.astype(F32)).astype(BF16)
-            df = jnp.where(left, df2[:C], df2[C:]) + mm_nt(part(2, j), r2b[j]) + mm(part(1, j), r1b[j])
-            df = df + mm(upper2, jnp.concatenate((hi, lo), axis=0)) + carry[0:1, pair_of(j)]
+            df2 = mm_tn(jnp.concatenate((db2[j], kept[rows, a_of(j)]), axis=0), jnp.concatenate((g[j], dn[j]), axis=0))
+            df = jnp.where(left, df2[:C], df2[C:]) + mm_nt(jnp.concatenate((part(2, j), part(1, j)), axis=1), rb[j])
+            df = df + sums[j] + carry[0:1, pair_of(j)]
             grad[here, 1536 + PAIR * j : 1536 + PAIR * (j + 1)] = (df * part(3, j).astype(F32)).astype(BF16)
             carry[0:1, pair_of(j)] += jnp.sum(dd[j], axis=0, keepdims=True)
         for j in PAIRS:
@@ -373,15 +389,15 @@
             dq = mm(da2, split_pair(part(1, j), left)) + mm_nt(dn[j], s1b[j])
             grad[here, pair_of(j)] = dq.astype(BF16)
             dk2 = mm_tn(da2, part(0, j))
-            dk = jnp.where(left, dk2[:C], dk2[C:]) + mm_nt(part(3, j), r1b[j])
+            dk = jnp.where(left, dk2[:C], dk2[C:]) + later[j][:, PAIR:]
             grad[here, 512 + PAIR * j : 512 + PAIR * (j + 1)] = dk.astype(BF16)
         for j in PAIRS:
-            r1[j] += jnp.where(same, mm_tn(part(0, j), dn[j]), 0.0)
-            r2[j] += jnp.where(same, mm_tn(g[j], do[j]), 0.0)
+            new = jnp.concatenate((mm_tn(g[j], do[j]), mm_tn(dn[j], part(0, j))), axis=1)
+            r[j] += jnp.where(same2, new, 0.0)
         return 0
 
     lax.fori_loop(0, count, step, 0, unroll=UNROLL)
-    for ref, end in zip((r1, r2, carry), ends):
+    for ref, end in zip((r, carry), ends):
         end[...] = ref[...]
 
 
@@ -389,9 +405,10 @@
     rows = count * CHUNK
     outs = [shape((rows, 2048))]
     if first - count >= 0:
-        outs += [shape((4, PAIR, PAIR), F32), shape((4, PAIR, PAIR), F32), shape((8, 512), F32)]
+        outs += [shape((4, PAIR, 2 * PAIR), F32), shape((8, 512), F32)]
     kernel = functools.partial(backward_kernel, first, count, qkvf.shape[0] // CHUNK - 1)
-    return call(clock, kernel, "attention_backward", outs, [qkvf, *saved, d_o, *states], state_scratch())
+    scratch = [pltpu.VMEM((4, PAIR, 2 * PAIR), F32), pltpu.VMEM((8, 512), F32)]
+    return call(clock, kernel, "attention_backward", outs, [qkvf, *saved, d_o, *states], scratch)
 
 
 def gelu_parts(v):
@@ -462,8 +479,11 @@
 def ffn_outer_kernel(token, resid, act, *refs):
     wu, vs, (out, bias, result, sem) = refs[:4], refs[4:8], refs[8:]
     put_blocks(bias, slice(None), jnp.broadcast_to(vector(vs, 512, 128), (8, 512)), blocks_of(token), 128)
-    total = mm(act[...], stack(wu))
-    result[...] = (total + resid[...] + bias[0:1, :]).astype(BF16)
+
+    def body(rows):
+        result[rows, :] = (mm(act[rows, :], stack(wu)) + resid[rows, :] + bias[0:1, :]).astype(BF16)
+
+    row_loop(act.shape[0], body)
     copy = pltpu.make_async_copy(result, out, sem)
     copy.start()
     copy.wait()
@@ -474,33 +494,41 @@
     return call(clock, ffn_outer_kernel, "ffn_outer", [shape(resid.shape)], [resid, act, *wu, *vecs], scratch, outside=(0,))[0]
 
 
-def inner_back_kernel(token, dy, slope, u0, u1, u2, u3, din, sums):
+def inner_back_kernel(which, more, token, dy, slope, *refs):
     cols = wide(blocks_of(token), 512)
-    sums[...] = jnp.zeros_like(sums)
-    sums[1:2, 0:512] = jnp.sum(dy[...].astype(F32), axis=0, keepdims=True)
-    for i, u in enumerate((u0, u1, u2, u3)):
+    wu, (din, sums) = refs[:2], refs[-2:]
+    if more:
+        sums[...] = refs[2][...]
+    else:
+        sums[...] = jnp.zeros_like(sums)
+        sums[1:2, 0:512] = jnp.sum(dy[...].astype(F32), axis=0, keepdims=True)
+    for i, u in zip(which, wu):
         d = (mm_nt(dy[...], u[...]) * slope[:, cols[i]].astype(F32)).astype(BF16)
         din[:, cols[i]] = d
         sums[0:1, cols[i]] = jnp.sum(d.astype(F32), axis=0, keepdims=True)
 
 
-def inner_back(clock, dy, slope, wu):
+def inner_back(clock, dy, slope, wu, which, sums=()):
     T = dy.shape[0]
-    return call(clock, inner_back_kernel, "inner_back", [shape((T, 2048)), shape((8, 2048), F32)], [dy, slope, *wu], aliases={1: 0})
-
-
-def inner_grad_kernel(n2, din, sums, keep, send):
+    kernel = functools.partial(inner_back_kernel, which, len(sums) > 0)
+    return call(clock, kernel, "inner_back", [shape((T, 2048)), shape((8, 2048), F32)], [dy, slope, *wu, *sums], aliases={1: 0})
+
+
+def inner_grad_kernel(first, _, n2, din, sums, out):
+    m = mm_tn(n2[:, 128 * first : 128 * (first + 2)], din[...]).astype(BF16)
     tail = jnp.concatenate((sums[...], jnp.zeros_like(sums)), axis=0).astype(BF16)
-    for i in range(4):
-        dest = keep if i < 2 else send
-        dest[i % 2, 0:128, :] = mm_tn(n2[:, 128 * i : 128 * (i + 1)], din[...]).astype(BF16)
-        dest[i % 2, 128:144, :] = tail
-
-
-def resid_back_kernel(token, dy, n2, r2, din, sums, *refs):
-    wo, wi, packs = refs[:4], refs[4:-9], refs[-9:-5]
-    keep, send, dres_out, do_out, scr = refs[-5:]
-    inner_grad_kernel(n2, din, sums, keep, send)
+    for k in range(2):
+        out[k, 0:128, :] = m[128 * k : 128 * (k + 1), :]
+        out[k, 128:144, :] = tail
+
+
+def inner_grad(clock, n2, din, sums, first):
+    return call(clock, functools.partial(inner_grad_kernel, first), "inner_grad", [shape((2, 144, 2048))], [n2, din, sums])[0]
+
+
+def resid_back_kernel(token, dy, n2, r2, din, *refs):
+    wo, wi, packs = refs[:4], refs[4:-7], refs[-7:-3]
+    dres_out, do_out, scr = refs[-3:]
     blocks = blocks_of(token)
     gain = vector(packs, 256, 128)
 
@@ -515,36 +543,32 @@
     row_loop(dy.shape[0], body)
 
 
-def resid_back(clock, dy, n2, r2, din, sums, wo, wi, packs):
+def resid_back(clock, dy, n2, r2, din, wo, wi, packs):
     T = dy.shape[0]
-    outs = [shape((2, 144, 2048))] * 2 + [shape((T, 512), F32), shape((T, 512))]
-    return call(clock, resid_back_kernel, "resid_back", outs, [dy, n2, r2, din, sums, *wo, *wi, *packs], [pltpu.VMEM((ROWS, 512), F32)])
-
-
-def project_grad_kernel(token, n1, early, late, mixed, dres, *dests):
+    outs = [shape((T, 512), F32), shape((T, 512))]
+    return call(clock, resid_back_kernel, "resid_back", outs, [dy, n2, r2, din, *wo, *wi, *packs], [pltpu.VMEM((ROWS, 512), F32)])
+
+
+def project_grad_kernel(first, token, n1, early, late, mixed, dres, out):
     half = early.shape[0]
     blocks = wide(blocks_of(token), 128)
-    for keep, send, start in ((*dests[:2], 0), (*dests[2:], 1024)):
+    n = n1[:, 128 * first : 128 * (first + 2)]
+    d = dres[...].astype(BF16)
+    for start in (0, 1024):
         cols = slice(start, start + 1024)
-        out = (mm_tn(n1[0:half, :], early[:, cols]) + mm_tn(n1[half:, :], late[:, cols])).astype(BF16)
+        m = (mm_tn(n[0:half], early[:, cols]) + mm_tn(n[half:], late[:, cols])).astype(BF16)
         total = sum(jnp.sum(r[:, cols].astype(F32), axis=0, keepdims=True) for r in (early, late))
         tail = jnp.broadcast_to(total, (16, 1024)).astype(BF16)
-        for i in range(4):
-            dest = keep if i < 2 else send
-            dest[i % 2, 0:128, 0:1024] = out[128 * i : 128 * (i + 1)]
-            dest[i % 2, 128:144, 0:1024] = tail
-    keep, send = dests[:2]
-    d = dres[...].astype(BF16)
-    for i in range(4):
-        dest = keep if i < 2 else send
-        dest[i % 2, 0:128, 1024:] = mm_tn(mixed[:, blocks[i]], d).astype(BF16)
-        dest[i % 2, 128:144, 1024:] = jnp.zeros((16, 512), BF16)
-
-
-def project_grad(clock, n1, early, late, mixed, dres):
-    outs = [shape((2, 144, 1536))] * 2 + [shape((2, 144, 1024))] * 2
-    keep_a, send_a, keep_b, send_b = call(clock, project_grad_kernel, "project_grad", outs, [n1, early, late, mixed, dres])
-    return (keep_a, send_a), (keep_b, send_b)
+        for k in range(2):
+            out[k, 0:128, cols] = m[128 * k : 128 * (k + 1)]
+            out[k, 128:144, cols] = tail
+    for k in range(2):
+        out[k, 0:128, 2048:] = mm_tn(mixed[:, blocks[first + k]], d).astype(BF16)
+        out[k, 128:144, 2048:] = jnp.zeros((16, 512), BF16)
+
+
+def project_grad(clock, n1, early, late, mixed, dres, first):
+    return call(clock, functools.partial(project_grad_kernel, first), "project_grad", [shape((2, 144, 2560))], [n1, early, late, mixed, dres])[0]
 
 
 def input_grad_kernel(token, tokens, early, late, dres, p0, p1, p2, p3, out, scr, result, sems):
@@ -601,76 +625,103 @@
     return call(clock, gate_kernel, "gate", outs, [*waited, *values], limit=1, aliases={n + k: k for k in range(len(values))})
 
 
-def join_core_kernel(_, keep, got, mine, *pieces):
-    mine[...] = add(keep[0], got[0]).astype(BF16)
-    start = 0
-    for piece in pieces:
-        rows = slice(start, start + piece.shape[0])
-        piece[...] = add(keep[1, rows, :], got[1, rows, :]).astype(BF16)
-        start += piece.shape[0]
-
-
-def join_kernel(split, place, token, keep, *refs):
-    outs_at = len(refs) - (1 if split is None else 3)
-    gots, refs = refs[:outs_at], refs[outs_at:]
-    if place is not None:
-        out = refs[0]
-        bit = lax.rem(lax.div(position(token, 1), place), 2)
-        out[:, half_at(bit, out.shape[1])] = keep[...]
-        out[:, half_at(1 - bit, out.shape[1])] = gots[0][...]
-        return
-    whole = refs[-1]
-    start = 0
-    for got in gots:
-        rows = slice(start, start + got.shape[0])
-        whole[rows, :] = add(keep[rows, :], got[...]).astype(BF16)
-        start += got.shape[0]
-    if split is not None:
-        mine, send, _ = refs
-        bit = lax.rem(lax.div(position(token, 1), split), 2)
-        mine[...] = whole[:, half_at(bit, whole.shape[1])]
-        send[...] = whole[:, half_at(1 - bit, whole.shape[1])]
+def quarter(ref, token, mask):
+    width = ref.shape[1] // 4
+    place = position(token, 1) ^ mask
+    return pl.ds(pl.multiple_of((2 * lax.rem(place, 2) + lax.rem(lax.div(place, 2), 2)) * width, width), width)
+
+
+def join_kernel(kind, mask, after, token, keep, *refs):
+    after_kind, after_mask, n_sends = after
+    n_outs = 1 + n_sends
+    gots, outs, whole = refs[: -1 - n_outs], refs[-1 - n_outs : -1], refs[-1]
+    bit = lambda m: lax.rem(lax.div(position(token, 1), m), 2)
+    if kind == "core":
+        rows = keep.shape[1]
+        for k in range(2):
+            whole[rows * k : rows * (k + 1), :] = add(keep[k], gots[0][k]).astype(BF16)
+    elif kind == "beside":
+        whole[:, half_at(bit(mask), whole.shape[1])] = keep[...]
+        whole[:, half_at(1 - bit(mask), whole.shape[1])] = gots[0][...]
+    elif kind == "besides":
+        for m, got in enumerate((keep, *gots)):
+            whole[:, quarter(whole, token, m)] = got[...]
+    elif kind == "x":
+        start = 0
+        for got in gots:
+            rows = slice(start, start + got.shape[0])
+            whole[rows, :] = add(keep[rows, :], got[...]).astype(BF16)
+            start += got.shape[0]
+    else:
+        total = keep[...].astype(F32)
+        for got in gots:
+            total = total + got[...].astype(F32)
+        whole[...] = total.astype(BF16)
+    if after_kind == "half":
+        outs[0][...] = whole[:, half_at(bit(after_mask), whole.shape[1])]
+        outs[1][...] = whole[:, half_at(1 - bit(after_mask), whole.shape[1])]
+    elif after_kind == "quarter":
+        for m, out in enumerate(outs):
+            out[...] = whole[:, quarter(whole, token, m)]
+    else:
+        start = 0
+        for out in outs:
+            out[...] = whole[start : start + out.shape[0], :]
+            start += out.shape[0]
 
 
 class Chain:
-    def __init__(self, clock, dp, halved, pieces, pair):
-        self.clock, self.dp, self.pieces = clock, dp, pieces
+    def __init__(self, clock, dp, steps, send, pieces=()):
+        self.clock, self.dp = clock, dp
+        self.pieces = pieces or (send.shape[1],)
         masks = [1 << k for k in range(dp.bit_length() - 1)]
-        self.todo = [("core", 0), ("x", 0)] + [("half" if m in halved else "all", m) for m in masks] + [("beside", m) for m in reversed(masks) if m in halved]
-        self.keep, self.send = pair
+        used = [1, 2] if "quarter" in steps else [m for m in masks if f"half{m}" in steps]
+        self.todo = []
+        for name in steps:
+            if name == "all":
+                self.todo += [("all", m) for m in masks if m not in used]
+            else:
+                kind = name.rstrip("0123456789")
+                self.todo.append((kind, int(name[len(kind) :] or 0)))
+        self.send = [send]
         self.busy = True
+        self.launch()
 
     def launch(self):
         self.kind, self.mask = self.todo.pop(0)
+        self.split = 0
         if self.kind == "core":
-            self.got = [over_core(self.send)]
+            self.got = [over_core(self.send[0])]
         elif self.kind == "x":
             self.got = [over_x(self.send.pop(0))]
+            self.split = len(self.send)
+        elif self.kind == "quarter":
+            self.got = [exchange(v, "dp", self.dp, m) for m, v in enumerate(self.send, 1)]
+        elif self.kind == "besides":
+            self.got = [exchange(self.keep, "dp", self.dp, m) for m in (1, 2, 3)]
         else:
-            self.got = [exchange(self.send, "dp", self.dp, self.mask)]
-
-    def more(self, *others):
-        piece, *sends = gate(self.clock, [self.got[-1]], [self.send.pop(0)] + [c.send for c in others])
-        self.got.append(over_x(piece))
-        for chain, send in zip(others, sends):
-            chain.send = send
-            chain.launch()
+            self.got = [exchange(self.send[0], "dp", self.dp, self.mask)]
+
+    def more(self):
+        self.got.append(over_x(gate(self.clock, [self.got[-1]], [self.send.pop(0)])[0]))
+        self.split -= 1
 
     def step(self):
         rows, width = self.keep.shape[-2:]
-        if self.kind == "core":
-            outs = [shape((rows, width))] + [shape((n, width)) for n in self.pieces]
-            self.keep, *self.send = call(self.clock, join_core_kernel, "join_core", outs, [self.keep, *self.got], limit=JOIN)
+        rows = 2 * rows if self.kind == "core" else rows
+        width = width * {"beside": 2, "besides": 4}.get(self.kind, 1)
+        kind, mask = self.todo[0] if self.todo else ("", 0)
+        if kind == "half":
+            dims = [(rows, width // 2)] * 2
+        elif kind == "quarter":
+            dims = [(rows, width // 4)] * 4
+        elif kind == "x":
+            dims = [(n, width) for n in (rows // 2, *self.pieces)]
         else:
-            split = self.todo[0][1] if self.todo and self.todo[0][0] == "half" else None
-            place = self.mask if self.kind == "beside" else None
-            kernel = functools.partial(join_kernel, split, place)
-            if split is None:
-                outs, scratch = [shape((rows, 2 * width if place else width))], []
-            else:
-                outs, scratch = [shape((rows, width // 2))] * 2, [pltpu.VMEM((rows, width), BF16)]
-            out = call(self.clock, kernel, "join", outs, [self.keep, *self.got], scratch, limit=JOIN)
-            self.keep, self.send = out if split else (out[0], out[0])
+            dims = [(rows, width)]
+        kernel = functools.partial(join_kernel, self.kind, self.mask, (kind, mask, len(dims) - 1))
+        self.keep, *self.send = call(self.clock, kernel, "join", [shape(d) for d in dims], [self.keep, *self.got], [pltpu.VMEM((rows, width), BF16)], limit=JOIN)
+        self.send = self.send or [self.keep]
         self.busy = bool(self.todo)
         if self.busy:
             self.launch()
@@ -725,40 +776,42 @@
     return call(clock, finish_inner_kernel, "finish_inner", outs, [total, w, pack], scratch, limit=JOIN, outside=range(5))
 
 
-def project_parts(total, pack, start, buf):
+def finish_project_kernel(_, total, pack, *refs):
+    outs, (buf, small, sems) = refs[:-3], refs[-3:]
     gain, shift = (column(pack[128:129, k : k + 128].astype(F32)) for k in (0, 128))
-    m = total[0:128, 0:1024].astype(F32)
-    tail = total[128:144, 0:1024].astype(F32)[0:1, :]
-    buf[:, 0:1024] = gain * m + shift * tail
-    w = pack[0:128, start : start + 1024].astype(F32)
-    return as_row(jnp.sum(w * m, axis=1, keepdims=True)), as_row(jnp.sum(w * tail, axis=1, keepdims=True))
-
-
-def finish_first_kernel(_, total, pack, out0, out1, out2, before, buf, sems):
-    gain, shift = project_parts(total, pack, 0, buf)
-    buf[:, 1024:1536] = total[0:128, 1024:1536].astype(F32)
-    before[0:1, :] = gain
-    before[1:2, :] = shift
-    send_out([(buf.at[:, 512 * n : 512 * (n + 1)], out) for n, out in enumerate((out0, out1, out2))], sems)
-
-
-def finish_first(clock, total, pack):
-    outs = [shape((128, 512), F32)] * 3 + [shape((8, 128), F32)]
-    scratch = [pltpu.VMEM((128, 1536), F32), pltpu.SemaphoreType.DMA((3,))]
-    return call(clock, finish_first_kernel, "finish_first", outs, [total, pack], scratch, limit=JOIN, outside=range(3))
-
-
-def finish_last_kernel(_, total, pack, before, out0, out1, gain_out, shift_out, buf, small, sems):
-    gain, shift = project_parts(total, pack, 1024, buf)
-    small[0:1, :] = before[0:1, :] + gain
-    small[1:2, :] = before[1:2, :] + shift
-    send_out([(buf.at[:, 0:512], out0), (buf.at[:, 512:1024], out1), (small.at[0], gain_out), (small.at[1], shift_out)], sems)
-
-
-def finish_last(clock, total, pack, before):
-    outs = [shape((128, 512), F32)] * 2 + [shape((128,), F32)] * 2
-    scratch = [pltpu.VMEM((128, 1024), F32), pltpu.VMEM((8, 128), F32), pltpu.SemaphoreType.DMA((4,))]
-    return call(clock, finish_last_kernel, "finish_last", outs, [total, pack, before], scratch, limit=JOIN, outside=range(4))
+    m = total[0:128, 0:2048].astype(F32)
+    tail = total[128:144, 0:2048].astype(F32)[0:1, :]
+    buf[:, 0:2048] = gain * m + shift * tail
+    buf[:, 2048:2560] = total[0:128, 2048:2560].astype(F32)
+    copies = [pltpu.make_async_copy(buf.at[:, 512 * k : 512 * (k + 1)], out, sems.at[k]) for k, out in enumerate(outs[:5])]
+    for copy in copies:
+        copy.start()
+    w = pack[0:128, :].astype(F32)
+    small[0:1, :] = as_row(jnp.sum(w * m, axis=1, keepdims=True))
+    small[1:2, :] = as_row(jnp.sum(w * tail, axis=1, keepdims=True))
+    more = [pltpu.make_async_copy(small.at[k], out, sems.at[5 + k]) for k, out in enumerate(outs[5:])]
+    for copy in more:
+        copy.start()
+    for copy in copies + more:
+        copy.wait()
+
+
+def finish_project(clock, total, pack):
+    outs = [shape((128, 512), F32)] * 5 + [shape((128,), F32)] * 2
+    scratch = [pltpu.VMEM((128, 2560), F32), pltpu.VMEM((8, 128), F32), pltpu.SemaphoreType.DMA((7,))]
+    return call(clock, finish_project_kernel, "finish_project", outs, [total, pack], scratch, limit=JOIN, outside=range(7))
+
+
+PLAN = (
+    "OG", "IA", "WU", "IB", "u", "IS", "IK", "i", "RB", "u", "AE", "u", "i", "AL", "u", "i", "PS", "PK",
+    "p", "IN", "i", "u", "FO", "u", "p", "i", "p", "u", "i", "p", "u",
+)
+STEPS = {
+    "u": ("core", "x", "half1", "half2", "all", "beside2", "beside1"),
+    "i": ("core", "quarter", "x", "all", "beside2", "beside1"),
+    "p": ("core", "x", "quarter", "all", "besides"),
+}
+PIECES = {"u": (272, 240), "i": (), "p": ()}
 
 
 def per_device(dp, tokens, first_gain, first_shift, w_query, w_key, w_value, w_control, w_output, second_gain, second_shift, w_inner, inner_bias, w_outer, outer_bias, cotangent):
@@ -770,55 +823,106 @@
     n1, n1_low = first_norm(clock, tokens)
     *mine, wi0, wi1, w_output = clock.sync(*mine, wi0, wi1, w_output)
     wi_x0 = over_x(wi0)
-    across = assemble(clock, mine, [exchange(v, "dp", dp, 1) for v in mine], wi_x0)
+    across = assemble(clock, mine, [exchange(v, "dp", dp, k + 1) for k, v in enumerate(mine)], wi_x0)
     packs = [own, across, own_core, over_core(across)]
     wi1, w_output = clock.sync(wi1, w_output)
     wi_x1, wo_x, wo_c = over_x(wi1), over_x(w_output), over_core(w_output)
     qkvf = project(clock, n1, packs)
+    w_outer = clock.sync(w_outer)
+    wu_x, wu_c = over_x(w_outer), over_core(w_outer)
     mixed, *saved = attention_forward(clock, qkvf)
-    wo_x, wi_x1, w_outer = clock.sync(wo_x, wi_x1, w_outer)
+    wo_x, wi_x1 = clock.sync(wo_x, wi_x1)
     wo = [w_output, wo_x, wo_c, over_core(wo_x)]
     wi = [w_inner, wi_x0, wi_x1, wi_c, over_core(wi_x0), over_core(wi_x1)]
-    wu_x, wu_c = over_x(w_outer), over_core(w_outer)
     resid, n2, r2, a2 = middle(clock, tokens, mixed, wo, packs)
     act, slope = ffn_inner(clock, a2, wi, packs)
-    u = Chain(clock, dp, (1, 2), (272, 240), outer_grad(clock, act, cotangent))
-    u.launch()
-    wu_x = clock.sync(wu_x)
-    wu = [w_outer, wu_x, wu_c, over_core(wu_x)]
-    din, sums = inner_back(clock, cotangent, slope, wu)
-    u.step()
-    *pair, dres, d_o = resid_back(clock, cotangent, n2, r2, din, sums, wo, wi, packs)
-    i = Chain(clock, dp, (1, 2), (48, 32, 64), pair)
-    u.more(i)
-    early = attention_backward(clock, qkvf, saved, d_o, 7, 4)
-    u.step()
-    i.step()
-    late = attention_backward(clock, qkvf, saved, d_o, 3, 4, early[1:])
-    i.more()
-    u.step()
-    pair_a, pair_b = project_grad(clock, n1_low, late[0], early[0], mixed, dres)
-    a, b = Chain(clock, dp, (1, 2), (144,), pair_a), Chain(clock, dp, (1,), (144,), pair_b)
-    u.step()
-    i.more(a, b)
-    a.step()
-    grad_tokens = input_grad(clock, tokens, late[0], early[0], dres, packs)
-    for c in (u, b, i):
-        c.step()
-    output = ffn_outer(clock, resid, act, wu, packs)
-    order = [a, u, i, a, i, b, a, u, b, i, a, b, i, a, i, b, a, b]
-    while any(c.busy for c in (u, i, a, b)):
-        c = order.pop(0) if order else next(c for c in (u, i, a, b) if c.busy)
+    chains, made = {}, {}
+
+    def start(name, send, keep):
+        chains[name] = Chain(clock, dp, STEPS[name], send, PIECES[name])
+        made[name] = keep
+
+    def outer():
+        keep, send = outer_grad(clock, act, cotangent)
+        start("u", send, lambda: keep)
+
+    def wait_outer():
+        wu_x = clock.sync(made["wu"])
+        made["wu"] = [w_outer, wu_x, wu_c, over_core(wu_x)]
+
+    def back_near():
+        made["din"] = inner_back(clock, cotangent, slope, [w_outer, wu_c], (0, 2))
+
+    def back_far():
+        d, partial = made["din"]
+        made["din"] = inner_back(clock, cotangent, d, [made["wu"][1], made["wu"][3]], (1, 3), [partial])
+
+    def inner_send():
+        start("i", inner_grad(clock, n2, *made["din"], 2), None)
+
+    def inner_keep():
+        made["i"] = inner_grad(clock, n2, *made["din"], 0)
+
+    def resid_grad():
+        made["dres"], made["do"] = resid_back(clock, cotangent, n2, r2, made["din"][0], wo, wi, packs)
+
+    def early():
+        made["early"] = attention_backward(clock, qkvf, saved, made["do"], 7, 4)
+
+    def late():
+        made["late"] = attention_backward(clock, qkvf, saved, made["do"], 3, 4, made["early"][1:])
+
+    def project_part(first):
+        return project_grad(clock, n1_low, made["late"][0], made["early"][0], mixed, made["dres"], first)
+
+    def project_send():
+        start("p", project_part(2), None)
+
+    def project_keep():
+        made["p"] = project_part(0)
+
+    def input_part():
+        made["tokens"] = input_grad(clock, tokens, made["late"][0], made["early"][0], made["dres"], packs)
+
+    def output_part():
+        made["output"] = ffn_outer(clock, resid, act, made["wu"], packs)
+
+    def finish(name):
+        total = chains[name].keep
+        if name == "u":
+            made["outer"] = finish_outer(clock, total)
+        elif name == "i":
+            made["inner"] = finish_inner(clock, total, w_inner, packs[0])
+        else:
+            made["project"] = finish_project(clock, total, packs[0])
+
+    def advance(name):
+        c = chains[name]
         if not c.busy:
-            continue
-        c.step()
-        if not c.busy and c is u:
-            grad_outer = finish_outer(clock, u.keep)
-        elif not c.busy and c is i:
-            grad_inner, *vectors = finish_inner(clock, i.keep, w_inner, packs[0])
-        elif not c.busy and c is a:
-            grad_query, grad_key, grad_output, before = finish_first(clock, a.keep, packs[0])
-    grad_value, grad_control, first_gain_grad, first_shift_grad = finish_last(clock, b.keep, packs[0], before)
+            return
+        if c.kind == "core":
+            keep = made[name]
+            c.keep = keep() if callable(keep) else keep
+        if c.split:
+            c.more()
+        else:
+            c.step()
+            if not c.busy:
+                finish(name)
+
+    made["wu"] = wu_x
+    kernels = dict(OG=outer, WU=wait_outer, IA=back_near, IB=back_far, IS=inner_send, IK=inner_keep, RB=resid_grad, AE=early, AL=late, PS=project_send, PK=project_keep, IN=input_part, FO=output_part)
+    for word in PLAN:
+        if word in kernels:
+            kernels[word]()
+        else:
+            advance(word)
+    while any(c.busy for c in chains.values()):
+        for name in "uip":
+            advance(name)
+    output, grad_tokens, grad_outer = made["output"], made["tokens"], made["outer"]
+    grad_inner, *vectors = made["inner"]
+    grad_query, grad_key, grad_value, grad_control, grad_output, first_gain_grad, first_shift_grad = made["project"]
     second_gain_grad, second_shift_grad, inner_bias_grad, outer_bias_grad = vectors
     return (
         output, grad_tokens, first_gain_grad, first_shift_grad, grad_query, grad_key, grad_value, grad_control,

time: 159 us -> 145 us (0.912)
  waiting for transfers between devices: 52.9 us -> 36.3 us
  starting transfers between devices: 38.4 us -> 41.1 us
    ppermute x47 -> x42, waiting for transfers between devices: 52.9 us -> 36.3 us  [exchange(): return lax.ppermute(value, axis, [(i, i ^ mask) for i in range(size)])]
    ppermute x47 -> x42, starting transfers between devices: 38.4 us -> 41.1 us  [exchange(): return lax.ppermute(value, axis, [(i, i ^ mask) for i in range(size)])]
    pallas_call x49 -> x41, Pallas kernels: 64.6 us -> 64.8 us  [call(): pl.pallas_call(body, in_specs=[VM] + [ANY if k in raw else VM for k in ra...]
  transfers between devices with their start and end apart: 47 -> 42, of which waited for: 22 -> 23; matrix products, arithmetic and copies ran while one was open for 0% -> 0% of each run, Pallas kernels for 38% -> 39%
where the time goes in v4:
time: 145 us
  Pallas kernels  64.8 us (45%)
  starting transfers between devices  41.1 us (28%)
  waiting for transfers between devices  36.3 us (25%)
    pallas_call x41, Pallas kernels, call(): pl.pallas_call(body, in_specs=[VM] + [ANY if k in raw else VM for k in ra...  64.8 us
    ppermute x42, starting transfers between devices, exchange(): return lax.ppermute(value, axis, [(i, i ^ mask) for i in range(size)])  41.1 us
    ppermute x42, waiting for transfers between devices, exchange(): return lax.ppermute(value, axis, [(i, i ^ mask) for i in range(size)])  36.3 us
  transfers between devices with their start and end apart: 42, of which 23 were waited for; matrix products, arithmetic and copies ran while one was open for 0% of the time, Pallas kernels for 39%

profile of v4, /device:TPU:0, one launch (start us, length us, event | category | flops | bytes accessed | tf_op | source)
XLA Modules:
  0.0 144.9 jit_solution(6839911644484020009)
XLA Ops:
  0.8 1.7 %begin.1 = (bf16[144,2048]{1,0:T(8,128)(2,1)S(1)}, bf16[144,512]{1,0:T(8,128)(2,1)S(1)}, bf16[144,512]{1,0:T(8,128)(2,1)S(1)}, bf16[64,2048]{1,0:T(8,128)(2,1)S(...) custom-call(s32[8,128]{1,0:T(8,128)S(1)} %iota.7.token, bf16[128,512]{1,0:T(8,128)(2,1)} %refs_0_.7, ...), custom_call_target="tpu_custom_call" | custom-call | flops 1000 | bytes 1024 | tf_op jit(solution)/shard_map/begin/pallas_call | solution.py:63
  2.5 3.0 %collective-permute-start = (bf16[144,512]{1,0:T(8,128)(2,1)S(1)}, bf16[144,512]{1,0:T(8,128)(2,1)S(1)}, u32[]{:S(2)}, u32[]{:S(2)}) collective-permute-start(bf16[144,512]{1,0:T(8,128)(2,1)S(1)} %get-tuple-element.154), channel_id=1, source_target_pairs={{0,2},{1,3},{2,0},{3,1},{4,6},{5,7},{6,4},{7,5},{8,10},{9,11},{10,... | collective-permute-start | bytes 442376 | tf_op jit(solution)/shard_map/ppermute | solution.py:599
  8.0 2.2 %collective-permute-done.refs_0_ = bf16[144,512]{1,0:T(8,128)(2,1)S(1)} collective-permute-done((bf16[144,512]{1,0:T(8,128)(2,1)S(1)}, bf16[144,512]{1,0:T(8,128)(2,1)S(1)}, u32[]{:S(2)}, u32[]{:S(2)}) %collective-permute-start) | collective-permute-done | bytes 147488 | tf_op jit(solution)/shard_map/ppermute | solution.py:599
  10.2 2.3 %collective-permute-done.1.refs_1_ = bf16[144,512]{1,0:T(8,128)(2,1)S(1)} collective-permute-done((bf16[144,512]{1,0:T(8,128)(2,1)S(1)}, bf16[144,512]{1,0:T(8,128)(2,1)S(1)}, u32[]{:S(2)}, u32[]{:S(2)}) %collective-permute-start.1) | collective-permute-done | bytes 147488 | tf_op jit(solution)/shard_map/ppermute | solution.py:599
  12.5 1.7 %collective-permute-start.4 = (bf16[64,2048]{1,0:T(8,128)(2,1)S(1)}, bf16[64,2048]{1,0:T(8,128)(2,1)S(1)}, u32[]{:S(2)}, u32[]{:S(2)}) collective-permute-start(bf16[64,2048]{1,0:T(8,128)(2,1)S(1)} %get-tuple-element.161), channel_id=1, source_target_pairs={{0,2},{1,3},{2,0},{3,1},{4,6},{5,7},{6,4},{7,5},{8,10},{9,11},{10,... | collective-permute-start | bytes 786440 | tf_op jit(solution)/shard_map/ppermute | solution.py:599
  17.3 2.0 %collective-permute-done.2.refs_2_ = bf16[144,512]{1,0:T(8,128)(2,1)S(1)} collective-permute-done((bf16[144,512]{1,0:T(8,128)(2,1)S(1)}, bf16[144,512]{1,0:T(8,128)(2,1)S(1)}, u32[]{:S(2)}, u32[]{:S(2)}) %collective-permute-start.2) | collective-permute-done | bytes 147488 | tf_op jit(solution)/shard_map/ppermute | solution.py:599
  23.6 2.5 %project.1 = (bf16[1024,2048]{1,0:T(8,128)(2,1)S(1)}, s32[8,128]{1,0:T(8,128)S(1)}) custom-call(s32[8,128]{1,0:T(8,128)S(1)} %get-tuple-element.165.token, f32[1024,512]{1,0:T(8,128)S(1)} %get-tuple-element.166.refs_0_, bf16[144,2048]{1,0:T(8,128)(2,1)S(1)} %get-tuple-element.167.refs_1_.refs_6_.refs_7_.refs_14_.refs_4_.refs_2_, ...), custom_call_target="tpu_custom_call" | custom-call | flops 1000 | bytes 1024 | tf_op jit(solution)/shard_map/project/pallas_call | solution.py:63
  26.1 7.4 %attention_forward.1 = (bf16[1024,512]{1,0:T(8,128)(2,1)S(1)}, bf16[1024,3072]{1,0:T(8,128)(2,1)S(1)}, bf16[8,128,1024]{2,1,0:T(8,128)(2,1)S(1)}, f32[8,8,512]{2,1,0:T(8,128)S(1)}, s32[8,128]{1,0:T(8,128)S(1)}) custom-call(s32[8,128]{1,0:T(8,128)S(1)} %get-tuple-element.170.token, bf16[1024,2048]{1,0:T(8,128)(2,1)S(1)} %get-tuple-element.171.refs_0_), custom_call_target="tpu_custom_call" | custom-call | flops 1000 | bytes 1024 | tf_op jit(solution)/shard_map/attention_forward/pallas_call | solution.py:63
  36.0 2.0 %middle.1 = (f32[1024,512]{1,0:T(8,128)S(1)}, bf16[1024,512]{1,0:T(8,128)(2,1)S(1)}, f32[1024,128]{1,0:T(8,128)S(1)}, bf16[1024,512]{1,0:T(8,128)(2,1)S(1)}, s32[8,128]{1,0:T(8,128)S(1)}) custom-call(s32[8,128]{1,0:T(8,128)S(1)} %get-tuple-element.175.token, bf16[1024,512]{1,0:T(8,128)(2,1)S(1)} %copy-done.2, ...), custom_call_target="tpu_custom_call" | custom-call | flops 1000 | bytes 1024 | tf_op jit(solution)/shard_map/middle/pallas_call | solution.py:63
  38.1 6.2 %ffn_inner.1 = (bf16[1024,2048]{1,0:T(8,128)(2,1)S(1)}, bf16[1024,2048]{1,0:T(8,128)(2,1)S(1)}, s32[8,128]{1,0:T(8,128)S(1)}) custom-call(s32[8,128]{1,0:T(8,128)S(1)} %get-tuple-element.178.token, bf16[1024,512]{1,0:T(8,128)(2,1)S(1)} %get-tuple-element.179.refs_0_, bf16[128,2048]{1,0:T(8,128)(2,1)S(1)} %copy-done.3, ...), custom_call_target="tpu_custom_call" | custom-call | flops 1000 | bytes 1024 | tf_op jit(solution)/shard_map/ffn_inner/pallas_call | solution.py:63
  44.3 2.4 %outer_grad.1 = (bf16[2,512,512]{2,1,0:T(8,128)(2,1)S(1)}, bf16[2,512,512]{2,1,0:T(8,128)(2,1)S(1)}, s32[8,128]{1,0:T(8,128)S(1)}) custom-call(s32[8,128]{1,0:T(8,128)S(1)} %get-tuple-element.181.token, bf16[1024,2048]{1,0:T(8,128)(2,1)S(1)} %get-tuple-element.182.refs_0_.refs_1_, bf16[1024,512]{1,0:T(8,128)(2,1)S(1)} %copy-done), custom_call_target="tpu_custom_call" | custom-call | flops 1000 | bytes 1024 | tf_op jit(solution)/shard_map/outer_grad/pallas_call | solution.py:63
  49.6 1.9 %collective-permute-done.16.refs_3_.refs_5_ = bf16[512,512]{1,0:T(8,128)(2,1)S(1)} collective-permute-done((bf16[512,512]{1,0:T(8,128)(2,1)S(1)}, bf16[512,512]{1,0:T(8,128)(2,1)S(1)}, u32[]{:S(2)}, u32[]{:S(2)}) %collective-permute-start.16) | collective-permute-done | bytes 524320 | tf_op jit(solution)/shard_map/ppermute | solution.py:599
  58.1 4.4 %resid_back.1 = (f32[1024,512]{1,0:T(8,128)S(1)}, bf16[1024,512]{1,0:T(8,128)(2,1)S(1)}, s32[8,128]{1,0:T(8,128)S(1)}) custom-call(s32[8,128]{1,0:T(8,128)S(1)} %get-tuple-element.202.token, bf16[1024,512]{1,0:T(8,128)(2,1)S(1)} %copy-done, bf16[1024,512]{1,0:T(8,128)(2,1)S(1)} %get-tuple-element.195.refs_0_.refs_1_, ...), custom_call_target="tpu_custom_call" | custom-call | flops 1000 | bytes 1024 | tf_op jit(solution)/shard_map/resid_back/pallas_call | solution.py:63
  67.9 5.3 %attention_backward.2 = (bf16[512,2048]{1,0:T(8,128)(2,1)S(1)}, f32[4,128,256]{2,1,0:T(8,128)S(1)}, f32[8,512]{1,0:T(8,128)S(1)}, s32[8,128]{1,0:T(8,128)S(1)}) custom-call(s32[8,128]{1,0:T(8,128)S(1)} %get-tuple-element.207.token, bf16[1024,2048]{1,0:T(8,128)(2,1)S(1)} %get-tuple-element.171.refs_0_, bf16[1024,3072]{1,0:T(8,128)(2,1)S(1)} %get-tuple-element.208.refs_1_, ...), custom_call_target="tpu_custom_call" | custom-call | flops 1000 | bytes 1024 | tf_op jit(solution)/shard_map/attention_backward/pallas_call | solution.py:63
  75.6 4.6 %collective-permute-done.23.refs_3_ = bf16[288,512]{1,0:T(8,128)(2,1)S(1)} collective-permute-done((bf16[288,512]{1,0:T(8,128)(2,1)S(1)}, bf16[288,512]{1,0:T(8,128)(2,1)S(1)}, u32[]{:S(2)}, u32[]{:S(2)}) %collective-permute-start.23) | collective-permute-done | bytes 294944 | tf_op jit(solution)/shard_map/ppermute | solution.py:599
  81.7 5.1 %attention_backward.3 = (bf16[512,2048]{1,0:T(8,128)(2,1)S(1)}, s32[8,128]{1,0:T(8,128)S(1)}) custom-call(s32[8,128]{1,0:T(8,128)S(1)} %get-tuple-element.220.token, bf16[1024,2048]{1,0:T(8,128)(2,1)S(1)} %get-tuple-element.171.refs_0_, bf16[1024,3072]{1,0:T(8,128)(2,1)S(1)} %get-tuple-element.208.refs_1_, ...), custom_call_target="tpu_custom_call" | custom-call | flops 1000 | bytes 1024 | tf_op jit(solution)/shard_map/attention_backward/pallas_call | solution.py:63
  87.1 1.6 %project_grad.2 = (bf16[2,144,2560]{2,1,0:T(8,128)(2,1)S(1)}, s32[8,128]{1,0:T(8,128)S(1)}) custom-call(s32[8,128]{1,0:T(8,128)S(1)} %get-tuple-element.229.token, bf16[1024,512]{1,0:T(8,128)(2,1)S(1)} %get-tuple-element.230.refs_0_, bf16[512,2048]{1,0:T(8,128)(2,1)S(1)} %get-tuple-element.231.refs_1_, bf16[512,2048]{1,0:T(8,128)(2,1)S(1)} %get-tuple-element.232.refs_2_, ...), custom_call_target="tpu_custom_call" | custom-call | flops 1000 | bytes 1024 | tf_op jit(solution)/shard_map/project_grad/pallas_call | solution.py:63
  88.8 1.6 %project_grad.3 = (bf16[2,144,2560]{2,1,0:T(8,128)(2,1)S(1)}, s32[8,128]{1,0:T(8,128)S(1)}) custom-call(s32[8,128]{1,0:T(8,128)S(1)} %get-tuple-element.234.token, bf16[1024,512]{1,0:T(8,128)(2,1)S(1)} %get-tuple-element.230.refs_0_, bf16[512,2048]{1,0:T(8,128)(2,1)S(1)} %get-tuple-element.231.refs_1_, bf16[512,2048]{1,0:T(8,128)(2,1)S(1)} %get-tuple-element.232.refs_2_, ...), custom_call_target="tpu_custom_call" | custom-call | flops 1000 | bytes 1024 | tf_op jit(solution)/shard_map/project_grad/pallas_call | solution.py:63
  90.4 1.7 %collective-permute-done.26.refs_1_ = bf16[2,144,2560]{2,1,0:T(8,128)(2,1)S(1)} collective-permute-done((bf16[2,144,2560]{2,1,0:T(8,128)(2,1)S(1)}, bf16[2,144,2560]{2,1,0:T(8,128)(2,1)S(1)}, u32[]{:S(2)}, u32[]{:S(2)}) %collective-permute-start.26) | collective-permute-done | bytes 1474592 | tf_op jit(solution)/shard_map/ppermute | solution.py:599
  93.2 2.6 %collective-permute-start.27 = (bf16[144,512]{1,0:T(8,128)(2,1)S(1)}, bf16[144,512]{1,0:T(8,128)(2,1)S(1)}, u32[]{:S(2)}, u32[]{:S(2)}) collective-permute-start(bf16[144,512]{1,0:T(8,128)(2,1)S(1)} %get-tuple-element.240.refs_0_), channel_id=1, source_target_pairs={{0,16},{4,20},{8,24},{12,28},{16,0},{20,4},{24,8},{28,12},{1,17},{... | collective-permute-start | bytes 442376 | tf_op jit(solution)/shard_map/ppermute | solution.py:599
  97.4 4.4 %input_grad.1 = (bf16[1024,512]{1,0:T(8,128)(2,1)}, s32[8,128]{1,0:T(8,128)S(1)}) custom-call(s32[8,128]{1,0:T(8,128)S(1)} %get-tuple-element.238.token, bf16[1024,512]{1,0:T(8,128)(2,1)S(1)} %copy-done.2, bf16[512,2048]{1,0:T(8,128)(2,1)S(1)} %get-tuple-element.231.refs_1_, bf16[512,2048]{1,0:T(8,128)(2,1)S(1)} %get-tuple-element.232.refs_2_, ...), custom_call_target="tpu_custom_call" | custom-call | flops 1000 | bytes 1024 | tf_op jit(solution)/shard_map/input_grad/pallas_call | solution.py:63
  104.3 2.8 %collective-permute-start.31 = (bf16[144,512]{1,0:T(8,128)(2,1)S(1)}, bf16[144,512]{1,0:T(8,128)(2,1)S(1)}, u32[]{:S(2)}, u32[]{:S(2)}) collective-permute-start(bf16[144,512]{1,0:T(8,128)(2,1)S(1)} %get-tuple-element.254.refs_0_), channel_id=1, source_target_pairs={{0,8},{4,12},{8,0},{12,4},{16,24},{20,28},{24,16},{28,20},{1,9},{5... | collective-permute-start | bytes 442376 | tf_op jit(solution)/shard_map/ppermute | solution.py:599
  107.2 3.9 %ffn_outer.1 = (bf16[1024,512]{1,0:T(8,128)(2,1)}, s32[8,128]{1,0:T(8,128)S(1)}) custom-call(s32[8,128]{1,0:T(8,128)S(1)} %get-tuple-element.244.token, f32[1024,512]{1,0:T(8,128)S(1)} %get-tuple-element.245.refs_0_, bf16[1024,2048]{1,0:T(8,128)(2,1)S(1)} %get-tuple-element.182.refs_0_.refs_1_, bf16[512,512]{1,0:T(8,128)(2,1)S(1)} %copy-done.4, ...), custom_call_target="tpu_custom_call" | custom-call | flops 1000 | bytes 1024 | tf_op jit(solution)/shard_map/ffn_outer/pallas_call | solution.py:63
  113.9 2.0 %collective-permute-start.34 = (bf16[144,640]{1,0:T(8,128)(2,1)S(1)}, bf16[144,640]{1,0:T(8,128)(2,1)S(1)}, u32[]{:S(2)}, u32[]{:S(2)}) collective-permute-start(bf16[144,640]{1,0:T(8,128)(2,1)S(1)} %get-tuple-element.259), channel_id=1, source_target_pairs={{0,12},{4,8},{8,4},{12,0},{16,28},{20,24},{24,20},{28,16},{1,13},{... | collective-permute-start | bytes 552968 | tf_op jit(solution)/shard_map/ppermute | solution.py:599
  117.7 3.4 %collective-permute-done.32.refs_1_ = bf16[144,640]{1,0:T(8,128)(2,1)S(1)} collective-permute-done((bf16[144,640]{1,0:T(8,128)(2,1)S(1)}, bf16[144,640]{1,0:T(8,128)(2,1)S(1)}, u32[]{:S(2)}, u32[]{:S(2)}) %collective-permute-start.32) | collective-permute-done | bytes 184352 | tf_op jit(solution)/shard_map/ppermute | solution.py:599
  121.2 3.2 %collective-permute-done.34.refs_3_ = bf16[144,640]{1,0:T(8,128)(2,1)S(1)} collective-permute-done((bf16[144,640]{1,0:T(8,128)(2,1)S(1)}, bf16[144,640]{1,0:T(8,128)(2,1)S(1)}, u32[]{:S(2)}, u32[]{:S(2)}) %collective-permute-start.34) | collective-permute-done | bytes 184352 | tf_op jit(solution)/shard_map/ppermute | solution.py:599
  124.6 2.2 %collective-permute-start.37 = (bf16[144,640]{1,0:T(8,128)(2,1)S(1)}, bf16[144,640]{1,0:T(8,128)(2,1)S(1)}, u32[]{:S(2)}, u32[]{:S(2)}) collective-permute-start(bf16[144,640]{1,0:T(8,128)(2,1)S(1)} %get-tuple-element.267.refs_0_), channel_id=1, source_target_pairs={{0,16},{4,20},{8,24},{12,28},{16,0},{20,4},{24,8},{28,12},{1,17},{... | collective-permute-start | bytes 552968 | tf_op jit(solution)/shard_map/ppermute | solution.py:599
  131.2 1.9 %collective-permute-done.37.refs_1_ = bf16[144,640]{1,0:T(8,128)(2,1)S(1)} collective-permute-done((bf16[144,640]{1,0:T(8,128)(2,1)S(1)}, bf16[144,640]{1,0:T(8,128)(2,1)S(1)}, u32[]{:S(2)}, u32[]{:S(2)}) %collective-permute-start.37) | collective-permute-done | bytes 184352 | tf_op jit(solution)/shard_map/ppermute | solution.py:599
  134.2 1.8 %collective-permute-start.40 = (bf16[144,640]{1,0:T(8,128)(2,1)S(1)}, bf16[144,640]{1,0:T(8,128)(2,1)S(1)}, u32[]{:S(2)}, u32[]{:S(2)}) collective-permute-start(bf16[144,640]{1,0:T(8,128)(2,1)S(1)} %get-tuple-element.273.refs_0_), channel_id=1, source_target_pairs={{0,8},{4,12},{8,0},{12,4},{16,24},{20,28},{24,16},{28,20},{1,9},{5... | collective-permute-start | bytes 552968 | tf_op jit(solution)/shard_map/ppermute | solution.py:599
  138.1 1.7 %collective-permute-done.41.refs_3_ = bf16[144,640]{1,0:T(8,128)(2,1)S(1)} collective-permute-done((bf16[144,640]{1,0:T(8,128)(2,1)S(1)}, bf16[144,640]{1,0:T(8,128)(2,1)S(1)}, u32[]{:S(2)}, u32[]{:S(2)}) %collective-permute-start.41) | collective-permute-done | bytes 184352 | tf_op jit(solution)/shard_map/ppermute | solution.py:599
  139.8 1.7 %collective-permute-done.40.refs_2_ = bf16[144,640]{1,0:T(8,128)(2,1)S(1)} collective-permute-done((bf16[144,640]{1,0:T(8,128)(2,1)S(1)}, bf16[144,640]{1,0:T(8,128)(2,1)S(1)}, u32[]{:S(2)}, u32[]{:S(2)}) %collective-permute-start.40) | collective-permute-done | bytes 184352 | tf_op jit(solution)/shard_map/ppermute | solution.py:599
  142.5 2.2 %finish_project.1 = (f32[128,512]{1,0:T(8,128)}, f32[128,512]{1,0:T(8,128)}, f32[128,512]{1,0:T(8,128)}, f32[128,512]{1,0:T(8,128)}, f32[128,512]{1,0:T(8,128)},...) custom-call(s32[8,128]{1,0:T(8,128)S(1)} %get-tuple-element.274.token, ...), custom_call_target="tpu_custom_call" | custom-call | flops 1000 | bytes 1024 | tf_op jit(solution)/shard_map/finish_project/pallas_call | solution.py:63
  (107 shorter events, 50.0 us)
Async XLA Ops:
  2.5 7.7 %collective-permute-start = (bf16[144,512]{1,0:T(8,128)(2,1)S(1)}, bf16[144,512]{1,0:T(8,128)(2,1)S(1)}, u32[]{:S(2)}, u32[]{:S(2)}) collective-permute-start(bf16[144,512]{1,0:T(8,128)(2,1)S(1)} %get-tuple-element.154), channel_id=1, source_target_pairs={{0,2},{1,3},{2,0},{3,1},{4,6},{5,7},{6,4},{7,5},{8,10},{9,11},{10,... | collective-permute-start | bytes 442376 | tf_op jit(solution)/shard_map/ppermute | solution.py:599
  5.5 7.0 %collective-permute-start.1 = (bf16[144,512]{1,0:T(8,128)(2,1)S(1)}, bf16[144,512]{1,0:T(8,128)(2,1)S(1)}, u32[]{:S(2)}, u32[]{:S(2)}) collective-permute-start(bf16[144,512]{1,0:T(8,128)(2,1)S(1)} %get-tuple-element.155), channel_id=1, source_target_pairs={{0,2},{1,3},{2,0},{3,1},{4,6},{5,7},{6,4},{7,5},{8,10},{9,11},{10,... | collective-permute-start | bytes 442376 | tf_op jit(solution)/shard_map/ppermute | solution.py:599
  12.5 8.4 %collective-permute-start.4 = (bf16[64,2048]{1,0:T(8,128)(2,1)S(1)}, bf16[64,2048]{1,0:T(8,128)(2,1)S(1)}, u32[]{:S(2)}, u32[]{:S(2)}) collective-permute-start(bf16[64,2048]{1,0:T(8,128)(2,1)S(1)} %get-tuple-element.161), channel_id=1, source_target_pairs={{0,2},{1,3},{2,0},{3,1},{4,6},{5,7},{6,4},{7,5},{8,10},{9,11},{10,... | collective-permute-start | bytes 786440 | tf_op jit(solution)/shard_map/ppermute | solution.py:599
  17.3 6.2 %collective-permute-start.5 = (bf16[144,2048]{1,0:T(8,128)(2,1)S(1)}, bf16[144,2048]{1,0:T(8,128)(2,1)S(1)}, u32[]{:S(2)}, u32[]{:S(2)}) collective-permute-start(bf16[144,2048]{1,0:T(8,128)(2,1)S(1)} %get-tuple-element.167.refs_1_.refs_6_.refs_7_.refs_14_.refs_4_.refs_2_), channel_id=1, source_target_pairs={{0,1},{1,0},{2,3},{3,2},{4,5},{5,4},{6,7},{7,6},{8,9},{9,8},{10,11... | collective-permute-start | bytes 1769480 | tf_op jit(solution)/shard_map/ppermute | solution.py:599
  21.2 12.3 %collective-permute-start.8 = (bf16[64,2048]{1,0:T(8,128)(2,1)S(1)}, bf16[64,2048]{1,0:T(8,128)(2,1)S(1)}, u32[]{:S(2)}, u32[]{:S(2)}) collective-permute-start(bf16[64,2048]{1,0:T(8,128)(2,1)S(1)} %get-tuple-element.174), channel_id=1, source_target_pairs={{0,2},{1,3},{2,0},{3,1},{4,6},{5,7},{6,4},{7,5},{8,10},{9,11},{10,... | collective-permute-start | bytes 786440 | tf_op jit(solution)/shard_map/ppermute | solution.py:599
  21.8 16.3 %collective-permute-start.11 = (bf16[128,2048]{1,0:T(8,128)(2,1)S(1)}, bf16[128,2048]{1,0:T(8,128)(2,1)S(1)}, u32[]{:S(2)}, u32[]{:S(2)}) collective-permute-start(bf16[128,2048]{1,0:T(8,128)(2,1)S(1)} %copy-done.3), channel_id=1, source_target_pairs={{0,1},{1,0},{2,3},{3,2},{4,5},{5,4},{6,7},{7,6},{8,9},{9,8},{10,11... | collective-permute-start | bytes 1572872 | tf_op jit(solution)/shard_map/ppermute | solution.py:599
  22.0 11.5 %collective-permute-start.7 = (bf16[128,512]{1,0:T(8,128)(2,1)S(1)}, bf16[128,512]{1,0:T(8,128)(2,1)S(1)}, u32[]{:S(2)}, u32[]{:S(2)}) collective-permute-start(bf16[128,512]{1,0:T(8,128)(2,1)S(1)} %copy-done.5), channel_id=1, source_target_pairs={{0,2},{1,3},{2,0},{3,1},{4,6},{5,7},{6,4},{7,5},{8,10},{9,11},{10,... | collective-permute-start | bytes 393224 | tf_op jit(solution)/shard_map/ppermute | solution.py:599
  23.5 14.6 %collective-permute-start.12 = (bf16[64,2048]{1,0:T(8,128)(2,1)S(1)}, bf16[64,2048]{1,0:T(8,128)(2,1)S(1)}, u32[]{:S(2)}, u32[]{:S(2)}) collective-permute-start(bf16[64,2048]{1,0:T(8,128)(2,1)S(1)} %collective-permute-done.4.refs_4_.refs_2_.refs_9_), channel_id=1, source_target_pairs={{0,1},{1,0},{2,3},{3,2},{4,5},{5,4},{6,7},{7,6},{8,9},{9,8},{10,11... | collective-permute-start | bytes 786440 | tf_op jit(solution)/shard_map/ppermute | solution.py:599
  35.4 14.2 %collective-permute-start.15 = (bf16[512,512]{1,0:T(8,128)(2,1)S(1)}, bf16[512,512]{1,0:T(8,128)(2,1)S(1)}, u32[]{:S(2)}, u32[]{:S(2)}) collective-permute-start(bf16[512,512]{1,0:T(8,128)(2,1)S(1)} %copy-done.4), channel_id=1, source_target_pairs={{0,2},{1,3},{2,0},{3,1},{4,6},{5,7},{6,4},{7,5},{8,10},{9,11},{10,... | collective-permute-start | bytes 1572872 | tf_op jit(solution)/shard_map/ppermute | solution.py:599
  35.9 11.3 %collective-permute-start.14 = (bf16[512,512]{1,0:T(8,128)(2,1)S(1)}, bf16[512,512]{1,0:T(8,128)(2,1)S(1)}, u32[]{:S(2)}, u32[]{:S(2)}) collective-permute-start(bf16[512,512]{1,0:T(8,128)(2,1)S(1)} %copy-done.4), channel_id=1, source_target_pairs={{0,1},{1,0},{2,3},{3,2},{4,5},{5,4},{6,7},{7,6},{8,9},{9,8},{10,11... | collective-permute-start | bytes 1572872 | tf_op jit(solution)/shard_map/ppermute | solution.py:599
  46.7 6.2 %collective-permute-start.17 = (bf16[2,512,512]{2,1,0:T(8,128)(2,1)S(1)}, bf16[2,512,512]{2,1,0:T(8,128)(2,1)S(1)}, u32[]{:S(2)}, u32[]{:S(2)}) collective-permute-start(bf16[2,512,512]{2,1,0:T(8,128)(2,1)S(1)} %get-tuple-element.193), channel_id=1, source_target_pairs={{0,1},{1,0},{2,3},{3,2},{4,5},{5,4},{6,7},{7,6},{8,9},{9,8},{10,11... | collective-permute-start | bytes 3145736 | tf_op jit(solution)/shard_map/ppermute | solution.py:599
  54.7 8.9 %collective-permute-start.19 = (bf16[272,512]{1,0:T(8,128)(2,1)S(1)}, bf16[272,512]{1,0:T(8,128)(2,1)S(1)}, u32[]{:S(2)}, u32[]{:S(2)}) collective-permute-start(bf16[272,512]{1,0:T(8,128)(2,1)S(1)} %get-tuple-element.205), channel_id=1, source_target_pairs={{0,2},{1,3},{2,0},{3,1},{4,6},{5,7},{6,4},{7,5},{8,10},{9,11},{10,... | collective-permute-start | bytes 835592 | tf_op jit(solution)/shard_map/ppermute | solution.py:599
  63.6 9.6 %collective-permute-start.20 = (bf16[240,512]{1,0:T(8,128)(2,1)S(1)}, bf16[240,512]{1,0:T(8,128)(2,1)S(1)}, u32[]{:S(2)}, u32[]{:S(2)}) collective-permute-start(bf16[240,512]{1,0:T(8,128)(2,1)S(1)} %get-tuple-element.214), channel_id=1, source_target_pairs={{0,2},{1,3},{2,0},{3,1},{4,6},{5,7},{6,4},{7,5},{8,10},{9,11},{10,... | collective-permute-start | bytes 737288 | tf_op jit(solution)/shard_map/ppermute | solution.py:599
  64.4 10.5 %collective-permute-start.21 = (bf16[288,512]{1,0:T(8,128)(2,1)S(1)}, bf16[288,512]{1,0:T(8,128)(2,1)S(1)}, u32[]{:S(2)}, u32[]{:S(2)}) collective-permute-start(bf16[288,512]{1,0:T(8,128)(2,1)S(1)} %get-tuple-element.217), channel_id=1, source_target_pairs={{0,4},{4,0},{8,12},{12,8},{16,20},{20,16},{24,28},{28,24},{1,5},{5... | collective-permute-start | bytes 884744 | tf_op jit(solution)/shard_map/ppermute | solution.py:599
  65.6 9.9 %collective-permute-start.22 = (bf16[288,512]{1,0:T(8,128)(2,1)S(1)}, bf16[288,512]{1,0:T(8,128)(2,1)S(1)}, u32[]{:S(2)}, u32[]{:S(2)}) collective-permute-start(bf16[288,512]{1,0:T(8,128)(2,1)S(1)} %get-tuple-element.218), channel_id=1, source_target_pairs={{0,8},{4,12},{8,0},{12,4},{16,24},{20,28},{24,16},{28,20},{1,9},{5... | collective-permute-start | bytes 884744 | tf_op jit(solution)/shard_map/ppermute | solution.py:599
  67.2 13.0 %collective-permute-start.23 = (bf16[288,512]{1,0:T(8,128)(2,1)S(1)}, bf16[288,512]{1,0:T(8,128)(2,1)S(1)}, u32[]{:S(2)}, u32[]{:S(2)}) collective-permute-start(bf16[288,512]{1,0:T(8,128)(2,1)S(1)} %get-tuple-element.219), channel_id=1, source_target_pairs={{0,12},{4,8},{8,4},{12,0},{16,28},{20,24},{24,20},{28,16},{1,13},{... | collective-permute-start | bytes 884744 | tf_op jit(solution)/shard_map/ppermute | solution.py:599
  73.6 13.2 %collective-permute-start.24 = (bf16[512,256]{1,0:T(8,128)(2,1)S(1)}, bf16[512,256]{1,0:T(8,128)(2,1)S(1)}, u32[]{:S(2)}, u32[]{:S(2)}) collective-permute-start(bf16[512,256]{1,0:T(8,128)(2,1)S(1)} %get-tuple-element.225), channel_id=1, source_target_pairs={{0,4},{4,0},{8,12},{12,8},{16,20},{20,16},{24,28},{28,24},{1,5},{5... | collective-permute-start | bytes 786440 | tf_op jit(solution)/shard_map/ppermute | solution.py:599
  80.3 6.7 %collective-permute-start.25 = (bf16[144,512]{1,0:T(8,128)(2,1)S(1)}, bf16[144,512]{1,0:T(8,128)(2,1)S(1)}, u32[]{:S(2)}, u32[]{:S(2)}) collective-permute-start(bf16[144,512]{1,0:T(8,128)(2,1)S(1)} %get-tuple-element.228), channel_id=1, source_target_pairs={{0,2},{1,3},{2,0},{3,1},{4,6},{5,7},{6,4},{7,5},{8,10},{9,11},{10,... | collective-permute-start | bytes 442376 | tf_op jit(solution)/shard_map/ppermute | solution.py:599
  92.4 19.5 %collective-permute-start.30 = (bf16[144,2560]{1,0:T(8,128)(2,1)S(1)}, bf16[144,2560]{1,0:T(8,128)(2,1)S(1)}, u32[]{:S(2)}, u32[]{:S(2)}) collective-permute-start(bf16[144,2560]{1,0:T(8,128)(2,1)S(1)} %get-tuple-element.252), channel_id=1, source_target_pairs={{0,2},{1,3},{2,0},{3,1},{4,6},{5,7},{6,4},{7,5},{8,10},{9,11},{10,... | collective-permute-start | bytes 2211848 | tf_op jit(solution)/shard_map/ppermute | solution.py:599
  93.2 9.7 %collective-permute-start.27 = (bf16[144,512]{1,0:T(8,128)(2,1)S(1)}, bf16[144,512]{1,0:T(8,128)(2,1)S(1)}, u32[]{:S(2)}, u32[]{:S(2)}) collective-permute-start(bf16[144,512]{1,0:T(8,128)(2,1)S(1)} %get-tuple-element.240.refs_0_), channel_id=1, source_target_pairs={{0,16},{4,20},{8,24},{12,28},{16,0},{20,4},{24,8},{28,12},{1,17},{... | collective-permute-start | bytes 442376 | tf_op jit(solution)/shard_map/ppermute | solution.py:599
  95.8 7.1 %collective-permute-start.28 = (bf16[512,128]{1,0:T(8,128)(2,1)S(1)}, bf16[512,128]{1,0:T(8,128)(2,1)S(1)}, u32[]{:S(2)}, u32[]{:S(2)}) collective-permute-start(bf16[512,128]{1,0:T(8,128)(2,1)S(1)} %get-tuple-element.243), channel_id=1, source_target_pairs={{0,8},{4,12},{8,0},{12,4},{16,24},{20,28},{24,16},{28,20},{1,9},{5... | collective-permute-start | bytes 393224 | tf_op jit(solution)/shard_map/ppermute | solution.py:599
  103.0 8.8 %collective-permute-start.29 = (bf16[512,128]{1,0:T(8,128)(2,1)S(1)}, bf16[512,128]{1,0:T(8,128)(2,1)S(1)}, u32[]{:S(2)}, u32[]{:S(2)}) collective-permute-start(bf16[512,128]{1,0:T(8,128)(2,1)S(1)} %get-tuple-element.249.refs_0_), channel_id=1, source_target_pairs={{0,16},{4,20},{8,24},{12,28},{16,0},{20,4},{24,8},{28,12},{1,17},{... | collective-permute-start | bytes 393224 | tf_op jit(solution)/shard_map/ppermute | solution.py:599
  104.3 11.6 %collective-permute-start.31 = (bf16[144,512]{1,0:T(8,128)(2,1)S(1)}, bf16[144,512]{1,0:T(8,128)(2,1)S(1)}, u32[]{:S(2)}, u32[]{:S(2)}) collective-permute-start(bf16[144,512]{1,0:T(8,128)(2,1)S(1)} %get-tuple-element.254.refs_0_), channel_id=1, source_target_pairs={{0,8},{4,12},{8,0},{12,4},{16,24},{20,28},{24,16},{28,20},{1,9},{5... | collective-permute-start | bytes 442376 | tf_op jit(solution)/shard_map/ppermute | solution.py:599
  112.4 8.8 %collective-permute-start.32 = (bf16[144,640]{1,0:T(8,128)(2,1)S(1)}, bf16[144,640]{1,0:T(8,128)(2,1)S(1)}, u32[]{:S(2)}, u32[]{:S(2)}) collective-permute-start(bf16[144,640]{1,0:T(8,128)(2,1)S(1)} %get-tuple-element.257), channel_id=1, source_target_pairs={{0,4},{4,0},{8,12},{12,8},{16,20},{20,16},{24,28},{28,24},{1,5},{5... | collective-permute-start | bytes 552968 | tf_op jit(solution)/shard_map/ppermute | solution.py:599
  113.7 7.6 %collective-permute-start.33 = (bf16[144,640]{1,0:T(8,128)(2,1)S(1)}, bf16[144,640]{1,0:T(8,128)(2,1)S(1)}, u32[]{:S(2)}, u32[]{:S(2)}) collective-permute-start(bf16[144,640]{1,0:T(8,128)(2,1)S(1)} %get-tuple-element.258), channel_id=1, source_target_pairs={{0,8},{4,12},{8,0},{12,4},{16,24},{20,28},{24,16},{28,20},{1,9},{5... | collective-permute-start | bytes 552968 | tf_op jit(solution)/shard_map/ppermute | solution.py:599
  113.9 10.5 %collective-permute-start.34 = (bf16[144,640]{1,0:T(8,128)(2,1)S(1)}, bf16[144,640]{1,0:T(8,128)(2,1)S(1)}, u32[]{:S(2)}, u32[]{:S(2)}) collective-permute-start(bf16[144,640]{1,0:T(8,128)(2,1)S(1)} %get-tuple-element.259), channel_id=1, source_target_pairs={{0,12},{4,8},{8,4},{12,0},{16,28},{20,24},{24,20},{28,16},{1,13},{... | collective-permute-start | bytes 552968 | tf_op jit(solution)/shard_map/ppermute | solution.py:599
  116.2 13.3 %collective-permute-start.36 = (bf16[144,1024]{1,0:T(8,128)(2,1)S(1)}, bf16[144,1024]{1,0:T(8,128)(2,1)S(1)}, u32[]{:S(2)}, u32[]{:S(2)}) collective-permute-start(bf16[144,1024]{1,0:T(8,128)(2,1)S(1)} %get-tuple-element.263.refs_0_), channel_id=1, source_target_pairs={{0,4},{4,0},{8,12},{12,8},{16,20},{20,16},{24,28},{28,24},{1,5},{5... | collective-permute-start | bytes 884744 | tf_op jit(solution)/shard_map/ppermute | solution.py:599
  117.5 10.0 %collective-permute-start.35 = (bf16[512,128]{1,0:T(8,128)(2,1)S(1)}, bf16[512,128]{1,0:T(8,128)(2,1)S(1)}, u32[]{:S(2)}, u32[]{:S(2)}) collective-permute-start(bf16[512,128]{1,0:T(8,128)(2,1)S(1)} %get-tuple-element.261.refs_0_), channel_id=1, source_target_pairs={{0,8},{4,12},{8,0},{12,4},{16,24},{20,28},{24,16},{28,20},{1,9},{5... | collective-permute-start | bytes 393224 | tf_op jit(solution)/shard_map/ppermute | solution.py:599
  124.6 8.5 %collective-permute-start.37 = (bf16[144,640]{1,0:T(8,128)(2,1)S(1)}, bf16[144,640]{1,0:T(8,128)(2,1)S(1)}, u32[]{:S(2)}, u32[]{:S(2)}) collective-permute-start(bf16[144,640]{1,0:T(8,128)(2,1)S(1)} %get-tuple-element.267.refs_0_), channel_id=1, source_target_pairs={{0,16},{4,20},{8,24},{12,28},{16,0},{20,4},{24,8},{28,12},{1,17},{... | collective-permute-start | bytes 552968 | tf_op jit(solution)/shard_map/ppermute | solution.py:599
  127.8 8.9 %collective-permute-start.38 = (bf16[512,256]{1,0:T(8,128)(2,1)S(1)}, bf16[512,256]{1,0:T(8,128)(2,1)S(1)}, u32[]{:S(2)}, u32[]{:S(2)}) collective-permute-start(bf16[512,256]{1,0:T(8,128)(2,1)S(1)} %get-tuple-element.269.refs_0_), channel_id=1, source_target_pairs={{0,4},{4,0},{8,12},{12,8},{16,20},{20,16},{24,28},{28,24},{1,5},{5... | collective-permute-start | bytes 786440 | tf_op jit(solution)/shard_map/ppermute | solution.py:599
  133.2 6.6 %collective-permute-start.41 = (bf16[144,640]{1,0:T(8,128)(2,1)S(1)}, bf16[144,640]{1,0:T(8,128)(2,1)S(1)}, u32[]{:S(2)}, u32[]{:S(2)}) collective-permute-start(bf16[144,640]{1,0:T(8,128)(2,1)S(1)} %get-tuple-element.273.refs_0_), channel_id=1, source_target_pairs={{0,12},{4,8},{8,4},{12,0},{16,28},{20,24},{24,20},{28,16},{1,13},{... | collective-permute-start | bytes 552968 | tf_op jit(solution)/shard_map/ppermute | solution.py:599
  134.2 7.3 %collective-permute-start.40 = (bf16[144,640]{1,0:T(8,128)(2,1)S(1)}, bf16[144,640]{1,0:T(8,128)(2,1)S(1)}, u32[]{:S(2)}, u32[]{:S(2)}) collective-permute-start(bf16[144,640]{1,0:T(8,128)(2,1)S(1)} %get-tuple-element.273.refs_0_), channel_id=1, source_target_pairs={{0,8},{4,12},{8,0},{12,4},{16,24},{20,28},{24,16},{28,20},{1,9},{5... | collective-permute-start | bytes 552968 | tf_op jit(solution)/shard_map/ppermute | solution.py:599
  (16 other events, 103.9 us)

commit v5 on v4

--- a/solution.py
+++ b/solution.py
@@ -16,6 +16,7 @@
 UNROLL = 2
 JOIN = 4
 ROWS = 512
+WHOLE = 1024
 EPS = 1e-5
 WEIGHT = 1000
 MASKS = (0, 2, 1, 3)
@@ -108,12 +109,15 @@
     return jnp.concatenate([r[128:129, start : start + width] for r in packs], axis=1).astype(F32)
 
 
-def row_loop(T, body):
+def row_loop(T, body, rows=ROWS):
     def step(c, _):
-        body(pl.ds(pl.multiple_of(c * ROWS, ROWS), ROWS))
+        body(pl.ds(pl.multiple_of(c * rows, rows), rows))
         return 0
 
-    lax.fori_loop(0, T // ROWS, step, 0)
+    if rows < T:
+        lax.fori_loop(0, T // rows, step, 0)
+    else:
+        body(slice(None))
 
 
 def stats(x):
@@ -196,7 +200,7 @@
             out = mm(a1, stack_packs(packs, cols))
             qkvf[rows, cols] = (jnp.exp(out) if n == 3 else out).astype(BF16)
 
-    row_loop(n1.shape[0], body)
+    row_loop(n1.shape[0], body, WHOLE)
 
 
 def project(clock, n1, packs):
@@ -549,26 +553,30 @@
     return call(clock, resid_back_kernel, "resid_back", outs, [dy, n2, r2, din, *wo, *wi, *packs], [pltpu.VMEM((ROWS, 512), F32)])
 
 
-def project_grad_kernel(first, token, n1, early, late, mixed, dres, out):
+def project_grad_kernel(first, starts, token, n1, early, late, mixed, dres, out):
     half = early.shape[0]
     blocks = wide(blocks_of(token), 128)
     n = n1[:, 128 * first : 128 * (first + 2)]
-    d = dres[...].astype(BF16)
-    for start in (0, 1024):
-        cols = slice(start, start + 1024)
+    for at, start in enumerate(starts):
+        cols, dest = slice(start, start + 1024), slice(1024 * at, 1024 * (at + 1))
         m = (mm_tn(n[0:half], early[:, cols]) + mm_tn(n[half:], late[:, cols])).astype(BF16)
         total = sum(jnp.sum(r[:, cols].astype(F32), axis=0, keepdims=True) for r in (early, late))
         tail = jnp.broadcast_to(total, (16, 1024)).astype(BF16)
         for k in range(2):
-            out[k, 0:128, cols] = m[128 * k : 128 * (k + 1)]
-            out[k, 128:144, cols] = tail
-    for k in range(2):
-        out[k, 0:128, 2048:] = mm_tn(mixed[:, blocks[first + k]], d).astype(BF16)
-        out[k, 128:144, 2048:] = jnp.zeros((16, 512), BF16)
-
-
-def project_grad(clock, n1, early, late, mixed, dres, first):
-    return call(clock, functools.partial(project_grad_kernel, first), "project_grad", [shape((2, 144, 2560))], [n1, early, late, mixed, dres])[0]
+            out[k, 0:128, dest] = m[128 * k : 128 * (k + 1)]
+            out[k, 128:144, dest] = tail
+    rest = 1024 * len(starts)
+    if rest < out.shape[2]:
+        d = dres[...].astype(BF16)
+        for k in range(2):
+            out[k, 0:128, rest:] = mm_tn(mixed[:, blocks[first + k]], d).astype(BF16)
+            out[k, 128:144, rest:] = jnp.zeros((16, 512), BF16)
+
+
+def project_grad(clock, n1, early, late, mixed, dres, first, starts=(0, 1024)):
+    width = 1024 * len(starts) + (512 if 1024 in starts else 0)
+    kernel = functools.partial(project_grad_kernel, first, starts)
+    return call(clock, kernel, "project_grad", [shape((2, 144, width))], [n1, early, late, mixed, dres])[0]
 
 
 def input_grad_kernel(token, tokens, early, late, dres, p0, p1, p2, p3, out, scr, result, sems):
@@ -637,9 +645,12 @@
     gots, outs, whole = refs[: -1 - n_outs], refs[-1 - n_outs : -1], refs[-1]
     bit = lambda m: lax.rem(lax.div(position(token, 1), m), 2)
     if kind == "core":
-        rows = keep.shape[1]
-        for k in range(2):
-            whole[rows * k : rows * (k + 1), :] = add(keep[k], gots[0][k]).astype(BF16)
+        rows, start = keep.shape[1], 0
+        for got in gots:
+            cols = slice(start, start + got.shape[2])
+            for k in range(2):
+                whole[rows * k : rows * (k + 1), cols] = add(keep[k, :, cols], got[k]).astype(BF16)
+            start += got.shape[2]
     elif kind == "beside":
         whole[:, half_at(bit(mask), whole.shape[1])] = keep[...]
         whole[:, half_at(1 - bit(mask), whole.shape[1])] = gots[0][...]
@@ -673,7 +684,7 @@
 class Chain:
     def __init__(self, clock, dp, steps, send, pieces=()):
         self.clock, self.dp = clock, dp
-        self.pieces = pieces or (send.shape[1],)
+        self.pieces = pieces or (send[0].shape[1],)
         masks = [1 << k for k in range(dp.bit_length() - 1)]
         used = [1, 2] if "quarter" in steps else [m for m in masks if f"half{m}" in steps]
         self.todo = []
@@ -683,7 +694,7 @@
             else:
                 kind = name.rstrip("0123456789")
                 self.todo.append((kind, int(name[len(kind) :] or 0)))
-        self.send = [send]
+        self.send = send
         self.busy = True
         self.launch()
 
@@ -691,7 +702,7 @@
         self.kind, self.mask = self.todo.pop(0)
         self.split = 0
         if self.kind == "core":
-            self.got = [over_core(self.send[0])]
+            self.got = [over_core(v) for v in self.send]
         elif self.kind == "x":
             self.got = [over_x(self.send.pop(0))]
             self.split = len(self.send)
@@ -779,13 +790,15 @@
 def finish_project_kernel(_, total, pack, *refs):
     outs, (buf, small, sems) = refs[:-3], refs[-3:]
     gain, shift = (column(pack[128:129, k : k + 128].astype(F32)) for k in (0, 128))
+    copies = []
+    for k, out in enumerate(outs[:5]):
+        cols = slice(512 * k, 512 * (k + 1))
+        part = total[0:128, cols].astype(F32)
+        buf[:, cols] = gain * part + shift * total[128:144, cols].astype(F32)[0:1, :] if k < 4 else part
+        copies.append(pltpu.make_async_copy(buf.at[:, cols], out, sems.at[k]))
+        copies[-1].start()
     m = total[0:128, 0:2048].astype(F32)
     tail = total[128:144, 0:2048].astype(F32)[0:1, :]
-    buf[:, 0:2048] = gain * m + shift * tail
-    buf[:, 2048:2560] = total[0:128, 2048:2560].astype(F32)
-    copies = [pltpu.make_async_copy(buf.at[:, 512 * k : 512 * (k + 1)], out, sems.at[k]) for k, out in enumerate(outs[:5])]
-    for copy in copies:
-        copy.start()
     w = pack[0:128, :].astype(F32)
     small[0:1, :] = as_row(jnp.sum(w * m, axis=1, keepdims=True))
     small[1:2, :] = as_row(jnp.sum(w * tail, axis=1, keepdims=True))
@@ -803,15 +816,15 @@
 
 
 PLAN = (
-    "OG", "IA", "WU", "IB", "u", "IS", "IK", "i", "RB", "u", "AE", "u", "i", "AL", "u", "i", "PS", "PK",
-    "p", "IN", "i", "u", "FO", "u", "p", "i", "p", "u", "i", "p", "u",
+    "OG", "IA", "WU", "IB", "u", "IS", "IK", "i", "RB", "AE", "u", "i", "AL", "u", "i", "PS", "PK", "p",
+    "IN", "u", "i", "FO", "u", "p", "i", "p", "u", "i", "p", "u",
 )
 STEPS = {
     "u": ("core", "x", "half1", "half2", "all", "beside2", "beside1"),
     "i": ("core", "quarter", "x", "all", "beside2", "beside1"),
     "p": ("core", "x", "quarter", "all", "besides"),
 }
-PIECES = {"u": (272, 240), "i": (), "p": ()}
+PIECES = {"u": (512,), "i": (), "p": ()}
 
 
 def per_device(dp, tokens, first_gain, first_shift, w_query, w_key, w_value, w_control, w_output, second_gain, second_shift, w_inner, inner_bias, w_outer, outer_bias, cotangent):
@@ -844,7 +857,7 @@
 
     def outer():
         keep, send = outer_grad(clock, act, cotangent)
-        start("u", send, lambda: keep)
+        start("u", [send], lambda: keep)
 
     def wait_outer():
         wu_x = clock.sync(made["wu"])
@@ -858,7 +871,7 @@
         made["din"] = inner_back(clock, cotangent, d, [made["wu"][1], made["wu"][3]], (1, 3), [partial])
 
     def inner_send():
-        start("i", inner_grad(clock, n2, *made["din"], 2), None)
+        start("i", [inner_grad(clock, n2, *made["din"], 2)], None)
 
     def inner_keep():
         made["i"] = inner_grad(clock, n2, *made["din"], 0)
@@ -876,7 +889,7 @@
         return project_grad(clock, n1_low, made["late"][0], made["early"][0], mixed, made["dres"], first)
 
     def project_send():
-        start("p", project_part(2), None)
+        start("p", [project_part(2)], None)
 
     def project_keep():
         made["p"] = project_part(0)

time: 145 us -> 139 us (0.959)
  waiting for transfers between devices: 36.3 us -> 30.5 us
    ppermute x42 -> x41, waiting for transfers between devices: 36.3 us -> 30.5 us  [exchange(): return lax.ppermute(value, axis, [(i, i ^ mask) for i in range(size)])]
    ppermute x42 -> x41, starting transfers between devices: 41.1 us -> 40.8 us  [exchange(): return lax.ppermute(value, axis, [(i, i ^ mask) for i in range(size)])]
    pallas_call x41 -> x40, Pallas kernels: 64.8 us -> 64.6 us  [call(): pl.pallas_call(body, in_specs=[VM] + [ANY if k in raw else VM for k in ra...]
  transfers between devices with their start and end apart: 42 -> 41, of which waited for: 23 -> 19; matrix products, arithmetic and copies ran while one was open for 0% -> 0% of each run, Pallas kernels for 39% -> 41%
where the time goes in v5:
time: 139 us
  Pallas kernels  64.6 us (46%)
  starting transfers between devices  40.8 us (29%)
  waiting for transfers between devices  30.5 us (22%)
    pallas_call x40, Pallas kernels, call(): pl.pallas_call(body, in_specs=[VM] + [ANY if k in raw else VM for k in ra...  64.6 us
    ppermute x41, starting transfers between devices, exchange(): return lax.ppermute(value, axis, [(i, i ^ mask) for i in range(size)])  40.8 us
    ppermute x41, waiting for transfers between devices, exchange(): return lax.ppermute(value, axis, [(i, i ^ mask) for i in range(size)])  30.5 us
  transfers between devices with their start and end apart: 41, of which 19 were waited for; matrix products, arithmetic and copies ran while one was open for 0% of the time, Pallas kernels for 41%

profile of v5, /device:TPU:0, one launch (start us, length us, event | category | flops | bytes accessed | tf_op | source)
XLA Modules:
  0.0 138.5 jit_solution(18198528422125851979)
XLA Ops:
  0.8 1.7 %begin.1 = (bf16[144,2048]{1,0:T(8,128)(2,1)S(1)}, bf16[144,512]{1,0:T(8,128)(2,1)S(1)}, bf16[144,512]{1,0:T(8,128)(2,1)S(1)}, bf16[64,2048]{1,0:T(8,128)(2,1)S(...) custom-call(s32[8,128]{1,0:T(8,128)S(1)} %iota.7.token, bf16[128,512]{1,0:T(8,128)(2,1)} %refs_0_.7, ...), custom_call_target="tpu_custom_call" | custom-call | flops 1000 | bytes 1024 | tf_op jit(solution)/shard_map/begin/pallas_call | solution.py:64
  2.5 3.0 %collective-permute-start = (bf16[144,512]{1,0:T(8,128)(2,1)S(1)}, bf16[144,512]{1,0:T(8,128)(2,1)S(1)}, u32[]{:S(2)}, u32[]{:S(2)}) collective-permute-start(bf16[144,512]{1,0:T(8,128)(2,1)S(1)} %get-tuple-element.151), channel_id=1, source_target_pairs={{0,2},{1,3},{2,0},{3,1},{4,6},{5,7},{6,4},{7,5},{8,10},{9,11},{10,... | collective-permute-start | bytes 442376 | tf_op jit(solution)/shard_map/ppermute | solution.py:607
  8.0 2.2 %collective-permute-done.refs_0_ = bf16[144,512]{1,0:T(8,128)(2,1)S(1)} collective-permute-done((bf16[144,512]{1,0:T(8,128)(2,1)S(1)}, bf16[144,512]{1,0:T(8,128)(2,1)S(1)}, u32[]{:S(2)}, u32[]{:S(2)}) %collective-permute-start) | collective-permute-done | bytes 147488 | tf_op jit(solution)/shard_map/ppermute | solution.py:607
  10.2 2.3 %collective-permute-done.1.refs_1_ = bf16[144,512]{1,0:T(8,128)(2,1)S(1)} collective-permute-done((bf16[144,512]{1,0:T(8,128)(2,1)S(1)}, bf16[144,512]{1,0:T(8,128)(2,1)S(1)}, u32[]{:S(2)}, u32[]{:S(2)}) %collective-permute-start.1) | collective-permute-done | bytes 147488 | tf_op jit(solution)/shard_map/ppermute | solution.py:607
  12.5 1.7 %collective-permute-start.4 = (bf16[64,2048]{1,0:T(8,128)(2,1)S(1)}, bf16[64,2048]{1,0:T(8,128)(2,1)S(1)}, u32[]{:S(2)}, u32[]{:S(2)}) collective-permute-start(bf16[64,2048]{1,0:T(8,128)(2,1)S(1)} %get-tuple-element.158), channel_id=1, source_target_pairs={{0,2},{1,3},{2,0},{3,1},{4,6},{5,7},{6,4},{7,5},{8,10},{9,11},{10,... | collective-permute-start | bytes 786440 | tf_op jit(solution)/shard_map/ppermute | solution.py:607
  17.3 2.0 %collective-permute-done.2.refs_2_ = bf16[144,512]{1,0:T(8,128)(2,1)S(1)} collective-permute-done((bf16[144,512]{1,0:T(8,128)(2,1)S(1)}, bf16[144,512]{1,0:T(8,128)(2,1)S(1)}, u32[]{:S(2)}, u32[]{:S(2)}) %collective-permute-start.2) | collective-permute-done | bytes 147488 | tf_op jit(solution)/shard_map/ppermute | solution.py:607
  23.6 2.4 %project.1 = (bf16[1024,2048]{1,0:T(8,128)(2,1)S(1)}, s32[8,128]{1,0:T(8,128)S(1)}) custom-call(s32[8,128]{1,0:T(8,128)S(1)} %get-tuple-element.162.token, f32[1024,512]{1,0:T(8,128)S(1)} %get-tuple-element.163.refs_0_, bf16[144,2048]{1,0:T(8,128)(2,1)S(1)} %get-tuple-element.164.refs_1_.refs_6_.refs_7_.refs_14_.refs_4_.refs_2_, ...), custom_call_target="tpu_custom_call" | custom-call | flops 1000 | bytes 1024 | tf_op jit(solution)/shard_map/project/pallas_call | solution.py:64
  26.0 7.4 %attention_forward.1 = (bf16[1024,512]{1,0:T(8,128)(2,1)S(1)}, bf16[1024,3072]{1,0:T(8,128)(2,1)S(1)}, bf16[8,128,1024]{2,1,0:T(8,128)(2,1)S(1)}, f32[8,8,512]{2,1,0:T(8,128)S(1)}, s32[8,128]{1,0:T(8,128)S(1)}) custom-call(s32[8,128]{1,0:T(8,128)S(1)} %get-tuple-element.167.token, bf16[1024,2048]{1,0:T(8,128)(2,1)S(1)} %get-tuple-element.168.refs_0_), custom_call_target="tpu_custom_call" | custom-call | flops 1000 | bytes 1024 | tf_op jit(solution)/shard_map/attention_forward/pallas_call | solution.py:64
  35.8 2.0 %middle.1 = (f32[1024,512]{1,0:T(8,128)S(1)}, bf16[1024,512]{1,0:T(8,128)(2,1)S(1)}, f32[1024,128]{1,0:T(8,128)S(1)}, bf16[1024,512]{1,0:T(8,128)(2,1)S(1)}, s32[8,128]{1,0:T(8,128)S(1)}) custom-call(s32[8,128]{1,0:T(8,128)S(1)} %get-tuple-element.172.token, bf16[1024,512]{1,0:T(8,128)(2,1)S(1)} %copy-done.2, ...), custom_call_target="tpu_custom_call" | custom-call | flops 1000 | bytes 1024 | tf_op jit(solution)/shard_map/middle/pallas_call | solution.py:64
  37.9 6.2 %ffn_inner.1 = (bf16[1024,2048]{1,0:T(8,128)(2,1)S(1)}, bf16[1024,2048]{1,0:T(8,128)(2,1)S(1)}, s32[8,128]{1,0:T(8,128)S(1)}) custom-call(s32[8,128]{1,0:T(8,128)S(1)} %get-tuple-element.175.token, bf16[1024,512]{1,0:T(8,128)(2,1)S(1)} %get-tuple-element.176.refs_0_, bf16[128,2048]{1,0:T(8,128)(2,1)S(1)} %copy-done.3, ...), custom_call_target="tpu_custom_call" | custom-call | flops 1000 | bytes 1024 | tf_op jit(solution)/shard_map/ffn_inner/pallas_call | solution.py:64
  44.1 2.4 %outer_grad.1 = (bf16[2,512,512]{2,1,0:T(8,128)(2,1)S(1)}, bf16[2,512,512]{2,1,0:T(8,128)(2,1)S(1)}, s32[8,128]{1,0:T(8,128)S(1)}) custom-call(s32[8,128]{1,0:T(8,128)S(1)} %get-tuple-element.178.token, bf16[1024,2048]{1,0:T(8,128)(2,1)S(1)} %get-tuple-element.179.refs_0_.refs_1_, bf16[1024,512]{1,0:T(8,128)(2,1)S(1)} %copy-done), custom_call_target="tpu_custom_call" | custom-call | flops 1000 | bytes 1024 | tf_op jit(solution)/shard_map/outer_grad/pallas_call | solution.py:64
  47.0 1.6 %inner_back.2 = (bf16[1024,2048]{1,0:T(8,128)(2,1)S(1)}, f32[8,2048]{1,0:T(8,128)S(1)}, s32[8,128]{1,0:T(8,128)S(1)}) custom-call(s32[8,128]{1,0:T(8,128)S(1)} %get-tuple-element.180.token, bf16[1024,512]{1,0:T(8,128)(2,1)S(1)} %copy-done, bf16[1024,2048]{1,0:T(8,128)(2,1)S(1)} %get-tuple-element.181.refs_1_, ...), custom_call_target="tpu_custom_call", output_to_operand_aliasing={{0}: (2, {})} | custom-call | flops 1000 | bytes 1024 | tf_op jit(solution)/shard_map/inner_back/pallas_call | solution.py:64
  49.4 1.9 %collective-permute-done.16.refs_3_.refs_5_ = bf16[512,512]{1,0:T(8,128)(2,1)S(1)} collective-permute-done((bf16[512,512]{1,0:T(8,128)(2,1)S(1)}, bf16[512,512]{1,0:T(8,128)(2,1)S(1)}, u32[]{:S(2)}, u32[]{:S(2)}) %collective-permute-start.16) | collective-permute-done | bytes 524320 | tf_op jit(solution)/shard_map/ppermute | solution.py:607
  61.5 4.4 %resid_back.1 = (f32[1024,512]{1,0:T(8,128)S(1)}, bf16[1024,512]{1,0:T(8,128)(2,1)S(1)}, s32[8,128]{1,0:T(8,128)S(1)}) custom-call(s32[8,128]{1,0:T(8,128)S(1)} %get-tuple-element.199.token, bf16[1024,512]{1,0:T(8,128)(2,1)S(1)} %copy-done, bf16[1024,512]{1,0:T(8,128)(2,1)S(1)} %get-tuple-element.192.refs_0_.refs_1_, ...), custom_call_target="tpu_custom_call" | custom-call | flops 1000 | bytes 1024 | tf_op jit(solution)/shard_map/resid_back/pallas_call | solution.py:64
  65.9 5.3 %attention_backward.2 = (bf16[512,2048]{1,0:T(8,128)(2,1)S(1)}, f32[4,128,256]{2,1,0:T(8,128)S(1)}, f32[8,512]{1,0:T(8,128)S(1)}, s32[8,128]{1,0:T(8,128)S(1)}) custom-call(s32[8,128]{1,0:T(8,128)S(1)} %get-tuple-element.201.token, bf16[1024,2048]{1,0:T(8,128)(2,1)S(1)} %get-tuple-element.168.refs_0_, bf16[1024,3072]{1,0:T(8,128)(2,1)S(1)} %get-tuple-element.202.refs_1_, ...), custom_call_target="tpu_custom_call" | custom-call | flops 1000 | bytes 1024 | tf_op jit(solution)/shard_map/attention_backward/pallas_call | solution.py:64
  72.4 2.2 %collective-permute-done.22.refs_3_ = bf16[288,512]{1,0:T(8,128)(2,1)S(1)} collective-permute-done((bf16[288,512]{1,0:T(8,128)(2,1)S(1)}, bf16[288,512]{1,0:T(8,128)(2,1)S(1)}, u32[]{:S(2)}, u32[]{:S(2)}) %collective-permute-start.22) | collective-permute-done | bytes 294944 | tf_op jit(solution)/shard_map/ppermute | solution.py:607
  75.7 5.1 %attention_backward.3 = (bf16[512,2048]{1,0:T(8,128)(2,1)S(1)}, s32[8,128]{1,0:T(8,128)S(1)}) custom-call(s32[8,128]{1,0:T(8,128)S(1)} %get-tuple-element.214.token, bf16[1024,2048]{1,0:T(8,128)(2,1)S(1)} %get-tuple-element.168.refs_0_, bf16[1024,3072]{1,0:T(8,128)(2,1)S(1)} %get-tuple-element.202.refs_1_, ...), custom_call_target="tpu_custom_call" | custom-call | flops 1000 | bytes 1024 | tf_op jit(solution)/shard_map/attention_backward/pallas_call | solution.py:64
  81.1 1.6 %project_grad.2 = (bf16[2,144,2560]{2,1,0:T(8,128)(2,1)S(1)}, s32[8,128]{1,0:T(8,128)S(1)}) custom-call(s32[8,128]{1,0:T(8,128)S(1)} %get-tuple-element.223.token, bf16[1024,512]{1,0:T(8,128)(2,1)S(1)} %get-tuple-element.224.refs_0_, bf16[512,2048]{1,0:T(8,128)(2,1)S(1)} %get-tuple-element.225.refs_1_, bf16[512,2048]{1,0:T(8,128)(2,1)S(1)} %get-tuple-element.226.refs_2_, ...), custom_call_target="tpu_custom_call" | custom-call | flops 1000 | bytes 1024 | tf_op jit(solution)/shard_map/project_grad/pallas_call | solution.py:64
  82.8 1.6 %project_grad.3 = (bf16[2,144,2560]{2,1,0:T(8,128)(2,1)S(1)}, s32[8,128]{1,0:T(8,128)S(1)}) custom-call(s32[8,128]{1,0:T(8,128)S(1)} %get-tuple-element.228.token, bf16[1024,512]{1,0:T(8,128)(2,1)S(1)} %get-tuple-element.224.refs_0_, bf16[512,2048]{1,0:T(8,128)(2,1)S(1)} %get-tuple-element.225.refs_1_, bf16[512,2048]{1,0:T(8,128)(2,1)S(1)} %get-tuple-element.226.refs_2_, ...), custom_call_target="tpu_custom_call" | custom-call | flops 1000 | bytes 1024 | tf_op jit(solution)/shard_map/project_grad/pallas_call | solution.py:64
  84.4 1.6 %collective-permute-done.25.refs_1_ = bf16[2,144,2560]{2,1,0:T(8,128)(2,1)S(1)} collective-permute-done((bf16[2,144,2560]{2,1,0:T(8,128)(2,1)S(1)}, bf16[2,144,2560]{2,1,0:T(8,128)(2,1)S(1)}, u32[]{:S(2)}, u32[]{:S(2)}) %collective-permute-start.25) | collective-permute-done | bytes 1474592 | tf_op jit(solution)/shard_map/ppermute | solution.py:607
  87.7 1.6 %collective-permute-start.26 = (bf16[512,128]{1,0:T(8,128)(2,1)S(1)}, bf16[512,128]{1,0:T(8,128)(2,1)S(1)}, u32[]{:S(2)}, u32[]{:S(2)}) collective-permute-start(bf16[512,128]{1,0:T(8,128)(2,1)S(1)} %get-tuple-element.235), channel_id=1, source_target_pairs={{0,8},{4,12},{8,0},{12,4},{16,24},{20,28},{24,16},{28,20},{1,9},{5... | collective-permute-start | bytes 393224 | tf_op jit(solution)/shard_map/ppermute | solution.py:607
  89.3 2.6 %collective-permute-start.27 = (bf16[144,512]{1,0:T(8,128)(2,1)S(1)}, bf16[144,512]{1,0:T(8,128)(2,1)S(1)}, u32[]{:S(2)}, u32[]{:S(2)}) collective-permute-start(bf16[144,512]{1,0:T(8,128)(2,1)S(1)} %get-tuple-element.237.refs_0_), channel_id=1, source_target_pairs={{0,16},{4,20},{8,24},{12,28},{16,0},{20,4},{24,8},{28,12},{1,17},{... | collective-permute-start | bytes 442376 | tf_op jit(solution)/shard_map/ppermute | solution.py:607
  91.9 4.4 %input_grad.1 = (bf16[1024,512]{1,0:T(8,128)(2,1)}, s32[8,128]{1,0:T(8,128)S(1)}) custom-call(s32[8,128]{1,0:T(8,128)S(1)} %get-tuple-element.232.token, bf16[1024,512]{1,0:T(8,128)(2,1)S(1)} %copy-done.2, bf16[512,2048]{1,0:T(8,128)(2,1)S(1)} %get-tuple-element.225.refs_1_, bf16[512,2048]{1,0:T(8,128)(2,1)S(1)} %get-tuple-element.226.refs_2_, ...), custom_call_target="tpu_custom_call" | custom-call | flops 1000 | bytes 1024 | tf_op jit(solution)/shard_map/input_grad/pallas_call | solution.py:64
  96.9 1.9 %collective-permute-done.27.refs_1_ = bf16[144,512]{1,0:T(8,128)(2,1)S(1)} collective-permute-done((bf16[144,512]{1,0:T(8,128)(2,1)S(1)}, bf16[144,512]{1,0:T(8,128)(2,1)S(1)}, u32[]{:S(2)}, u32[]{:S(2)}) %collective-permute-start.27) | collective-permute-done | bytes 147488 | tf_op jit(solution)/shard_map/ppermute | solution.py:607
  98.8 2.1 %collective-permute-start.30 = (bf16[144,512]{1,0:T(8,128)(2,1)S(1)}, bf16[144,512]{1,0:T(8,128)(2,1)S(1)}, u32[]{:S(2)}, u32[]{:S(2)}) collective-permute-start(bf16[144,512]{1,0:T(8,128)(2,1)S(1)} %get-tuple-element.248.refs_0_), channel_id=1, source_target_pairs={{0,8},{4,12},{8,0},{12,4},{16,24},{20,28},{24,16},{28,20},{1,9},{5... | collective-permute-start | bytes 442376 | tf_op jit(solution)/shard_map/ppermute | solution.py:607
  100.9 3.9 %ffn_outer.1 = (bf16[1024,512]{1,0:T(8,128)(2,1)}, s32[8,128]{1,0:T(8,128)S(1)}) custom-call(s32[8,128]{1,0:T(8,128)S(1)} %get-tuple-element.238.token, f32[1024,512]{1,0:T(8,128)S(1)} %get-tuple-element.239.refs_0_, bf16[1024,2048]{1,0:T(8,128)(2,1)S(1)} %get-tuple-element.179.refs_0_.refs_1_, bf16[512,512]{1,0:T(8,128)(2,1)S(1)} %copy-done.4, ...), custom_call_target="tpu_custom_call" | custom-call | flops 1000 | bytes 1024 | tf_op jit(solution)/shard_map/ffn_outer/pallas_call | solution.py:64
  112.2 1.8 %collective-permute-done.31.refs_1_ = bf16[144,640]{1,0:T(8,128)(2,1)S(1)} collective-permute-done((bf16[144,640]{1,0:T(8,128)(2,1)S(1)}, bf16[144,640]{1,0:T(8,128)(2,1)S(1)}, u32[]{:S(2)}, u32[]{:S(2)}) %collective-permute-start.31) | collective-permute-done | bytes 184352 | tf_op jit(solution)/shard_map/ppermute | solution.py:607
  114.4 4.1 %collective-permute-done.33.refs_3_ = bf16[144,640]{1,0:T(8,128)(2,1)S(1)} collective-permute-done((bf16[144,640]{1,0:T(8,128)(2,1)S(1)}, bf16[144,640]{1,0:T(8,128)(2,1)S(1)}, u32[]{:S(2)}, u32[]{:S(2)}) %collective-permute-start.33) | collective-permute-done | bytes 184352 | tf_op jit(solution)/shard_map/ppermute | solution.py:607
  118.7 2.5 %collective-permute-start.36 = (bf16[144,640]{1,0:T(8,128)(2,1)S(1)}, bf16[144,640]{1,0:T(8,128)(2,1)S(1)}, u32[]{:S(2)}, u32[]{:S(2)}) collective-permute-start(bf16[144,640]{1,0:T(8,128)(2,1)S(1)} %get-tuple-element.261.refs_0_), channel_id=1, source_target_pairs={{0,16},{4,20},{8,24},{12,28},{16,0},{20,4},{24,8},{28,12},{1,17},{... | collective-permute-start | bytes 552968 | tf_op jit(solution)/shard_map/ppermute | solution.py:607
  124.9 2.4 %collective-permute-done.36.refs_1_ = bf16[144,640]{1,0:T(8,128)(2,1)S(1)} collective-permute-done((bf16[144,640]{1,0:T(8,128)(2,1)S(1)}, bf16[144,640]{1,0:T(8,128)(2,1)S(1)}, u32[]{:S(2)}, u32[]{:S(2)}) %collective-permute-start.36) | collective-permute-done | bytes 184352 | tf_op jit(solution)/shard_map/ppermute | solution.py:607
  132.3 1.6 %collective-permute-done.40.refs_3_ = bf16[144,640]{1,0:T(8,128)(2,1)S(1)} collective-permute-done((bf16[144,640]{1,0:T(8,128)(2,1)S(1)}, bf16[144,640]{1,0:T(8,128)(2,1)S(1)}, u32[]{:S(2)}, u32[]{:S(2)}) %collective-permute-start.40) | collective-permute-done | bytes 184352 | tf_op jit(solution)/shard_map/ppermute | solution.py:607
  136.2 2.1 %finish_project.1 = (f32[128,512]{1,0:T(8,128)}, f32[128,512]{1,0:T(8,128)}, f32[128,512]{1,0:T(8,128)}, f32[128,512]{1,0:T(8,128)}, f32[128,512]{1,0:T(8,128)},...) custom-call(s32[8,128]{1,0:T(8,128)S(1)} %get-tuple-element.268.token, ...), custom_call_target="tpu_custom_call" | custom-call | flops 1000 | bytes 1024 | tf_op jit(solution)/shard_map/finish_project/pallas_call | solution.py:64
  (104 shorter events, 47.4 us)
Async XLA Ops:
  2.5 7.7 %collective-permute-start = (bf16[144,512]{1,0:T(8,128)(2,1)S(1)}, bf16[144,512]{1,0:T(8,128)(2,1)S(1)}, u32[]{:S(2)}, u32[]{:S(2)}) collective-permute-start(bf16[144,512]{1,0:T(8,128)(2,1)S(1)} %get-tuple-element.151), channel_id=1, source_target_pairs={{0,2},{1,3},{2,0},{3,1},{4,6},{5,7},{6,4},{7,5},{8,10},{9,11},{10,... | collective-permute-start | bytes 442376 | tf_op jit(solution)/shard_map/ppermute | solution.py:607
  5.5 7.0 %collective-permute-start.1 = (bf16[144,512]{1,0:T(8,128)(2,1)S(1)}, bf16[144,512]{1,0:T(8,128)(2,1)S(1)}, u32[]{:S(2)}, u32[]{:S(2)}) collective-permute-start(bf16[144,512]{1,0:T(8,128)(2,1)S(1)} %get-tuple-element.152), channel_id=1, source_target_pairs={{0,2},{1,3},{2,0},{3,1},{4,6},{5,7},{6,4},{7,5},{8,10},{9,11},{10,... | collective-permute-start | bytes 442376 | tf_op jit(solution)/shard_map/ppermute | solution.py:607
  12.5 8.4 %collective-permute-start.4 = (bf16[64,2048]{1,0:T(8,128)(2,1)S(1)}, bf16[64,2048]{1,0:T(8,128)(2,1)S(1)}, u32[]{:S(2)}, u32[]{:S(2)}) collective-permute-start(bf16[64,2048]{1,0:T(8,128)(2,1)S(1)} %get-tuple-element.158), channel_id=1, source_target_pairs={{0,2},{1,3},{2,0},{3,1},{4,6},{5,7},{6,4},{7,5},{8,10},{9,11},{10,... | collective-permute-start | bytes 786440 | tf_op jit(solution)/shard_map/ppermute | solution.py:607
  17.3 6.2 %collective-permute-start.5 = (bf16[144,2048]{1,0:T(8,128)(2,1)S(1)}, bf16[144,2048]{1,0:T(8,128)(2,1)S(1)}, u32[]{:S(2)}, u32[]{:S(2)}) collective-permute-start(bf16[144,2048]{1,0:T(8,128)(2,1)S(1)} %get-tuple-element.164.refs_1_.refs_6_.refs_7_.refs_14_.refs_4_.refs_2_), channel_id=1, source_target_pairs={{0,1},{1,0},{2,3},{3,2},{4,5},{5,4},{6,7},{7,6},{8,9},{9,8},{10,11... | collective-permute-start | bytes 1769480 | tf_op jit(solution)/shard_map/ppermute | solution.py:607
  21.2 12.1 %collective-permute-start.8 = (bf16[64,2048]{1,0:T(8,128)(2,1)S(1)}, bf16[64,2048]{1,0:T(8,128)(2,1)S(1)}, u32[]{:S(2)}, u32[]{:S(2)}) collective-permute-start(bf16[64,2048]{1,0:T(8,128)(2,1)S(1)} %get-tuple-element.171), channel_id=1, source_target_pairs={{0,2},{1,3},{2,0},{3,1},{4,6},{5,7},{6,4},{7,5},{8,10},{9,11},{10,... | collective-permute-start | bytes 786440 | tf_op jit(solution)/shard_map/ppermute | solution.py:607
  21.8 16.1 %collective-permute-start.11 = (bf16[128,2048]{1,0:T(8,128)(2,1)S(1)}, bf16[128,2048]{1,0:T(8,128)(2,1)S(1)}, u32[]{:S(2)}, u32[]{:S(2)}) collective-permute-start(bf16[128,2048]{1,0:T(8,128)(2,1)S(1)} %copy-done.3), channel_id=1, source_target_pairs={{0,1},{1,0},{2,3},{3,2},{4,5},{5,4},{6,7},{7,6},{8,9},{9,8},{10,11... | collective-permute-start | bytes 1572872 | tf_op jit(solution)/shard_map/ppermute | solution.py:607
  22.0 11.3 %collective-permute-start.7 = (bf16[128,512]{1,0:T(8,128)(2,1)S(1)}, bf16[128,512]{1,0:T(8,128)(2,1)S(1)}, u32[]{:S(2)}, u32[]{:S(2)}) collective-permute-start(bf16[128,512]{1,0:T(8,128)(2,1)S(1)} %copy-done.5), channel_id=1, source_target_pairs={{0,2},{1,3},{2,0},{3,1},{4,6},{5,7},{6,4},{7,5},{8,10},{9,11},{10,... | collective-permute-start | bytes 393224 | tf_op jit(solution)/shard_map/ppermute | solution.py:607
  23.5 14.4 %collective-permute-start.12 = (bf16[64,2048]{1,0:T(8,128)(2,1)S(1)}, bf16[64,2048]{1,0:T(8,128)(2,1)S(1)}, u32[]{:S(2)}, u32[]{:S(2)}) collective-permute-start(bf16[64,2048]{1,0:T(8,128)(2,1)S(1)} %collective-permute-done.4.refs_4_.refs_2_.refs_9_), channel_id=1, source_target_pairs={{0,1},{1,0},{2,3},{3,2},{4,5},{5,4},{6,7},{7,6},{8,9},{9,8},{10,11... | collective-permute-start | bytes 786440 | tf_op jit(solution)/shard_map/ppermute | solution.py:607
  35.2 14.2 %collective-permute-start.15 = (bf16[512,512]{1,0:T(8,128)(2,1)S(1)}, bf16[512,512]{1,0:T(8,128)(2,1)S(1)}, u32[]{:S(2)}, u32[]{:S(2)}) collective-permute-start(bf16[512,512]{1,0:T(8,128)(2,1)S(1)} %copy-done.4), channel_id=1, source_target_pairs={{0,2},{1,3},{2,0},{3,1},{4,6},{5,7},{6,4},{7,5},{8,10},{9,11},{10,... | collective-permute-start | bytes 1572872 | tf_op jit(solution)/shard_map/ppermute | solution.py:607
  35.8 11.3 %collective-permute-start.14 = (bf16[512,512]{1,0:T(8,128)(2,1)S(1)}, bf16[512,512]{1,0:T(8,128)(2,1)S(1)}, u32[]{:S(2)}, u32[]{:S(2)}) collective-permute-start(bf16[512,512]{1,0:T(8,128)(2,1)S(1)} %copy-done.4), channel_id=1, source_target_pairs={{0,1},{1,0},{2,3},{3,2},{4,5},{5,4},{6,7},{7,6},{8,9},{9,8},{10,11... | collective-permute-start | bytes 1572872 | tf_op jit(solution)/shard_map/ppermute | solution.py:607
  46.5 6.2 %collective-permute-start.17 = (bf16[2,512,512]{2,1,0:T(8,128)(2,1)S(1)}, bf16[2,512,512]{2,1,0:T(8,128)(2,1)S(1)}, u32[]{:S(2)}, u32[]{:S(2)}) collective-permute-start(bf16[2,512,512]{2,1,0:T(8,128)(2,1)S(1)} %get-tuple-element.190), channel_id=1, source_target_pairs={{0,1},{1,0},{2,3},{3,2},{4,5},{5,4},{6,7},{7,6},{8,9},{9,8},{10,11... | collective-permute-start | bytes 3145736 | tf_op jit(solution)/shard_map/ppermute | solution.py:607
  54.5 16.7 %collective-permute-start.19 = (bf16[512,512]{1,0:T(8,128)(2,1)S(1)}, bf16[512,512]{1,0:T(8,128)(2,1)S(1)}, u32[]{:S(2)}, u32[]{:S(2)}) collective-permute-start(bf16[512,512]{1,0:T(8,128)(2,1)S(1)} %get-tuple-element.208), channel_id=1, source_target_pairs={{0,2},{1,3},{2,0},{3,1},{4,6},{5,7},{6,4},{7,5},{8,10},{9,11},{10,... | collective-permute-start | bytes 1572872 | tf_op jit(solution)/shard_map/ppermute | solution.py:607
  58.0 14.5 %collective-permute-start.20 = (bf16[288,512]{1,0:T(8,128)(2,1)S(1)}, bf16[288,512]{1,0:T(8,128)(2,1)S(1)}, u32[]{:S(2)}, u32[]{:S(2)}) collective-permute-start(bf16[288,512]{1,0:T(8,128)(2,1)S(1)} %get-tuple-element.211), channel_id=1, source_target_pairs={{0,4},{4,0},{8,12},{12,8},{16,20},{20,16},{24,28},{28,24},{1,5},{5... | collective-permute-start | bytes 884744 | tf_op jit(solution)/shard_map/ppermute | solution.py:607
  58.8 13.6 %collective-permute-start.21 = (bf16[288,512]{1,0:T(8,128)(2,1)S(1)}, bf16[288,512]{1,0:T(8,128)(2,1)S(1)}, u32[]{:S(2)}, u32[]{:S(2)}) collective-permute-start(bf16[288,512]{1,0:T(8,128)(2,1)S(1)} %get-tuple-element.212), channel_id=1, source_target_pairs={{0,8},{4,12},{8,0},{12,4},{16,24},{20,28},{24,16},{28,20},{1,9},{5... | collective-permute-start | bytes 884744 | tf_op jit(solution)/shard_map/ppermute | solution.py:607
  60.4 14.3 %collective-permute-start.22 = (bf16[288,512]{1,0:T(8,128)(2,1)S(1)}, bf16[288,512]{1,0:T(8,128)(2,1)S(1)}, u32[]{:S(2)}, u32[]{:S(2)}) collective-permute-start(bf16[288,512]{1,0:T(8,128)(2,1)S(1)} %get-tuple-element.213), channel_id=1, source_target_pairs={{0,12},{4,8},{8,4},{12,0},{16,28},{20,24},{24,20},{28,16},{1,13},{... | collective-permute-start | bytes 884744 | tf_op jit(solution)/shard_map/ppermute | solution.py:607
  71.6 9.2 %collective-permute-start.23 = (bf16[512,256]{1,0:T(8,128)(2,1)S(1)}, bf16[512,256]{1,0:T(8,128)(2,1)S(1)}, u32[]{:S(2)}, u32[]{:S(2)}) collective-permute-start(bf16[512,256]{1,0:T(8,128)(2,1)S(1)} %get-tuple-element.219), channel_id=1, source_target_pairs={{0,4},{4,0},{8,12},{12,8},{16,20},{20,16},{24,28},{28,24},{1,5},{5... | collective-permute-start | bytes 786440 | tf_op jit(solution)/shard_map/ppermute | solution.py:607
  74.8 6.2 %collective-permute-start.24 = (bf16[144,512]{1,0:T(8,128)(2,1)S(1)}, bf16[144,512]{1,0:T(8,128)(2,1)S(1)}, u32[]{:S(2)}, u32[]{:S(2)}) collective-permute-start(bf16[144,512]{1,0:T(8,128)(2,1)S(1)} %get-tuple-element.222), channel_id=1, source_target_pairs={{0,2},{1,3},{2,0},{3,1},{4,6},{5,7},{6,4},{7,5},{8,10},{9,11},{10,... | collective-permute-start | bytes 442376 | tf_op jit(solution)/shard_map/ppermute | solution.py:607
  86.4 18.6 %collective-permute-start.29 = (bf16[144,2560]{1,0:T(8,128)(2,1)S(1)}, bf16[144,2560]{1,0:T(8,128)(2,1)S(1)}, u32[]{:S(2)}, u32[]{:S(2)}) collective-permute-start(bf16[144,2560]{1,0:T(8,128)(2,1)S(1)} %get-tuple-element.246), channel_id=1, source_target_pairs={{0,2},{1,3},{2,0},{3,1},{4,6},{5,7},{6,4},{7,5},{8,10},{9,11},{10,... | collective-permute-start | bytes 2211848 | tf_op jit(solution)/shard_map/ppermute | solution.py:607
  87.7 8.6 %collective-permute-start.26 = (bf16[512,128]{1,0:T(8,128)(2,1)S(1)}, bf16[512,128]{1,0:T(8,128)(2,1)S(1)}, u32[]{:S(2)}, u32[]{:S(2)}) collective-permute-start(bf16[512,128]{1,0:T(8,128)(2,1)S(1)} %get-tuple-element.235), channel_id=1, source_target_pairs={{0,8},{4,12},{8,0},{12,4},{16,24},{20,28},{24,16},{28,20},{1,9},{5... | collective-permute-start | bytes 393224 | tf_op jit(solution)/shard_map/ppermute | solution.py:607
  89.3 9.4 %collective-permute-start.27 = (bf16[144,512]{1,0:T(8,128)(2,1)S(1)}, bf16[144,512]{1,0:T(8,128)(2,1)S(1)}, u32[]{:S(2)}, u32[]{:S(2)}) collective-permute-start(bf16[144,512]{1,0:T(8,128)(2,1)S(1)} %get-tuple-element.237.refs_0_), channel_id=1, source_target_pairs={{0,16},{4,20},{8,24},{12,28},{16,0},{20,4},{24,8},{28,12},{1,17},{... | collective-permute-start | bytes 442376 | tf_op jit(solution)/shard_map/ppermute | solution.py:607
  96.4 8.5 %collective-permute-start.28 = (bf16[512,128]{1,0:T(8,128)(2,1)S(1)}, bf16[512,128]{1,0:T(8,128)(2,1)S(1)}, u32[]{:S(2)}, u32[]{:S(2)}) collective-permute-start(bf16[512,128]{1,0:T(8,128)(2,1)S(1)} %get-tuple-element.243.refs_0_), channel_id=1, source_target_pairs={{0,16},{4,20},{8,24},{12,28},{16,0},{20,4},{24,8},{28,12},{1,17},{... | collective-permute-start | bytes 393224 | tf_op jit(solution)/shard_map/ppermute | solution.py:607
  98.8 10.3 %collective-permute-start.30 = (bf16[144,512]{1,0:T(8,128)(2,1)S(1)}, bf16[144,512]{1,0:T(8,128)(2,1)S(1)}, u32[]{:S(2)}, u32[]{:S(2)}) collective-permute-start(bf16[144,512]{1,0:T(8,128)(2,1)S(1)} %get-tuple-element.248.refs_0_), channel_id=1, source_target_pairs={{0,8},{4,12},{8,0},{12,4},{16,24},{20,28},{24,16},{28,20},{1,9},{5... | collective-permute-start | bytes 442376 | tf_op jit(solution)/shard_map/ppermute | solution.py:607
  105.5 8.5 %collective-permute-start.31 = (bf16[144,640]{1,0:T(8,128)(2,1)S(1)}, bf16[144,640]{1,0:T(8,128)(2,1)S(1)}, u32[]{:S(2)}, u32[]{:S(2)}) collective-permute-start(bf16[144,640]{1,0:T(8,128)(2,1)S(1)} %get-tuple-element.251), channel_id=1, source_target_pairs={{0,4},{4,0},{8,12},{12,8},{16,20},{20,16},{24,28},{28,24},{1,5},{5... | collective-permute-start | bytes 552968 | tf_op jit(solution)/shard_map/ppermute | solution.py:607
  106.8 7.6 %collective-permute-start.32 = (bf16[144,640]{1,0:T(8,128)(2,1)S(1)}, bf16[144,640]{1,0:T(8,128)(2,1)S(1)}, u32[]{:S(2)}, u32[]{:S(2)}) collective-permute-start(bf16[144,640]{1,0:T(8,128)(2,1)S(1)} %get-tuple-element.252), channel_id=1, source_target_pairs={{0,8},{4,12},{8,0},{12,4},{16,24},{20,28},{24,16},{28,20},{1,9},{5... | collective-permute-start | bytes 552968 | tf_op jit(solution)/shard_map/ppermute | solution.py:607
  108.4 10.1 %collective-permute-start.33 = (bf16[144,640]{1,0:T(8,128)(2,1)S(1)}, bf16[144,640]{1,0:T(8,128)(2,1)S(1)}, u32[]{:S(2)}, u32[]{:S(2)}) collective-permute-start(bf16[144,640]{1,0:T(8,128)(2,1)S(1)} %get-tuple-element.253), channel_id=1, source_target_pairs={{0,12},{4,8},{8,4},{12,0},{16,28},{20,24},{24,20},{28,16},{1,13},{... | collective-permute-start | bytes 552968 | tf_op jit(solution)/shard_map/ppermute | solution.py:607
  109.3 13.8 %collective-permute-start.35 = (bf16[144,1024]{1,0:T(8,128)(2,1)S(1)}, bf16[144,1024]{1,0:T(8,128)(2,1)S(1)}, u32[]{:S(2)}, u32[]{:S(2)}) collective-permute-start(bf16[144,1024]{1,0:T(8,128)(2,1)S(1)} %get-tuple-element.257.refs_0_), channel_id=1, source_target_pairs={{0,4},{4,0},{8,12},{12,8},{16,20},{20,16},{24,28},{28,24},{1,5},{5... | collective-permute-start | bytes 884744 | tf_op jit(solution)/shard_map/ppermute | solution.py:607
  110.6 10.5 %collective-permute-start.34 = (bf16[512,128]{1,0:T(8,128)(2,1)S(1)}, bf16[512,128]{1,0:T(8,128)(2,1)S(1)}, u32[]{:S(2)}, u32[]{:S(2)}) collective-permute-start(bf16[512,128]{1,0:T(8,128)(2,1)S(1)} %get-tuple-element.255.refs_0_), channel_id=1, source_target_pairs={{0,8},{4,12},{8,0},{12,4},{16,24},{20,28},{24,16},{28,20},{1,9},{5... | collective-permute-start | bytes 393224 | tf_op jit(solution)/shard_map/ppermute | solution.py:607
  118.7 8.6 %collective-permute-start.36 = (bf16[144,640]{1,0:T(8,128)(2,1)S(1)}, bf16[144,640]{1,0:T(8,128)(2,1)S(1)}, u32[]{:S(2)}, u32[]{:S(2)}) collective-permute-start(bf16[144,640]{1,0:T(8,128)(2,1)S(1)} %get-tuple-element.261.refs_0_), channel_id=1, source_target_pairs={{0,16},{4,20},{8,24},{12,28},{16,0},{20,4},{24,8},{28,12},{1,17},{... | collective-permute-start | bytes 552968 | tf_op jit(solution)/shard_map/ppermute | solution.py:607
  121.5 9.5 %collective-permute-start.37 = (bf16[512,256]{1,0:T(8,128)(2,1)S(1)}, bf16[512,256]{1,0:T(8,128)(2,1)S(1)}, u32[]{:S(2)}, u32[]{:S(2)}) collective-permute-start(bf16[512,256]{1,0:T(8,128)(2,1)S(1)} %get-tuple-element.263.refs_0_), channel_id=1, source_target_pairs={{0,4},{4,0},{8,12},{12,8},{16,20},{20,16},{24,28},{28,24},{1,5},{5... | collective-permute-start | bytes 786440 | tf_op jit(solution)/shard_map/ppermute | solution.py:607
  127.4 6.6 %collective-permute-start.40 = (bf16[144,640]{1,0:T(8,128)(2,1)S(1)}, bf16[144,640]{1,0:T(8,128)(2,1)S(1)}, u32[]{:S(2)}, u32[]{:S(2)}) collective-permute-start(bf16[144,640]{1,0:T(8,128)(2,1)S(1)} %get-tuple-element.267.refs_0_), channel_id=1, source_target_pairs={{0,12},{4,8},{8,4},{12,0},{16,28},{20,24},{24,20},{28,16},{1,13},{... | collective-permute-start | bytes 552968 | tf_op jit(solution)/shard_map/ppermute | solution.py:607
  128.3 7.0 %collective-permute-start.39 = (bf16[144,640]{1,0:T(8,128)(2,1)S(1)}, bf16[144,640]{1,0:T(8,128)(2,1)S(1)}, u32[]{:S(2)}, u32[]{:S(2)}) collective-permute-start(bf16[144,640]{1,0:T(8,128)(2,1)S(1)} %get-tuple-element.267.refs_0_), channel_id=1, source_target_pairs={{0,8},{4,12},{8,0},{12,4},{16,24},{20,28},{24,16},{28,20},{1,9},{5... | collective-permute-start | bytes 552968 | tf_op jit(solution)/shard_map/ppermute | solution.py:607
  129.7 6.1 %collective-permute-start.38 = (bf16[144,640]{1,0:T(8,128)(2,1)S(1)}, bf16[144,640]{1,0:T(8,128)(2,1)S(1)}, u32[]{:S(2)}, u32[]{:S(2)}) collective-permute-start(bf16[144,640]{1,0:T(8,128)(2,1)S(1)} %get-tuple-element.267.refs_0_), channel_id=1, source_target_pairs={{0,4},{4,0},{8,12},{12,8},{16,20},{20,16},{24,28},{28,24},{1,5},{5... | collective-permute-start | bytes 552968 | tf_op jit(solution)/shard_map/ppermute | solution.py:607
  (15 other events, 97.7 us)

commit v6 on v5

--- a/solution.py
+++ b/solution.py
@@ -518,16 +518,14 @@
     return call(clock, kernel, "inner_back", [shape((T, 2048)), shape((8, 2048), F32)], [dy, slope, *wu, *sums], aliases={1: 0})
 
 
-def inner_grad_kernel(first, _, n2, din, sums, out):
+def inner_grad_kernel(first, _, n2, din, out):
     m = mm_tn(n2[:, 128 * first : 128 * (first + 2)], din[...]).astype(BF16)
-    tail = jnp.concatenate((sums[...], jnp.zeros_like(sums)), axis=0).astype(BF16)
     for k in range(2):
-        out[k, 0:128, :] = m[128 * k : 128 * (k + 1), :]
-        out[k, 128:144, :] = tail
-
-
-def inner_grad(clock, n2, din, sums, first):
-    return call(clock, functools.partial(inner_grad_kernel, first), "inner_grad", [shape((2, 144, 2048))], [n2, din, sums])[0]
+        out[k] = m[128 * k : 128 * (k + 1), :]
+
+
+def inner_grad(clock, n2, din, first):
+    return call(clock, functools.partial(inner_grad_kernel, first), "inner_grad", [shape((2, 128, 2048))], [n2, din])[0]
 
 
 def resid_back_kernel(token, dy, n2, r2, din, *refs):
@@ -553,7 +551,7 @@
     return call(clock, resid_back_kernel, "resid_back", outs, [dy, n2, r2, din, *wo, *wi, *packs], [pltpu.VMEM((ROWS, 512), F32)])
 
 
-def project_grad_kernel(first, starts, token, n1, early, late, mixed, dres, out):
+def project_grad_kernel(first, starts, token, n1, early, late, mixed, dres, sums, out):
     half = early.shape[0]
     blocks = wide(blocks_of(token), 128)
     n = n1[:, 128 * first : 128 * (first + 2)]
@@ -561,7 +559,8 @@
         cols, dest = slice(start, start + 1024), slice(1024 * at, 1024 * (at + 1))
         m = (mm_tn(n[0:half], early[:, cols]) + mm_tn(n[half:], late[:, cols])).astype(BF16)
         total = sum(jnp.sum(r[:, cols].astype(F32), axis=0, keepdims=True) for r in (early, late))
-        tail = jnp.broadcast_to(total, (16, 1024)).astype(BF16)
+        row = lax.broadcasted_iota(jnp.int32, (16, 1024), 0)
+        tail = jnp.where(row == 0, total, jnp.where(row == 1, sums[0:1, cols], sums[1:2, cols])).astype(BF16)
         for k in range(2):
             out[k, 0:128, dest] = m[128 * k : 128 * (k + 1)]
             out[k, 128:144, dest] = tail
@@ -573,10 +572,10 @@
             out[k, 128:144, rest:] = jnp.zeros((16, 512), BF16)
 
 
-def project_grad(clock, n1, early, late, mixed, dres, first, starts=(0, 1024)):
+def project_grad(clock, n1, early, late, mixed, dres, sums, first, starts=(0, 1024)):
     width = 1024 * len(starts) + (512 if 1024 in starts else 0)
     kernel = functools.partial(project_grad_kernel, first, starts)
-    return call(clock, kernel, "project_grad", [shape((2, 144, width))], [n1, early, late, mixed, dres])[0]
+    return call(clock, kernel, "project_grad", [shape((2, 144, width))], [n1, early, late, mixed, dres, sums])[0]
 
 
 def input_grad_kernel(token, tokens, early, late, dres, p0, p1, p2, p3, out, scr, result, sems):
@@ -767,52 +766,42 @@
     return call(clock, finish_outer_kernel, "finish_outer", [shape(u.shape, F32)], [u], [pltpu.VMEM(u.shape, F32), pltpu.SemaphoreType.DMA((1,))], limit=JOIN, outside=(0,))[0]
 
 
-def finish_inner_kernel(token, total, w, pack, out, gain_out, shift_out, inner_out, outer_out, buf, small, sems):
-    gain, shift = (column(pack[128:129, k : k + 128].astype(F32)) for k in (256, 384))
-    m = total[0:128, :].astype(F32)
-    tail = total[128:144, :].astype(F32)
-    buf[...] = gain * m + shift * tail[0:1, :]
-    wf = w[...].astype(F32)
-    small[0:1, 0:128] = as_row(jnp.sum(wf * m, axis=1, keepdims=True))
-    small[1:2, 0:128] = as_row(jnp.sum(wf * tail[0:1, :], axis=1, keepdims=True))
-    me = position(token, 0)
-    small[2:3, :] = total[128:144, pl.ds(pl.multiple_of(me * 512, 512), 512)].astype(F32)[0:1, :]
-    small[3:4, 0:128] = total[128:144, pl.ds(pl.multiple_of(me * 128, 128), 128)].astype(F32)[1:2, :]
-    send_out([(buf, out), (small.at[0, 0:128], gain_out), (small.at[1, 0:128], shift_out), (small.at[2], inner_out), (small.at[3, 0:128], outer_out)], sems)
-
-
-def finish_inner(clock, total, w, pack):
-    outs = [shape((128, 2048), F32), shape((128,), F32), shape((128,), F32), shape((512,), F32), shape((128,), F32)]
-    scratch = [pltpu.VMEM((128, 2048), F32), pltpu.VMEM((8, 512), F32), pltpu.SemaphoreType.DMA((5,))]
-    return call(clock, finish_inner_kernel, "finish_inner", outs, [total, w, pack], scratch, limit=JOIN, outside=range(5))
-
-
-def finish_project_kernel(_, total, pack, *refs):
-    outs, (buf, small, sems) = refs[:-3], refs[-3:]
-    gain, shift = (column(pack[128:129, k : k + 128].astype(F32)) for k in (0, 128))
+def finish_kernel(token, total, inner, w_inner, pack, *refs):
+    outs, (buf, buf_inner, small, sems) = refs[:-4], refs[-4:]
+    gain, shift, gain_two, shift_two = (column(pack[128:129, k : k + 128].astype(F32)) for k in (0, 128, 256, 384))
     copies = []
-    for k, out in enumerate(outs[:5]):
+
+    def leave(source, k):
+        copies.append(pltpu.make_async_copy(source, outs[k], sems.at[k]))
+        copies[-1].start()
+
+    sums = total[128:144, 0:2048].astype(F32)
+    n = inner[...].astype(F32)
+    buf_inner[...] = gain_two * n + shift_two * sums[1:2, :]
+    leave(buf_inner, 5)
+    for k in range(5):
         cols = slice(512 * k, 512 * (k + 1))
         part = total[0:128, cols].astype(F32)
-        buf[:, cols] = gain * part + shift * total[128:144, cols].astype(F32)[0:1, :] if k < 4 else part
-        copies.append(pltpu.make_async_copy(buf.at[:, cols], out, sems.at[k]))
-        copies[-1].start()
-    m = total[0:128, 0:2048].astype(F32)
-    tail = total[128:144, 0:2048].astype(F32)[0:1, :]
+        buf[:, cols] = gain * part + shift * sums[0:1, cols] if k < 4 else part
+        leave(buf.at[:, cols], k)
     w = pack[0:128, :].astype(F32)
-    small[0:1, :] = as_row(jnp.sum(w * m, axis=1, keepdims=True))
-    small[1:2, :] = as_row(jnp.sum(w * tail, axis=1, keepdims=True))
-    more = [pltpu.make_async_copy(small.at[k], out, sems.at[5 + k]) for k, out in enumerate(outs[5:])]
-    for copy in more:
-        copy.start()
-    for copy in copies + more:
+    v = w_inner[...].astype(F32)
+    for k, product in enumerate((w * total[0:128, 0:2048].astype(F32), w * sums[0:1, :], v * n, v * sums[1:2, :])):
+        small[k : k + 1, 0:128] = as_row(jnp.sum(product, axis=1, keepdims=True))
+        leave(small.at[k, 0:128], 6 + k)
+    me = position(token, 0)
+    small[4:5, :] = total[128:144, pl.ds(pl.multiple_of(me * 512, 512), 512)].astype(F32)[1:2, :]
+    leave(small.at[4], 10)
+    small[5:6, 0:128] = total[128:144, pl.ds(pl.multiple_of(me * 128, 128), 128)].astype(F32)[2:3, :]
+    leave(small.at[5, 0:128], 11)
+    for copy in copies:
         copy.wait()
 
 
-def finish_project(clock, total, pack):
-    outs = [shape((128, 512), F32)] * 5 + [shape((128,), F32)] * 2
-    scratch = [pltpu.VMEM((128, 2560), F32), pltpu.VMEM((8, 128), F32), pltpu.SemaphoreType.DMA((7,))]
-    return call(clock, finish_project_kernel, "finish_project", outs, [total, pack], scratch, limit=JOIN, outside=range(7))
+def finish_all(clock, total, inner, w_inner, pack):
+    outs = [shape((128, 512), F32)] * 5 + [shape((128, 2048), F32)] + [shape((128,), F32)] * 4 + [shape((512,), F32), shape((128,), F32)]
+    scratch = [pltpu.VMEM((128, 2560), F32), pltpu.VMEM((128, 2048), F32), pltpu.VMEM((8, 512), F32), pltpu.SemaphoreType.DMA((12,))]
+    return call(clock, finish_kernel, "finish_all", outs, [total, inner, w_inner, pack], scratch, limit=12, outside=range(12))
 
 
 PLAN = (
@@ -871,10 +860,10 @@
         made["din"] = inner_back(clock, cotangent, d, [made["wu"][1], made["wu"][3]], (1, 3), [partial])
 
     def inner_send():
-        start("i", [inner_grad(clock, n2, *made["din"], 2)], None)
+        start("i", [inner_grad(clock, n2, made["din"][0], 2)], None)
 
     def inner_keep():
-        made["i"] = inner_grad(clock, n2, *made["din"], 0)
+        made["i"] = inner_grad(clock, n2, made["din"][0], 0)
 
     def resid_grad():
         made["dres"], made["do"] = resid_back(clock, cotangent, n2, r2, made["din"][0], wo, wi, packs)
@@ -886,7 +875,7 @@
         made["late"] = attention_backward(clock, qkvf, saved, made["do"], 3, 4, made["early"][1:])
 
     def project_part(first):
-        return project_grad(clock, n1_low, made["late"][0], made["early"][0], mixed, made["dres"], first)
+        return project_grad(clock, n1_low, made["late"][0], made["early"][0], mixed, made["dres"], made["din"][1], first)
 
     def project_send():
         start("p", [project_part(2)], None)
@@ -901,13 +890,10 @@
         made["output"] = ffn_outer(clock, resid, act, made["wu"], packs)
 
     def finish(name):
-        total = chains[name].keep
         if name == "u":
-            made["outer"] = finish_outer(clock, total)
-        elif name == "i":
-            made["inner"] = finish_inner(clock, total, w_inner, packs[0])
-        else:
-            made["project"] = finish_project(clock, total, packs[0])
+            made["outer"] = finish_outer(clock, chains[name].keep)
+        elif not (chains["i"].busy or chains["p"].busy):
+            made["rest"] = finish_all(clock, chains["p"].keep, chains["i"].keep, w_inner, packs[0])
 
     def advance(name):
         c = chains[name]
@@ -933,13 +919,13 @@
     while any(c.busy for c in chains.values()):
         for name in "uip":
             advance(name)
-    output, grad_tokens, grad_outer = made["output"], made["tokens"], made["outer"]
-    grad_inner, *vectors = made["inner"]
-    grad_query, grad_key, grad_value, grad_control, grad_output, first_gain_grad, first_shift_grad = made["project"]
-    second_gain_grad, second_shift_grad, inner_bias_grad, outer_bias_grad = vectors
+    (
+        grad_query, grad_key, grad_value, grad_control, grad_output, grad_inner, first_gain_grad, first_shift_grad,
+        second_gain_grad, second_shift_grad, inner_bias_grad, outer_bias_grad,
+    ) = made["rest"]
     return (
-        output, grad_tokens, first_gain_grad, first_shift_grad, grad_query, grad_key, grad_value, grad_control,
-        grad_output, second_gain_grad, second_shift_grad, grad_inner, inner_bias_grad, grad_outer, outer_bias_grad,
+        made["output"], made["tokens"], first_gain_grad, first_shift_grad, grad_query, grad_key, grad_value, grad_control, grad_output,
+        second_gain_grad, second_shift_grad, grad_inner, inner_bias_grad, made["outer"], outer_bias_grad,
     )
 
 

time: 139 us -> 138 us (level)
    pallas_call x40 -> x39, Pallas kernels: 64.6 us -> 63.7 us  [call(): pl.pallas_call(body, in_specs=[VM] + [ANY if k in raw else VM for k in ra...]
  transfers between devices with their start and end apart: 41 -> 41, of which waited for: 19 -> 20; matrix products, arithmetic and copies ran while one was open for 0% -> 0% of each run, Pallas kernels for 41% -> 40%
where the time goes in v6:
time: 138 us; the launch traced here: 137 us
  Pallas kernels  63.7 us (46%)
  starting transfers between devices  39.6 us (29%)
  waiting for transfers between devices  31.4 us (23%)
    pallas_call x39, Pallas kernels, call(): pl.pallas_call(body, in_specs=[VM] + [ANY if k in raw else VM for k in ra...  63.7 us
    ppermute x41, starting transfers between devices, exchange(): return lax.ppermute(value, axis, [(i, i ^ mask) for i in range(size)])  39.6 us
    ppermute x41, waiting for transfers between devices, exchange(): return lax.ppermute(value, axis, [(i, i ^ mask) for i in range(size)])  31.4 us
  transfers between devices with their start and end apart: 41, of which 20 were waited for; matrix products, arithmetic and copies ran while one was open for 0% of the time, Pallas kernels for 40%

profile of v6, /device:TPU:0, one launch (start us, length us, event | category | flops | bytes accessed | tf_op | source)
XLA Modules:
  0.0 137.4 jit_solution(7480859805101957175)
XLA Ops:
  0.8 1.7 %begin.1 = (bf16[144,2048]{1,0:T(8,128)(2,1)S(1)}, bf16[144,512]{1,0:T(8,128)(2,1)S(1)}, bf16[144,512]{1,0:T(8,128)(2,1)S(1)}, bf16[64,2048]{1,0:T(8,128)(2,1)S(...) custom-call(s32[8,128]{1,0:T(8,128)S(1)} %iota.7.token, bf16[128,512]{1,0:T(8,128)(2,1)} %refs_0_.7, ...), custom_call_target="tpu_custom_call" | custom-call | flops 1000 | bytes 1024 | tf_op jit(solution)/shard_map/begin/pallas_call | solution.py:64
  2.5 3.0 %collective-permute-start = (bf16[144,512]{1,0:T(8,128)(2,1)S(1)}, bf16[144,512]{1,0:T(8,128)(2,1)S(1)}, u32[]{:S(2)}, u32[]{:S(2)}) collective-permute-start(bf16[144,512]{1,0:T(8,128)(2,1)S(1)} %get-tuple-element.150), channel_id=1, source_target_pairs={{0,2},{1,3},{2,0},{3,1},{4,6},{5,7},{6,4},{7,5},{8,10},{9,11},{10,... | collective-permute-start | bytes 442376 | tf_op jit(solution)/shard_map/ppermute | solution.py:606
  8.0 2.2 %collective-permute-done.refs_0_ = bf16[144,512]{1,0:T(8,128)(2,1)S(1)} collective-permute-done((bf16[144,512]{1,0:T(8,128)(2,1)S(1)}, bf16[144,512]{1,0:T(8,128)(2,1)S(1)}, u32[]{:S(2)}, u32[]{:S(2)}) %collective-permute-start) | collective-permute-done | bytes 147488 | tf_op jit(solution)/shard_map/ppermute | solution.py:606
  10.2 2.3 %collective-permute-done.1.refs_1_ = bf16[144,512]{1,0:T(8,128)(2,1)S(1)} collective-permute-done((bf16[144,512]{1,0:T(8,128)(2,1)S(1)}, bf16[144,512]{1,0:T(8,128)(2,1)S(1)}, u32[]{:S(2)}, u32[]{:S(2)}) %collective-permute-start.1) | collective-permute-done | bytes 147488 | tf_op jit(solution)/shard_map/ppermute | solution.py:606
  12.5 1.7 %collective-permute-start.4 = (bf16[64,2048]{1,0:T(8,128)(2,1)S(1)}, bf16[64,2048]{1,0:T(8,128)(2,1)S(1)}, u32[]{:S(2)}, u32[]{:S(2)}) collective-permute-start(bf16[64,2048]{1,0:T(8,128)(2,1)S(1)} %get-tuple-element.157), channel_id=1, source_target_pairs={{0,2},{1,3},{2,0},{3,1},{4,6},{5,7},{6,4},{7,5},{8,10},{9,11},{10,... | collective-permute-start | bytes 786440 | tf_op jit(solution)/shard_map/ppermute | solution.py:606
  15.8 1.6 %collective-permute-start.3 = (bf16[144,512]{1,0:T(8,128)(2,1)S(1)}, bf16[144,512]{1,0:T(8,128)(2,1)S(1)}, u32[]{:S(2)}, u32[]{:S(2)}) collective-permute-start(bf16[144,512]{1,0:T(8,128)(2,1)S(1)} %collective-permute-done.1.refs_1_), channel_id=1, source_target_pairs={{0,8},{4,12},{8,0},{12,4},{16,24},{20,28},{24,16},{28,20},{1,9},{5... | collective-permute-start | bytes 442376 | tf_op jit(solution)/shard_map/ppermute | solution.py:606
  17.3 2.0 %collective-permute-done.2.refs_2_ = bf16[144,512]{1,0:T(8,128)(2,1)S(1)} collective-permute-done((bf16[144,512]{1,0:T(8,128)(2,1)S(1)}, bf16[144,512]{1,0:T(8,128)(2,1)S(1)}, u32[]{:S(2)}, u32[]{:S(2)}) %collective-permute-start.2) | collective-permute-done | bytes 147488 | tf_op jit(solution)/shard_map/ppermute | solution.py:606
  23.6 2.4 %project.1 = (bf16[1024,2048]{1,0:T(8,128)(2,1)S(1)}, s32[8,128]{1,0:T(8,128)S(1)}) custom-call(s32[8,128]{1,0:T(8,128)S(1)} %get-tuple-element.161.token, f32[1024,512]{1,0:T(8,128)S(1)} %get-tuple-element.162.refs_0_, bf16[144,2048]{1,0:T(8,128)(2,1)S(1)} %get-tuple-element.163.refs_1_.refs_6_.refs_7_.refs_14_.refs_4_.refs_3_, ...), custom_call_target="tpu_custom_call" | custom-call | flops 1000 | bytes 1024 | tf_op jit(solution)/shard_map/project/pallas_call | solution.py:64
  25.9 7.4 %attention_forward.1 = (bf16[1024,512]{1,0:T(8,128)(2,1)S(1)}, bf16[1024,3072]{1,0:T(8,128)(2,1)S(1)}, bf16[8,128,1024]{2,1,0:T(8,128)(2,1)S(1)}, f32[8,8,512]{2,1,0:T(8,128)S(1)}, s32[8,128]{1,0:T(8,128)S(1)}) custom-call(s32[8,128]{1,0:T(8,128)S(1)} %get-tuple-element.166.token, bf16[1024,2048]{1,0:T(8,128)(2,1)S(1)} %get-tuple-element.167.refs_0_), custom_call_target="tpu_custom_call" | custom-call | flops 1000 | bytes 1024 | tf_op jit(solution)/shard_map/attention_forward/pallas_call | solution.py:64
  35.8 2.0 %middle.1 = (f32[1024,512]{1,0:T(8,128)S(1)}, bf16[1024,512]{1,0:T(8,128)(2,1)S(1)}, f32[1024,128]{1,0:T(8,128)S(1)}, bf16[1024,512]{1,0:T(8,128)(2,1)S(1)}, s32[8,128]{1,0:T(8,128)S(1)}) custom-call(s32[8,128]{1,0:T(8,128)S(1)} %get-tuple-element.171.token, bf16[1024,512]{1,0:T(8,128)(2,1)S(1)} %copy-done.2, ...), custom_call_target="tpu_custom_call" | custom-call | flops 1000 | bytes 1024 | tf_op jit(solution)/shard_map/middle/pallas_call | solution.py:64
  37.9 6.2 %ffn_inner.1 = (bf16[1024,2048]{1,0:T(8,128)(2,1)S(1)}, bf16[1024,2048]{1,0:T(8,128)(2,1)S(1)}, s32[8,128]{1,0:T(8,128)S(1)}) custom-call(s32[8,128]{1,0:T(8,128)S(1)} %get-tuple-element.174.token, bf16[1024,512]{1,0:T(8,128)(2,1)S(1)} %get-tuple-element.175.refs_0_, bf16[128,2048]{1,0:T(8,128)(2,1)S(1)} %copy-done.3, ...), custom_call_target="tpu_custom_call" | custom-call | flops 1000 | bytes 1024 | tf_op jit(solution)/shard_map/ffn_inner/pallas_call | solution.py:64
  44.1 2.4 %outer_grad.1 = (bf16[2,512,512]{2,1,0:T(8,128)(2,1)S(1)}, bf16[2,512,512]{2,1,0:T(8,128)(2,1)S(1)}, s32[8,128]{1,0:T(8,128)S(1)}) custom-call(s32[8,128]{1,0:T(8,128)S(1)} %get-tuple-element.177.token, bf16[1024,2048]{1,0:T(8,128)(2,1)S(1)} %get-tuple-element.178.refs_0_.refs_1_, bf16[1024,512]{1,0:T(8,128)(2,1)S(1)} %copy-done), custom_call_target="tpu_custom_call" | custom-call | flops 1000 | bytes 1024 | tf_op jit(solution)/shard_map/outer_grad/pallas_call | solution.py:64
  47.0 1.6 %inner_back.2 = (bf16[1024,2048]{1,0:T(8,128)(2,1)S(1)}, f32[8,2048]{1,0:T(8,128)S(1)}, s32[8,128]{1,0:T(8,128)S(1)}) custom-call(s32[8,128]{1,0:T(8,128)S(1)} %get-tuple-element.179.token, bf16[1024,512]{1,0:T(8,128)(2,1)S(1)} %copy-done, bf16[1024,2048]{1,0:T(8,128)(2,1)S(1)} %get-tuple-element.180.refs_1_, ...), custom_call_target="tpu_custom_call", output_to_operand_aliasing={{0}: (2, {})} | custom-call | flops 1000 | bytes 1024 | tf_op jit(solution)/shard_map/inner_back/pallas_call | solution.py:64
  49.4 1.9 %collective-permute-done.16.refs_3_.refs_5_ = bf16[512,512]{1,0:T(8,128)(2,1)S(1)} collective-permute-done((bf16[512,512]{1,0:T(8,128)(2,1)S(1)}, bf16[512,512]{1,0:T(8,128)(2,1)S(1)}, u32[]{:S(2)}, u32[]{:S(2)}) %collective-permute-start.16) | collective-permute-done | bytes 524320 | tf_op jit(solution)/shard_map/ppermute | solution.py:606
  58.6 1.6 %collective-permute-start.21 = (bf16[256,512]{1,0:T(8,128)(2,1)S(1)}, bf16[256,512]{1,0:T(8,128)(2,1)S(1)}, u32[]{:S(2)}, u32[]{:S(2)}) collective-permute-start(bf16[256,512]{1,0:T(8,128)(2,1)S(1)} %get-tuple-element.210), channel_id=1, source_target_pairs={{0,8},{4,12},{8,0},{12,4},{16,24},{20,28},{24,16},{28,20},{1,9},{5... | collective-permute-start | bytes 786440 | tf_op jit(solution)/shard_map/ppermute | solution.py:606
  61.3 4.4 %resid_back.1 = (f32[1024,512]{1,0:T(8,128)S(1)}, bf16[1024,512]{1,0:T(8,128)(2,1)S(1)}, s32[8,128]{1,0:T(8,128)S(1)}) custom-call(s32[8,128]{1,0:T(8,128)S(1)} %get-tuple-element.197.token, bf16[1024,512]{1,0:T(8,128)(2,1)S(1)} %copy-done, bf16[1024,512]{1,0:T(8,128)(2,1)S(1)} %get-tuple-element.191.refs_0_.refs_1_, ...), custom_call_target="tpu_custom_call" | custom-call | flops 1000 | bytes 1024 | tf_op jit(solution)/shard_map/resid_back/pallas_call | solution.py:64
  65.7 5.3 %attention_backward.2 = (bf16[512,2048]{1,0:T(8,128)(2,1)S(1)}, f32[4,128,256]{2,1,0:T(8,128)S(1)}, f32[8,512]{1,0:T(8,128)S(1)}, s32[8,128]{1,0:T(8,128)S(1)}) custom-call(s32[8,128]{1,0:T(8,128)S(1)} %get-tuple-element.199.token, bf16[1024,2048]{1,0:T(8,128)(2,1)S(1)} %get-tuple-element.167.refs_0_, bf16[1024,3072]{1,0:T(8,128)(2,1)S(1)} %get-tuple-element.200.refs_1_, ...), custom_call_target="tpu_custom_call" | custom-call | flops 1000 | bytes 1024 | tf_op jit(solution)/shard_map/attention_backward/pallas_call | solution.py:64
  73.9 5.1 %attention_backward.3 = (bf16[512,2048]{1,0:T(8,128)(2,1)S(1)}, s32[8,128]{1,0:T(8,128)S(1)}) custom-call(s32[8,128]{1,0:T(8,128)S(1)} %get-tuple-element.212.token, bf16[1024,2048]{1,0:T(8,128)(2,1)S(1)} %get-tuple-element.167.refs_0_, bf16[1024,3072]{1,0:T(8,128)(2,1)S(1)} %get-tuple-element.200.refs_1_, ...), custom_call_target="tpu_custom_call" | custom-call | flops 1000 | bytes 1024 | tf_op jit(solution)/shard_map/attention_backward/pallas_call | solution.py:64
  79.3 1.6 %project_grad.2 = (bf16[2,144,2560]{2,1,0:T(8,128)(2,1)S(1)}, s32[8,128]{1,0:T(8,128)S(1)}) custom-call(s32[8,128]{1,0:T(8,128)S(1)} %get-tuple-element.221.token, bf16[1024,512]{1,0:T(8,128)(2,1)S(1)} %get-tuple-element.222.refs_0_, bf16[512,2048]{1,0:T(8,128)(2,1)S(1)} %get-tuple-element.223.refs_1_, bf16[512,2048]{1,0:T(8,128)(2,1)S(1)} %get-tuple-element.224.refs_2_, ...), custom_call_target="tpu_custom_call" | custom-call | flops 1000 | bytes 1024 | tf_op jit(solution)/shard_map/project_grad/pallas_call | solution.py:64
  81.0 1.6 %project_grad.3 = (bf16[2,144,2560]{2,1,0:T(8,128)(2,1)S(1)}, s32[8,128]{1,0:T(8,128)S(1)}) custom-call(s32[8,128]{1,0:T(8,128)S(1)} %get-tuple-element.227.token, bf16[1024,512]{1,0:T(8,128)(2,1)S(1)} %get-tuple-element.222.refs_0_, bf16[512,2048]{1,0:T(8,128)(2,1)S(1)} %get-tuple-element.223.refs_1_, bf16[512,2048]{1,0:T(8,128)(2,1)S(1)} %get-tuple-element.224.refs_2_, ...), custom_call_target="tpu_custom_call" | custom-call | flops 1000 | bytes 1024 | tf_op jit(solution)/shard_map/project_grad/pallas_call | solution.py:64
  82.6 1.6 %collective-permute-done.25.refs_1_ = bf16[2,144,2560]{2,1,0:T(8,128)(2,1)S(1)} collective-permute-done((bf16[2,144,2560]{2,1,0:T(8,128)(2,1)S(1)}, bf16[2,144,2560]{2,1,0:T(8,128)(2,1)S(1)}, u32[]{:S(2)}, u32[]{:S(2)}) %collective-permute-start.25) | collective-permute-done | bytes 1474592 | tf_op jit(solution)/shard_map/ppermute | solution.py:606
  87.5 2.6 %collective-permute-start.27 = (bf16[128,512]{1,0:T(8,128)(2,1)S(1)}, bf16[128,512]{1,0:T(8,128)(2,1)S(1)}, u32[]{:S(2)}, u32[]{:S(2)}) collective-permute-start(bf16[128,512]{1,0:T(8,128)(2,1)S(1)} %get-tuple-element.236.refs_0_), channel_id=1, source_target_pairs={{0,16},{4,20},{8,24},{12,28},{16,0},{20,4},{24,8},{28,12},{1,17},{... | collective-permute-start | bytes 393224 | tf_op jit(solution)/shard_map/ppermute | solution.py:606
  90.1 4.4 %input_grad.1 = (bf16[1024,512]{1,0:T(8,128)(2,1)}, s32[8,128]{1,0:T(8,128)S(1)}) custom-call(s32[8,128]{1,0:T(8,128)S(1)} %get-tuple-element.231.token, bf16[1024,512]{1,0:T(8,128)(2,1)S(1)} %copy-done.2, bf16[512,2048]{1,0:T(8,128)(2,1)S(1)} %get-tuple-element.223.refs_1_, bf16[512,2048]{1,0:T(8,128)(2,1)S(1)} %get-tuple-element.224.refs_2_, ...), custom_call_target="tpu_custom_call" | custom-call | flops 1000 | bytes 1024 | tf_op jit(solution)/shard_map/input_grad/pallas_call | solution.py:64
  97.2 3.9 %ffn_outer.1 = (bf16[1024,512]{1,0:T(8,128)(2,1)}, s32[8,128]{1,0:T(8,128)S(1)}) custom-call(s32[8,128]{1,0:T(8,128)S(1)} %get-tuple-element.237.token, f32[1024,512]{1,0:T(8,128)S(1)} %get-tuple-element.238.refs_0_, bf16[1024,2048]{1,0:T(8,128)(2,1)S(1)} %get-tuple-element.178.refs_0_.refs_1_, bf16[512,512]{1,0:T(8,128)(2,1)S(1)} %copy-done.4, ...), custom_call_target="tpu_custom_call" | custom-call | flops 1000 | bytes 1024 | tf_op jit(solution)/shard_map/ffn_outer/pallas_call | solution.py:64
  101.1 2.0 %collective-permute-done.28.refs_1_ = bf16[512,128]{1,0:T(8,128)(2,1)S(1)} collective-permute-done((bf16[512,128]{1,0:T(8,128)(2,1)S(1)}, bf16[512,128]{1,0:T(8,128)(2,1)S(1)}, u32[]{:S(2)}, u32[]{:S(2)}) %collective-permute-start.28) | collective-permute-done | bytes 131104 | tf_op jit(solution)/shard_map/ppermute | solution.py:606
  110.4 1.9 %collective-permute-done.31.refs_1_ = bf16[144,640]{1,0:T(8,128)(2,1)S(1)} collective-permute-done((bf16[144,640]{1,0:T(8,128)(2,1)S(1)}, bf16[144,640]{1,0:T(8,128)(2,1)S(1)}, u32[]{:S(2)}, u32[]{:S(2)}) %collective-permute-start.31) | collective-permute-done | bytes 184352 | tf_op jit(solution)/shard_map/ppermute | solution.py:606
  112.6 4.0 %collective-permute-done.33.refs_3_ = bf16[144,640]{1,0:T(8,128)(2,1)S(1)} collective-permute-done((bf16[144,640]{1,0:T(8,128)(2,1)S(1)}, bf16[144,640]{1,0:T(8,128)(2,1)S(1)}, u32[]{:S(2)}, u32[]{:S(2)}) %collective-permute-start.33) | collective-permute-done | bytes 184352 | tf_op jit(solution)/shard_map/ppermute | solution.py:606
  116.8 2.3 %collective-permute-start.36 = (bf16[144,640]{1,0:T(8,128)(2,1)S(1)}, bf16[144,640]{1,0:T(8,128)(2,1)S(1)}, u32[]{:S(2)}, u32[]{:S(2)}) collective-permute-start(bf16[144,640]{1,0:T(8,128)(2,1)S(1)} %get-tuple-element.258.refs_0_), channel_id=1, source_target_pairs={{0,16},{4,20},{8,24},{12,28},{16,0},{20,4},{24,8},{28,12},{1,17},{... | collective-permute-start | bytes 552968 | tf_op jit(solution)/shard_map/ppermute | solution.py:606
  119.4 1.8 %collective-permute-start.37 = (bf16[512,256]{1,0:T(8,128)(2,1)S(1)}, bf16[512,256]{1,0:T(8,128)(2,1)S(1)}, u32[]{:S(2)}, u32[]{:S(2)}) collective-permute-start(bf16[512,256]{1,0:T(8,128)(2,1)S(1)} %get-tuple-element.260.refs_0_), channel_id=1, source_target_pairs={{0,4},{4,0},{8,12},{12,8},{16,20},{20,16},{24,28},{28,24},{1,5},{5... | collective-permute-start | bytes 786440 | tf_op jit(solution)/shard_map/ppermute | solution.py:606
  121.5 3.9 %collective-permute-done.36.refs_1_ = bf16[144,640]{1,0:T(8,128)(2,1)S(1)} collective-permute-done((bf16[144,640]{1,0:T(8,128)(2,1)S(1)}, bf16[144,640]{1,0:T(8,128)(2,1)S(1)}, u32[]{:S(2)}, u32[]{:S(2)}) %collective-permute-start.36) | collective-permute-done | bytes 184352 | tf_op jit(solution)/shard_map/ppermute | solution.py:606
  130.4 1.6 %collective-permute-done.40.refs_3_ = bf16[144,640]{1,0:T(8,128)(2,1)S(1)} collective-permute-done((bf16[144,640]{1,0:T(8,128)(2,1)S(1)}, bf16[144,640]{1,0:T(8,128)(2,1)S(1)}, u32[]{:S(2)}, u32[]{:S(2)}) %collective-permute-start.40) | collective-permute-done | bytes 184352 | tf_op jit(solution)/shard_map/ppermute | solution.py:606
  134.3 2.9 %finish_all.1 = (f32[128,512]{1,0:T(8,128)}, f32[128,512]{1,0:T(8,128)}, f32[128,512]{1,0:T(8,128)}, f32[128,512]{1,0:T(8,128)}, f32[128,512]{1,0:T(8,128)}, /*i...) custom-call(s32[8,128]{1,0:T(8,128)S(1)} %get-tuple-element.265.toke, ...), custom_call_target="tpu_custom_call" | custom-call | flops 1000 | bytes 1024 | tf_op jit(solution)/shard_map/finish_all/pallas_call | solution.py:64
  (103 shorter events, 45.2 us)
Async XLA Ops:
  2.5 7.7 %collective-permute-start = (bf16[144,512]{1,0:T(8,128)(2,1)S(1)}, bf16[144,512]{1,0:T(8,128)(2,1)S(1)}, u32[]{:S(2)}, u32[]{:S(2)}) collective-permute-start(bf16[144,512]{1,0:T(8,128)(2,1)S(1)} %get-tuple-element.150), channel_id=1, source_target_pairs={{0,2},{1,3},{2,0},{3,1},{4,6},{5,7},{6,4},{7,5},{8,10},{9,11},{10,... | collective-permute-start | bytes 442376 | tf_op jit(solution)/shard_map/ppermute | solution.py:606
  5.5 7.0 %collective-permute-start.1 = (bf16[144,512]{1,0:T(8,128)(2,1)S(1)}, bf16[144,512]{1,0:T(8,128)(2,1)S(1)}, u32[]{:S(2)}, u32[]{:S(2)}) collective-permute-start(bf16[144,512]{1,0:T(8,128)(2,1)S(1)} %get-tuple-element.151), channel_id=1, source_target_pairs={{0,2},{1,3},{2,0},{3,1},{4,6},{5,7},{6,4},{7,5},{8,10},{9,11},{10,... | collective-permute-start | bytes 442376 | tf_op jit(solution)/shard_map/ppermute | solution.py:606
  12.5 8.4 %collective-permute-start.4 = (bf16[64,2048]{1,0:T(8,128)(2,1)S(1)}, bf16[64,2048]{1,0:T(8,128)(2,1)S(1)}, u32[]{:S(2)}, u32[]{:S(2)}) collective-permute-start(bf16[64,2048]{1,0:T(8,128)(2,1)S(1)} %get-tuple-element.157), channel_id=1, source_target_pairs={{0,2},{1,3},{2,0},{3,1},{4,6},{5,7},{6,4},{7,5},{8,10},{9,11},{10,... | collective-permute-start | bytes 786440 | tf_op jit(solution)/shard_map/ppermute | solution.py:606
  17.3 6.2 %collective-permute-start.5 = (bf16[144,2048]{1,0:T(8,128)(2,1)S(1)}, bf16[144,2048]{1,0:T(8,128)(2,1)S(1)}, u32[]{:S(2)}, u32[]{:S(2)}) collective-permute-start(bf16[144,2048]{1,0:T(8,128)(2,1)S(1)} %get-tuple-element.163.refs_1_.refs_6_.refs_7_.refs_14_.refs_4_.refs_3_), channel_id=1, source_target_pairs={{0,1},{1,0},{2,3},{3,2},{4,5},{5,4},{6,7},{7,6},{8,9},{9,8},{10,11... | collective-permute-start | bytes 1769480 | tf_op jit(solution)/shard_map/ppermute | solution.py:606
  21.2 12.1 %collective-permute-start.8 = (bf16[64,2048]{1,0:T(8,128)(2,1)S(1)}, bf16[64,2048]{1,0:T(8,128)(2,1)S(1)}, u32[]{:S(2)}, u32[]{:S(2)}) collective-permute-start(bf16[64,2048]{1,0:T(8,128)(2,1)S(1)} %get-tuple-element.170), channel_id=1, source_target_pairs={{0,2},{1,3},{2,0},{3,1},{4,6},{5,7},{6,4},{7,5},{8,10},{9,11},{10,... | collective-permute-start | bytes 786440 | tf_op jit(solution)/shard_map/ppermute | solution.py:606
  21.8 16.1 %collective-permute-start.11 = (bf16[128,2048]{1,0:T(8,128)(2,1)S(1)}, bf16[128,2048]{1,0:T(8,128)(2,1)S(1)}, u32[]{:S(2)}, u32[]{:S(2)}) collective-permute-start(bf16[128,2048]{1,0:T(8,128)(2,1)S(1)} %copy-done.3), channel_id=1, source_target_pairs={{0,1},{1,0},{2,3},{3,2},{4,5},{5,4},{6,7},{7,6},{8,9},{9,8},{10,11... | collective-permute-start | bytes 1572872 | tf_op jit(solution)/shard_map/ppermute | solution.py:606
  22.0 11.3 %collective-permute-start.7 = (bf16[128,512]{1,0:T(8,128)(2,1)S(1)}, bf16[128,512]{1,0:T(8,128)(2,1)S(1)}, u32[]{:S(2)}, u32[]{:S(2)}) collective-permute-start(bf16[128,512]{1,0:T(8,128)(2,1)S(1)} %copy-done.5), channel_id=1, source_target_pairs={{0,2},{1,3},{2,0},{3,1},{4,6},{5,7},{6,4},{7,5},{8,10},{9,11},{10,... | collective-permute-start | bytes 393224 | tf_op jit(solution)/shard_map/ppermute | solution.py:606
  23.5 14.4 %collective-permute-start.12 = (bf16[64,2048]{1,0:T(8,128)(2,1)S(1)}, bf16[64,2048]{1,0:T(8,128)(2,1)S(1)}, u32[]{:S(2)}, u32[]{:S(2)}) collective-permute-start(bf16[64,2048]{1,0:T(8,128)(2,1)S(1)} %collective-permute-done.4.refs_4_.refs_2_.refs_9_), channel_id=1, source_target_pairs={{0,1},{1,0},{2,3},{3,2},{4,5},{5,4},{6,7},{7,6},{8,9},{9,8},{10,11... | collective-permute-start | bytes 786440 | tf_op jit(solution)/shard_map/ppermute | solution.py:606
  35.2 14.2 %collective-permute-start.15 = (bf16[512,512]{1,0:T(8,128)(2,1)S(1)}, bf16[512,512]{1,0:T(8,128)(2,1)S(1)}, u32[]{:S(2)}, u32[]{:S(2)}) collective-permute-start(bf16[512,512]{1,0:T(8,128)(2,1)S(1)} %copy-done.4), channel_id=1, source_target_pairs={{0,2},{1,3},{2,0},{3,1},{4,6},{5,7},{6,4},{7,5},{8,10},{9,11},{10,... | collective-permute-start | bytes 1572872 | tf_op jit(solution)/shard_map/ppermute | solution.py:606
  35.8 11.2 %collective-permute-start.14 = (bf16[512,512]{1,0:T(8,128)(2,1)S(1)}, bf16[512,512]{1,0:T(8,128)(2,1)S(1)}, u32[]{:S(2)}, u32[]{:S(2)}) collective-permute-start(bf16[512,512]{1,0:T(8,128)(2,1)S(1)} %copy-done.4), channel_id=1, source_target_pairs={{0,1},{1,0},{2,3},{3,2},{4,5},{5,4},{6,7},{7,6},{8,9},{9,8},{10,11... | collective-permute-start | bytes 1572872 | tf_op jit(solution)/shard_map/ppermute | solution.py:606
  46.5 6.3 %collective-permute-start.17 = (bf16[2,512,512]{2,1,0:T(8,128)(2,1)S(1)}, bf16[2,512,512]{2,1,0:T(8,128)(2,1)S(1)}, u32[]{:S(2)}, u32[]{:S(2)}) collective-permute-start(bf16[2,512,512]{2,1,0:T(8,128)(2,1)S(1)} %get-tuple-element.189), channel_id=1, source_target_pairs={{0,1},{1,0},{2,3},{3,2},{4,5},{5,4},{6,7},{7,6},{8,9},{9,8},{10,11... | collective-permute-start | bytes 3145736 | tf_op jit(solution)/shard_map/ppermute | solution.py:606
  54.5 16.4 %collective-permute-start.19 = (bf16[512,512]{1,0:T(8,128)(2,1)S(1)}, bf16[512,512]{1,0:T(8,128)(2,1)S(1)}, u32[]{:S(2)}, u32[]{:S(2)}) collective-permute-start(bf16[512,512]{1,0:T(8,128)(2,1)S(1)} %get-tuple-element.206), channel_id=1, source_target_pairs={{0,2},{1,3},{2,0},{3,1},{4,6},{5,7},{6,4},{7,5},{8,10},{9,11},{10,... | collective-permute-start | bytes 1572872 | tf_op jit(solution)/shard_map/ppermute | solution.py:606
  57.7 14.5 %collective-permute-start.20 = (bf16[256,512]{1,0:T(8,128)(2,1)S(1)}, bf16[256,512]{1,0:T(8,128)(2,1)S(1)}, u32[]{:S(2)}, u32[]{:S(2)}) collective-permute-start(bf16[256,512]{1,0:T(8,128)(2,1)S(1)} %get-tuple-element.209), channel_id=1, source_target_pairs={{0,4},{4,0},{8,12},{12,8},{16,20},{20,16},{24,28},{28,24},{1,5},{5... | collective-permute-start | bytes 786440 | tf_op jit(solution)/shard_map/ppermute | solution.py:606
  58.6 13.6 %collective-permute-start.21 = (bf16[256,512]{1,0:T(8,128)(2,1)S(1)}, bf16[256,512]{1,0:T(8,128)(2,1)S(1)}, u32[]{:S(2)}, u32[]{:S(2)}) collective-permute-start(bf16[256,512]{1,0:T(8,128)(2,1)S(1)} %get-tuple-element.210), channel_id=1, source_target_pairs={{0,8},{4,12},{8,0},{12,4},{16,24},{20,28},{24,16},{28,20},{1,9},{5... | collective-permute-start | bytes 786440 | tf_op jit(solution)/shard_map/ppermute | solution.py:606
  60.2 12.8 %collective-permute-start.22 = (bf16[256,512]{1,0:T(8,128)(2,1)S(1)}, bf16[256,512]{1,0:T(8,128)(2,1)S(1)}, u32[]{:S(2)}, u32[]{:S(2)}) collective-permute-start(bf16[256,512]{1,0:T(8,128)(2,1)S(1)} %get-tuple-element.211), channel_id=1, source_target_pairs={{0,12},{4,8},{8,4},{12,0},{16,28},{20,24},{24,20},{28,16},{1,13},{... | collective-permute-start | bytes 786440 | tf_op jit(solution)/shard_map/ppermute | solution.py:606
  71.3 7.6 %collective-permute-start.23 = (bf16[512,256]{1,0:T(8,128)(2,1)S(1)}, bf16[512,256]{1,0:T(8,128)(2,1)S(1)}, u32[]{:S(2)}, u32[]{:S(2)}) collective-permute-start(bf16[512,256]{1,0:T(8,128)(2,1)S(1)} %get-tuple-element.217), channel_id=1, source_target_pairs={{0,4},{4,0},{8,12},{12,8},{16,20},{20,16},{24,28},{28,24},{1,5},{5... | collective-permute-start | bytes 786440 | tf_op jit(solution)/shard_map/ppermute | solution.py:606
  73.1 6.2 %collective-permute-start.24 = (bf16[128,512]{1,0:T(8,128)(2,1)S(1)}, bf16[128,512]{1,0:T(8,128)(2,1)S(1)}, u32[]{:S(2)}, u32[]{:S(2)}) collective-permute-start(bf16[128,512]{1,0:T(8,128)(2,1)S(1)} %get-tuple-element.220), channel_id=1, source_target_pairs={{0,2},{1,3},{2,0},{3,1},{4,6},{5,7},{6,4},{7,5},{8,10},{9,11},{10,... | collective-permute-start | bytes 393224 | tf_op jit(solution)/shard_map/ppermute | solution.py:606
  84.6 18.6 %collective-permute-start.29 = (bf16[144,2560]{1,0:T(8,128)(2,1)S(1)}, bf16[144,2560]{1,0:T(8,128)(2,1)S(1)}, u32[]{:S(2)}, u32[]{:S(2)}) collective-permute-start(bf16[144,2560]{1,0:T(8,128)(2,1)S(1)} %get-tuple-element.245), channel_id=1, source_target_pairs={{0,2},{1,3},{2,0},{3,1},{4,6},{5,7},{6,4},{7,5},{8,10},{9,11},{10,... | collective-permute-start | bytes 2211848 | tf_op jit(solution)/shard_map/ppermute | solution.py:606
  86.0 8.6 %collective-permute-start.26 = (bf16[512,128]{1,0:T(8,128)(2,1)S(1)}, bf16[512,128]{1,0:T(8,128)(2,1)S(1)}, u32[]{:S(2)}, u32[]{:S(2)}) collective-permute-start(bf16[512,128]{1,0:T(8,128)(2,1)S(1)} %get-tuple-element.234), channel_id=1, source_target_pairs={{0,8},{4,12},{8,0},{12,4},{16,24},{20,28},{24,16},{28,20},{1,9},{5... | collective-permute-start | bytes 393224 | tf_op jit(solution)/shard_map/ppermute | solution.py:606
  87.5 8.7 %collective-permute-start.27 = (bf16[128,512]{1,0:T(8,128)(2,1)S(1)}, bf16[128,512]{1,0:T(8,128)(2,1)S(1)}, u32[]{:S(2)}, u32[]{:S(2)}) collective-permute-start(bf16[128,512]{1,0:T(8,128)(2,1)S(1)} %get-tuple-element.236.refs_0_), channel_id=1, source_target_pairs={{0,16},{4,20},{8,24},{12,28},{16,0},{20,4},{24,8},{28,12},{1,17},{... | collective-permute-start | bytes 393224 | tf_op jit(solution)/shard_map/ppermute | solution.py:606
  94.6 8.5 %collective-permute-start.28 = (bf16[512,128]{1,0:T(8,128)(2,1)S(1)}, bf16[512,128]{1,0:T(8,128)(2,1)S(1)}, u32[]{:S(2)}, u32[]{:S(2)}) collective-permute-start(bf16[512,128]{1,0:T(8,128)(2,1)S(1)} %get-tuple-element.242.refs_0_), channel_id=1, source_target_pairs={{0,16},{4,20},{8,24},{12,28},{16,0},{20,4},{24,8},{28,12},{1,17},{... | collective-permute-start | bytes 393224 | tf_op jit(solution)/shard_map/ppermute | solution.py:606
  96.3 11.0 %collective-permute-start.30 = (bf16[128,512]{1,0:T(8,128)(2,1)S(1)}, bf16[128,512]{1,0:T(8,128)(2,1)S(1)}, u32[]{:S(2)}, u32[]{:S(2)}) collective-permute-start(bf16[128,512]{1,0:T(8,128)(2,1)S(1)} %get-tuple-element.247.refs_0_), channel_id=1, source_target_pairs={{0,8},{4,12},{8,0},{12,4},{16,24},{20,28},{24,16},{28,20},{1,9},{5... | collective-permute-start | bytes 393224 | tf_op jit(solution)/shard_map/ppermute | solution.py:606
  103.7 8.6 %collective-permute-start.31 = (bf16[144,640]{1,0:T(8,128)(2,1)S(1)}, bf16[144,640]{1,0:T(8,128)(2,1)S(1)}, u32[]{:S(2)}, u32[]{:S(2)}) collective-permute-start(bf16[144,640]{1,0:T(8,128)(2,1)S(1)} %get-tuple-element.250), channel_id=1, source_target_pairs={{0,4},{4,0},{8,12},{12,8},{16,20},{20,16},{24,28},{28,24},{1,5},{5... | collective-permute-start | bytes 552968 | tf_op jit(solution)/shard_map/ppermute | solution.py:606
  105.0 7.6 %collective-permute-start.32 = (bf16[144,640]{1,0:T(8,128)(2,1)S(1)}, bf16[144,640]{1,0:T(8,128)(2,1)S(1)}, u32[]{:S(2)}, u32[]{:S(2)}) collective-permute-start(bf16[144,640]{1,0:T(8,128)(2,1)S(1)} %get-tuple-element.251), channel_id=1, source_target_pairs={{0,8},{4,12},{8,0},{12,4},{16,24},{20,28},{24,16},{28,20},{1,9},{5... | collective-permute-start | bytes 552968 | tf_op jit(solution)/shard_map/ppermute | solution.py:606
  106.6 10.0 %collective-permute-start.33 = (bf16[144,640]{1,0:T(8,128)(2,1)S(1)}, bf16[144,640]{1,0:T(8,128)(2,1)S(1)}, u32[]{:S(2)}, u32[]{:S(2)}) collective-permute-start(bf16[144,640]{1,0:T(8,128)(2,1)S(1)} %get-tuple-element.252), channel_id=1, source_target_pairs={{0,12},{4,8},{8,4},{12,0},{16,28},{20,24},{24,20},{28,16},{1,13},{... | collective-permute-start | bytes 552968 | tf_op jit(solution)/shard_map/ppermute | solution.py:606
  107.5 13.7 %collective-permute-start.35 = (bf16[128,1024]{1,0:T(8,128)(2,1)S(1)}, bf16[128,1024]{1,0:T(8,128)(2,1)S(1)}, u32[]{:S(2)}, u32[]{:S(2)}) collective-permute-start(bf16[128,1024]{1,0:T(8,128)(2,1)S(1)} %get-tuple-element.256.refs_0_), channel_id=1, source_target_pairs={{0,4},{4,0},{8,12},{12,8},{16,20},{20,16},{24,28},{28,24},{1,5},{5... | collective-permute-start | bytes 786440 | tf_op jit(solution)/shard_map/ppermute | solution.py:606
  108.8 10.2 %collective-permute-start.34 = (bf16[512,128]{1,0:T(8,128)(2,1)S(1)}, bf16[512,128]{1,0:T(8,128)(2,1)S(1)}, u32[]{:S(2)}, u32[]{:S(2)}) collective-permute-start(bf16[512,128]{1,0:T(8,128)(2,1)S(1)} %get-tuple-element.254.refs_0_), channel_id=1, source_target_pairs={{0,8},{4,12},{8,0},{12,4},{16,24},{20,28},{24,16},{28,20},{1,9},{5... | collective-permute-start | bytes 393224 | tf_op jit(solution)/shard_map/ppermute | solution.py:606
  116.8 8.6 %collective-permute-start.36 = (bf16[144,640]{1,0:T(8,128)(2,1)S(1)}, bf16[144,640]{1,0:T(8,128)(2,1)S(1)}, u32[]{:S(2)}, u32[]{:S(2)}) collective-permute-start(bf16[144,640]{1,0:T(8,128)(2,1)S(1)} %get-tuple-element.258.refs_0_), channel_id=1, source_target_pairs={{0,16},{4,20},{8,24},{12,28},{16,0},{20,4},{24,8},{28,12},{1,17},{... | collective-permute-start | bytes 552968 | tf_op jit(solution)/shard_map/ppermute | solution.py:606
  119.4 9.6 %collective-permute-start.37 = (bf16[512,256]{1,0:T(8,128)(2,1)S(1)}, bf16[512,256]{1,0:T(8,128)(2,1)S(1)}, u32[]{:S(2)}, u32[]{:S(2)}) collective-permute-start(bf16[512,256]{1,0:T(8,128)(2,1)S(1)} %get-tuple-element.260.refs_0_), channel_id=1, source_target_pairs={{0,4},{4,0},{8,12},{12,8},{16,20},{20,16},{24,28},{28,24},{1,5},{5... | collective-permute-start | bytes 786440 | tf_op jit(solution)/shard_map/ppermute | solution.py:606
  125.5 6.5 %collective-permute-start.40 = (bf16[144,640]{1,0:T(8,128)(2,1)S(1)}, bf16[144,640]{1,0:T(8,128)(2,1)S(1)}, u32[]{:S(2)}, u32[]{:S(2)}) collective-permute-start(bf16[144,640]{1,0:T(8,128)(2,1)S(1)} %get-tuple-element.264.refs_0_), channel_id=1, source_target_pairs={{0,12},{4,8},{8,4},{12,0},{16,28},{20,24},{24,20},{28,16},{1,13},{... | collective-permute-start | bytes 552968 | tf_op jit(solution)/shard_map/ppermute | solution.py:606
  126.5 7.0 %collective-permute-start.39 = (bf16[144,640]{1,0:T(8,128)(2,1)S(1)}, bf16[144,640]{1,0:T(8,128)(2,1)S(1)}, u32[]{:S(2)}, u32[]{:S(2)}) collective-permute-start(bf16[144,640]{1,0:T(8,128)(2,1)S(1)} %get-tuple-element.264.refs_0_), channel_id=1, source_target_pairs={{0,8},{4,12},{8,0},{12,4},{16,24},{20,28},{24,16},{28,20},{1,9},{5... | collective-permute-start | bytes 552968 | tf_op jit(solution)/shard_map/ppermute | solution.py:606
  128.0 5.9 %collective-permute-start.38 = (bf16[144,640]{1,0:T(8,128)(2,1)S(1)}, bf16[144,640]{1,0:T(8,128)(2,1)S(1)}, u32[]{:S(2)}, u32[]{:S(2)}) collective-permute-start(bf16[144,640]{1,0:T(8,128)(2,1)S(1)} %get-tuple-element.264.refs_0_), channel_id=1, source_target_pairs={{0,4},{4,0},{8,12},{12,8},{16,20},{20,16},{24,28},{28,24},{1,5},{5... | collective-permute-start | bytes 552968 | tf_op jit(solution)/shard_map/ppermute | solution.py:606
  (15 other events, 97.5 us)

commit v7 on v6

--- a/solution.py
+++ b/solution.py
@@ -500,9 +500,9 @@
 
 def inner_back_kernel(which, more, token, dy, slope, *refs):
     cols = wide(blocks_of(token), 512)
-    wu, (din, sums) = refs[:2], refs[-2:]
+    wu, (din, sums) = refs[: len(which)], refs[-2:]
     if more:
-        sums[...] = refs[2][...]
+        sums[...] = refs[len(which)][...]
     else:
         sums[...] = jnp.zeros_like(sums)
         sums[1:2, 0:512] = jnp.sum(dy[...].astype(F32), axis=0, keepdims=True)
@@ -805,7 +805,7 @@
 
 
 PLAN = (
-    "OG", "IA", "WU", "IB", "u", "IS", "IK", "i", "RB", "AE", "u", "i", "AL", "u", "i", "PS", "PK", "p",
+    "OG", "IA", "WU", "IB", "u", "IC", "IS", "IK", "i", "RB", "AE", "u", "i", "AL", "u", "i", "PS", "PK", "p",
     "IN", "u", "i", "FO", "u", "p", "i", "p", "u", "i", "p", "u",
 )
 STEPS = {
@@ -857,7 +857,11 @@
 
     def back_far():
         d, partial = made["din"]
-        made["din"] = inner_back(clock, cotangent, d, [made["wu"][1], made["wu"][3]], (1, 3), [partial])
+        made["din"] = inner_back(clock, cotangent, d, [made["wu"][1]], (1,), [partial])
+
+    def back_last():
+        d, partial = made["din"]
+        made["din"] = inner_back(clock, cotangent, d, [made["wu"][3]], (3,), [partial])
 
     def inner_send():
         start("i", [inner_grad(clock, n2, made["din"][0], 2)], None)
@@ -910,7 +914,7 @@
                 finish(name)
 
     made["wu"] = wu_x
-    kernels = dict(OG=outer, WU=wait_outer, IA=back_near, IB=back_far, IS=inner_send, IK=inner_keep, RB=resid_grad, AE=early, AL=late, PS=project_send, PK=project_keep, IN=input_part, FO=output_part)
+    kernels = dict(OG=outer, WU=wait_outer, IA=back_near, IB=back_far, IC=back_last, IS=inner_send, IK=inner_keep, RB=resid_grad, AE=early, AL=late, PS=project_send, PK=project_keep, IN=input_part, FO=output_part)
     for word in PLAN:
         if word in kernels:
             kernels[word]()

time: 138 us -> 137 us (level)
    pallas_call x39 -> x40, Pallas kernels: 63.7 us -> 64 us  [call(): pl.pallas_call(body, in_specs=[VM] + [ANY if k in raw else VM for k in ra...]
where the time goes in v7:
time: 137 us
  Pallas kernels  64 us (47%)
  starting transfers between devices  39.6 us (29%)
  waiting for transfers between devices  30.2 us (22%)
    pallas_call x40, Pallas kernels, call(): pl.pallas_call(body, in_specs=[VM] + [ANY if k in raw else VM for k in ra...  64 us
    ppermute x41, starting transfers between devices, exchange(): return lax.ppermute(value, axis, [(i, i ^ mask) for i in range(size)])  39.6 us
    ppermute x41, waiting for transfers between devices, exchange(): return lax.ppermute(value, axis, [(i, i ^ mask) for i in range(size)])  30.2 us
  transfers between devices with their start and end apart: 41, of which 20 were waited for; matrix products, arithmetic and copies ran while one was open for 0% of the time, Pallas kernels for 40%

profile of v7, /device:TPU:0, one launch (start us, length us, event | category | flops | bytes accessed | tf_op | source)
XLA Modules:
  0.0 136.5 jit_solution(9243468526260557996)
XLA Ops:
  0.8 1.7 %begin.1 = (bf16[144,2048]{1,0:T(8,128)(2,1)S(1)}, bf16[144,512]{1,0:T(8,128)(2,1)S(1)}, bf16[144,512]{1,0:T(8,128)(2,1)S(1)}, bf16[64,2048]{1,0:T(8,128)(2,1)S(...) custom-call(s32[8,128]{1,0:T(8,128)S(1)} %iota.7.token, bf16[128,512]{1,0:T(8,128)(2,1)} %refs_0_.8, ...), custom_call_target="tpu_custom_call" | custom-call | flops 1000 | bytes 1024 | tf_op jit(solution)/shard_map/begin/pallas_call | solution.py:64
  2.5 3.0 %collective-permute-start = (bf16[144,512]{1,0:T(8,128)(2,1)S(1)}, bf16[144,512]{1,0:T(8,128)(2,1)S(1)}, u32[]{:S(2)}, u32[]{:S(2)}) collective-permute-start(bf16[144,512]{1,0:T(8,128)(2,1)S(1)} %get-tuple-element.153), channel_id=1, source_target_pairs={{0,2},{1,3},{2,0},{3,1},{4,6},{5,7},{6,4},{7,5},{8,10},{9,11},{10,... | collective-permute-start | bytes 442376 | tf_op jit(solution)/shard_map/ppermute | solution.py:606
  8.0 2.2 %collective-permute-done.refs_0_ = bf16[144,512]{1,0:T(8,128)(2,1)S(1)} collective-permute-done((bf16[144,512]{1,0:T(8,128)(2,1)S(1)}, bf16[144,512]{1,0:T(8,128)(2,1)S(1)}, u32[]{:S(2)}, u32[]{:S(2)}) %collective-permute-start) | collective-permute-done | bytes 147488 | tf_op jit(solution)/shard_map/ppermute | solution.py:606
  10.2 2.3 %collective-permute-done.1.refs_1_ = bf16[144,512]{1,0:T(8,128)(2,1)S(1)} collective-permute-done((bf16[144,512]{1,0:T(8,128)(2,1)S(1)}, bf16[144,512]{1,0:T(8,128)(2,1)S(1)}, u32[]{:S(2)}, u32[]{:S(2)}) %collective-permute-start.1) | collective-permute-done | bytes 147488 | tf_op jit(solution)/shard_map/ppermute | solution.py:606
  12.5 1.7 %collective-permute-start.4 = (bf16[64,2048]{1,0:T(8,128)(2,1)S(1)}, bf16[64,2048]{1,0:T(8,128)(2,1)S(1)}, u32[]{:S(2)}, u32[]{:S(2)}) collective-permute-start(bf16[64,2048]{1,0:T(8,128)(2,1)S(1)} %get-tuple-element.160), channel_id=1, source_target_pairs={{0,2},{1,3},{2,0},{3,1},{4,6},{5,7},{6,4},{7,5},{8,10},{9,11},{10,... | collective-permute-start | bytes 786440 | tf_op jit(solution)/shard_map/ppermute | solution.py:606
  15.8 1.6 %collective-permute-start.3 = (bf16[144,512]{1,0:T(8,128)(2,1)S(1)}, bf16[144,512]{1,0:T(8,128)(2,1)S(1)}, u32[]{:S(2)}, u32[]{:S(2)}) collective-permute-start(bf16[144,512]{1,0:T(8,128)(2,1)S(1)} %collective-permute-done.1.refs_1_), channel_id=1, source_target_pairs={{0,8},{4,12},{8,0},{12,4},{16,24},{20,28},{24,16},{28,20},{1,9},{5... | collective-permute-start | bytes 442376 | tf_op jit(solution)/shard_map/ppermute | solution.py:606
  17.3 2.0 %collective-permute-done.2.refs_2_ = bf16[144,512]{1,0:T(8,128)(2,1)S(1)} collective-permute-done((bf16[144,512]{1,0:T(8,128)(2,1)S(1)}, bf16[144,512]{1,0:T(8,128)(2,1)S(1)}, u32[]{:S(2)}, u32[]{:S(2)}) %collective-permute-start.2) | collective-permute-done | bytes 147488 | tf_op jit(solution)/shard_map/ppermute | solution.py:606
  23.6 2.4 %project.1 = (bf16[1024,2048]{1,0:T(8,128)(2,1)S(1)}, s32[8,128]{1,0:T(8,128)S(1)}) custom-call(s32[8,128]{1,0:T(8,128)S(1)} %get-tuple-element.164.token, f32[1024,512]{1,0:T(8,128)S(1)} %get-tuple-element.165.refs_0_, bf16[144,2048]{1,0:T(8,128)(2,1)S(1)} %get-tuple-element.166.refs_1_.refs_6_.refs_7_.refs_14_.refs_4_.refs_3_, ...), custom_call_target="tpu_custom_call" | custom-call | flops 1000 | bytes 1024 | tf_op jit(solution)/shard_map/project/pallas_call | solution.py:64
  25.9 7.4 %attention_forward.1 = (bf16[1024,512]{1,0:T(8,128)(2,1)S(1)}, bf16[1024,3072]{1,0:T(8,128)(2,1)S(1)}, bf16[8,128,1024]{2,1,0:T(8,128)(2,1)S(1)}, f32[8,8,512]{2,1,0:T(8,128)S(1)}, s32[8,128]{1,0:T(8,128)S(1)}) custom-call(s32[8,128]{1,0:T(8,128)S(1)} %get-tuple-element.169.token, bf16[1024,2048]{1,0:T(8,128)(2,1)S(1)} %get-tuple-element.170.refs_0_), custom_call_target="tpu_custom_call" | custom-call | flops 1000 | bytes 1024 | tf_op jit(solution)/shard_map/attention_forward/pallas_call | solution.py:64
  35.8 2.0 %middle.1 = (f32[1024,512]{1,0:T(8,128)S(1)}, bf16[1024,512]{1,0:T(8,128)(2,1)S(1)}, f32[1024,128]{1,0:T(8,128)S(1)}, bf16[1024,512]{1,0:T(8,128)(2,1)S(1)}, s32[8,128]{1,0:T(8,128)S(1)}) custom-call(s32[8,128]{1,0:T(8,128)S(1)} %get-tuple-element.174.token, bf16[1024,512]{1,0:T(8,128)(2,1)S(1)} %copy-done.2, ...), custom_call_target="tpu_custom_call" | custom-call | flops 1000 | bytes 1024 | tf_op jit(solution)/shard_map/middle/pallas_call | solution.py:64
  37.9 6.2 %ffn_inner.1 = (bf16[1024,2048]{1,0:T(8,128)(2,1)S(1)}, bf16[1024,2048]{1,0:T(8,128)(2,1)S(1)}, s32[8,128]{1,0:T(8,128)S(1)}) custom-call(s32[8,128]{1,0:T(8,128)S(1)} %get-tuple-element.177.token, bf16[1024,512]{1,0:T(8,128)(2,1)S(1)} %get-tuple-element.178.refs_0_, bf16[128,2048]{1,0:T(8,128)(2,1)S(1)} %copy-done.3, ...), custom_call_target="tpu_custom_call" | custom-call | flops 1000 | bytes 1024 | tf_op jit(solution)/shard_map/ffn_inner/pallas_call | solution.py:64
  44.1 2.4 %outer_grad.1 = (bf16[2,512,512]{2,1,0:T(8,128)(2,1)S(1)}, bf16[2,512,512]{2,1,0:T(8,128)(2,1)S(1)}, s32[8,128]{1,0:T(8,128)S(1)}) custom-call(s32[8,128]{1,0:T(8,128)S(1)} %get-tuple-element.180.token, bf16[1024,2048]{1,0:T(8,128)(2,1)S(1)} %get-tuple-element.181.refs_0_.refs_1_, bf16[1024,512]{1,0:T(8,128)(2,1)S(1)} %copy-done), custom_call_target="tpu_custom_call" | custom-call | flops 1000 | bytes 1024 | tf_op jit(solution)/shard_map/outer_grad/pallas_call | solution.py:64
  47.0 1.6 %inner_back.3 = (bf16[1024,2048]{1,0:T(8,128)(2,1)S(1)}, f32[8,2048]{1,0:T(8,128)S(1)}, s32[8,128]{1,0:T(8,128)S(1)}) custom-call(s32[8,128]{1,0:T(8,128)S(1)} %get-tuple-element.182.token, bf16[1024,512]{1,0:T(8,128)(2,1)S(1)} %copy-done, bf16[1024,2048]{1,0:T(8,128)(2,1)S(1)} %get-tuple-element.183.refs_1_, ...), custom_call_target="tpu_custom_call", output_to_operand_aliasing={{0}: (2, {})} | custom-call | flops 1000 | bytes 1024 | tf_op jit(solution)/shard_map/inner_back/pallas_call | solution.py:64
  57.7 1.6 %collective-permute-start.21 = (bf16[256,512]{1,0:T(8,128)(2,1)S(1)}, bf16[256,512]{1,0:T(8,128)(2,1)S(1)}, u32[]{:S(2)}, u32[]{:S(2)}) collective-permute-start(bf16[256,512]{1,0:T(8,128)(2,1)S(1)} %get-tuple-element.216), channel_id=1, source_target_pairs={{0,8},{4,12},{8,0},{12,4},{16,24},{20,28},{24,16},{28,20},{1,9},{5... | collective-permute-start | bytes 786440 | tf_op jit(solution)/shard_map/ppermute | solution.py:606
  60.4 4.4 %resid_back.1 = (f32[1024,512]{1,0:T(8,128)S(1)}, bf16[1024,512]{1,0:T(8,128)(2,1)S(1)}, s32[8,128]{1,0:T(8,128)S(1)}) custom-call(s32[8,128]{1,0:T(8,128)S(1)} %get-tuple-element.203.token, bf16[1024,512]{1,0:T(8,128)(2,1)S(1)} %copy-done, bf16[1024,512]{1,0:T(8,128)(2,1)S(1)} %get-tuple-element.197.refs_0_.refs_1_, ...), custom_call_target="tpu_custom_call" | custom-call | flops 1000 | bytes 1024 | tf_op jit(solution)/shard_map/resid_back/pallas_call | solution.py:64
  64.9 5.3 %attention_backward.2 = (bf16[512,2048]{1,0:T(8,128)(2,1)S(1)}, f32[4,128,256]{2,1,0:T(8,128)S(1)}, f32[8,512]{1,0:T(8,128)S(1)}, s32[8,128]{1,0:T(8,128)S(1)}) custom-call(s32[8,128]{1,0:T(8,128)S(1)} %get-tuple-element.205.token, bf16[1024,2048]{1,0:T(8,128)(2,1)S(1)} %get-tuple-element.170.refs_0_, bf16[1024,3072]{1,0:T(8,128)(2,1)S(1)} %get-tuple-element.206.refs_1_, ...), custom_call_target="tpu_custom_call" | custom-call | flops 1000 | bytes 1024 | tf_op jit(solution)/shard_map/attention_backward/pallas_call | solution.py:64
  73.1 5.1 %attention_backward.3 = (bf16[512,2048]{1,0:T(8,128)(2,1)S(1)}, s32[8,128]{1,0:T(8,128)S(1)}) custom-call(s32[8,128]{1,0:T(8,128)S(1)} %get-tuple-element.218.token, bf16[1024,2048]{1,0:T(8,128)(2,1)S(1)} %get-tuple-element.170.refs_0_, bf16[1024,3072]{1,0:T(8,128)(2,1)S(1)} %get-tuple-element.206.refs_1_, ...), custom_call_target="tpu_custom_call" | custom-call | flops 1000 | bytes 1024 | tf_op jit(solution)/shard_map/attention_backward/pallas_call | solution.py:64
  78.5 1.6 %project_grad.2 = (bf16[2,144,2560]{2,1,0:T(8,128)(2,1)S(1)}, s32[8,128]{1,0:T(8,128)S(1)}) custom-call(s32[8,128]{1,0:T(8,128)S(1)} %get-tuple-element.227.token, bf16[1024,512]{1,0:T(8,128)(2,1)S(1)} %get-tuple-element.228.refs_0_, bf16[512,2048]{1,0:T(8,128)(2,1)S(1)} %get-tuple-element.229.refs_1_, bf16[512,2048]{1,0:T(8,128)(2,1)S(1)} %get-tuple-element.230.refs_2_, ...), custom_call_target="tpu_custom_call" | custom-call | flops 1000 | bytes 1024 | tf_op jit(solution)/shard_map/project_grad/pallas_call | solution.py:64
  80.2 1.6 %project_grad.3 = (bf16[2,144,2560]{2,1,0:T(8,128)(2,1)S(1)}, s32[8,128]{1,0:T(8,128)S(1)}) custom-call(s32[8,128]{1,0:T(8,128)S(1)} %get-tuple-element.233.token, bf16[1024,512]{1,0:T(8,128)(2,1)S(1)} %get-tuple-element.228.refs_0_, bf16[512,2048]{1,0:T(8,128)(2,1)S(1)} %get-tuple-element.229.refs_1_, bf16[512,2048]{1,0:T(8,128)(2,1)S(1)} %get-tuple-element.230.refs_2_, ...), custom_call_target="tpu_custom_call" | custom-call | flops 1000 | bytes 1024 | tf_op jit(solution)/shard_map/project_grad/pallas_call | solution.py:64
  81.8 1.6 %collective-permute-done.25.refs_1_ = bf16[2,144,2560]{2,1,0:T(8,128)(2,1)S(1)} collective-permute-done((bf16[2,144,2560]{2,1,0:T(8,128)(2,1)S(1)}, bf16[2,144,2560]{2,1,0:T(8,128)(2,1)S(1)}, u32[]{:S(2)}, u32[]{:S(2)}) %collective-permute-start.25) | collective-permute-done | bytes 1474592 | tf_op jit(solution)/shard_map/ppermute | solution.py:606
  86.7 2.6 %collective-permute-start.27 = (bf16[128,512]{1,0:T(8,128)(2,1)S(1)}, bf16[128,512]{1,0:T(8,128)(2,1)S(1)}, u32[]{:S(2)}, u32[]{:S(2)}) collective-permute-start(bf16[128,512]{1,0:T(8,128)(2,1)S(1)} %get-tuple-element.242.refs_0_), channel_id=1, source_target_pairs={{0,16},{4,20},{8,24},{12,28},{16,0},{20,4},{24,8},{28,12},{1,17},{... | collective-permute-start | bytes 393224 | tf_op jit(solution)/shard_map/ppermute | solution.py:606
  89.3 4.4 %input_grad.1 = (bf16[1024,512]{1,0:T(8,128)(2,1)}, s32[8,128]{1,0:T(8,128)S(1)}) custom-call(s32[8,128]{1,0:T(8,128)S(1)} %get-tuple-element.237.token, bf16[1024,512]{1,0:T(8,128)(2,1)S(1)} %copy-done.2, bf16[512,2048]{1,0:T(8,128)(2,1)S(1)} %get-tuple-element.229.refs_1_, bf16[512,2048]{1,0:T(8,128)(2,1)S(1)} %get-tuple-element.230.refs_2_, ...), custom_call_target="tpu_custom_call" | custom-call | flops 1000 | bytes 1024 | tf_op jit(solution)/shard_map/input_grad/pallas_call | solution.py:64
  96.3 3.9 %ffn_outer.1 = (bf16[1024,512]{1,0:T(8,128)(2,1)}, s32[8,128]{1,0:T(8,128)S(1)}) custom-call(s32[8,128]{1,0:T(8,128)S(1)} %get-tuple-element.243.token, f32[1024,512]{1,0:T(8,128)S(1)} %get-tuple-element.244.refs_0_, bf16[1024,2048]{1,0:T(8,128)(2,1)S(1)} %get-tuple-element.181.refs_0_.refs_1_, bf16[512,512]{1,0:T(8,128)(2,1)S(1)} %copy-done.4, ...), custom_call_target="tpu_custom_call" | custom-call | flops 1000 | bytes 1024 | tf_op jit(solution)/shard_map/ffn_outer/pallas_call | solution.py:64
  100.3 2.0 %collective-permute-done.28.refs_1_ = bf16[512,128]{1,0:T(8,128)(2,1)S(1)} collective-permute-done((bf16[512,128]{1,0:T(8,128)(2,1)S(1)}, bf16[512,128]{1,0:T(8,128)(2,1)S(1)}, u32[]{:S(2)}, u32[]{:S(2)}) %collective-permute-start.28) | collective-permute-done | bytes 131104 | tf_op jit(solution)/shard_map/ppermute | solution.py:606
  104.2 1.6 %collective-permute-start.32 = (bf16[144,640]{1,0:T(8,128)(2,1)S(1)}, bf16[144,640]{1,0:T(8,128)(2,1)S(1)}, u32[]{:S(2)}, u32[]{:S(2)}) collective-permute-start(bf16[144,640]{1,0:T(8,128)(2,1)S(1)} %get-tuple-element.257), channel_id=1, source_target_pairs={{0,8},{4,12},{8,0},{12,4},{16,24},{20,28},{24,16},{28,20},{1,9},{5... | collective-permute-start | bytes 552968 | tf_op jit(solution)/shard_map/ppermute | solution.py:606
  109.6 1.9 %collective-permute-done.31.refs_1_ = bf16[144,640]{1,0:T(8,128)(2,1)S(1)} collective-permute-done((bf16[144,640]{1,0:T(8,128)(2,1)S(1)}, bf16[144,640]{1,0:T(8,128)(2,1)S(1)}, u32[]{:S(2)}, u32[]{:S(2)}) %collective-permute-start.31) | collective-permute-done | bytes 184352 | tf_op jit(solution)/shard_map/ppermute | solution.py:606
  111.8 4.0 %collective-permute-done.33.refs_3_ = bf16[144,640]{1,0:T(8,128)(2,1)S(1)} collective-permute-done((bf16[144,640]{1,0:T(8,128)(2,1)S(1)}, bf16[144,640]{1,0:T(8,128)(2,1)S(1)}, u32[]{:S(2)}, u32[]{:S(2)}) %collective-permute-start.33) | collective-permute-done | bytes 184352 | tf_op jit(solution)/shard_map/ppermute | solution.py:606
  115.9 2.3 %collective-permute-start.36 = (bf16[144,640]{1,0:T(8,128)(2,1)S(1)}, bf16[144,640]{1,0:T(8,128)(2,1)S(1)}, u32[]{:S(2)}, u32[]{:S(2)}) collective-permute-start(bf16[144,640]{1,0:T(8,128)(2,1)S(1)} %get-tuple-element.264.refs_0_), channel_id=1, source_target_pairs={{0,16},{4,20},{8,24},{12,28},{16,0},{20,4},{24,8},{28,12},{1,17},{... | collective-permute-start | bytes 552968 | tf_op jit(solution)/shard_map/ppermute | solution.py:606
  118.6 1.8 %collective-permute-start.37 = (bf16[512,256]{1,0:T(8,128)(2,1)S(1)}, bf16[512,256]{1,0:T(8,128)(2,1)S(1)}, u32[]{:S(2)}, u32[]{:S(2)}) collective-permute-start(bf16[512,256]{1,0:T(8,128)(2,1)S(1)} %get-tuple-element.266.refs_0_), channel_id=1, source_target_pairs={{0,4},{4,0},{8,12},{12,8},{16,20},{20,16},{24,28},{28,24},{1,5},{5... | collective-permute-start | bytes 786440 | tf_op jit(solution)/shard_map/ppermute | solution.py:606
  120.7 3.9 %collective-permute-done.36.refs_1_ = bf16[144,640]{1,0:T(8,128)(2,1)S(1)} collective-permute-done((bf16[144,640]{1,0:T(8,128)(2,1)S(1)}, bf16[144,640]{1,0:T(8,128)(2,1)S(1)}, u32[]{:S(2)}, u32[]{:S(2)}) %collective-permute-start.36) | collective-permute-done | bytes 184352 | tf_op jit(solution)/shard_map/ppermute | solution.py:606
  129.6 1.6 %collective-permute-done.40.refs_3_ = bf16[144,640]{1,0:T(8,128)(2,1)S(1)} collective-permute-done((bf16[144,640]{1,0:T(8,128)(2,1)S(1)}, bf16[144,640]{1,0:T(8,128)(2,1)S(1)}, u32[]{:S(2)}, u32[]{:S(2)}) %collective-permute-start.40) | collective-permute-done | bytes 184352 | tf_op jit(solution)/shard_map/ppermute | solution.py:606
  133.4 2.9 %finish_all.1 = (f32[128,512]{1,0:T(8,128)}, f32[128,512]{1,0:T(8,128)}, f32[128,512]{1,0:T(8,128)}, f32[128,512]{1,0:T(8,128)}, f32[128,512]{1,0:T(8,128)}, /*i...) custom-call(s32[8,128]{1,0:T(8,128)S(1)} %get-tuple-element.271.toke, ...), custom_call_target="tpu_custom_call" | custom-call | flops 1000 | bytes 1024 | tf_op jit(solution)/shard_map/finish_all/pallas_call | solution.py:64
  (104 shorter events, 44.6 us)
Async XLA Ops:
  2.5 7.7 %collective-permute-start = (bf16[144,512]{1,0:T(8,128)(2,1)S(1)}, bf16[144,512]{1,0:T(8,128)(2,1)S(1)}, u32[]{:S(2)}, u32[]{:S(2)}) collective-permute-start(bf16[144,512]{1,0:T(8,128)(2,1)S(1)} %get-tuple-element.153), channel_id=1, source_target_pairs={{0,2},{1,3},{2,0},{3,1},{4,6},{5,7},{6,4},{7,5},{8,10},{9,11},{10,... | collective-permute-start | bytes 442376 | tf_op jit(solution)/shard_map/ppermute | solution.py:606
  5.5 7.0 %collective-permute-start.1 = (bf16[144,512]{1,0:T(8,128)(2,1)S(1)}, bf16[144,512]{1,0:T(8,128)(2,1)S(1)}, u32[]{:S(2)}, u32[]{:S(2)}) collective-permute-start(bf16[144,512]{1,0:T(8,128)(2,1)S(1)} %get-tuple-element.154), channel_id=1, source_target_pairs={{0,2},{1,3},{2,0},{3,1},{4,6},{5,7},{6,4},{7,5},{8,10},{9,11},{10,... | collective-permute-start | bytes 442376 | tf_op jit(solution)/shard_map/ppermute | solution.py:606
  12.5 8.4 %collective-permute-start.4 = (bf16[64,2048]{1,0:T(8,128)(2,1)S(1)}, bf16[64,2048]{1,0:T(8,128)(2,1)S(1)}, u32[]{:S(2)}, u32[]{:S(2)}) collective-permute-start(bf16[64,2048]{1,0:T(8,128)(2,1)S(1)} %get-tuple-element.160), channel_id=1, source_target_pairs={{0,2},{1,3},{2,0},{3,1},{4,6},{5,7},{6,4},{7,5},{8,10},{9,11},{10,... | collective-permute-start | bytes 786440 | tf_op jit(solution)/shard_map/ppermute | solution.py:606
  14.2 5.1 %collective-permute-start.2 = (bf16[144,512]{1,0:T(8,128)(2,1)S(1)}, bf16[144,512]{1,0:T(8,128)(2,1)S(1)}, u32[]{:S(2)}, u32[]{:S(2)}) collective-permute-start(bf16[144,512]{1,0:T(8,128)(2,1)S(1)} %collective-permute-done.refs_0_), channel_id=1, source_target_pairs={{0,4},{4,0},{8,12},{12,8},{16,20},{20,16},{24,28},{28,24},{1,5},{5... | collective-permute-start | bytes 442376 | tf_op jit(solution)/shard_map/ppermute | solution.py:606
  17.3 6.2 %collective-permute-start.5 = (bf16[144,2048]{1,0:T(8,128)(2,1)S(1)}, bf16[144,2048]{1,0:T(8,128)(2,1)S(1)}, u32[]{:S(2)}, u32[]{:S(2)}) collective-permute-start(bf16[144,2048]{1,0:T(8,128)(2,1)S(1)} %get-tuple-element.166.refs_1_.refs_6_.refs_7_.refs_14_.refs_4_.refs_3_), channel_id=1, source_target_pairs={{0,1},{1,0},{2,3},{3,2},{4,5},{5,4},{6,7},{7,6},{8,9},{9,8},{10,11... | collective-permute-start | bytes 1769480 | tf_op jit(solution)/shard_map/ppermute | solution.py:606
  21.2 12.1 %collective-permute-start.8 = (bf16[64,2048]{1,0:T(8,128)(2,1)S(1)}, bf16[64,2048]{1,0:T(8,128)(2,1)S(1)}, u32[]{:S(2)}, u32[]{:S(2)}) collective-permute-start(bf16[64,2048]{1,0:T(8,128)(2,1)S(1)} %get-tuple-element.173), channel_id=1, source_target_pairs={{0,2},{1,3},{2,0},{3,1},{4,6},{5,7},{6,4},{7,5},{8,10},{9,11},{10,... | collective-permute-start | bytes 786440 | tf_op jit(solution)/shard_map/ppermute | solution.py:606
  21.8 16.1 %collective-permute-start.11 = (bf16[128,2048]{1,0:T(8,128)(2,1)S(1)}, bf16[128,2048]{1,0:T(8,128)(2,1)S(1)}, u32[]{:S(2)}, u32[]{:S(2)}) collective-permute-start(bf16[128,2048]{1,0:T(8,128)(2,1)S(1)} %copy-done.3), channel_id=1, source_target_pairs={{0,1},{1,0},{2,3},{3,2},{4,5},{5,4},{6,7},{7,6},{8,9},{9,8},{10,11... | collective-permute-start | bytes 1572872 | tf_op jit(solution)/shard_map/ppermute | solution.py:606
  22.0 11.3 %collective-permute-start.7 = (bf16[128,512]{1,0:T(8,128)(2,1)S(1)}, bf16[128,512]{1,0:T(8,128)(2,1)S(1)}, u32[]{:S(2)}, u32[]{:S(2)}) collective-permute-start(bf16[128,512]{1,0:T(8,128)(2,1)S(1)} %copy-done.5), channel_id=1, source_target_pairs={{0,2},{1,3},{2,0},{3,1},{4,6},{5,7},{6,4},{7,5},{8,10},{9,11},{10,... | collective-permute-start | bytes 393224 | tf_op jit(solution)/shard_map/ppermute | solution.py:606
  23.5 14.4 %collective-permute-start.12 = (bf16[64,2048]{1,0:T(8,128)(2,1)S(1)}, bf16[64,2048]{1,0:T(8,128)(2,1)S(1)}, u32[]{:S(2)}, u32[]{:S(2)}) collective-permute-start(bf16[64,2048]{1,0:T(8,128)(2,1)S(1)} %collective-permute-done.4.refs_4_.refs_2_.refs_9_), channel_id=1, source_target_pairs={{0,1},{1,0},{2,3},{3,2},{4,5},{5,4},{6,7},{7,6},{8,9},{9,8},{10,11... | collective-permute-start | bytes 786440 | tf_op jit(solution)/shard_map/ppermute | solution.py:606
  35.2 14.2 %collective-permute-start.15 = (bf16[512,512]{1,0:T(8,128)(2,1)S(1)}, bf16[512,512]{1,0:T(8,128)(2,1)S(1)}, u32[]{:S(2)}, u32[]{:S(2)}) collective-permute-start(bf16[512,512]{1,0:T(8,128)(2,1)S(1)} %copy-done.4), channel_id=1, source_target_pairs={{0,2},{1,3},{2,0},{3,1},{4,6},{5,7},{6,4},{7,5},{8,10},{9,11},{10,... | collective-permute-start | bytes 1572872 | tf_op jit(solution)/shard_map/ppermute | solution.py:606
  35.8 11.3 %collective-permute-start.14 = (bf16[512,512]{1,0:T(8,128)(2,1)S(1)}, bf16[512,512]{1,0:T(8,128)(2,1)S(1)}, u32[]{:S(2)}, u32[]{:S(2)}) collective-permute-start(bf16[512,512]{1,0:T(8,128)(2,1)S(1)} %copy-done.4), channel_id=1, source_target_pairs={{0,1},{1,0},{2,3},{3,2},{4,5},{5,4},{6,7},{7,6},{8,9},{9,8},{10,11... | collective-permute-start | bytes 1572872 | tf_op jit(solution)/shard_map/ppermute | solution.py:606
  53.7 16.5 %collective-permute-start.19 = (bf16[512,512]{1,0:T(8,128)(2,1)S(1)}, bf16[512,512]{1,0:T(8,128)(2,1)S(1)}, u32[]{:S(2)}, u32[]{:S(2)}) collective-permute-start(bf16[512,512]{1,0:T(8,128)(2,1)S(1)} %get-tuple-element.212), channel_id=1, source_target_pairs={{0,2},{1,3},{2,0},{3,1},{4,6},{5,7},{6,4},{7,5},{8,10},{9,11},{10,... | collective-permute-start | bytes 1572872 | tf_op jit(solution)/shard_map/ppermute | solution.py:606
  56.9 14.5 %collective-permute-start.20 = (bf16[256,512]{1,0:T(8,128)(2,1)S(1)}, bf16[256,512]{1,0:T(8,128)(2,1)S(1)}, u32[]{:S(2)}, u32[]{:S(2)}) collective-permute-start(bf16[256,512]{1,0:T(8,128)(2,1)S(1)} %get-tuple-element.215), channel_id=1, source_target_pairs={{0,4},{4,0},{8,12},{12,8},{16,20},{20,16},{24,28},{28,24},{1,5},{5... | collective-permute-start | bytes 786440 | tf_op jit(solution)/shard_map/ppermute | solution.py:606
  57.7 13.7 %collective-permute-start.21 = (bf16[256,512]{1,0:T(8,128)(2,1)S(1)}, bf16[256,512]{1,0:T(8,128)(2,1)S(1)}, u32[]{:S(2)}, u32[]{:S(2)}) collective-permute-start(bf16[256,512]{1,0:T(8,128)(2,1)S(1)} %get-tuple-element.216), channel_id=1, source_target_pairs={{0,8},{4,12},{8,0},{12,4},{16,24},{20,28},{24,16},{28,20},{1,9},{5... | collective-permute-start | bytes 786440 | tf_op jit(solution)/shard_map/ppermute | solution.py:606
  59.3 12.8 %collective-permute-start.22 = (bf16[256,512]{1,0:T(8,128)(2,1)S(1)}, bf16[256,512]{1,0:T(8,128)(2,1)S(1)}, u32[]{:S(2)}, u32[]{:S(2)}) collective-permute-start(bf16[256,512]{1,0:T(8,128)(2,1)S(1)} %get-tuple-element.217), channel_id=1, source_target_pairs={{0,12},{4,8},{8,4},{12,0},{16,28},{20,24},{24,20},{28,16},{1,13},{... | collective-permute-start | bytes 786440 | tf_op jit(solution)/shard_map/ppermute | solution.py:606
  70.5 7.6 %collective-permute-start.23 = (bf16[512,256]{1,0:T(8,128)(2,1)S(1)}, bf16[512,256]{1,0:T(8,128)(2,1)S(1)}, u32[]{:S(2)}, u32[]{:S(2)}) collective-permute-start(bf16[512,256]{1,0:T(8,128)(2,1)S(1)} %get-tuple-element.223), channel_id=1, source_target_pairs={{0,4},{4,0},{8,12},{12,8},{16,20},{20,16},{24,28},{28,24},{1,5},{5... | collective-permute-start | bytes 786440 | tf_op jit(solution)/shard_map/ppermute | solution.py:606
  72.2 6.2 %collective-permute-start.24 = (bf16[128,512]{1,0:T(8,128)(2,1)S(1)}, bf16[128,512]{1,0:T(8,128)(2,1)S(1)}, u32[]{:S(2)}, u32[]{:S(2)}) collective-permute-start(bf16[128,512]{1,0:T(8,128)(2,1)S(1)} %get-tuple-element.226), channel_id=1, source_target_pairs={{0,2},{1,3},{2,0},{3,1},{4,6},{5,7},{6,4},{7,5},{8,10},{9,11},{10,... | collective-permute-start | bytes 393224 | tf_op jit(solution)/shard_map/ppermute | solution.py:606
  83.8 18.6 %collective-permute-start.29 = (bf16[144,2560]{1,0:T(8,128)(2,1)S(1)}, bf16[144,2560]{1,0:T(8,128)(2,1)S(1)}, u32[]{:S(2)}, u32[]{:S(2)}) collective-permute-start(bf16[144,2560]{1,0:T(8,128)(2,1)S(1)} %get-tuple-element.251), channel_id=1, source_target_pairs={{0,2},{1,3},{2,0},{3,1},{4,6},{5,7},{6,4},{7,5},{8,10},{9,11},{10,... | collective-permute-start | bytes 2211848 | tf_op jit(solution)/shard_map/ppermute | solution.py:606
  85.1 8.6 %collective-permute-start.26 = (bf16[512,128]{1,0:T(8,128)(2,1)S(1)}, bf16[512,128]{1,0:T(8,128)(2,1)S(1)}, u32[]{:S(2)}, u32[]{:S(2)}) collective-permute-start(bf16[512,128]{1,0:T(8,128)(2,1)S(1)} %get-tuple-element.240), channel_id=1, source_target_pairs={{0,8},{4,12},{8,0},{12,4},{16,24},{20,28},{24,16},{28,20},{1,9},{5... | collective-permute-start | bytes 393224 | tf_op jit(solution)/shard_map/ppermute | solution.py:606
  86.7 8.7 %collective-permute-start.27 = (bf16[128,512]{1,0:T(8,128)(2,1)S(1)}, bf16[128,512]{1,0:T(8,128)(2,1)S(1)}, u32[]{:S(2)}, u32[]{:S(2)}) collective-permute-start(bf16[128,512]{1,0:T(8,128)(2,1)S(1)} %get-tuple-element.242.refs_0_), channel_id=1, source_target_pairs={{0,16},{4,20},{8,24},{12,28},{16,0},{20,4},{24,8},{28,12},{1,17},{... | collective-permute-start | bytes 393224 | tf_op jit(solution)/shard_map/ppermute | solution.py:606
  93.8 8.5 %collective-permute-start.28 = (bf16[512,128]{1,0:T(8,128)(2,1)S(1)}, bf16[512,128]{1,0:T(8,128)(2,1)S(1)}, u32[]{:S(2)}, u32[]{:S(2)}) collective-permute-start(bf16[512,128]{1,0:T(8,128)(2,1)S(1)} %get-tuple-element.248.refs_0_), channel_id=1, source_target_pairs={{0,16},{4,20},{8,24},{12,28},{16,0},{20,4},{24,8},{28,12},{1,17},{... | collective-permute-start | bytes 393224 | tf_op jit(solution)/shard_map/ppermute | solution.py:606
  95.5 11.0 %collective-permute-start.30 = (bf16[128,512]{1,0:T(8,128)(2,1)S(1)}, bf16[128,512]{1,0:T(8,128)(2,1)S(1)}, u32[]{:S(2)}, u32[]{:S(2)}) collective-permute-start(bf16[128,512]{1,0:T(8,128)(2,1)S(1)} %get-tuple-element.253.refs_0_), channel_id=1, source_target_pairs={{0,8},{4,12},{8,0},{12,4},{16,24},{20,28},{24,16},{28,20},{1,9},{5... | collective-permute-start | bytes 393224 | tf_op jit(solution)/shard_map/ppermute | solution.py:606
  102.9 8.6 %collective-permute-start.31 = (bf16[144,640]{1,0:T(8,128)(2,1)S(1)}, bf16[144,640]{1,0:T(8,128)(2,1)S(1)}, u32[]{:S(2)}, u32[]{:S(2)}) collective-permute-start(bf16[144,640]{1,0:T(8,128)(2,1)S(1)} %get-tuple-element.256), channel_id=1, source_target_pairs={{0,4},{4,0},{8,12},{12,8},{16,20},{20,16},{24,28},{28,24},{1,5},{5... | collective-permute-start | bytes 552968 | tf_op jit(solution)/shard_map/ppermute | solution.py:606
  104.2 7.6 %collective-permute-start.32 = (bf16[144,640]{1,0:T(8,128)(2,1)S(1)}, bf16[144,640]{1,0:T(8,128)(2,1)S(1)}, u32[]{:S(2)}, u32[]{:S(2)}) collective-permute-start(bf16[144,640]{1,0:T(8,128)(2,1)S(1)} %get-tuple-element.257), channel_id=1, source_target_pairs={{0,8},{4,12},{8,0},{12,4},{16,24},{20,28},{24,16},{28,20},{1,9},{5... | collective-permute-start | bytes 552968 | tf_op jit(solution)/shard_map/ppermute | solution.py:606
  105.8 10.0 %collective-permute-start.33 = (bf16[144,640]{1,0:T(8,128)(2,1)S(1)}, bf16[144,640]{1,0:T(8,128)(2,1)S(1)}, u32[]{:S(2)}, u32[]{:S(2)}) collective-permute-start(bf16[144,640]{1,0:T(8,128)(2,1)S(1)} %get-tuple-element.258), channel_id=1, source_target_pairs={{0,12},{4,8},{8,4},{12,0},{16,28},{20,24},{24,20},{28,16},{1,13},{... | collective-permute-start | bytes 552968 | tf_op jit(solution)/shard_map/ppermute | solution.py:606
  106.7 13.7 %collective-permute-start.35 = (bf16[128,1024]{1,0:T(8,128)(2,1)S(1)}, bf16[128,1024]{1,0:T(8,128)(2,1)S(1)}, u32[]{:S(2)}, u32[]{:S(2)}) collective-permute-start(bf16[128,1024]{1,0:T(8,128)(2,1)S(1)} %get-tuple-element.262.refs_0_), channel_id=1, source_target_pairs={{0,4},{4,0},{8,12},{12,8},{16,20},{20,16},{24,28},{28,24},{1,5},{5... | collective-permute-start | bytes 786440 | tf_op jit(solution)/shard_map/ppermute | solution.py:606
  108.0 10.3 %collective-permute-start.34 = (bf16[512,128]{1,0:T(8,128)(2,1)S(1)}, bf16[512,128]{1,0:T(8,128)(2,1)S(1)}, u32[]{:S(2)}, u32[]{:S(2)}) collective-permute-start(bf16[512,128]{1,0:T(8,128)(2,1)S(1)} %get-tuple-element.260.refs_0_), channel_id=1, source_target_pairs={{0,8},{4,12},{8,0},{12,4},{16,24},{20,28},{24,16},{28,20},{1,9},{5... | collective-permute-start | bytes 393224 | tf_op jit(solution)/shard_map/ppermute | solution.py:606
  115.9 8.6 %collective-permute-start.36 = (bf16[144,640]{1,0:T(8,128)(2,1)S(1)}, bf16[144,640]{1,0:T(8,128)(2,1)S(1)}, u32[]{:S(2)}, u32[]{:S(2)}) collective-permute-start(bf16[144,640]{1,0:T(8,128)(2,1)S(1)} %get-tuple-element.264.refs_0_), channel_id=1, source_target_pairs={{0,16},{4,20},{8,24},{12,28},{16,0},{20,4},{24,8},{28,12},{1,17},{... | collective-permute-start | bytes 552968 | tf_op jit(solution)/shard_map/ppermute | solution.py:606
  118.6 9.6 %collective-permute-start.37 = (bf16[512,256]{1,0:T(8,128)(2,1)S(1)}, bf16[512,256]{1,0:T(8,128)(2,1)S(1)}, u32[]{:S(2)}, u32[]{:S(2)}) collective-permute-start(bf16[512,256]{1,0:T(8,128)(2,1)S(1)} %get-tuple-element.266.refs_0_), channel_id=1, source_target_pairs={{0,4},{4,0},{8,12},{12,8},{16,20},{20,16},{24,28},{28,24},{1,5},{5... | collective-permute-start | bytes 786440 | tf_op jit(solution)/shard_map/ppermute | solution.py:606
  124.6 6.5 %collective-permute-start.40 = (bf16[144,640]{1,0:T(8,128)(2,1)S(1)}, bf16[144,640]{1,0:T(8,128)(2,1)S(1)}, u32[]{:S(2)}, u32[]{:S(2)}) collective-permute-start(bf16[144,640]{1,0:T(8,128)(2,1)S(1)} %get-tuple-element.270.refs_0_), channel_id=1, source_target_pairs={{0,12},{4,8},{8,4},{12,0},{16,28},{20,24},{24,20},{28,16},{1,13},{... | collective-permute-start | bytes 552968 | tf_op jit(solution)/shard_map/ppermute | solution.py:606
  125.7 7.0 %collective-permute-start.39 = (bf16[144,640]{1,0:T(8,128)(2,1)S(1)}, bf16[144,640]{1,0:T(8,128)(2,1)S(1)}, u32[]{:S(2)}, u32[]{:S(2)}) collective-permute-start(bf16[144,640]{1,0:T(8,128)(2,1)S(1)} %get-tuple-element.270.refs_0_), channel_id=1, source_target_pairs={{0,8},{4,12},{8,0},{12,4},{16,24},{20,28},{24,16},{28,20},{1,9},{5... | collective-permute-start | bytes 552968 | tf_op jit(solution)/shard_map/ppermute | solution.py:606
  127.2 5.9 %collective-permute-start.38 = (bf16[144,640]{1,0:T(8,128)(2,1)S(1)}, bf16[144,640]{1,0:T(8,128)(2,1)S(1)}, u32[]{:S(2)}, u32[]{:S(2)}) collective-permute-start(bf16[144,640]{1,0:T(8,128)(2,1)S(1)} %get-tuple-element.270.refs_0_), channel_id=1, source_target_pairs={{0,4},{4,0},{8,12},{12,8},{16,20},{20,16},{24,28},{28,24},{1,5},{5... | collective-permute-start | bytes 552968 | tf_op jit(solution)/shard_map/ppermute | solution.py:606
  (15 other events, 96.2 us)
